TPU v7x, 32 devices: a whole 2x2x4 slice. The times are simulated.
32 devices in a mesh: groups: 2 (over y), col: 8 (over z, x), rep: 2 (over core).
Axes of the slice: x: 2, y: 2, z: 4, core: 2. Of those that a mesh axis runs over, the one named last changes fastest.
Arguments:
- features: bfloat16 [768, 131072], P('col', ('groups', 'rep')), parts along dimension 1, may hold values from -6 to 6
- self_ids: int32 [11264], P(('groups', 'rep')), parts along dimension 0, may hold values from 0 to 65535
- neighbour_ids: int32 [15, 11264], P(None, ('groups', 'rep')), parts along dimension 1, may hold values from 0 to 65535
- count_one: int32 [11264], P(('groups', 'rep')), parts along dimension 0, may hold values from 1 to 15
- count_two: int32 [1024], P(('groups', 'col', 'rep')), parts along dimension 0, may hold values from 1 to 10
- self_one: bfloat16 [768, 256], P('col'), may hold values from -0.21875 to 0.21875
- neigh_one: bfloat16 [768, 256], P('col'), may hold values from -0.21875 to 0.21875
- bias_one: float32 [256], replicated, may hold values from -3 to 3
- self_two: bfloat16 [256, 256], replicated, may hold values from -0.375 to 0.375
- neigh_two: bfloat16 [256, 256], replicated, may hold values from -0.375 to 0.375
- bias_two: float32 [256], replicated, may hold values from -3 to 3
- out_weight: bfloat16 [256, 153], replicated, may hold values from -0.375 to 0.375
- out_bias: float32 [153], replicated, may hold values from -3 to 3
Outputs:
- logits: float32 [1024, 153], P(('groups', 'col', 'rep')), parts along dimension 0
There are 2 independent parts, one for each index of `groups`. A program takes and returns all parts, laid end to end along the dimension named above; an argument that names none is the same for every part. Nothing has to cross between parts.
All inputs are finite; a program needn't handle non-finite values.
Results may differ from a plain program's by a relative error of at most 0.0039.
Values may be sent and summed in bfloat16 or wider, within the bound.
No kernel may reach another device: no remote copies, remote signals or barrier semaphores. Data moves between devices by JAX's collectives and lax.ppermute only.
A program may use at most 256 MiB of HBM per device.

v0:
```python
import jax
import jax.numpy as jnp
from jax import lax
from jax.sharding import PartitionSpec as P


def local(
    features,
    self_ids,
    neighbour_ids,
    count_one,
    count_two,
    self_one,
    neigh_one,
    bias_one,
    self_two,
    neigh_two,
    bias_two,
    out_weight,
    out_bias,
):
    table_cols = lax.all_gather(features, "rep", axis=1, tiled=True)
    table_rows = table_cols.T
    blocks = lax.axis_size("col")
    total_rows = self_ids.shape[0]
    per_owner = total_rows // blocks
    fanout = neighbour_ids.shape[0]
    width = table_rows.shape[1]
    all_ids = jnp.concatenate([self_ids[None, :], neighbour_ids], axis=0)
    fetched = jnp.take(table_rows, all_ids, axis=0)
    self_x = fetched[0]
    mask = (jnp.arange(fanout)[:, None] < count_one[None, :]).astype(jnp.bfloat16)
    summed = jnp.einsum("kmc,km->mc", fetched[1:], mask, preferred_element_type=jnp.float32)
    mean_one = (summed / count_one[:, None].astype(jnp.float32)).astype(jnp.bfloat16)
    full_self, full_neigh = (
        lax.all_gather(self_one, "col", axis=0, tiled=True),
        lax.all_gather(neigh_one, "col", axis=0, tiled=True),
    )
    stacked = jnp.stack([self_x, mean_one], axis=0).reshape(2, blocks, per_owner, width)
    pieces = lax.all_to_all(stacked, "col", split_axis=1, concat_axis=3, tiled=True)
    pre_one = jnp.dot(pieces[0, 0], full_self, preferred_element_type=jnp.float32) + jnp.dot(
        pieces[1, 0], full_neigh, preferred_element_type=jnp.float32
    )
    hidden_one = jax.nn.relu(pre_one + bias_one).astype(jnp.bfloat16)
    seeds = count_two.shape[0]
    hidden = hidden_one.shape[1]
    grouped = hidden_one.reshape(seeds, per_owner // seeds, hidden)
    mask_two = (jnp.arange(grouped.shape[1] - 1)[None, :] < count_two[:, None]).astype(jnp.bfloat16)
    summed_two = jnp.einsum(
        "skh,sk->sh", grouped[:, 1:, :], mask_two, preferred_element_type=jnp.float32
    )
    mean_two = (summed_two / count_two[:, None].astype(jnp.float32)).astype(jnp.bfloat16)
    pre_two = jnp.dot(grouped[:, 0, :], self_two, preferred_element_type=jnp.float32) + jnp.dot(
        mean_two, neigh_two, preferred_element_type=jnp.float32
    )
    hidden_two = jax.nn.relu(pre_two + bias_two).astype(jnp.bfloat16)
    return jnp.dot(hidden_two, out_weight, preferred_element_type=jnp.float32) + out_bias


def solution(mesh):
    placed = (
        P("col", ("groups", "rep")),
        P(("groups", "rep")),
        P(None, ("groups", "rep")),
        P(("groups", "rep")),
        P(("groups", "col", "rep")),
        P("col", None),
        P("col", None),
        P(),
        P(),
        P(),
        P(),
        P(),
        P(),
    )
    return jax.shard_map(
        local,
        mesh=mesh,
        in_specs=placed,
        out_specs=P(("groups", "col", "rep"), None),
        check_vma=False,
    )
```

profile of v0, /device:TPU:0, one launch (start us, length us, event | category | flops | bytes accessed | tf_op | source)
XLA Modules:
  0.0 334.7 jit_solution(17689635609885637757)
XLA Ops:
  6.5 0.0 copy-start
  6.5 0.0 copy-start.7
  6.5 0.0 copy-start.1
  6.5 0.0 copy-start.6
  6.5 0.0 all-gather.2.cloned.1.call-start
  6.6 10.1 %copy.20 = bf16[96,32768]{0,1:T(8,128)(2,1)} copy(bf16[96,32768]{1,0:T(8,128)(2,1)} %param.13) | data formatting | bytes 12582912 | tf_op args[0]
  16.7 0.0 all-gather.2.cloned.1.call-update
  16.7 0.0 copy-done.7
  16.8 0.0 copy-done.1
  16.9 0.0 copy-done.6
  16.9 0.1 compare_and_fusion
  17.0 32.6 %all-gather.2.cloned.1.call-done = bf16[96,65536]{0,1:T(8,128)(2,1)} async-done(((bf16[96,32768]{0,1:T(8,128)(2,1)}), bf16[96,65536]{0,1:T(8,128)(2,1)}) %all-gather.2.cloned.1.call-update) | async-done | bytes 12582928 | tf_op jit(solution)/shard_map/all_gather | solution.py:22
  49.7 158.0 %gather_fusion = bf16[45056,96]{1,0:T(8,128)(2,1)} fusion(bf16[65536,96]{1,0:T(8,128)(2,1)} %bitcast.40, s32[45056]{0:T(1024)S(1)} %broadcast_clamp_fusion), kind=kCustom, calls=%fused_computation | custom fusion | bytes 17481728 | tf_op jit(solution)/shard_map/jit(_take)/gather | solution.py:30
  207.6 14.4 %copy.21 = bf16[16,2816,96]{1,2,0:T(8,128)(2,1)} copy(bf16[16,2816,96]{2,1,0:T(8,128)(2,1)} %bitcast.41) | data formatting | bytes 17301504 | tf_op jit(solution)/shard_map/jit(_take)/gather | solution.py:30
  222.0 7.7 %broadcast_select_fusion = bf16[16,2816,96]{1,2,0:T(8,128)(2,1)} fusion(bf16[16,2816,96]{1,2,0:T(8,128)(2,1)} %copy.21, pred[16,2816]{1,0:T(8,128)(4,1)S(1)} %compare_and_fusion), kind=kLoop, calls=%fused_computation.2 | loop fusion | flops 4325376 | bytes 17346560 | tf_op jit(solution)/shard_map/jit(_take)/select_n | solution.py:30
  229.7 0.0 slice-start
  229.8 0.0 copy-start.10
  229.8 0.0 copy-start.4
  229.8 0.0 copy-start.5
  229.8 5.1 %multiply_reduce_fusion = f32[2816,96]{0,1:T(8,128)S(1)} fusion(bf16[16,2816,96]{1,2,0:T(8,128)(2,1)} %broadcast_select_fusion, f32[2816,15]{0,1:T(8,128)S(1)} %fusion.9), kind=kLoop, calls=%fused_computation.1 | loop fusion | flops 11894784 | bytes 9360384 | tf_op jit(solution)/shard_map/kmc,km->mc/dot_general | solution.py:33
  234.8 0.0 copy-start.11
  234.9 0.1 divide_convert_fusion
  234.9 0.0 copy-start.2
  234.9 0.0 copy-start.3
  235.0 0.0 copy-start.8
  235.0 0.0 copy-start.9
  235.0 1.0 stack.9
  236.0 0.0 slice-done
  236.0 1.0 stack.8
  237.0 0.2 pad_maximum_fusion
  237.2 1.2 copy.22
  238.5 5.8 %all-to-all-start = ((bf16[2,8,352,96]{2,3,0,1:T(8,128)(2,1)}), bf16[2,8,352,96]{2,3,0,1:T(8,128)(2,1)S(1)}, u32[]{:S(2)}, u32[]{:S(2)}) async-start(bf16[2,8,352,96]{2,3,0,1:T(8,128)(2,1)} %copy.22), calls=%async_computation | async-start | bytes 2359296 | tf_op jit(solution)/shard_map/all_to_all | solution.py:40
  244.2 0.0 copy-done.10
  244.2 0.0 copy-done.4
  244.3 50.0 %all_gather.10 = bf16[768,256]{1,0:T(8,128)(2,1)S(1)} all-gather(bf16[96,256]{1,0:T(8,128)(2,1)S(1)} %copy-done.4), channel_id=1, replica_groups=mesh['groups'=2,'col'=8,'rep'=2] {'col'}, dimensions={0}, use_global_device_ids=true | all-gather | bytes 442368 | tf_op jit(solution)/shard_map/all_gather | solution.py:36
  294.2 0.0 copy-done.5
  294.2 31.2 %all_gather.11 = bf16[768,256]{1,0:T(8,128)(2,1)S(1)} all-gather(bf16[96,256]{1,0:T(8,128)(2,1)S(1)} %copy-done.5), channel_id=1, replica_groups=mesh['groups'=2,'col'=8,'rep'=2] {'col'}, dimensions={0}, use_global_device_ids=true | all-gather | bytes 442368 | tf_op jit(solution)/shard_map/all_gather | solution.py:37
  325.5 0.1 fusion.21
  325.6 0.0 all-to-all-done
  325.6 0.1 fusion.23
  325.7 0.4 fusion.24
  326.0 0.0 copy-done.11
  326.1 0.4 fusion.2
  326.4 0.1 reshape.115
  326.5 0.2 fusion.6
  326.7 0.0 copy-done
  326.7 0.1 fusion.14
  326.9 0.0 copy-done.2
  326.9 0.0 copy-done.3
  326.9 0.0 copy-done.8
  326.9 0.0 copy-done.9
  326.9 0.9 convolution_add_fusion.1
  (9 shorter events, 0.1 us)
Async XLA Ops:
  6.5 320.2 %copy-start = (bf16[256,256]{1,0:T(8,128)(2,1)S(1)}, bf16[256,256]{1,0:T(8,128)(2,1)}, u32[]{:S(2)}) copy-start(bf16[256,256]{1,0:T(8,128)(2,1)} %param.21) | copy-start | bytes 393220
  6.5 10.2 %copy-start.7 = (s32[2816]{0:T(1024)S(1)}, s32[2816]{0:T(1024)}, u32[]{:S(2)}) copy-start(s32[2816]{0:T(1024)} %param.14) | copy-start | bytes 33796
  6.5 10.2 %copy-start.1 = (s32[15,2816]{1,0:T(8,128)S(1)}, s32[15,2816]{1,0:T(8,128)}, u32[]{:S(2)}) copy-start(s32[15,2816]{1,0:T(8,128)} %param.15) | copy-start | bytes 506884
  6.5 10.3 %copy-start.6 = (s32[2816]{0:T(1024)S(1)}, s32[2816]{0:T(1024)}, u32[]{:S(2)}) copy-start(s32[2816]{0:T(1024)} %param.16) | copy-start | bytes 33796
  6.5 43.1 %all-gather.2.cloned.1.call-start = ((), (), s32[]{:S(2)}) async-start(), calls=%async_computation.1 | async-start | bytes 25165824 | tf_op jit(solution)/shard_map/all_gather | solution.py:22
  229.7 6.2 %slice-start = ((bf16[16,2816,96]{1,2,0:T(8,128)(2,1)}), bf16[1,2816,96]{1,2,0:T(8,128)(2,1)S(1)}, s32[]{:S(2)}) async-start(bf16[16,2816,96]{1,2,0:T(8,128)(2,1)} %broadcast_select_fusion), calls=%async_computation.2 | async-start | bytes 1081344 | tf_op jit(solution)/shard_map/slice | solution.py:31
  229.8 14.5 %copy-start.10 = (s32[32]{0:T(128)S(1)}, s32[32]{0:T(128)}, u32[]{:S(2)}) copy-start(s32[32]{0:T(128)} %param.17) | copy-start | bytes 388
  229.8 14.5 %copy-start.4 = (bf16[96,256]{1,0:T(8,128)(2,1)S(1)}, bf16[96,256]{1,0:T(8,128)(2,1)}, u32[]{:S(2)}) copy-start(bf16[96,256]{1,0:T(8,128)(2,1)} %param.18) | copy-start | bytes 147460
  229.8 64.5 %copy-start.5 = (bf16[96,256]{1,0:T(8,128)(2,1)S(1)}, bf16[96,256]{1,0:T(8,128)(2,1)}, u32[]{:S(2)}) copy-start(bf16[96,256]{1,0:T(8,128)(2,1)} %param.19) | copy-start | bytes 147460
  234.8 91.2 %copy-start.11 = (f32[256]{0:T(256)S(1)}, f32[256]{0:T(256)}, u32[]{:S(2)}) copy-start(f32[256]{0:T(256)} %param.20) | copy-start | bytes 3076
  234.9 91.9 %copy-start.2 = (bf16[256,256]{1,0:T(8,128)(2,1)S(1)}, bf16[256,256]{1,0:T(8,128)(2,1)}, u32[]{:S(2)}) copy-start(bf16[256,256]{1,0:T(8,128)(2,1)} %param.22) | copy-start | bytes 393220
  234.9 91.9 %copy-start.3 = (bf16[256,153]{0,1:T(8,128)(2,1)S(1)}, bf16[256,153]{0,1:T(8,128)(2,1)}, u32[]{:S(2)}) copy-start(bf16[256,153]{0,1:T(8,128)(2,1)} %param.24) | copy-start | bytes 235012
  235.0 91.9 %copy-start.8 = (f32[153]{0:T(256)S(1)}, f32[153]{0:T(256)}, u32[]{:S(2)}) copy-start(f32[153]{0:T(256)} %param.25) | copy-start | bytes 1840
  235.0 91.9 %copy-start.9 = (f32[256]{0:T(256)S(1)}, f32[256]{0:T(256)}, u32[]{:S(2)}) copy-start(f32[256]{0:T(256)} %param.23) | copy-start | bytes 3076
  238.5 87.1 %all-to-all-start = ((bf16[2,8,352,96]{2,3,0,1:T(8,128)(2,1)}), bf16[2,8,352,96]{2,3,0,1:T(8,128)(2,1)S(1)}, u32[]{:S(2)}, u32[]{:S(2)}) async-start(bf16[2,8,352,96]{2,3,0,1:T(8,128)(2,1)} %copy.22), calls=%async_computation | async-start | bytes 2359296 | tf_op jit(solution)/shard_map/all_to_all | solution.py:40
Sparse Core Ops, SparseCore 0:
  16.9 32.7 all-gather.1
where the time goes:
time: 335 us
  local copies, waits for them, and re-layouts  186 us (56%)
  blocking collectives  81.2 us (24%)
  waiting for transfers between devices  32.7 us (10%)
  between operations  13.7 us (4%)
  other arithmetic  13.3 us (4%)
  starting transfers between devices  5.8 us (2%)
    gather x2, local copies, waits for them, and re-layouts, local(): fetched = jnp.take(table_rows, all_ids, axis=0)  172 us
    all_gather x1, blocking collectives, local(): lax.all_gather(self_one, 'col', axis=0, tiled=True)  50 us
    all_gather x1, waiting for transfers between devices, local(): table_cols = lax.all_gather(features, 'rep', axis=1, tiled=True)  32.6 us
    all_gather x1, blocking collectives, local(): lax.all_gather(neigh_one, 'col', axis=0, tiled=True)  31.2 us
    unnamed x25, local copies, waits for them, and re-layouts  10.2 us
    select_n x2, other arithmetic, local(): fetched = jnp.take(table_rows, all_ids, axis=0)  7.74 us
  transfers between devices with their start and end apart: 2, of which 1 were waited for; matrix products, arithmetic and copies ran while one was open for 0% of the time, Pallas kernels for 0%

commit v1 on v0

v1 whole, which is shorter than its diff:
```python
import functools

import jax
import jax.numpy as jnp
import numpy as np
from jax import lax
from jax.experimental import pallas as pl
from jax.experimental.pallas import tpu as pltpu
from jax.sharding import PartitionSpec as P

CAP = 256
UNROLL = 4
LANES = 128
MIB = 2**20
BF16 = jnp.bfloat16
F32 = jnp.float32
I32 = jnp.int32


def general(
    features,
    self_ids,
    neighbour_ids,
    count_one,
    count_two,
    self_one,
    neigh_one,
    bias_one,
    self_two,
    neigh_two,
    bias_two,
    out_weight,
    out_bias,
):
    table_cols = lax.all_gather(features, "rep", axis=1, tiled=True)
    table_rows = table_cols.T
    blocks = lax.axis_size("col")
    total_rows = self_ids.shape[0]
    per_owner = total_rows // blocks
    fanout = neighbour_ids.shape[0]
    width = table_rows.shape[1]
    all_ids = jnp.concatenate([self_ids[None, :], neighbour_ids], axis=0)
    fetched = jnp.take(table_rows, all_ids, axis=0)
    self_x = fetched[0]
    mask = (jnp.arange(fanout)[:, None] < count_one[None, :]).astype(BF16)
    summed = jnp.einsum("kmc,km->mc", fetched[1:], mask, preferred_element_type=F32)
    mean_one = (summed / count_one[:, None].astype(F32)).astype(BF16)
    full_self, full_neigh = (
        lax.all_gather(self_one, "col", axis=0, tiled=True),
        lax.all_gather(neigh_one, "col", axis=0, tiled=True),
    )
    stacked = jnp.stack([self_x, mean_one], axis=0).reshape(2, blocks, per_owner, width)
    pieces = lax.all_to_all(stacked, "col", split_axis=1, concat_axis=3, tiled=True)
    pre_one = jnp.dot(pieces[0, 0], full_self, preferred_element_type=F32) + jnp.dot(
        pieces[1, 0], full_neigh, preferred_element_type=F32
    )
    hidden_one = jax.nn.relu(pre_one + bias_one).astype(BF16)
    seeds = count_two.shape[0]
    hidden = hidden_one.shape[1]
    grouped = hidden_one.reshape(seeds, per_owner // seeds, hidden)
    mask_two = (jnp.arange(grouped.shape[1] - 1)[None, :] < count_two[:, None]).astype(BF16)
    summed_two = jnp.einsum("skh,sk->sh", grouped[:, 1:, :], mask_two, preferred_element_type=F32)
    mean_two = (summed_two / count_two[:, None].astype(F32)).astype(BF16)
    pre_two = jnp.dot(grouped[:, 0, :], self_two, preferred_element_type=F32) + jnp.dot(
        mean_two, neigh_two, preferred_element_type=F32
    )
    hidden_two = jax.nn.relu(pre_two + bias_two).astype(BF16)
    return jnp.dot(hidden_two, out_weight, preferred_element_type=F32) + out_bias


def iota(shape, dim):
    return lax.broadcasted_iota(I32, shape, dim)


def tree_sum(terms):
    while len(terms) > 1:
        odd = [terms[-1]] if len(terms) % 2 else []
        terms = [a + b for a, b in zip(terms[::2], terms[1::2])] + odd
    return terms[0]


VMEM = pl.BlockSpec(memory_space=pltpu.VMEM)
SMEM = pl.BlockSpec(memory_space=pltpu.SMEM)
HBM = pl.BlockSpec(memory_space=pltpu.HBM)
ANY = pl.BlockSpec(memory_space=pl.ANY)


def start_all(copies):
    for copy in copies:
        copy.start()


def turn(copies, staged, table, base, done=None):
    blocks, width, length = staged.shape
    step = 512
    unroll = 2
    for block in range(blocks):
        copies[block].wait()

        def body(i, carry, block=block):
            for u in range(unroll):
                off = pl.multiple_of((i * unroll + u) * step, step)
                rows = staged[block, :, pl.ds(off, step)].T.astype(F32)
                at = pl.multiple_of(base + block * length + off, step)
                table[pl.ds(at, step), 0:width] = rows
            return carry

        lax.fori_loop(0, length // step // unroll, body, 0)
        if done is not None:
            done[block].start()


def feature_copies(features, staged, sems):
    blocks, _, length = staged.shape
    return [
        pltpu.make_async_copy(features.at[:, pl.ds(b * length, length)], staged.at[b], sems.at[b])
        for b in range(blocks)
    ]


def own_rows_kernel(me, features, rows, table, staged, sems, out_sems):
    copies = feature_copies(features, staged, sems)
    start_all(copies)
    blocks, _, length = staged.shape
    done = []
    for b in range(blocks):
        to = pl.multiple_of((me[2] * blocks + b) * length, length)
        done.append(
            pltpu.make_async_copy(
                table.at[pl.ds(b * length, length), :], rows.at[pl.ds(to, length), :], out_sems.at[b]
            )
        )
    turn(copies, staged, table, 0, done)
    for copy in done:
        copy.wait()


def order_kernel(fanout, per_seed, counts_rel, me, count_one, lists):
    owners, seeds = counts_rel.shape
    per_owner = count_one.shape[1]
    half = owners // 2
    mine = me[0]
    counts = jnp.concatenate(
        [counts_rel[pl.ds(jnp.bitwise_xor(mine, c), 1), :] for c in range(owners)], axis=0
    ).astype(F32)
    needs = (counts + 1.0).astype(BF16)
    before = (iota((seeds, seeds), 0) < iota((seeds, seeds), 1)).astype(BF16)
    offset = jnp.dot(needs, before, preferred_element_type=F32)
    off_hi = jnp.floor(offset * (1.0 / 16.0))
    off_lo = offset - off_hi * 16.0
    shift = iota((seeds, per_owner), 1) - iota((seeds, per_owner), 0) * per_seed
    spread = ((shift >= 0) & (shift < per_seed)).astype(BF16)
    place = jnp.dot(iota((8, seeds), 1).astype(BF16), spread, preferred_element_type=F32)
    t = iota((owners, per_owner), 1).astype(F32) - place[0:1, :] * per_seed
    of_row = jnp.dot(counts.astype(BF16), spread, preferred_element_type=F32)
    row_hi = jnp.dot(off_hi.astype(BF16), spread, preferred_element_type=F32)
    row_lo = jnp.dot(off_lo.astype(BF16), spread, preferred_element_type=F32)
    slot = row_hi * 16.0 + row_lo + t
    used = (t <= of_row) & (slot < CAP)
    key = jnp.where(used, count_one[...], 0)
    slot = slot.astype(I32)
    kinds = [
        (iota((16, per_owner), 0) == jnp.broadcast_to(key[c : c + 1, :], (16, per_owner)))
        for c in range(owners)
    ]
    stacked = jnp.concatenate([k.astype(F32).astype(BF16) for k in kinds], axis=0)
    left = (iota((per_owner, per_owner), 0) < iota((per_owner, per_owner), 1)).astype(BF16)
    prefix = jnp.dot(stacked, left, preferred_element_type=F32)
    total = jnp.dot(stacked, jnp.ones((per_owner, LANES), BF16), preferred_element_type=F32)
    for h in range(2):
        carry = jnp.zeros((16, LANES), F32)
        carries = []
        for c in range(h * half, (h + 1) * half):
            carries.append(carry)
            carry = carry + total[c * 16 : (c + 1) * 16, :]
        sizes = jnp.floor((carry + (UNROLL - 1)) * (1.0 / UNROLL)) * UNROLL
        bases = [jnp.zeros((1, LANES), F32)]
        for v in range(1, 16):
            bases.append(bases[-1] + sizes[v : v + 1, :])
        first = jnp.concatenate([bases[0]] + bases[:15], axis=0)
        gathered = jnp.zeros((64, LANES), F32)
        for i, c in enumerate(range(h * half, (h + 1) * half)):
            begin = (first + carries[i])[:, 0:1]
            spot = jnp.where(kinds[c], prefix[c * 16 : (c + 1) * 16, :] + begin, 0.0)
            spot = jnp.sum(spot, axis=0, keepdims=True).astype(I32)
            spot = jnp.where(key[c : c + 1, :] > 0, spot, -1)
            spot_lo = jnp.bitwise_and(spot, LANES - 1)
            spot_hi = jnp.right_shift(spot, 7)
            lane = (iota((LANES, per_owner), 0) == spot_lo).astype(F32).astype(BF16)
            row = iota((1, per_owner), 1) + c * per_owner
            back = half * CAP - (slot[c : c + 1, :] + i * CAP)
            at_hi = iota((16, per_owner), 0) == spot_hi
            values = jnp.concatenate(
                [
                    jnp.where(at_hi, jnp.broadcast_to(x, (16, per_owner)).astype(F32), 0.0)
                    for x in (
                        jnp.right_shift(row, 8),
                        jnp.bitwise_and(row, 255),
                        jnp.right_shift(back, 8),
                        jnp.bitwise_and(back, 255),
                    )
                ],
                axis=0,
            ).astype(BF16)
            gathered = gathered + lax.dot_general(
                values, lane, (((1,), (1,)), ((), ())), preferred_element_type=F32
            )
        lists[h, 0:16, :] = (gathered[0:16, :] * 256.0 + gathered[16:32, :]).astype(I32)
        lists[h, 16:32, :] = half * CAP - (
            gathered[32:48, :] * 256.0 + gathered[48:64, :]
        ).astype(I32)
        lists[h, 32:48, :] = jnp.concatenate(bases, axis=0).astype(I32)


def look_up(fanout, table, ids, lists, self_rows, mean_rows):
    def entry(kind, at):
        return lists[kind + jnp.right_shift(at, 7), jnp.bitwise_and(at, LANES - 1)]

    for v in range(1, fanout + 1):
        begin = lists[32 + v - 1, 0]
        end = lists[32 + v, 0]

        def body(i, carry, v=v, begin=begin):
            for u in range(UNROLL):
                at = begin + i * UNROLL + u
                row = entry(0, at)
                to = entry(16, at)
                self_rows[pl.ds(to, 1), :] = table[pl.ds(ids[0][row], 1), :]
                total = tree_sum([table[pl.ds(ids[k][row], 1), :] for k in range(1, v + 1)])
                mean_rows[pl.ds(to, 1), :] = total * (1.0 / v)
            return carry

        lax.fori_loop(0, jnp.right_shift(end - begin, UNROLL.bit_length() - 1), body, 0)


def write_out(x, width, self_rows, mean_rows, keep, send):
    valid = iota((CAP, LANES), 1) < width
    for z in range(2):
        for ref, side in ((keep, x), (send, 1 - x)):
            at = pl.multiple_of((z * 2 + side) * CAP, CAP)
            for part, rows in enumerate((self_rows, mean_rows)):
                block = jnp.where(valid, rows[pl.ds(at, CAP), :], 0.0).astype(BF16)
                ref[z, :, part * LANES : (part + 1) * LANES] = block


def first_kernel(
    fanout, me, lists_hbm, ids_hbm, table_in, other, table, keep, send, *scratch
):
    ids = scratch[: fanout + 1]
    lists, self_rows, mean_rows, staged, sems, small = scratch[fanout + 1 :]
    width = other.shape[0]
    length = other.shape[1]
    x, h, rep = me[0], me[1], me[2]
    copies = feature_copies(other, staged, sems)
    start_all(copies)
    rest = [pltpu.make_async_copy(lists_hbm.at[h], lists, small.at[1])]
    rest += [pltpu.make_async_copy(ids_hbm.at[k], ids[k], small.at[2 + k]) for k in range(fanout + 1)]
    start_all(rest)
    self_rows[...] = jnp.zeros_like(self_rows)
    mean_rows[...] = jnp.zeros_like(mean_rows)
    turn(copies, staged, table, pl.multiple_of((1 - rep) * length, length))
    for copy in rest:
        copy.wait()
    look_up(fanout, table, ids, lists, self_rows, mean_rows)
    write_out(x, width, self_rows, mean_rows, keep, send)


def second_kernel(fanout, width, me, lists_hbm, ids_hbm, table, keep, send, *scratch):
    ids = scratch[: fanout + 1]
    lists, self_rows, mean_rows, small = scratch[fanout + 1 :]
    x, h = me[0], 1 - me[1]
    rest = [pltpu.make_async_copy(lists_hbm.at[h], lists, small.at[1])]
    rest += [pltpu.make_async_copy(ids_hbm.at[k], ids[k], small.at[2 + k]) for k in range(fanout + 1)]
    start_all(rest)
    self_rows[...] = jnp.zeros_like(self_rows)
    mean_rows[...] = jnp.zeros_like(mean_rows)
    for copy in rest:
        copy.wait()
    look_up(fanout, table, ids, lists, self_rows, mean_rows)
    write_out(x, width, self_rows, mean_rows, keep, send)


def project_kernel(me, keep, got, weight, weight_got, out_0, out_1):
    zl = me[3]
    for which, out in ((zl, out_0), (1 - zl, out_1)):
        out[...] = (
            jnp.dot(keep[which], weight[...], preferred_element_type=F32)
            + jnp.dot(got[which], weight_got[...], preferred_element_type=F32)
        ).astype(out.dtype)


def last_kernel(
    mine, a, b, c, counts, bias_one, self_two, neigh_two, bias_two, out_weight, out_bias, out
):
    pre = mine[...] + a[...].astype(F32) + b[...].astype(F32) + c[...].astype(F32)
    hidden = jnp.maximum(pre + bias_one[...], 0.0).astype(BF16)
    seeds = counts.shape[0]
    count = counts[...]
    earlier = (iota((seeds, seeds), 0) > iota((seeds, seeds), 1)).astype(BF16)
    needs = jnp.broadcast_to((count + 1).astype(F32), (seeds, LANES)).astype(BF16)
    offset = jnp.dot(earlier, needs, preferred_element_type=F32)[:, 0:1].astype(I32)
    place = iota((seeds, CAP), 1) - offset
    is_self = (place == 0).astype(F32).astype(BF16)
    is_near = ((place >= 1) & (place <= count)).astype(F32).astype(BF16)
    own = jnp.dot(is_self, hidden, preferred_element_type=F32).astype(BF16)
    total = jnp.dot(is_near, hidden, preferred_element_type=F32)
    mean = (total / count.astype(F32)).astype(BF16)
    pre_two = (
        jnp.dot(own, self_two[...], preferred_element_type=F32)
        + jnp.dot(mean, neigh_two[...], preferred_element_type=F32)
        + bias_two[...]
    )
    hidden_two = jnp.maximum(pre_two, 0.0).astype(BF16)
    out[...] = jnp.dot(hidden_two, out_weight[...], preferred_element_type=F32) + out_bias[...]


def params(limit):
    return pltpu.CompilerParams(vmem_limit_bytes=limit * MIB)


def shape(dims, dtype):
    return jax.ShapeDtypeStruct(dims, dtype)


def own_rows_call(me, features):
    width, length = features.shape
    return pl.pallas_call(
        own_rows_kernel,
        out_shape=shape((2 * length, LANES), F32),
        in_specs=[SMEM, ANY],
        out_specs=HBM,
        scratch_shapes=[
            pltpu.VMEM((length, LANES), F32),
            pltpu.VMEM((4, width, length // 4), BF16),
            pltpu.SemaphoreType.DMA((4,)),
            pltpu.SemaphoreType.DMA((4,)),
        ],
        compiler_params=params(28),
        name="own_rows",
    )(me, features)


def order_call(fanout, per_seed, counts_rel, col, count_one):
    return pl.pallas_call(
        functools.partial(order_kernel, fanout, per_seed),
        out_shape=shape((2, 48, LANES), I32),
        in_specs=[VMEM, SMEM, VMEM],
        out_specs=VMEM,
        compiler_params=params(10),
        name="order",
    )(counts_rel, col, count_one)


def id_scratch(fanout, rows):
    return [pltpu.SMEM((rows,), I32) for _ in range(fanout + 1)] + [
        pltpu.SMEM((48, LANES), I32),
        pltpu.VMEM((4 * CAP + 8, LANES), F32),
        pltpu.VMEM((4 * CAP + 8, LANES), F32),
    ]


def first_call(me, lists, ids, own_rows, other):
    width, length = other.shape
    fanout = ids.shape[0] - 1
    halves = shape((2, CAP, 2 * LANES), BF16)
    return pl.pallas_call(
        functools.partial(first_kernel, fanout),
        out_shape=(shape((2 * length, LANES), F32), halves, halves),
        in_specs=[SMEM, ANY, ANY, VMEM, ANY],
        out_specs=(VMEM, VMEM, VMEM),
        scratch_shapes=id_scratch(fanout, ids.shape[1])
        + [
            pltpu.VMEM((4, width, length // 4), BF16),
            pltpu.SemaphoreType.DMA((4,)),
            pltpu.SemaphoreType.DMA((fanout + 3,)),
        ],
        input_output_aliases={3: 0},
        compiler_params=params(10),
        name="first_half",
    )(me, lists, ids, own_rows, other)


def second_call(width, me, lists, ids, table):
    fanout = ids.shape[0] - 1
    halves = shape((2, CAP, 2 * LANES), BF16)
    return pl.pallas_call(
        functools.partial(second_kernel, fanout, width),
        out_shape=(halves, halves),
        in_specs=[SMEM, ANY, ANY, VMEM],
        out_specs=(VMEM, VMEM),
        scratch_shapes=id_scratch(fanout, ids.shape[1])
        + [pltpu.SemaphoreType.DMA((fanout + 3,))],
        compiler_params=params(10),
        name="second_half",
    )(me, lists, ids, table)


def project_call(me, keep, got, weight, weight_got, kinds):
    hidden = weight.shape[1]
    return pl.pallas_call(
        project_kernel,
        out_shape=tuple(shape((CAP, hidden), kind) for kind in kinds),
        in_specs=[SMEM, VMEM, VMEM, VMEM, VMEM],
        out_specs=(VMEM, VMEM),
        compiler_params=params(10),
        name="project",
    )(me, keep, got, weight, weight_got)


def last_call(*args):
    seeds = args[4].shape[0]
    classes = args[-1].shape[1]
    return pl.pallas_call(
        last_kernel,
        out_shape=shape((seeds, classes), F32),
        in_specs=[VMEM] * len(args),
        out_specs=VMEM,
        compiler_params=params(10),
        name="layer_two",
    )(*args)


def main(
    features,
    self_ids,
    neighbour_ids,
    count_one,
    count_two,
    self_one,
    neigh_one,
    bias_one,
    self_two,
    neigh_two,
    bias_two,
    out_weight,
    out_bias,
):
    owners = lax.axis_size("col")
    seeds = count_two.shape[0]
    rows = self_ids.shape[0]
    per_owner = rows // owners
    per_seed = per_owner // seeds
    fanout = neighbour_ids.shape[0]
    width = features.shape[0]
    col = lax.axis_index("col")
    rep = lax.axis_index("rep")
    z = col // 2
    me = jnp.stack([col % 2, 1 - z // 2, rep, z % 2]).astype(I32)

    def across(value, bit):
        return lax.ppermute(value, "col", [(i, i ^ bit) for i in range(owners)])

    other = lax.ppermute(features, "rep", [(0, 1), (1, 0)])
    weight = jnp.concatenate(
        [jnp.pad(w, ((0, LANES - width), (0, 0))) for w in (self_one, neigh_one)], axis=0
    )
    counts = count_two[None, :]
    for bit in (1, 2, 4):
        counts = jnp.concatenate([counts, across(counts, bit)], axis=0)
    weight_got = across(weight, 1)
    own_rows = own_rows_call(me, features)
    ids = jnp.concatenate([self_ids[None, :], neighbour_ids], axis=0)
    lists = order_call(
        fanout, per_seed, counts, col.reshape(1).astype(I32), count_one.reshape(owners, per_owner)
    )
    lists, weight_got = lax.optimization_barrier((lists, weight_got))
    table, keep_far, send_far = first_call(me, lists, ids, own_rows, other)
    got_far = across(send_far, 1)
    keep_near, send_near = second_call(width, me, lists, ids, table)
    far = project_call(me, keep_far, got_far, weight, weight_got, (BF16, BF16))
    got_near = across(send_near, 1)
    got = [across(far[0], 4), across(far[1], 6)]
    near = project_call(me, keep_near, got_near, weight, weight_got, (F32, BF16))
    got.append(across(near[1], 2))
    fast = last_call(
        near[0],
        *got,
        count_two[:, None],
        bias_one[None, :],
        self_two,
        neigh_two,
        bias_two[None, :],
        out_weight,
        out_bias[None, :],
    )
    most = jnp.max(jnp.sum(counts + 1, axis=1)).reshape(1)
    most = jnp.maximum(most, lax.ppermute(most, "rep", [(0, 1), (1, 0)]))
    most = jnp.maximum(most, lax.ppermute(most, "groups", [(0, 1), (1, 0)]))
    return lax.cond(
        most[0] > CAP,
        lambda: general(
            features,
            self_ids,
            neighbour_ids,
            count_one,
            count_two,
            self_one,
            neigh_one,
            bias_one,
            self_two,
            neigh_two,
            bias_two,
            out_weight,
            out_bias,
        ),
        lambda: fast,
    )


def local(*args):
    features, self_ids, neighbour_ids = args[0], args[1], args[2]
    sizes = (lax.axis_size("groups"), lax.axis_size("col"), lax.axis_size("rep"))
    small = (
        sizes == (2, 8, 2)
        and features.shape[0] <= LANES
        and features.shape[1] <= 32768
        and self_ids.shape[0] * (neighbour_ids.shape[0] + 1) <= 2**17
        and neighbour_ids.shape[0] <= 15
    )
    return main(*args) if small else general(*args)


def solution(mesh):
    placed = (
        P("col", ("groups", "rep")),
        P(("groups", "rep")),
        P(None, ("groups", "rep")),
        P(("groups", "rep")),
        P(("groups", "col", "rep")),
        P("col", None),
        P("col", None),
        P(),
        P(),
        P(),
        P(),
        P(),
        P(),
    )
    return jax.shard_map(
        local,
        mesh=mesh,
        in_specs=placed,
        out_specs=P(("groups", "col", "rep"), None),
        check_vma=False,
    )
```

time: 335 us -> 104 us (0.31)
  local copies, waits for them, and re-layouts: 186 us -> 12.9 us
  blocking collectives: 81.2 us -> 0 us
  Pallas kernels: 0 us -> 46.1 us
  waiting for transfers between devices: 32.7 us -> 7.93 us
  starting transfers between devices: 5.8 us -> 17.3 us
  other arithmetic: 13.3 us -> 3.94 us
    gather x2 -> x0, local copies, waits for them, and re-layouts: 172 us -> none  [local(): fetched = jnp.take(table_rows, all_ids, axis=0)]
    all_gather x2 -> x0, blocking collectives: 81.2 us -> none  [the longest x1 50 us: local(): lax.all_gather(self_one, 'col', axis=0, tiled=True)]
    pallas_call x0 -> x7, Pallas kernels: none -> 46.1 us  [the longest x1 18.3 us: first_call(): pl.pallas_call(functools.partial(first_kernel, fanout), out_shape=(shape(...]
    all_gather x1 -> x0, waiting for transfers between devices: 32.6 us -> none  [local(): table_cols = lax.all_gather(features, 'rep', axis=1, tiled=True)]
    ppermute x0 -> x12, starting transfers between devices: none -> 17.3 us  [the longest x9 15.4 us: across(): return lax.ppermute(value, 'col', [(i, i ^ bit) for i in range(owners)])]
    ppermute x0 -> x12, waiting for transfers between devices: none -> 7.93 us  [the longest x9 4.21 us: across(): return lax.ppermute(value, 'col', [(i, i ^ bit) for i in range(owners)])]
    select_n x2 -> x0, other arithmetic: 7.74 us -> none  [local(): fetched = jnp.take(table_rows, all_ids, axis=0)]
    all_to_all x1 -> x0, starting transfers between devices: 5.77 us -> none  [local(): lax.all_to_all(stacked, 'col', split_axis=1, concat_axis=3, tiled=True)]
  transfers between devices with their start and end apart: 2 -> 12, of which waited for: 1 -> 4; matrix products, arithmetic and copies ran while one was open for 0% -> 5% of each run, Pallas kernels for 0% -> 26%
where the time goes in v1:
time: 104 us
  Pallas kernels  46.1 us (44%)
  starting transfers between devices  17.3 us (17%)
  between operations  15.5 us (15%)
  local copies, waits for them, and re-layouts  12.9 us (12%)
  waiting for transfers between devices  7.93 us (8%)
  other arithmetic  3.94 us (4%)
    pallas_call x1, Pallas kernels, first_call(): pl.pallas_call(functools.partial(first_kernel, fanout), out_shape=(shape(...  18.3 us
    pallas_call x1, Pallas kernels, second_call(): pl.pallas_call(functools.partial(second_kernel, fanout, width), out_shape...  15.6 us
    ppermute x9, starting transfers between devices, across(): return lax.ppermute(value, 'col', [(i, i ^ bit) for i in range(owners)])  15.4 us
    unnamed x29, local copies, waits for them, and re-layouts  11.3 us
    pallas_call x1, Pallas kernels, own_rows_call(): pl.pallas_call(own_rows_kernel, out_shape=shape((2 * length, LANES), F32)...  8.79 us
    ppermute x9, waiting for transfers between devices, across(): return lax.ppermute(value, 'col', [(i, i ^ bit) for i in range(owners)])  4.21 us
    ppermute x1, waiting for transfers between devices, main(): most = jnp.maximum(most, lax.ppermute(most, 'groups', [(0, 1), (1, 0)]))  2.34 us
  transfers between devices with their start and end apart: 12, of which 4 were waited for; matrix products, arithmetic and copies ran while one was open for 5% of the time, Pallas kernels for 26%

profile of v1, /device:TPU:0, one launch (start us, length us, event | category | flops | bytes accessed | tf_op | source)
XLA Modules:
  0.0 103.9 jit_solution(12243031441039852610)
XLA Ops:
  6.5 0.5 collective-permute-start.6
  7.0 2.5 %collective-permute-start = (s32[1,32]{1,0:T(1,128)}, s32[1,32]{1,0:T(1,128)S(1)}, u32[]{:S(2)}, u32[]{:S(2)}) collective-permute-start(s32[1,32]{1,0:T(1,128)} %bitcast.58), channel_id=1, source_target_pairs={{0,2},{2,0},{4,6},{6,4},{8,10},{10,8},{12,14},{14,12},{1,3},{3,1},... | collective-permute-start | bytes 392 | tf_op jit(solution)/shard_map/ppermute | solution.py:451
  9.5 0.8 fusion.25.weight
  10.3 0.1 collective-permute-start.5
  10.4 0.7 broadcast_in_dim.39
  11.2 0.9 pad_add_fusion.ids_hbm
  12.1 0.0 collective-permute-done
  12.1 0.7 pad_add_fusion.3
  12.8 2.1 %collective-permute-start.1 = (s32[2,32]{1,0:T(2,128)S(1)}, s32[2,32]{1,0:T(2,128)S(1)}, u32[]{:S(2)}, u32[]{:S(2)}) collective-permute-start(s32[2,32]{1,0:T(2,128)S(1)} %pad_add_fusion.3), channel_id=1, source_target_pairs={{0,4},{2,6},{4,0},{6,2},{8,12},{10,14},{12,8},{14,10},{1,5},{3,7},... | collective-permute-start | bytes 776 | tf_op jit(solution)/shard_map/ppermute | solution.py:451
  14.8 1.5 %collective-permute-done.1 = s32[2,32]{1,0:T(2,128)S(1)} collective-permute-done((s32[2,32]{1,0:T(2,128)S(1)}, s32[2,32]{1,0:T(2,128)S(1)}, u32[]{:S(2)}, u32[]{:S(2)}) %collective-permute-start.1) | collective-permute-done | bytes 288 | tf_op jit(solution)/shard_map/ppermute | solution.py:451
  16.4 0.7 pad_add_fusion.2
  17.0 3.0 %collective-permute-start.2 = (s32[4,32]{1,0:T(4,128)S(1)}, s32[4,32]{1,0:T(4,128)S(1)}, u32[]{:S(2)}, u32[]{:S(2)}) collective-permute-start(s32[4,32]{1,0:T(4,128)S(1)} %pad_add_fusion.2), channel_id=1, source_target_pairs={{0,8},{2,10},{4,12},{6,14},{8,0},{10,2},{12,4},{14,6},{1,9},{3,11}... | collective-permute-start | bytes 1544 | tf_op jit(solution)/shard_map/ppermute | solution.py:451
  20.1 0.1 pad_add_fusion.4.me
  20.2 0.8 reshape.130.count_one
  20.9 8.8 %own_rows.1.table_in = f32[65536,128]{1,0:T(8,128)} custom-call(s32[4]{0:T(128)S(1)} %pad_add_fusion.4.me, bf16[96,32768]{1,0:T(8,128)(2,1)} %features.1), custom_call_target="tpu_custom_call" | custom-call | tf_op jit(solution)/shard_map/own_rows/pallas_call | solution.py:327
  29.7 0.0 collective-permute-done.2
  29.8 0.0 copy-done.10
  29.8 0.1 pad_add_fusion.1
  29.9 1.1 %order.1.lists_hbm = s32[2,48,128]{2,1,0:T(8,128)S(1)} custom-call(s32[8,32]{1,0:T(8,128)S(1)} %get-tuple-element.125.counts_rel, s32[1]{0:T(128)} %bitcast.19.me, s32[8,352]{1,0:T(8,128)S(1)} %reshape.130.count_one), custom_call_target="tpu_custom_call" | custom-call | tf_op jit(solution)/shard_map/order/pallas_call | solution.py:344
  31.0 0.0 collective-permute-done.5.weight_got
  31.0 0.0 collective-permute-done.6.other
  31.0 0.0 copy-start
  31.0 10.5 %copy-done = f32[65536,128]{1,0:T(8,128)S(1)} copy-done((f32[65536,128]{1,0:T(8,128)S(1)}, f32[65536,128]{1,0:T(8,128)}, u32[]{:S(2)}) %copy-start) | copy-done | bytes 33554456
  41.5 18.3 %first_half.1 = (f32[65536,128]{1,0:T(8,128)S(1)}, bf16[2,256,256]{2,1,0:T(8,128)(2,1)S(1)}, bf16[2,256,256]{2,1,0:T(8,128)(2,1)S(1)}) custom-call(s32[4]{0:T(128)S(1)} %pad_add_fusion.4.me, s32[2,48,128]{2,1,0:T(8,128)S(1)} %order.1.lists_hbm, s32[16,2816]{1,0:T(8,128)S(1)} %pad_add_fusion.ids_hbm, ...), custom_call_target="tpu_custom_call", output_to_operand_aliasing={{0}: (3, {})} | custom-call | tf_op jit(solution)/shard_map/first_half/pallas_call | solution.py:366
  59.9 1.6 %collective-permute-start.8 = (bf16[2,256,256]{2,1,0:T(8,128)(2,1)S(1)}, bf16[2,256,256]{2,1,0:T(8,128)(2,1)S(1)}, u32[]{:S(2)}, u32[]{:S(2)}) collective-permute-start(bf16[2,256,256]{2,1,0:T(8,128)(2,1)S(1)} %get-tuple-element.66), channel_id=1, source_target_pairs={{0,2},{2,0},{4,6},{6,4},{8,10},{10,8},{12,14},{14,12},{1,3},{3,1},... | collective-permute-start | bytes 786440 | tf_op jit(solution)/shard_map/ppermute | solution.py:451
  61.4 0.0 copy-start.12
  61.5 0.0 copy-start.13
  61.5 0.0 copy-start.1
  61.5 0.0 copy-start.5
  61.5 0.0 copy-start.6
  61.5 0.0 copy-start.7
  61.5 0.0 copy-start.8
  61.5 15.6 %second_half.1 = (bf16[2,256,256]{2,1,0:T(8,128)(2,1)S(1)}, bf16[2,256,256]{2,1,0:T(8,128)(2,1)S(1)}) custom-call(s32[4]{0:T(128)S(1)} %pad_add_fusion.4.me, s32[2,48,128]{2,1,0:T(8,128)S(1)} %order.1.lists_hbm, s32[16,2816]{1,0:T(8,128)S(1)} %pad_add_fusion.ids_hbm, f32[65536,128]{1,0:T(8,128)S(1)} %get-tuple-element.60.table), custom_call_target="tpu_custom_call" | custom-call | tf_op jit(solution)/shard_map/second_half/pallas_call | solution.py:386
  77.1 0.6 collective-permute-start.7
  77.7 0.0 collective-permute-done.8.got
  77.7 0.8 project.3
  78.5 0.1 collective-permute-start.9
  78.6 3.9 %collective-permute-start.10 = (bf16[256,256]{1,0:T(8,128)(2,1)S(1)}, bf16[256,256]{1,0:T(8,128)(2,1)S(1)}, u32[]{:S(2)}, u32[]{:S(2)}) collective-permute-start(bf16[256,256]{1,0:T(8,128)(2,1)S(1)} %get-tuple-element.68), channel_id=1, source_target_pairs={{0,12},{2,14},{4,8},{6,10},{8,4},{10,6},{12,0},{14,2},{1,13},{3,15... | collective-permute-start | bytes 393224 | tf_op jit(solution)/shard_map/ppermute | solution.py:451
  82.5 2.6 %collective-permute-done.7.got = bf16[2,256,256]{2,1,0:T(8,128)(2,1)S(1)} collective-permute-done((bf16[2,256,256]{2,1,0:T(8,128)(2,1)S(1)}, bf16[2,256,256]{2,1,0:T(8,128)(2,1)S(1)}, u32[]{:S(2)}, u32[]{:S(2)}) %collective-permute-start.7) | collective-permute-done | bytes 262176 | tf_op jit(solution)/shard_map/ppermute | solution.py:451
  85.2 0.8 project.2
  86.0 1.6 %collective-permute-start.11 = (bf16[256,256]{1,0:T(8,128)(2,1)S(1)}, bf16[256,256]{1,0:T(8,128)(2,1)S(1)}, u32[]{:S(2)}, u32[]{:S(2)}) collective-permute-start(bf16[256,256]{1,0:T(8,128)(2,1)S(1)} %get-tuple-element.69), channel_id=1, source_target_pairs={{0,4},{2,6},{4,0},{6,2},{8,12},{10,14},{12,8},{14,10},{1,5},{3,7},... | collective-permute-start | bytes 393224 | tf_op jit(solution)/shard_map/ppermute | solution.py:451
  87.7 0.1 copy.34.counts
  87.7 0.0 copy-done.4
  87.8 0.1 copy.35.out_weight
  87.9 0.6 reduce_max.9
  88.5 0.0 collective-permute-start.3
  88.5 1.4 %collective-permute-done.3 = s32[1]{0:T(128)} collective-permute-done((s32[1]{0:T(128)}, s32[1]{0:T(128)}, u32[]{:S(2)}, u32[]{:S(2)}) %collective-permute-start.3) | collective-permute-done | bytes 36 | tf_op jit(solution)/shard_map/ppermute | solution.py:487
  91.1 1.4 %collective-permute-start.4 = (s32[1]{0:T(128)}, s32[1]{0:T(128)}, u32[]{:S(2)}, u32[]{:S(2)}) collective-permute-start(s32[1]{0:T(128)} %max.22), channel_id=1, source_target_pairs={{0,16},{16,0},{1,17},{17,1},{2,18},{18,2},{3,19},{19,3},{4,20},{20... | collective-permute-start | bytes 20 | tf_op jit(solution)/shard_map/ppermute | solution.py:488
  92.5 2.3 %collective-permute-done.4 = s32[1]{0:T(128)} collective-permute-done((s32[1]{0:T(128)}, s32[1]{0:T(128)}, u32[]{:S(2)}, u32[]{:S(2)}) %collective-permute-start.4) | collective-permute-done | bytes 36 | tf_op jit(solution)/shard_map/ppermute | solution.py:488
  95.4 0.0 collective-permute-done.9.a
  95.4 0.0 collective-permute-done.10.b
  95.4 0.0 collective-permute-done.11.c
  95.4 0.0 copy-done.2
  95.4 0.0 copy-done.3
  95.4 0.0 copy-done.11
  95.5 0.7 layer_two.1
  96.1 0.0 copy-done.1
  96.1 0.0 copy-done.5
  96.1 0.0 copy-done.6
  96.2 0.0 copy-done.7
  96.2 0.0 copy-done.8
  96.2 0.2 conditional.1
  96.4 0.0 copy-start.9
  96.4 0.6 copy-done.9
  (7 shorter events, 0.0 us)
Async XLA Ops:
  6.5 24.4 %collective-permute-start.6 = (bf16[96,32768]{1,0:T(8,128)(2,1)}, bf16[96,32768]{1,0:T(8,128)(2,1)}, u32[]{:S(2)}, u32[]{:S(2)}) collective-permute-start(bf16[96,32768]{1,0:T(8,128)(2,1)} %features.1), channel_id=1, source_target_pairs={{0,1},{1,0},{2,3},{3,2},{4,5},{5,4},{6,7},{7,6},{8,9},{9,8},{10,11... | collective-permute-start | bytes 18874376 | tf_op jit(solution)/shard_map/ppermute | solution.py:453
  7.0 5.1 %collective-permute-start = (s32[1,32]{1,0:T(1,128)}, s32[1,32]{1,0:T(1,128)S(1)}, u32[]{:S(2)}, u32[]{:S(2)}) collective-permute-start(s32[1,32]{1,0:T(1,128)} %bitcast.58), channel_id=1, source_target_pairs={{0,2},{2,0},{4,6},{6,4},{8,10},{10,8},{12,14},{14,12},{1,3},{3,1},... | collective-permute-start | bytes 392 | tf_op jit(solution)/shard_map/ppermute | solution.py:451
  10.3 20.6 %collective-permute-start.5 = (bf16[256,256]{1,0:T(8,128)(2,1)S(1)}, bf16[256,256]{1,0:T(8,128)(2,1)S(1)}, u32[]{:S(2)}, u32[]{:S(2)}) collective-permute-start(bf16[256,256]{1,0:T(8,128)(2,1)S(1)} %fusion.25.weight), channel_id=1, source_target_pairs={{0,2},{2,0},{4,6},{6,4},{8,10},{10,8},{12,14},{14,12},{1,3},{3,1},... | collective-permute-start | bytes 393224 | tf_op jit(solution)/shard_map/ppermute | solution.py:451
  12.8 3.6 %collective-permute-start.1 = (s32[2,32]{1,0:T(2,128)S(1)}, s32[2,32]{1,0:T(2,128)S(1)}, u32[]{:S(2)}, u32[]{:S(2)}) collective-permute-start(s32[2,32]{1,0:T(2,128)S(1)} %pad_add_fusion.3), channel_id=1, source_target_pairs={{0,4},{2,6},{4,0},{6,2},{8,12},{10,14},{12,8},{14,10},{1,5},{3,7},... | collective-permute-start | bytes 776 | tf_op jit(solution)/shard_map/ppermute | solution.py:451
  17.0 12.7 %collective-permute-start.2 = (s32[4,32]{1,0:T(4,128)S(1)}, s32[4,32]{1,0:T(4,128)S(1)}, u32[]{:S(2)}, u32[]{:S(2)}) collective-permute-start(s32[4,32]{1,0:T(4,128)S(1)} %pad_add_fusion.2), channel_id=1, source_target_pairs={{0,8},{2,10},{4,12},{6,14},{8,0},{10,2},{12,4},{14,6},{1,9},{3,11}... | collective-permute-start | bytes 1544 | tf_op jit(solution)/shard_map/ppermute | solution.py:451
  20.9 8.8 %copy-start.10 = (s32[32]{0:T(128)S(1)}, s32[32]{0:T(128)}, u32[]{:S(2)}) copy-start(s32[32]{0:T(128)} %param.19) | copy-start | bytes 388
  31.0 10.5 %copy-start = (f32[65536,128]{1,0:T(8,128)S(1)}, f32[65536,128]{1,0:T(8,128)}, u32[]{:S(2)}) copy-start(f32[65536,128]{1,0:T(8,128)} %own_rows.1.table_in) | copy-start | bytes 100663296
  59.9 17.8 %collective-permute-start.8 = (bf16[2,256,256]{2,1,0:T(8,128)(2,1)S(1)}, bf16[2,256,256]{2,1,0:T(8,128)(2,1)S(1)}, u32[]{:S(2)}, u32[]{:S(2)}) collective-permute-start(bf16[2,256,256]{2,1,0:T(8,128)(2,1)S(1)} %get-tuple-element.66), channel_id=1, source_target_pairs={{0,2},{2,0},{4,6},{6,4},{8,10},{10,8},{12,14},{14,12},{1,3},{3,1},... | collective-permute-start | bytes 786440 | tf_op jit(solution)/shard_map/ppermute | solution.py:451
  61.4 26.3 %copy-start.4 = (bf16[256,153]{0,1:T(8,128)(2,1)S(1)}, bf16[256,153]{0,1:T(8,128)(2,1)}, u32[]{:S(2)}) copy-start(bf16[256,153]{0,1:T(8,128)(2,1)} %param.26) | copy-start | bytes 235012
  61.4 34.0 %copy-start.2 = (bf16[256,256]{1,0:T(8,128)(2,1)S(1)}, bf16[256,256]{1,0:T(8,128)(2,1)}, u32[]{:S(2)}) copy-start(bf16[256,256]{1,0:T(8,128)(2,1)} %neigh_two.1) | copy-start | bytes 393220
  61.4 34.0 %copy-start.3 = (bf16[256,256]{1,0:T(8,128)(2,1)S(1)}, bf16[256,256]{1,0:T(8,128)(2,1)}, u32[]{:S(2)}) copy-start(bf16[256,256]{1,0:T(8,128)(2,1)} %self_two.1) | copy-start | bytes 393220
  61.4 34.0 %copy-start.11 = (f32[256]{0:T(256)S(1)}, f32[256]{0:T(256)}, u32[]{:S(2)}) copy-start(f32[256]{0:T(256)} %param.25) | copy-start | bytes 3076
  61.4 34.0 %copy-start.12 = (f32[153]{0:T(256)S(1)}, f32[153]{0:T(256)}, u32[]{:S(2)}) copy-start(f32[153]{0:T(256)} %param.27) | copy-start | bytes 1840
  61.5 34.0 %copy-start.13 = (f32[256]{0:T(256)S(1)}, f32[256]{0:T(256)}, u32[]{:S(2)}) copy-start(f32[256]{0:T(256)} %param.22) | copy-start | bytes 3076
  61.5 34.7 %copy-start.1 = (s32[15,2816]{1,0:T(8,128)S(1)}, s32[15,2816]{1,0:T(8,128)}, u32[]{:S(2)}) copy-start(s32[15,2816]{1,0:T(8,128)} %param.17) | copy-start | bytes 506884
  61.5 34.7 %copy-start.5 = (bf16[96,256]{1,0:T(8,128)(2,1)S(1)}, bf16[96,256]{1,0:T(8,128)(2,1)}, u32[]{:S(2)}) copy-start(bf16[96,256]{1,0:T(8,128)(2,1)} %param.21) | copy-start | bytes 147460
  61.5 34.7 %copy-start.6 = (bf16[96,256]{1,0:T(8,128)(2,1)S(1)}, bf16[96,256]{1,0:T(8,128)(2,1)}, u32[]{:S(2)}) copy-start(bf16[96,256]{1,0:T(8,128)(2,1)} %param.20) | copy-start | bytes 147460
  61.5 34.7 %copy-start.7 = (s32[2816]{0:T(1024)S(1)}, s32[2816]{0:T(1024)}, u32[]{:S(2)}) copy-start(s32[2816]{0:T(1024)} %param.18) | copy-start | bytes 33796
  61.5 34.7 %copy-start.8 = (s32[2816]{0:T(1024)S(1)}, s32[2816]{0:T(1024)}, u32[]{:S(2)}) copy-start(s32[2816]{0:T(1024)} %param.16) | copy-start | bytes 33796
  77.1 8.1 %collective-permute-start.7 = (bf16[2,256,256]{2,1,0:T(8,128)(2,1)S(1)}, bf16[2,256,256]{2,1,0:T(8,128)(2,1)S(1)}, u32[]{:S(2)}, u32[]{:S(2)}) collective-permute-start(bf16[2,256,256]{2,1,0:T(8,128)(2,1)S(1)} %get-tuple-element.62), channel_id=1, source_target_pairs={{0,2},{2,0},{4,6},{6,4},{8,10},{10,8},{12,14},{14,12},{1,3},{3,1},... | collective-permute-start | bytes 786440 | tf_op jit(solution)/shard_map/ppermute | solution.py:451
  78.5 16.9 %collective-permute-start.9 = (bf16[256,256]{1,0:T(8,128)(2,1)S(1)}, bf16[256,256]{1,0:T(8,128)(2,1)S(1)}, u32[]{:S(2)}, u32[]{:S(2)}) collective-permute-start(bf16[256,256]{1,0:T(8,128)(2,1)S(1)} %get-tuple-element.67), channel_id=1, source_target_pairs={{0,8},{2,10},{4,12},{6,14},{8,0},{10,2},{12,4},{14,6},{1,9},{3,11}... | collective-permute-start | bytes 393224 | tf_op jit(solution)/shard_map/ppermute | solution.py:451
  78.6 16.8 %collective-permute-start.10 = (bf16[256,256]{1,0:T(8,128)(2,1)S(1)}, bf16[256,256]{1,0:T(8,128)(2,1)S(1)}, u32[]{:S(2)}, u32[]{:S(2)}) collective-permute-start(bf16[256,256]{1,0:T(8,128)(2,1)S(1)} %get-tuple-element.68), channel_id=1, source_target_pairs={{0,12},{2,14},{4,8},{6,10},{8,4},{10,6},{12,0},{14,2},{1,13},{3,15... | collective-permute-start | bytes 393224 | tf_op jit(solution)/shard_map/ppermute | solution.py:451
  86.0 9.4 %collective-permute-start.11 = (bf16[256,256]{1,0:T(8,128)(2,1)S(1)}, bf16[256,256]{1,0:T(8,128)(2,1)S(1)}, u32[]{:S(2)}, u32[]{:S(2)}) collective-permute-start(bf16[256,256]{1,0:T(8,128)(2,1)S(1)} %get-tuple-element.69), channel_id=1, source_target_pairs={{0,4},{2,6},{4,0},{6,2},{8,12},{10,14},{12,8},{14,10},{1,5},{3,7},... | collective-permute-start | bytes 393224 | tf_op jit(solution)/shard_map/ppermute | solution.py:451
  88.5 1.4 %collective-permute-start.3 = (s32[1]{0:T(128)}, s32[1]{0:T(128)}, u32[]{:S(2)}, u32[]{:S(2)}) collective-permute-start(s32[1]{0:T(128)} %bitcast.13), channel_id=1, source_target_pairs={{0,1},{1,0},{2,3},{3,2},{4,5},{5,4},{6,7},{7,6},{8,9},{9,8},{10,11... | collective-permute-start | bytes 20 | tf_op jit(solution)/shard_map/ppermute | solution.py:487
  91.1 3.7 %collective-permute-start.4 = (s32[1]{0:T(128)}, s32[1]{0:T(128)}, u32[]{:S(2)}, u32[]{:S(2)}) collective-permute-start(s32[1]{0:T(128)} %max.22), channel_id=1, source_target_pairs={{0,16},{16,0},{1,17},{17,1},{2,18},{18,2},{3,19},{19,3},{4,20},{20... | collective-permute-start | bytes 20 | tf_op jit(solution)/shard_map/ppermute | solution.py:488
  96.4 0.6 copy-start.9

commit v2 on v1

v2 whole, which is shorter than its diff:
```python
import functools

import jax
import jax.numpy as jnp
import numpy as np
from jax import lax
from jax.experimental import pallas as pl
from jax.experimental.pallas import tpu as pltpu
from jax.sharding import PartitionSpec as P

CAP = 256
UNROLL = 8
POSITIONS = 9 * 128
FIRST_MIB = 20
LANES = 128
MIB = 2**20
BF16 = jnp.bfloat16
F32 = jnp.float32
I32 = jnp.int32


def gathered(value, axis):
    copies = jnp.broadcast_to(value[None], (lax.axis_size(axis),) + value.shape)
    pieces = lax.all_to_all(copies, axis, split_axis=0, concat_axis=0, tiled=True)
    return pieces.reshape((-1,) + value.shape[1:])


def general(
    other,
    features,
    self_ids,
    neighbour_ids,
    count_one,
    count_two,
    self_one,
    neigh_one,
    bias_one,
    self_two,
    neigh_two,
    bias_two,
    out_weight,
    out_bias,
):
    mine = jnp.where(lax.axis_index("rep") == 0, 0, 1)
    table_cols = jnp.where(
        mine == 0,
        jnp.concatenate([features, other], axis=1),
        jnp.concatenate([other, features], axis=1),
    )
    table_rows = table_cols.T
    blocks = lax.axis_size("col")
    total_rows = self_ids.shape[0]
    per_owner = total_rows // blocks
    fanout = neighbour_ids.shape[0]
    width = table_rows.shape[1]
    all_ids = jnp.concatenate([self_ids[None, :], neighbour_ids], axis=0)
    fetched = jnp.take(table_rows, all_ids, axis=0)
    self_x = fetched[0]
    mask = (jnp.arange(fanout)[:, None] < count_one[None, :]).astype(BF16)
    summed = jnp.einsum("kmc,km->mc", fetched[1:], mask, preferred_element_type=F32)
    mean_one = (summed / count_one[:, None].astype(F32)).astype(BF16)
    full_self, full_neigh = gathered(self_one, "col"), gathered(neigh_one, "col")
    stacked = jnp.stack([self_x, mean_one], axis=0).reshape(2, blocks, per_owner, width)
    pieces = lax.all_to_all(stacked, "col", split_axis=1, concat_axis=3, tiled=True)
    pre_one = jnp.dot(pieces[0, 0], full_self, preferred_element_type=F32) + jnp.dot(
        pieces[1, 0], full_neigh, preferred_element_type=F32
    )
    hidden_one = jax.nn.relu(pre_one + bias_one).astype(BF16)
    seeds = count_two.shape[0]
    hidden = hidden_one.shape[1]
    grouped = hidden_one.reshape(seeds, per_owner // seeds, hidden)
    mask_two = (jnp.arange(grouped.shape[1] - 1)[None, :] < count_two[:, None]).astype(BF16)
    summed_two = jnp.einsum("skh,sk->sh", grouped[:, 1:, :], mask_two, preferred_element_type=F32)
    mean_two = (summed_two / count_two[:, None].astype(F32)).astype(BF16)
    pre_two = jnp.dot(grouped[:, 0, :], self_two, preferred_element_type=F32) + jnp.dot(
        mean_two, neigh_two, preferred_element_type=F32
    )
    hidden_two = jax.nn.relu(pre_two + bias_two).astype(BF16)
    return jnp.dot(hidden_two, out_weight, preferred_element_type=F32) + out_bias


def iota(shape, dim):
    return lax.broadcasted_iota(I32, shape, dim)


def tree_sum(terms):
    while len(terms) > 1:
        odd = [terms[-1]] if len(terms) % 2 else []
        terms = [a + b for a, b in zip(terms[::2], terms[1::2])] + odd
    return terms[0]


VMEM = pl.BlockSpec(memory_space=pltpu.VMEM)
SMEM = pl.BlockSpec(memory_space=pltpu.SMEM)
HBM = pl.BlockSpec(memory_space=pltpu.HBM)
ANY = pl.BlockSpec(memory_space=pl.ANY)


def start_all(copies):
    for copy in copies:
        copy.start()


def turn(source, table, base):
    width, length = source.shape
    step = 512
    unroll = 4

    def body(i, carry):
        for u in range(unroll):
            off = pl.multiple_of((i * unroll + u) * step, step)
            rows = source[:, pl.ds(off, step)].T.astype(F32)
            table[pl.ds(pl.multiple_of(base + off, step), step), 0:width] = rows
        return carry

    lax.fori_loop(0, length // step // unroll, body, 0)


def order_kernel(per_seed, counts_rel, me, self_ids, neighbour_ids, count_one, lists):
    owners, seeds = counts_rel.shape
    fanout = neighbour_ids.shape[0]
    per_owner = count_one.shape[1] // owners
    half = owners // 2
    mine = me[0]
    counts = jnp.concatenate(
        [counts_rel[pl.ds(jnp.bitwise_xor(mine, c), 1), :] for c in range(owners)], axis=0
    ).astype(F32)
    needs = (counts + 1.0).astype(BF16)
    before = (iota((seeds, seeds), 0) < iota((seeds, seeds), 1)).astype(BF16)
    offset = jnp.dot(needs, before, preferred_element_type=F32)
    off_hi = jnp.floor(offset * (1.0 / 16.0))
    off_lo = offset - off_hi * 16.0
    shift = iota((seeds, per_owner), 1) - iota((seeds, per_owner), 0) * per_seed
    spread = ((shift >= 0) & (shift < per_seed)).astype(BF16)
    place = jnp.dot(iota((8, seeds), 1).astype(BF16), spread, preferred_element_type=F32)
    t = iota((owners, per_owner), 1).astype(F32) - place[0:1, :] * per_seed
    of_row = jnp.dot(counts.astype(BF16), spread, preferred_element_type=F32)
    row_hi = jnp.dot(off_hi.astype(BF16), spread, preferred_element_type=F32)
    row_lo = jnp.dot(off_lo.astype(BF16), spread, preferred_element_type=F32)
    slot = row_hi * 16.0 + row_lo + t
    used = (t <= of_row) & (slot < CAP)
    slot = slot.astype(I32)
    keys = [
        jnp.where(used[c : c + 1, :], count_one[:, c * per_owner : (c + 1) * per_owner], 0)
        for c in range(owners)
    ]
    kinds = [
        iota((16, per_owner), 0) == jnp.broadcast_to(key, (16, per_owner)) for key in keys
    ]
    stacked = jnp.concatenate([k.astype(F32).astype(BF16) for k in kinds], axis=0)
    left = (iota((per_owner, per_owner), 0) < iota((per_owner, per_owner), 1)).astype(BF16)
    prefix = jnp.dot(stacked, left, preferred_element_type=F32)
    total = jnp.dot(stacked, jnp.ones((per_owner, LANES), BF16), preferred_element_type=F32)
    for h in range(2):
        carry = jnp.zeros((16, LANES), F32)
        carries = []
        for c in range(h * half, (h + 1) * half):
            carries.append(carry)
            carry = carry + total[c * 16 : (c + 1) * 16, :]
        sizes = jnp.floor((carry + (UNROLL - 1)) * (1.0 / UNROLL)) * UNROLL
        bases = [jnp.zeros((1, LANES), F32)]
        for v in range(1, 16):
            bases.append(bases[-1] + sizes[v : v + 1, :])
        first = jnp.concatenate([bases[0]] + bases[:15], axis=0)
        sums = jnp.zeros((2 * (fanout + 2) * 16, LANES), F32)
        for i, c in enumerate(range(h * half, (h + 1) * half)):
            begin = (first + carries[i])[:, 0:1]
            spot = jnp.where(kinds[c], prefix[c * 16 : (c + 1) * 16, :] + begin, 0.0)
            spot = jnp.sum(spot, axis=0, keepdims=True).astype(I32)
            spot = jnp.where(keys[c] > 0, spot, -1)
            spot_lo = jnp.bitwise_and(spot, LANES - 1)
            spot_hi = jnp.right_shift(spot, 7)
            lane = (iota((LANES, per_owner), 0) == spot_lo).astype(F32).astype(BF16)
            at_hi = (iota((16, per_owner), 0) == spot_hi).astype(F32)
            columns = slice(c * per_owner, (c + 1) * per_owner)
            rows = [self_ids[:, columns]]
            rows += [neighbour_ids[k : k + 1, columns] for k in range(fanout)]
            rows += [half * CAP - (slot[c : c + 1, :] + i * CAP)]
            parts = []
            for row in rows:
                for byte in (jnp.right_shift(row, 8), jnp.bitwise_and(row, 255)):
                    value = jnp.broadcast_to(byte.astype(F32), (16, per_owner))
                    parts.append((at_hi * value).astype(BF16))
            sums = sums + lax.dot_general(
                jnp.concatenate(parts, axis=0),
                lane,
                (((1,), (1,)), ((), ())),
                preferred_element_type=F32,
            )
        for k in range(fanout + 2):
            hi = sums[32 * k : 32 * k + 16, :]
            lo = sums[32 * k + 16 : 32 * k + 32, :]
            value = (hi * 256.0 + lo).astype(I32)
            lists[h, k, :, :] = value if k <= fanout else half * CAP - value
        lane = iota((8, LANES), 1)
        begins = jnp.zeros((8, LANES), F32)
        for v in range(16):
            begins = begins + jnp.where(lane == v, bases[v], 0.0)
        lists[h, fanout + 2, 0:8, :] = begins.astype(I32)
        lists[h, fanout + 2, 8:16, :] = jnp.zeros((8, LANES), I32)


def list_copies(fanout, h, lists, ids, places, begins, sems):
    block = 16 * LANES

    def piece(k, length):
        at = pl.multiple_of((h * (fanout + 3) + k) * block, block)
        return lists.at[pl.ds(at, length)]

    copies = [
        pltpu.make_async_copy(piece(k, POSITIONS), ref, sems.at[k])
        for k, ref in enumerate(list(ids) + [places])
    ]
    last = fanout + 2
    return copies + [pltpu.make_async_copy(piece(last, LANES), begins, sems.at[last])]


def look_up(fanout, table, ids, places, begins, self_rows, mean_rows):
    for v in range(1, fanout + 1):
        begin = begins[v - 1]
        end = begins[v]

        def body(i, carry, v=v, begin=begin):
            for u in range(UNROLL):
                at = begin + i * UNROLL + u
                to = places[at]
                self_rows[pl.ds(to, 1), :] = table[pl.ds(ids[0][at], 1), :]
                total = tree_sum([table[pl.ds(ids[k][at], 1), :] for k in range(1, v + 1)])
                mean_rows[pl.ds(to, 1), :] = total * (1.0 / v)
            return carry

        lax.fori_loop(0, jnp.right_shift(end - begin, UNROLL.bit_length() - 1), body, 0)


def write_out(x, width, self_rows, mean_rows, keep, send):
    valid = iota((CAP, LANES), 1) < width
    for z in range(2):
        for ref, side in ((keep, x), (send, 1 - x)):
            at = pl.multiple_of((z * 2 + side) * CAP, CAP)
            for part, rows in enumerate((self_rows, mean_rows)):
                block = jnp.where(valid, rows[pl.ds(at, CAP), :], 0.0).astype(BF16)
                ref[z, :, part * LANES : (part + 1) * LANES] = block


def first_kernel(
    fanout, me, lists, features, other, weight, table, keep, send, *scratch
):
    ids = scratch[: fanout + 1]
    places, begins, self_rows, mean_rows, sems, staged, staged_sems = scratch[fanout + 1 :]
    width, length = other.shape
    x, h, rep = me[0], me[1], me[2]
    blocks, _, part = staged.shape
    stages = [
        pltpu.make_async_copy(
            features.at[:, pl.ds(b * part, part)], staged.at[b], staged_sems.at[b]
        )
        for b in range(blocks)
    ]
    start_all(stages)
    copies = list_copies(fanout, h, lists, ids, places, begins, sems)
    start_all(copies)
    self_rows[...] = jnp.zeros_like(self_rows)
    mean_rows[...] = jnp.zeros_like(mean_rows)
    turn(other, table, pl.multiple_of((1 - rep) * length, length))
    for b, stage in enumerate(stages):
        stage.wait()
        turn(staged.at[b], table, pl.multiple_of(rep * length + b * part, part))
    for copy in copies:
        copy.wait()
    look_up(fanout, table, ids, places, begins, self_rows, mean_rows)
    write_out(x, width, self_rows, mean_rows, keep, send)
    send[2, :, :] = weight[...]


def second_kernel(fanout, width, me, lists, table, keep_hbm, send_hbm, *scratch):
    ids = scratch[: fanout + 1]
    places, begins, self_rows, mean_rows, sems, keep, send, out_sems = scratch[fanout + 1 :]
    x, h = me[0], 1 - me[1]
    copies = list_copies(fanout, h, lists, ids, places, begins, sems)
    start_all(copies)
    self_rows[...] = jnp.zeros_like(self_rows)
    mean_rows[...] = jnp.zeros_like(mean_rows)
    for copy in copies:
        copy.wait()
    look_up(fanout, table, ids, places, begins, self_rows, mean_rows)
    write_out(x, width, self_rows, mean_rows, keep, send)
    outs = [
        pltpu.make_async_copy(send, send_hbm, out_sems.at[0]),
        pltpu.make_async_copy(keep, keep_hbm, out_sems.at[1]),
    ]
    start_all(outs)
    for copy in outs:
        copy.wait()


def project_kernel(me, keep, got, weight, weight_got, out_0, out_1):
    zl = me[3]
    theirs = weight_got[2]
    for which, out in ((zl, out_0), (1 - zl, out_1)):
        out[...] = (
            jnp.dot(keep[which], weight[...], preferred_element_type=F32)
            + jnp.dot(got[which], theirs, preferred_element_type=F32)
        ).astype(out.dtype)


def last_kernel(
    mine, a, b, c, counts, bias_one, self_two, neigh_two, bias_two, out_weight, out_bias, out
):
    pre = mine[...] + a[...].astype(F32) + b[...].astype(F32) + c[...].astype(F32)
    hidden = jnp.maximum(pre + bias_one[...], 0.0).astype(BF16)
    seeds = counts.shape[0]
    count = counts[...]
    earlier = (iota((seeds, seeds), 0) > iota((seeds, seeds), 1)).astype(BF16)
    needs = jnp.broadcast_to((count + 1).astype(F32), (seeds, LANES)).astype(BF16)
    offset = jnp.dot(earlier, needs, preferred_element_type=F32)[:, 0:1].astype(I32)
    place = iota((seeds, CAP), 1) - offset
    is_self = (place == 0).astype(F32).astype(BF16)
    is_near = ((place >= 1) & (place <= count)).astype(F32).astype(BF16)
    own = jnp.dot(is_self, hidden, preferred_element_type=F32).astype(BF16)
    total = jnp.dot(is_near, hidden, preferred_element_type=F32)
    mean = (total / count.astype(F32)).astype(BF16)
    pre_two = (
        jnp.dot(own, self_two[...], preferred_element_type=F32)
        + jnp.dot(mean, neigh_two[...], preferred_element_type=F32)
        + bias_two[...]
    )
    hidden_two = jnp.maximum(pre_two, 0.0).astype(BF16)
    out[...] = jnp.dot(hidden_two, out_weight[...], preferred_element_type=F32) + out_bias[...]


def params(limit):
    return pltpu.CompilerParams(vmem_limit_bytes=limit * MIB)


def shape(dims, dtype):
    return jax.ShapeDtypeStruct(dims, dtype)


def order_call(per_seed, counts_rel, col, self_ids, neighbour_ids, count_one):
    lists = pl.pallas_call(
        functools.partial(order_kernel, per_seed),
        out_shape=shape((2, neighbour_ids.shape[0] + 3, 16, LANES), I32),
        in_specs=[VMEM, SMEM, VMEM, VMEM, VMEM],
        out_specs=VMEM,
        compiler_params=params(10),
        name="order",
    )(counts_rel, col, self_ids, neighbour_ids, count_one)
    return lists.reshape(-1)


def list_scratch(fanout):
    return (
        [pltpu.SMEM((POSITIONS,), I32) for _ in range(fanout + 2)]
        + [pltpu.SMEM((LANES,), I32)]
        + [pltpu.VMEM((4 * CAP + 8, LANES), F32) for _ in range(2)]
        + [pltpu.SemaphoreType.DMA((fanout + 3,))]
    )


def first_call(fanout, me, lists, features, other, weight):
    return pl.pallas_call(
        functools.partial(first_kernel, fanout),
        out_shape=(
            shape((2 * features.shape[1], LANES), F32),
            shape((2, CAP, 2 * LANES), BF16),
            shape((3, CAP, 2 * LANES), BF16),
        ),
        in_specs=[SMEM, ANY, ANY, VMEM, VMEM],
        out_specs=(VMEM, VMEM, VMEM),
        scratch_shapes=list_scratch(fanout)
        + [
            pltpu.VMEM((4, features.shape[0], features.shape[1] // 4), BF16),
            pltpu.SemaphoreType.DMA((4,)),
        ],
        compiler_params=params(FIRST_MIB),
        name="first_half",
    )(me, lists, features, other, weight)


def second_call(fanout, width, me, lists, table):
    dims = (2, CAP, 2 * LANES)
    halves = pltpu.HBM(dims, BF16)
    return pl.pallas_call(
        functools.partial(second_kernel, fanout, width),
        out_shape=(halves, halves),
        in_specs=[SMEM, ANY, VMEM],
        out_specs=(HBM, HBM),
        scratch_shapes=list_scratch(fanout)
        + [pltpu.VMEM(dims, BF16) for _ in range(2)]
        + [pltpu.SemaphoreType.DMA((2,))],
        compiler_params=params(10),
        name="second_half",
    )(me, lists, table)


def project_call(me, keep, got, weight, weight_got, kinds):
    hidden = weight.shape[1]
    return pl.pallas_call(
        project_kernel,
        out_shape=tuple(shape((CAP, hidden), kind) for kind in kinds),
        in_specs=[SMEM, VMEM, VMEM, VMEM, VMEM],
        out_specs=(VMEM, VMEM),
        compiler_params=params(10),
        name="project",
    )(me, keep, got, weight, weight_got)


def last_call(*args):
    seeds = args[4].shape[0]
    classes = args[-1].shape[1]
    return pl.pallas_call(
        last_kernel,
        out_shape=shape((seeds, classes), F32),
        in_specs=[VMEM] * len(args),
        out_specs=VMEM,
        compiler_params=params(10),
        name="layer_two",
    )(*args)


def main(
    features,
    self_ids,
    neighbour_ids,
    count_one,
    count_two,
    self_one,
    neigh_one,
    bias_one,
    self_two,
    neigh_two,
    bias_two,
    out_weight,
    out_bias,
):
    owners = lax.axis_size("col")
    seeds = count_two.shape[0]
    per_owner = self_ids.shape[0] // owners
    per_seed = per_owner // seeds
    fanout = neighbour_ids.shape[0]
    width = features.shape[0]
    col = lax.axis_index("col")
    rep = lax.axis_index("rep")
    z = col // 2
    me = jnp.stack([col % 2, 1 - z // 2, rep, z % 2]).astype(I32)

    def across(value, bit):
        return lax.ppermute(value, "col", [(i, i ^ bit) for i in range(owners)])

    def swapped(value):
        return lax.ppermute(value, "rep", [(0, 1), (1, 0)])

    other = swapped(features)
    weight = jnp.concatenate(
        [jnp.pad(w, ((0, LANES - width), (0, 0))) for w in (self_one, neigh_one)], axis=0
    )
    counts = count_two[None, :]
    for bit in (1, 2, 4):
        counts = jnp.concatenate([counts, across(counts, bit)], axis=0)
    lists = order_call(
        per_seed,
        counts,
        col.reshape(1).astype(I32),
        self_ids[None, :],
        neighbour_ids,
        count_one[None, :],
    )
    table, keep_far, send_far = first_call(fanout, me, lists, features, other, weight)
    got_far = across(send_far, 1)
    keep_near, send_near = second_call(fanout, width, me, lists, table)
    far = project_call(me, keep_far, got_far, weight, got_far, (BF16, BF16))
    got_near = across(send_near, 1)
    got = [across(far[0], 4), across(far[1], 6)]
    near = project_call(me, keep_near, got_near, weight, got_far, (F32, BF16))
    got.append(across(near[1], 2))
    fast = last_call(
        near[0],
        *got,
        count_two[:, None],
        bias_one[None, :],
        self_two,
        neigh_two,
        bias_two[None, :],
        out_weight,
        out_bias[None, :],
    )
    most = jnp.max(jnp.sum(counts + 1, axis=1)).reshape(1)
    most = jnp.maximum(most, swapped(most))
    most = jnp.maximum(most, lax.ppermute(most, "groups", [(0, 1), (1, 0)]))
    return lax.cond(
        most[0] > CAP,
        lambda: general(
            other,
            features,
            self_ids,
            neighbour_ids,
            count_one,
            count_two,
            self_one,
            neigh_one,
            bias_one,
            self_two,
            neigh_two,
            bias_two,
            out_weight,
            out_bias,
        ),
        lambda: fast,
    )


def local(*args):
    features, self_ids, neighbour_ids = args[0], args[1], args[2]
    sizes = (lax.axis_size("groups"), lax.axis_size("col"), lax.axis_size("rep"))
    small = (
        sizes == (2, 8, 2)
        and features.shape[0] <= LANES
        and features.shape[1] <= 32768
        and self_ids.shape[0] * (neighbour_ids.shape[0] + 1) <= 2**17
        and neighbour_ids.shape[0] <= 15
    )
    if small:
        return main(*args)
    return general(lax.ppermute(features, "rep", [(0, 1), (1, 0)]), *args)


def solution(mesh):
    placed = (
        P("col", ("groups", "rep")),
        P(("groups", "rep")),
        P(None, ("groups", "rep")),
        P(("groups", "rep")),
        P(("groups", "col", "rep")),
        P("col", None),
        P("col", None),
        P(),
        P(),
        P(),
        P(),
        P(),
        P(),
    )
    return jax.shard_map(
        local,
        mesh=mesh,
        in_specs=placed,
        out_specs=P(("groups", "col", "rep"), None),
        check_vma=False,
    )
```

time: 104 us -> 65.9 us (0.63)
  Pallas kernels: 46.1 us -> 31 us
  between operations: 15.5 us -> 2.07 us
  local copies, waits for them, and re-layouts: 12.9 us -> 3.24 us
  waiting for transfers between devices: 7.93 us -> 5.97 us
  starting transfers between devices: 17.3 us -> 19 us
    unnamed x29, local copies, waits for them, and re-layouts: 11.3 us -> 1.72 us
    pallas_call x2 -> x1, Pallas kernels: 9.85 us -> 2.73 us  [order_call(): pl.pallas_call(functools.partial(order_kernel, per_seed), out_shape=shape...]
    pallas_call x1, Pallas kernels: 15.6 us -> 9.54 us  [second_call(): pl.pallas_call(functools.partial(second_kernel, fanout, width), out_shape...]
    pallas_call x1, Pallas kernels: 18.3 us -> 16.4 us  [first_call(): pl.pallas_call(functools.partial(first_kernel, fanout), out_shape=(shape(...]
    ppermute x1, starting transfers between devices: 1.37 us -> 2.74 us  [main(): most = jnp.maximum(most, lax.ppermute(most, 'groups', [(0, 1), (1, 0)]))]
    ppermute x1, waiting for transfers between devices: 2.34 us -> 0.97 us  [main(): most = jnp.maximum(most, lax.ppermute(most, 'groups', [(0, 1), (1, 0)]))]
    ppermute x9 -> x8, waiting for transfers between devices: 4.21 us -> 3.61 us  [across(): return lax.ppermute(value, 'col', [(i, i ^ bit) for i in range(owners)])]
    ppermute x9 -> x8, starting transfers between devices: 15.4 us -> 15.8 us  [across(): return lax.ppermute(value, 'col', [(i, i ^ bit) for i in range(owners)])]
  transfers between devices with their start and end apart: 12 -> 11, of which waited for: 4 -> 6; matrix products, arithmetic and copies ran while one was open for 5% -> 8% of each run, Pallas kernels for 26% -> 21%
where the time goes in v2:
time: 65.9 us; the launch traced here: 65.2 us
  Pallas kernels  31 us (47%)
  starting transfers between devices  19 us (29%)
  waiting for transfers between devices  5.97 us (9%)
  other arithmetic  3.64 us (6%)
  local copies, waits for them, and re-layouts  3.24 us (5%)
  between operations  2.07 us (3%)
    pallas_call x1, Pallas kernels, first_call(): pl.pallas_call(functools.partial(first_kernel, fanout), out_shape=(shape(...  16.4 us
    ppermute x8, starting transfers between devices, across(): return lax.ppermute(value, 'col', [(i, i ^ bit) for i in range(owners)])  15.8 us
    pallas_call x1, Pallas kernels, second_call(): pl.pallas_call(functools.partial(second_kernel, fanout, width), out_shape...  9.54 us
    ppermute x8, waiting for transfers between devices, across(): return lax.ppermute(value, 'col', [(i, i ^ bit) for i in range(owners)])  3.61 us
    ppermute x1, starting transfers between devices, main(): most = jnp.maximum(most, lax.ppermute(most, 'groups', [(0, 1), (1, 0)]))  2.74 us
    pallas_call x1, Pallas kernels, order_call(): pl.pallas_call(functools.partial(order_kernel, per_seed), out_shape=shape...  2.73 us
    concatenate x3, other arithmetic, main(): counts = jnp.concatenate([counts, across(counts, bit)], axis=0)  2.1 us
    unnamed x29, local copies, waits for them, and re-layouts  1.72 us
  transfers between devices with their start and end apart: 11, of which 6 were waited for; matrix products, arithmetic and copies ran while one was open for 8% of the time, Pallas kernels for 21%

profile of v2, /device:TPU:0, one launch (start us, length us, event | category | flops | bytes accessed | tf_op | source)
XLA Modules:
  0.0 65.2 jit_solution(16717936509374417641)
XLA Ops:
  0.0 0.5 collective-permute-start.5
  0.5 2.5 %collective-permute-start = (s32[1,32]{1,0:T(1,128)}, s32[1,32]{1,0:T(1,128)S(1)}, u32[]{:S(2)}, u32[]{:S(2)}) collective-permute-start(s32[1,32]{1,0:T(1,128)} %bitcast.65), channel_id=1, source_target_pairs={{0,2},{2,0},{4,6},{6,4},{8,10},{10,8},{12,14},{14,12},{1,3},{3,1},... | collective-permute-start | bytes 392 | tf_op jit(solution)/shard_map/ppermute | solution.py:448
  2.9 0.8 %fusion.26.weight = bf16[256,256]{1,0:T(8,128)(2,1)S(1)} fusion(bf16[96,256]{1,0:T(8,128)(2,1)} %param.21, bf16[96,256]{1,0:T(8,128)(2,1)} %param.20), kind=kLoop, calls=%fused_computation.42 | loop fusion | flops 524288 | bytes 229376 | tf_op jit(solution)/shard_map/concatenate | solution.py:454
  3.8 0.8 %collective-permute-done = s32[1,32]{1,0:T(1,128)S(1)} collective-permute-done((s32[1,32]{1,0:T(1,128)}, s32[1,32]{1,0:T(1,128)S(1)}, u32[]{:S(2)}, u32[]{:S(2)}) %collective-permute-start) | collective-permute-done | bytes 160 | tf_op jit(solution)/shard_map/ppermute | solution.py:448
  4.6 0.7 %pad_add_fusion.2 = s32[2,32]{1,0:T(2,128)S(1)} fusion(s32[1,32]{1,0:T(1,128)S(1)} %collective-permute-done, s32[1,32]{1,0:T(1,128)} %bitcast.66), kind=kLoop, calls=%fused_computation.46 | loop fusion | flops 64 | bytes 512 | tf_op jit(solution)/shard_map/concatenate | solution.py:459
  5.3 2.1 %collective-permute-start.1 = (s32[2,32]{1,0:T(2,128)S(1)}, s32[2,32]{1,0:T(2,128)S(1)}, u32[]{:S(2)}, u32[]{:S(2)}) collective-permute-start(s32[2,32]{1,0:T(2,128)S(1)} %pad_add_fusion.2), channel_id=1, source_target_pairs={{0,4},{2,6},{4,0},{6,2},{8,12},{10,14},{12,8},{14,10},{1,5},{3,7},... | collective-permute-start | bytes 776 | tf_op jit(solution)/shard_map/ppermute | solution.py:448
  7.4 1.5 %collective-permute-done.1 = s32[2,32]{1,0:T(2,128)S(1)} collective-permute-done((s32[2,32]{1,0:T(2,128)S(1)}, s32[2,32]{1,0:T(2,128)S(1)}, u32[]{:S(2)}, u32[]{:S(2)}) %collective-permute-start.1) | collective-permute-done | bytes 288 | tf_op jit(solution)/shard_map/ppermute | solution.py:448
  8.9 0.7 %pad_add_fusion.1 = s32[4,32]{1,0:T(4,128)S(1)} fusion(s32[2,32]{1,0:T(2,128)S(1)} %collective-permute-done.1, s32[1,32]{1,0:T(1,128)S(1)} %collective-permute-done, s32[1,32]{1,0:T(1,128)} %bitcast.67), kind=kLoop, calls=%fused_computation.45 | loop fusion | flops 256 | bytes 1024 | tf_op jit(solution)/shard_map/concatenate | solution.py:459
  9.6 3.0 %collective-permute-start.2 = (s32[4,32]{1,0:T(4,128)S(1)}, s32[4,32]{1,0:T(4,128)S(1)}, u32[]{:S(2)}, u32[]{:S(2)}) collective-permute-start(s32[4,32]{1,0:T(4,128)S(1)} %pad_add_fusion.1), channel_id=1, source_target_pairs={{0,8},{2,10},{4,12},{6,14},{8,0},{10,2},{12,4},{14,6},{1,9},{3,11}... | collective-permute-start | bytes 1544 | tf_op jit(solution)/shard_map/ppermute | solution.py:448
  12.6 0.1 pad_add_fusion.3.me
  12.7 0.7 %broadcast_in_dim.29.self_ids = s32[1,2816]{1,0:T(1,128)S(1)} reshape(s32[2816]{0:T(1024)} %param.16) | data formatting | bytes 22528 | tf_op jit(solution)/shard_map/broadcast_in_dim | solution.py:464
  13.4 0.7 %broadcast_in_dim.30.count_one = s32[1,2816]{1,0:T(1,128)S(1)} reshape(s32[2816]{0:T(1024)} %param.18) | data formatting | bytes 22528 | tf_op jit(solution)/shard_map/broadcast_in_dim | solution.py:466
  14.1 0.1 collective-permute-done.2
  14.2 0.8 %pad_add_fusion = (s32[8,32]{1,0:T(8,128)S(1)}, s32[8]{0:T(128)S(1)}) fusion(s32[4,32]{1,0:T(4,128)S(1)} %collective-permute-done.2, s32[2,32]{1,0:T(2,128)S(1)} %collective-permute-done.1, s32[1,32]{1,0:T(1,128)S(1)} %collective-permute-done, s32[1,32]{1,0:T(1,128)} %bitcast.68), kind=kLoop, calls=%fused_computation.43 | loop fusion | flops 1272 | bytes 2080 | tf_op jit(solution)/shard_map/concatenate | solution.py:459
  15.0 2.7 %order.1 = s32[2,18,16,128]{3,2,1,0:T(8,128)S(1)} custom-call(s32[8,32]{1,0:T(8,128)S(1)} %get-tuple-element.128.counts_rel, s32[1]{0:T(128)} %bitcast.21.me, s32[1,2816]{1,0:T(1,128)S(1)} %broadcast_in_dim.29.self_ids, s32[15,2816]{1,0:T(8,128)} %neighbour_ids.1, s32[1,2816]{1,0:T(1,128)S(1)} %broadcast_in_dim.30.count_one), custom_call_target="tpu_custom_call" | custom-call | tf_op jit(solution)/shard_map/order/pallas_call | solution.py:340
  17.7 0.0 collective-permute-done.5.other
  17.7 16.4 %first_half.1 = (f32[65536,128]{1,0:T(8,128)S(1)}, bf16[2,256,256]{2,1,0:T(8,128)(2,1)S(1)}, bf16[3,256,256]{2,1,0:T(8,128)(2,1)S(1)}) custom-call(s32[4]{0:T(128)S(1)} %pad_add_fusion.3.me, s32[73728]{0:T(1024)S(1)} %bitcast.56, bf16[96,32768]{1,0:T(8,128)(2,1)} %features.1, bf16[96,32768]{1,0:T(8,128)(2,1)} %collective-permute-done.5.other, ...), custom_call_target="tpu_custom_call" | custom-call | tf_op jit(solution)/shard_map/first_half/pallas_call | solution.py:361
  34.2 1.9 %collective-permute-start.7 = (bf16[3,256,256]{2,1,0:T(8,128)(2,1)S(1)}, bf16[3,256,256]{2,1,0:T(8,128)(2,1)S(1)}, u32[]{:S(2)}, u32[]{:S(2)}) collective-permute-start(bf16[3,256,256]{2,1,0:T(8,128)(2,1)S(1)} %get-tuple-element.63), channel_id=1, source_target_pairs={{0,2},{2,0},{4,6},{6,4},{8,10},{10,8},{12,14},{14,12},{1,3},{3,1},... | collective-permute-start | bytes 1179656 | tf_op jit(solution)/shard_map/ppermute | solution.py:448
  36.0 0.0 copy-start.4
  36.1 0.0 copy-start.10
  36.1 0.0 copy-start.11
  36.1 0.0 copy-start.12
  36.1 0.0 copy-start.13
  36.1 0.0 copy-start.1
  36.1 0.0 copy-start.5
  36.1 0.0 copy-start.6
  36.1 0.0 copy-start.7
  36.1 0.0 copy-start.8
  36.2 9.5 %second_half.1 = (bf16[2,256,256]{2,1,0:T(8,128)(2,1)}, bf16[2,256,256]{2,1,0:T(8,128)(2,1)}) custom-call(s32[4]{0:T(128)S(1)} %pad_add_fusion.3.me, s32[73728]{0:T(1024)S(1)} %bitcast.57, f32[65536,128]{1,0:T(8,128)S(1)} %get-tuple-element.60.table), custom_call_target="tpu_custom_call" | custom-call | tf_op jit(solution)/shard_map/second_half/pallas_call | solution.py:383
  45.7 0.3 collective-permute-start.6
  46.0 0.0 collective-permute-done.7.weight_got.got
  46.0 0.8 %project.3 = (bf16[256,256]{1,0:T(8,128)(2,1)S(1)}, bf16[256,256]{1,0:T(8,128)(2,1)S(1)}) custom-call(s32[4]{0:T(128)S(1)} %pad_add_fusion.3.me, bf16[2,256,256]{2,1,0:T(8,128)(2,1)S(1)} %get-tuple-element.65.keep, bf16[3,256,256]{2,1,0:T(8,128)(2,1)S(1)} %collective-permute-done.7.weight_got.got, bf16[256,256]{1,0:T(8,128)(2,1)S(1)} %fusion.26.weight, ...), custom_call_target="tpu_custom_call" | custom-call | tf_op jit(solution)/shard_map/project/pallas_call | solution.py:398
  46.8 3.0 %collective-permute-start.8 = (bf16[256,256]{1,0:T(8,128)(2,1)S(1)}, bf16[256,256]{1,0:T(8,128)(2,1)S(1)}, u32[]{:S(2)}, u32[]{:S(2)}) collective-permute-start(bf16[256,256]{1,0:T(8,128)(2,1)S(1)} %get-tuple-element.66), channel_id=1, source_target_pairs={{0,8},{2,10},{4,12},{6,14},{8,0},{10,2},{12,4},{14,6},{1,9},{3,11}... | collective-permute-start | bytes 393224 | tf_op jit(solution)/shard_map/ppermute | solution.py:448
  49.8 1.4 %collective-permute-start.9 = (bf16[256,256]{1,0:T(8,128)(2,1)S(1)}, bf16[256,256]{1,0:T(8,128)(2,1)S(1)}, u32[]{:S(2)}, u32[]{:S(2)}) collective-permute-start(bf16[256,256]{1,0:T(8,128)(2,1)S(1)} %get-tuple-element.67), channel_id=1, source_target_pairs={{0,12},{2,14},{4,8},{6,10},{8,4},{10,6},{12,0},{14,2},{1,13},{3,15... | collective-permute-start | bytes 393224 | tf_op jit(solution)/shard_map/ppermute | solution.py:448
  51.2 1.2 %collective-permute-done.6.got = bf16[2,256,256]{2,1,0:T(8,128)(2,1)S(1)} collective-permute-done((bf16[2,256,256]{2,1,0:T(8,128)(2,1)}, bf16[2,256,256]{2,1,0:T(8,128)(2,1)S(1)}, u32[]{:S(2)}, u32[]{:S(2)}) %collective-permute-start.6) | collective-permute-done | bytes 262176 | tf_op jit(solution)/shard_map/ppermute | solution.py:448
  52.4 0.9 %copy-done = bf16[2,256,256]{2,1,0:T(8,128)(2,1)S(1)} copy-done((bf16[2,256,256]{2,1,0:T(8,128)(2,1)S(1)}, bf16[2,256,256]{2,1,0:T(8,128)(2,1)}, u32[]{:S(2)}) %copy-start) | copy-done | bytes 262168
  53.3 0.8 %project.2 = (f32[256,256]{1,0:T(8,128)S(1)}, bf16[256,256]{1,0:T(8,128)(2,1)S(1)}) custom-call(s32[4]{0:T(128)S(1)} %pad_add_fusion.3.me, bf16[2,256,256]{2,1,0:T(8,128)(2,1)S(1)} %copy-done, bf16[2,256,256]{2,1,0:T(8,128)(2,1)S(1)} %collective-permute-done.6.got, bf16[256,256]{1,0:T(8,128)(2,1)S(1)} %fusion.26.weight, ...), custom_call_target="tpu_custom_call" | custom-call | tf_op jit(solution)/shard_map/project/pallas_call | solution.py:398
  54.1 1.6 %collective-permute-start.10 = (bf16[256,256]{1,0:T(8,128)(2,1)S(1)}, bf16[256,256]{1,0:T(8,128)(2,1)S(1)}, u32[]{:S(2)}, u32[]{:S(2)}) collective-permute-start(bf16[256,256]{1,0:T(8,128)(2,1)S(1)} %get-tuple-element.68), channel_id=1, source_target_pairs={{0,4},{2,6},{4,0},{6,2},{8,12},{10,14},{12,8},{14,10},{1,5},{3,7},... | collective-permute-start | bytes 393224 | tf_op jit(solution)/shard_map/ppermute | solution.py:448
  55.8 0.0 copy-done.4
  55.8 0.1 copy.37.out_weight
  55.9 0.0 copy-done.10
  55.9 0.1 copy.36.counts
  56.0 0.6 reduce_max.9
  56.6 0.0 collective-permute-start.3
  56.6 1.4 %collective-permute-done.3 = s32[1]{0:T(128)} collective-permute-done((s32[1]{0:T(128)}, s32[1]{0:T(128)}, u32[]{:S(2)}, u32[]{:S(2)}) %collective-permute-start.3) | collective-permute-done | bytes 36 | tf_op jit(solution)/shard_map/ppermute | solution.py:451
  59.2 2.7 %collective-permute-start.4 = (s32[1]{0:T(128)}, s32[1]{0:T(128)}, u32[]{:S(2)}, u32[]{:S(2)}) collective-permute-start(s32[1]{0:T(128)} %max.22), channel_id=1, source_target_pairs={{0,16},{16,0},{1,17},{17,1},{2,18},{18,2},{3,19},{19,3},{4,20},{20... | collective-permute-start | bytes 20 | tf_op jit(solution)/shard_map/ppermute | solution.py:489
  62.0 1.0 %collective-permute-done.4 = s32[1]{0:T(128)} collective-permute-done((s32[1]{0:T(128)}, s32[1]{0:T(128)}, u32[]{:S(2)}, u32[]{:S(2)}) %collective-permute-start.4) | collective-permute-done | bytes 36 | tf_op jit(solution)/shard_map/ppermute | solution.py:489
  63.5 0.0 collective-permute-done.8.a
  63.5 0.0 collective-permute-done.9.b
  63.5 0.0 collective-permute-done.10.c
  63.6 0.0 copy-done.2
  63.6 0.0 copy-done.3
  63.6 0.0 copy-done.11
  63.6 0.0 copy-done.12
  63.6 0.0 copy-done.13
  63.6 0.7 %layer_two.1 = f32[32,153]{1,0:T(8,128)S(1)} custom-call(f32[256,256]{1,0:T(8,128)S(1)} %get-tuple-element.64.mine, bf16[256,256]{1,0:T(8,128)(2,1)S(1)} %collective-permute-done.8.a, bf16[256,256]{1,0:T(8,128)(2,1)S(1)} %collective-permute-done.9.b, bf16[256,256]{1,0:T(8,128)(2,1)S(1)} %collective-permute-done.10.c, s32[32,1]{1,0:T(8,128)S(1)} %copy.36.counts, ...), custom_call_target="tpu_custom_call" | custom-call | tf_op jit(solution)/shard_map/layer_two/pallas_call | solution.py:411
  64.3 0.0 copy-done.1
  64.3 0.0 copy-done.5
  64.3 0.0 copy-done.6
  64.3 0.0 copy-done.7
  64.3 0.0 copy-done.8
  64.3 0.2 conditional.1
  64.5 0.0 copy-start.9
  64.6 0.6 copy-done.9
  (3 shorter events, 0.0 us)
Async XLA Ops:
  0.0 17.7 %collective-permute-start.5 = (bf16[96,32768]{1,0:T(8,128)(2,1)}, bf16[96,32768]{1,0:T(8,128)(2,1)}, u32[]{:S(2)}, u32[]{:S(2)}) collective-permute-start(bf16[96,32768]{1,0:T(8,128)(2,1)} %features.1), channel_id=1, source_target_pairs={{0,1},{1,0},{2,3},{3,2},{4,5},{5,4},{6,7},{7,6},{8,9},{9,8},{10,11... | collective-permute-start | bytes 18874376 | tf_op jit(solution)/shard_map/ppermute | solution.py:451
  0.5 4.1 %collective-permute-start = (s32[1,32]{1,0:T(1,128)}, s32[1,32]{1,0:T(1,128)S(1)}, u32[]{:S(2)}, u32[]{:S(2)}) collective-permute-start(s32[1,32]{1,0:T(1,128)} %bitcast.65), channel_id=1, source_target_pairs={{0,2},{2,0},{4,6},{6,4},{8,10},{10,8},{12,14},{14,12},{1,3},{3,1},... | collective-permute-start | bytes 392 | tf_op jit(solution)/shard_map/ppermute | solution.py:448
  5.3 3.7 %collective-permute-start.1 = (s32[2,32]{1,0:T(2,128)S(1)}, s32[2,32]{1,0:T(2,128)S(1)}, u32[]{:S(2)}, u32[]{:S(2)}) collective-permute-start(s32[2,32]{1,0:T(2,128)S(1)} %pad_add_fusion.2), channel_id=1, source_target_pairs={{0,4},{2,6},{4,0},{6,2},{8,12},{10,14},{12,8},{14,10},{1,5},{3,7},... | collective-permute-start | bytes 776 | tf_op jit(solution)/shard_map/ppermute | solution.py:448
  9.6 4.6 %collective-permute-start.2 = (s32[4,32]{1,0:T(4,128)S(1)}, s32[4,32]{1,0:T(4,128)S(1)}, u32[]{:S(2)}, u32[]{:S(2)}) collective-permute-start(s32[4,32]{1,0:T(4,128)S(1)} %pad_add_fusion.1), channel_id=1, source_target_pairs={{0,8},{2,10},{4,12},{6,14},{8,0},{10,2},{12,4},{14,6},{1,9},{3,11}... | collective-permute-start | bytes 1544 | tf_op jit(solution)/shard_map/ppermute | solution.py:448
  34.2 11.8 %collective-permute-start.7 = (bf16[3,256,256]{2,1,0:T(8,128)(2,1)S(1)}, bf16[3,256,256]{2,1,0:T(8,128)(2,1)S(1)}, u32[]{:S(2)}, u32[]{:S(2)}) collective-permute-start(bf16[3,256,256]{2,1,0:T(8,128)(2,1)S(1)} %get-tuple-element.63), channel_id=1, source_target_pairs={{0,2},{2,0},{4,6},{6,4},{8,10},{10,8},{12,14},{14,12},{1,3},{3,1},... | collective-permute-start | bytes 1179656 | tf_op jit(solution)/shard_map/ppermute | solution.py:448
  36.0 19.7 %copy-start.4 = (bf16[256,153]{0,1:T(8,128)(2,1)S(1)}, bf16[256,153]{0,1:T(8,128)(2,1)}, u32[]{:S(2)}) copy-start(bf16[256,153]{0,1:T(8,128)(2,1)} %param.26) | copy-start | bytes 235012
  36.1 19.8 %copy-start.10 = (s32[32]{0:T(128)S(1)}, s32[32]{0:T(128)}, u32[]{:S(2)}) copy-start(s32[32]{0:T(128)} %param.19) | copy-start | bytes 388
  36.1 27.5 %copy-start.2 = (bf16[256,256]{1,0:T(8,128)(2,1)S(1)}, bf16[256,256]{1,0:T(8,128)(2,1)}, u32[]{:S(2)}) copy-start(bf16[256,256]{1,0:T(8,128)(2,1)} %neigh_two.1) | copy-start | bytes 393220
  36.1 27.5 %copy-start.3 = (bf16[256,256]{1,0:T(8,128)(2,1)S(1)}, bf16[256,256]{1,0:T(8,128)(2,1)}, u32[]{:S(2)}) copy-start(bf16[256,256]{1,0:T(8,128)(2,1)} %self_two.1) | copy-start | bytes 393220
  36.1 27.5 %copy-start.11 = (f32[256]{0:T(256)S(1)}, f32[256]{0:T(256)}, u32[]{:S(2)}) copy-start(f32[256]{0:T(256)} %param.25) | copy-start | bytes 3076
  36.1 27.5 %copy-start.12 = (f32[153]{0:T(256)S(1)}, f32[153]{0:T(256)}, u32[]{:S(2)}) copy-start(f32[153]{0:T(256)} %param.27) | copy-start | bytes 1840
  36.1 27.5 %copy-start.13 = (f32[256]{0:T(256)S(1)}, f32[256]{0:T(256)}, u32[]{:S(2)}) copy-start(f32[256]{0:T(256)} %param.22) | copy-start | bytes 3076
  36.1 28.2 %copy-start.1 = (s32[15,2816]{1,0:T(8,128)S(1)}, s32[15,2816]{1,0:T(8,128)}, u32[]{:S(2)}) copy-start(s32[15,2816]{1,0:T(8,128)} %neighbour_ids.1) | copy-start | bytes 506884
  36.1 28.2 %copy-start.5 = (bf16[96,256]{1,0:T(8,128)(2,1)S(1)}, bf16[96,256]{1,0:T(8,128)(2,1)}, u32[]{:S(2)}) copy-start(bf16[96,256]{1,0:T(8,128)(2,1)} %param.21) | copy-start | bytes 147460
  36.1 28.2 %copy-start.6 = (bf16[96,256]{1,0:T(8,128)(2,1)S(1)}, bf16[96,256]{1,0:T(8,128)(2,1)}, u32[]{:S(2)}) copy-start(bf16[96,256]{1,0:T(8,128)(2,1)} %param.20) | copy-start | bytes 147460
  36.1 28.2 %copy-start.7 = (s32[2816]{0:T(1024)S(1)}, s32[2816]{0:T(1024)}, u32[]{:S(2)}) copy-start(s32[2816]{0:T(1024)} %param.16) | copy-start | bytes 33796
  36.1 28.2 %copy-start.8 = (s32[2816]{0:T(1024)S(1)}, s32[2816]{0:T(1024)}, u32[]{:S(2)}) copy-start(s32[2816]{0:T(1024)} %param.18) | copy-start | bytes 33796
  45.7 6.6 %collective-permute-start.6 = (bf16[2,256,256]{2,1,0:T(8,128)(2,1)}, bf16[2,256,256]{2,1,0:T(8,128)(2,1)S(1)}, u32[]{:S(2)}, u32[]{:S(2)}) collective-permute-start(bf16[2,256,256]{2,1,0:T(8,128)(2,1)} %get-tuple-element.62), channel_id=1, source_target_pairs={{0,2},{2,0},{4,6},{6,4},{8,10},{10,8},{12,14},{14,12},{1,3},{3,1},... | collective-permute-start | bytes 786440 | tf_op jit(solution)/shard_map/ppermute | solution.py:448
  46.8 16.7 %collective-permute-start.8 = (bf16[256,256]{1,0:T(8,128)(2,1)S(1)}, bf16[256,256]{1,0:T(8,128)(2,1)S(1)}, u32[]{:S(2)}, u32[]{:S(2)}) collective-permute-start(bf16[256,256]{1,0:T(8,128)(2,1)S(1)} %get-tuple-element.66), channel_id=1, source_target_pairs={{0,8},{2,10},{4,12},{6,14},{8,0},{10,2},{12,4},{14,6},{1,9},{3,11}... | collective-permute-start | bytes 393224 | tf_op jit(solution)/shard_map/ppermute | solution.py:448
  49.8 13.7 %collective-permute-start.9 = (bf16[256,256]{1,0:T(8,128)(2,1)S(1)}, bf16[256,256]{1,0:T(8,128)(2,1)S(1)}, u32[]{:S(2)}, u32[]{:S(2)}) collective-permute-start(bf16[256,256]{1,0:T(8,128)(2,1)S(1)} %get-tuple-element.67), channel_id=1, source_target_pairs={{0,12},{2,14},{4,8},{6,10},{8,4},{10,6},{12,0},{14,2},{1,13},{3,15... | collective-permute-start | bytes 393224 | tf_op jit(solution)/shard_map/ppermute | solution.py:448
  52.4 1.0 %copy-start = (bf16[2,256,256]{2,1,0:T(8,128)(2,1)S(1)}, bf16[2,256,256]{2,1,0:T(8,128)(2,1)}, u32[]{:S(2)}) copy-start(bf16[2,256,256]{2,1,0:T(8,128)(2,1)} %get-tuple-element.61.keep) | copy-start | bytes 786436
  54.1 9.4 %collective-permute-start.10 = (bf16[256,256]{1,0:T(8,128)(2,1)S(1)}, bf16[256,256]{1,0:T(8,128)(2,1)S(1)}, u32[]{:S(2)}, u32[]{:S(2)}) collective-permute-start(bf16[256,256]{1,0:T(8,128)(2,1)S(1)} %get-tuple-element.68), channel_id=1, source_target_pairs={{0,4},{2,6},{4,0},{6,2},{8,12},{10,14},{12,8},{14,10},{1,5},{3,7},... | collective-permute-start | bytes 393224 | tf_op jit(solution)/shard_map/ppermute | solution.py:448
  56.6 1.4 %collective-permute-start.3 = (s32[1]{0:T(128)}, s32[1]{0:T(128)}, u32[]{:S(2)}, u32[]{:S(2)}) collective-permute-start(s32[1]{0:T(128)} %bitcast.15), channel_id=1, source_target_pairs={{0,1},{1,0},{2,3},{3,2},{4,5},{5,4},{6,7},{7,6},{8,9},{9,8},{10,11... | collective-permute-start | bytes 20 | tf_op jit(solution)/shard_map/ppermute | solution.py:451
  59.2 3.7 %collective-permute-start.4 = (s32[1]{0:T(128)}, s32[1]{0:T(128)}, u32[]{:S(2)}, u32[]{:S(2)}) collective-permute-start(s32[1]{0:T(128)} %max.22), channel_id=1, source_target_pairs={{0,16},{16,0},{1,17},{17,1},{2,18},{18,2},{3,19},{19,3},{4,20},{20... | collective-permute-start | bytes 20 | tf_op jit(solution)/shard_map/ppermute | solution.py:489
  64.5 0.6 copy-start.9

commit v3 on v2

--- a/solution.py
+++ b/solution.py
@@ -8,10 +8,10 @@
 from jax.experimental.pallas import tpu as pltpu
 from jax.sharding import PartitionSpec as P
 
-CAP = 256
+CAP = 272
 UNROLL = 8
-POSITIONS = 9 * 128
-FIRST_MIB = 20
+POSITIONS = 10 * 128
+FIRST_MIB = 18
 LANES = 128
 MIB = 2**20
 BF16 = jnp.bfloat16
@@ -116,12 +116,20 @@
     lax.fori_loop(0, length // step // unroll, body, 0)
 
 
-def order_kernel(per_seed, counts_rel, me, self_ids, neighbour_ids, count_one, lists):
+def order_kernel(
+    per_seed, me, own, got_1, got_2, got_4, self_ids, neighbour_ids, count_one, lists, counts_rel
+):
     owners, seeds = counts_rel.shape
     fanout = neighbour_ids.shape[0]
-    per_owner = count_one.shape[1] // owners
+    per_owner = count_one.shape[0] // owners
     half = owners // 2
-    mine = me[0]
+    mine = me[4]
+    counts_rel[0:1, :] = own[...]
+    counts_rel[1:2, :] = got_1[...]
+    counts_rel[2:4, :] = got_2[...]
+    counts_rel[4:8, :] = got_4[...]
+    own_ids = self_ids[...].reshape(1, owners * per_owner)
+    ones = count_one[...].reshape(1, owners * per_owner)
     counts = jnp.concatenate(
         [counts_rel[pl.ds(jnp.bitwise_xor(mine, c), 1), :] for c in range(owners)], axis=0
     ).astype(F32)
@@ -141,7 +149,7 @@
     used = (t <= of_row) & (slot < CAP)
     slot = slot.astype(I32)
     keys = [
-        jnp.where(used[c : c + 1, :], count_one[:, c * per_owner : (c + 1) * per_owner], 0)
+        jnp.where(used[c : c + 1, :], ones[:, c * per_owner : (c + 1) * per_owner], 0)
         for c in range(owners)
     ]
     kinds = [
@@ -173,7 +181,7 @@
             lane = (iota((LANES, per_owner), 0) == spot_lo).astype(F32).astype(BF16)
             at_hi = (iota((16, per_owner), 0) == spot_hi).astype(F32)
             columns = slice(c * per_owner, (c + 1) * per_owner)
-            rows = [self_ids[:, columns]]
+            rows = [own_ids[:, columns]]
             rows += [neighbour_ids[k : k + 1, columns] for k in range(fanout)]
             rows += [half * CAP - (slot[c : c + 1, :] + i * CAP)]
             parts = []
@@ -207,16 +215,21 @@
         at = pl.multiple_of((h * (fanout + 3) + k) * block, block)
         return lists.at[pl.ds(at, length)]
 
+    last = fanout + 2
     copies = [
         pltpu.make_async_copy(piece(k, POSITIONS), ref, sems.at[k])
         for k, ref in enumerate(list(ids) + [places])
     ]
-    last = fanout + 2
-    return copies + [pltpu.make_async_copy(piece(last, LANES), begins, sems.at[last])]
-
-
-def look_up(fanout, table, ids, places, begins, self_rows, mean_rows):
+    copies.append(pltpu.make_async_copy(piece(last, LANES), begins, sems.at[last]))
+    start_all(copies[fanout + 1 :] + copies[: fanout + 1])
+    return copies
+
+
+def look_up(fanout, copies, table, ids, places, begins, self_rows, mean_rows):
+    for copy in [copies[0]] + copies[fanout + 1 :]:
+        copy.wait()
     for v in range(1, fanout + 1):
+        copies[v].wait()
         begin = begins[v - 1]
         end = begins[v]
 
@@ -242,34 +255,41 @@
                 ref[z, :, part * LANES : (part + 1) * LANES] = block
 
 
+def stage(source, staged, sems):
+    blocks, _, part = staged.shape
+    copies = [
+        pltpu.make_async_copy(source.at[:, pl.ds(b * part, part)], staged.at[b], sems.at[b])
+        for b in range(blocks)
+    ]
+    start_all(copies)
+    return copies
+
+
 def first_kernel(
-    fanout, me, lists, features, other, weight, table, keep, send, *scratch
+    fanout, me, lists, features, other, self_one, neigh_one, table, keep, send, *scratch
 ):
     ids = scratch[: fanout + 1]
-    places, begins, self_rows, mean_rows, sems, staged, staged_sems = scratch[fanout + 1 :]
+    places, begins, self_rows, mean_rows, sems = scratch[fanout + 1 : -4]
+    staged_0, sems_0, staged_1, sems_1 = scratch[-4:]
     width, length = other.shape
     x, h, rep = me[0], me[1], me[2]
-    blocks, _, part = staged.shape
     stages = [
-        pltpu.make_async_copy(
-            features.at[:, pl.ds(b * part, part)], staged.at[b], staged_sems.at[b]
-        )
-        for b in range(blocks)
+        (stage(features, staged_0, sems_0), staged_0, rep * length),
+        (stage(other, staged_1, sems_1), staged_1, (1 - rep) * length),
     ]
-    start_all(stages)
     copies = list_copies(fanout, h, lists, ids, places, begins, sems)
-    start_all(copies)
     self_rows[...] = jnp.zeros_like(self_rows)
     mean_rows[...] = jnp.zeros_like(mean_rows)
-    turn(other, table, pl.multiple_of((1 - rep) * length, length))
-    for b, stage in enumerate(stages):
-        stage.wait()
-        turn(staged.at[b], table, pl.multiple_of(rep * length + b * part, part))
-    for copy in copies:
-        copy.wait()
-    look_up(fanout, table, ids, places, begins, self_rows, mean_rows)
+    send[2, :, :] = jnp.zeros(send.shape[1:], BF16)
+    send[2, 0:width, :] = self_one[...]
+    send[2, LANES : LANES + width, :] = neigh_one[...]
+    for parts, staged, base in stages:
+        length_of = staged.shape[2]
+        for b, part in enumerate(parts):
+            part.wait()
+            turn(staged.at[b], table, pl.multiple_of(base + b * length_of, length_of))
+    look_up(fanout, copies, table, ids, places, begins, self_rows, mean_rows)
     write_out(x, width, self_rows, mean_rows, keep, send)
-    send[2, :, :] = weight[...]
 
 
 def second_kernel(fanout, width, me, lists, table, keep_hbm, send_hbm, *scratch):
@@ -277,12 +297,9 @@
     places, begins, self_rows, mean_rows, sems, keep, send, out_sems = scratch[fanout + 1 :]
     x, h = me[0], 1 - me[1]
     copies = list_copies(fanout, h, lists, ids, places, begins, sems)
-    start_all(copies)
     self_rows[...] = jnp.zeros_like(self_rows)
     mean_rows[...] = jnp.zeros_like(mean_rows)
-    for copy in copies:
-        copy.wait()
-    look_up(fanout, table, ids, places, begins, self_rows, mean_rows)
+    look_up(fanout, copies, table, ids, places, begins, self_rows, mean_rows)
     write_out(x, width, self_rows, mean_rows, keep, send)
     outs = [
         pltpu.make_async_copy(send, send_hbm, out_sems.at[0]),
@@ -293,14 +310,23 @@
         copy.wait()
 
 
-def project_kernel(me, keep, got, weight, weight_got, out_0, out_1):
-    zl = me[3]
-    theirs = weight_got[2]
-    for which, out in ((zl, out_0), (1 - zl, out_1)):
+def project(zl, keep, got, weight, weight_got, outs):
+    for which, out in ((zl, outs[0]), (1 - zl, outs[1])):
         out[...] = (
-            jnp.dot(keep[which], weight[...], preferred_element_type=F32)
-            + jnp.dot(got[which], theirs, preferred_element_type=F32)
+            jnp.dot(keep[which], weight[2, 0 : 2 * LANES, :], preferred_element_type=F32)
+            + jnp.dot(got[which], weight_got[2, 0 : 2 * LANES, :], preferred_element_type=F32)
         ).astype(out.dtype)
+
+
+def project_far_kernel(me, keep, got, sent, later, out_0, out_1, loaded, sem):
+    copy = pltpu.make_async_copy(later, loaded, sem)
+    copy.start()
+    project(me[3], keep, got, sent, got, (out_0, out_1))
+    copy.wait()
+
+
+def project_near_kernel(me, keep, got, weight, weight_got, out_0, out_1):
+    project(me[3], keep, got, weight, weight_got, (out_0, out_1))
 
 
 def last_kernel(
@@ -336,15 +362,17 @@
     return jax.ShapeDtypeStruct(dims, dtype)
 
 
-def order_call(per_seed, counts_rel, col, self_ids, neighbour_ids, count_one):
+def order_call(per_seed, me, own, got, self_ids, neighbour_ids, count_one):
+    owners = sum(x.shape[0] for x in (own, *got))
     lists = pl.pallas_call(
         functools.partial(order_kernel, per_seed),
         out_shape=shape((2, neighbour_ids.shape[0] + 3, 16, LANES), I32),
-        in_specs=[VMEM, SMEM, VMEM, VMEM, VMEM],
+        in_specs=[SMEM] + [VMEM] * 7,
         out_specs=VMEM,
+        scratch_shapes=[pltpu.VMEM((owners, own.shape[1]), I32)],
         compiler_params=params(10),
         name="order",
-    )(counts_rel, col, self_ids, neighbour_ids, count_one)
+    )(me, own, *got, self_ids, neighbour_ids, count_one)
     return lists.reshape(-1)
 
 
@@ -357,24 +385,22 @@
     )
 
 
-def first_call(fanout, me, lists, features, other, weight):
+def first_call(fanout, me, lists, features, other, self_one, neigh_one):
+    width, length = features.shape
+    staging = [pltpu.VMEM((4, width, length // 4), BF16), pltpu.SemaphoreType.DMA((4,))]
     return pl.pallas_call(
         functools.partial(first_kernel, fanout),
         out_shape=(
-            shape((2 * features.shape[1], LANES), F32),
+            shape((2 * length, LANES), F32),
             shape((2, CAP, 2 * LANES), BF16),
             shape((3, CAP, 2 * LANES), BF16),
         ),
-        in_specs=[SMEM, ANY, ANY, VMEM, VMEM],
+        in_specs=[SMEM, ANY, ANY, ANY, VMEM, VMEM],
         out_specs=(VMEM, VMEM, VMEM),
-        scratch_shapes=list_scratch(fanout)
-        + [
-            pltpu.VMEM((4, features.shape[0], features.shape[1] // 4), BF16),
-            pltpu.SemaphoreType.DMA((4,)),
-        ],
+        scratch_shapes=list_scratch(fanout) + staging + staging,
         compiler_params=params(FIRST_MIB),
         name="first_half",
-    )(me, lists, features, other, weight)
+    )(me, lists, features, other, self_one, neigh_one)
 
 
 def second_call(fanout, width, me, lists, table):
@@ -393,15 +419,28 @@
     )(me, lists, table)
 
 
-def project_call(me, keep, got, weight, weight_got, kinds):
-    hidden = weight.shape[1]
+def project_far_call(me, keep, got, sent, later):
+    part = shape((CAP, sent.shape[2]), BF16)
     return pl.pallas_call(
-        project_kernel,
-        out_shape=tuple(shape((CAP, hidden), kind) for kind in kinds),
+        project_far_kernel,
+        out_shape=(part, part, shape(later.shape, BF16)),
+        in_specs=[SMEM, VMEM, VMEM, VMEM, ANY],
+        out_specs=(VMEM, VMEM, VMEM),
+        scratch_shapes=[pltpu.SemaphoreType.DMA],
+        compiler_params=params(10),
+        name="project_far",
+    )(me, keep, got, sent, later)
+
+
+def project_near_call(me, keep, got, weight, weight_got):
+    dims = (CAP, weight.shape[2])
+    return pl.pallas_call(
+        project_near_kernel,
+        out_shape=(shape(dims, F32), shape(dims, BF16)),
         in_specs=[SMEM, VMEM, VMEM, VMEM, VMEM],
         out_specs=(VMEM, VMEM),
         compiler_params=params(10),
-        name="project",
+        name="project_near",
     )(me, keep, got, weight, weight_got)
 
 
@@ -442,40 +481,31 @@
     col = lax.axis_index("col")
     rep = lax.axis_index("rep")
     z = col // 2
-    me = jnp.stack([col % 2, 1 - z // 2, rep, z % 2]).astype(I32)
+    me = jnp.stack([col % 2, 1 - z // 2, rep, z % 2, col]).astype(I32)
 
     def across(value, bit):
         return lax.ppermute(value, "col", [(i, i ^ bit) for i in range(owners)])
 
-    def swapped(value):
-        return lax.ppermute(value, "rep", [(0, 1), (1, 0)])
-
-    other = swapped(features)
-    weight = jnp.concatenate(
-        [jnp.pad(w, ((0, LANES - width), (0, 0))) for w in (self_one, neigh_one)], axis=0
-    )
-    counts = count_two[None, :]
-    for bit in (1, 2, 4):
-        counts = jnp.concatenate([counts, across(counts, bit)], axis=0)
-    lists = order_call(
-        per_seed,
-        counts,
-        col.reshape(1).astype(I32),
-        self_ids[None, :],
-        neighbour_ids,
-        count_one[None, :],
-    )
-    table, keep_far, send_far = first_call(fanout, me, lists, features, other, weight)
+    other = lax.ppermute(features, "rep", [(0, 1), (1, 0)])
+    own = count_two[None, :]
+    got_1 = across(own, 1)
+    got_2 = across(jnp.concatenate([own, got_1], axis=0), 2)
+    got_4 = across(jnp.concatenate([own, got_1, got_2], axis=0), 4)
+    got = (got_1, got_2, got_4)
+    lists = order_call(per_seed, me, own, got, self_ids, neighbour_ids, count_one)
+    table, keep_far, send_far = first_call(
+        fanout, me, lists, features, other, self_one, neigh_one
+    )
     got_far = across(send_far, 1)
     keep_near, send_near = second_call(fanout, width, me, lists, table)
-    far = project_call(me, keep_far, got_far, weight, got_far, (BF16, BF16))
     got_near = across(send_near, 1)
-    got = [across(far[0], 4), across(far[1], 6)]
-    near = project_call(me, keep_near, got_near, weight, got_far, (F32, BF16))
-    got.append(across(near[1], 2))
+    far_0, far_1, keep_near = project_far_call(me, keep_far, got_far, send_far, keep_near)
+    far = [across(far_0, 4), across(far_1, 6)]
+    near_0, near_1 = project_near_call(me, keep_near, got_near, send_far, got_far)
+    far.append(across(near_1, 2))
     fast = last_call(
-        near[0],
-        *got,
+        near_0,
+        *far,
         count_two[:, None],
         bias_one[None, :],
         self_two,
@@ -484,11 +514,9 @@
         out_weight,
         out_bias[None, :],
     )
-    most = jnp.max(jnp.sum(counts + 1, axis=1)).reshape(1)
-    most = jnp.maximum(most, swapped(most))
-    most = jnp.maximum(most, lax.ppermute(most, "groups", [(0, 1), (1, 0)]))
+    most = functools.reduce(jnp.maximum, [jnp.max(jnp.sum(x + 1, axis=1)) for x in (own, *got)])
     return lax.cond(
-        most[0] > CAP,
+        most > CAP,
         lambda: general(
             other,
             features,

time: 65.9 us -> 65 us (0.986)
  waiting for transfers between devices: 5.97 us -> 10.5 us
  starting transfers between devices: 19 us -> 14.7 us
  local copies, waits for them, and re-layouts: 3.24 us -> 1.89 us
  between operations: 2.07 us -> 2.83 us
    ppermute x8, waiting for transfers between devices: 3.61 us -> 10.5 us  [across(): return lax.ppermute(value, 'col', [(i, i ^ bit) for i in range(owners)])]
    ppermute x3 -> x1, starting transfers between devices: 3.19 us -> 0.45 us  [main(): other = lax.ppermute(features, 'rep', [(0, 1), (1, 0)])]
    ppermute x3 -> x1, waiting for transfers between devices: 2.36 us -> 0.01 us  [main(): other = lax.ppermute(features, 'rep', [(0, 1), (1, 0)])]
    concatenate x4 -> x2, other arithmetic: 2.94 us -> 1.33 us  [the longest x1 0.66 us: main(): got_4 = across(jnp.concatenate([own, got_1, got_2], axis=0), 4)]
    ppermute x8, starting transfers between devices: 15.8 us -> 14.2 us  [across(): return lax.ppermute(value, 'col', [(i, i ^ bit) for i in range(owners)])]
    reduce_sum x0 -> x4, other arithmetic: none -> 1.51 us  [main(): jnp.sum(x + 1, axis=1)]
    broadcast_in_dim x2 -> x0, local copies, waits for them, and re-layouts: 1.43 us -> none  [the longest x1 0.72 us: main(): self_ids[None, :]]
  transfers between devices with their start and end apart: 11 -> 9, of which waited for: 6 -> 7; matrix products, arithmetic and copies ran while one was open for 8% -> 7% of each run, Pallas kernels for 21% -> 20%
where the time goes in v3:
time: 65 us; the launch traced here: 64.9 us
  Pallas kernels  30.7 us (47%)
  starting transfers between devices  14.7 us (23%)
  waiting for transfers between devices  10.5 us (16%)
  other arithmetic  4.12 us (6%)
  between operations  2.83 us (4%)
  local copies, waits for them, and re-layouts  1.89 us (3%)
    pallas_call x1, Pallas kernels, first_call(): pl.pallas_call(functools.partial(first_kernel, fanout), out_shape=(shape(...  16.2 us
    ppermute x8, starting transfers between devices, across(): return lax.ppermute(value, 'col', [(i, i ^ bit) for i in range(owners)])  14.2 us
    ppermute x8, waiting for transfers between devices, across(): return lax.ppermute(value, 'col', [(i, i ^ bit) for i in range(owners)])  10.5 us
    pallas_call x1, Pallas kernels, second_call(): pl.pallas_call(functools.partial(second_kernel, fanout, width), out_shape...  9.34 us
    pallas_call x1, Pallas kernels, order_call(): pl.pallas_call(functools.partial(order_kernel, per_seed), out_shape=shape...  2.77 us
    unnamed x29, local copies, waits for them, and re-layouts  1.72 us
    reduce_sum x4, other arithmetic, main(): jnp.sum(x + 1, axis=1)  1.51 us
  transfers between devices with their start and end apart: 9, of which 7 were waited for; matrix products, arithmetic and copies ran while one was open for 7% of the time, Pallas kernels for 20%

profile of v3, /device:TPU:0, one launch (start us, length us, event | category | flops | bytes accessed | tf_op | source)
XLA Modules:
  0.0 64.9 jit_solution(2485465139637912420)
XLA Ops:
  0.0 0.5 collective-permute-start.3
  0.5 2.5 %collective-permute-start = (s32[1,32]{1,0:T(1,128)}, s32[1,32]{1,0:T(1,128)S(1)}, u32[]{:S(2)}, u32[]{:S(2)}) collective-permute-start(s32[1,32]{1,0:T(1,128)} %bitcast.63), channel_id=1, source_target_pairs={{0,2},{2,0},{4,6},{6,4},{8,10},{10,8},{12,14},{14,12},{1,3},{3,1},... | collective-permute-start | bytes 392 | tf_op jit(solution)/shard_map/ppermute | solution.py:487
  2.9 1.7 %collective-permute-done.got_1 = s32[1,32]{1,0:T(1,128)S(1)} collective-permute-done((s32[1,32]{1,0:T(1,128)}, s32[1,32]{1,0:T(1,128)S(1)}, u32[]{:S(2)}, u32[]{:S(2)}) %collective-permute-start) | collective-permute-done | bytes 160 | tf_op jit(solution)/shard_map/ppermute | solution.py:487
  4.6 0.7 %pad_add_fusion.1 = s32[2,32]{1,0:T(2,128)S(1)} fusion(s32[1,32]{1,0:T(1,128)S(1)} %collective-permute-done.got_1, s32[1,32]{1,0:T(1,128)} %bitcast.64), kind=kLoop, calls=%fused_computation.40 | loop fusion | flops 64 | bytes 512 | tf_op jit(solution)/shard_map/concatenate | solution.py:492
  5.3 2.1 %collective-permute-start.1 = (s32[2,32]{1,0:T(2,128)S(1)}, s32[2,32]{1,0:T(2,128)S(1)}, u32[]{:S(2)}, u32[]{:S(2)}) collective-permute-start(s32[2,32]{1,0:T(2,128)S(1)} %pad_add_fusion.1), channel_id=1, source_target_pairs={{0,4},{2,6},{4,0},{6,2},{8,12},{10,14},{12,8},{14,10},{1,5},{3,7},... | collective-permute-start | bytes 776 | tf_op jit(solution)/shard_map/ppermute | solution.py:487
  7.4 1.5 %collective-permute-done.1.got_2 = s32[2,32]{1,0:T(2,128)S(1)} collective-permute-done((s32[2,32]{1,0:T(2,128)S(1)}, s32[2,32]{1,0:T(2,128)S(1)}, u32[]{:S(2)}, u32[]{:S(2)}) %collective-permute-start.1) | collective-permute-done | bytes 288 | tf_op jit(solution)/shard_map/ppermute | solution.py:487
  8.9 0.7 %pad_add_fusion = s32[4,32]{1,0:T(4,128)S(1)} fusion(s32[2,32]{1,0:T(2,128)S(1)} %collective-permute-done.1.got_2, s32[1,32]{1,0:T(1,128)S(1)} %collective-permute-done.got_1, s32[1,32]{1,0:T(1,128)} %bitcast.65), kind=kLoop, calls=%fused_computation.38 | loop fusion | flops 256 | bytes 1024 | tf_op jit(solution)/shard_map/concatenate | solution.py:493
  9.6 3.0 %collective-permute-start.2 = (s32[4,32]{1,0:T(4,128)S(1)}, s32[4,32]{1,0:T(4,128)S(1)}, u32[]{:S(2)}, u32[]{:S(2)}) collective-permute-start(s32[4,32]{1,0:T(4,128)S(1)} %pad_add_fusion), channel_id=1, source_target_pairs={{0,8},{2,10},{4,12},{6,14},{8,0},{10,2},{12,4},{14,6},{1,9},{3,11}... | collective-permute-start | bytes 1544 | tf_op jit(solution)/shard_map/ppermute | solution.py:487
  12.6 0.1 stack.31.me
  12.7 1.5 %collective-permute-done.2.got_4 = s32[4,32]{1,0:T(4,128)S(1)} collective-permute-done((s32[4,32]{1,0:T(4,128)S(1)}, s32[4,32]{1,0:T(4,128)S(1)}, u32[]{:S(2)}, u32[]{:S(2)}) %collective-permute-start.2) | collective-permute-done | bytes 544 | tf_op jit(solution)/shard_map/ppermute | solution.py:487
  14.2 2.8 %order.1 = s32[2,18,16,128]{3,2,1,0:T(8,128)S(1)} custom-call(s32[5]{0:T(128)S(1)} %stack.31.me, s32[1,32]{1,0:T(1,128)} %bitcast.66, s32[1,32]{1,0:T(1,128)S(1)} %collective-permute-done.got_1, s32[2,32]{1,0:T(2,128)S(1)} %collective-permute-done.1.got_2, s32[4,32]{1,0:T(4,128)S(1)} %collective-permute-done.2.got_4, s32[2816]{0:T(1024)} %self_ids.1, ...), custom_call_target="tpu_custom_call" | custom-call | tf_op jit(solution)/shard_map/order/pallas_call | solution.py:367
  16.9 0.0 collective-permute-done.3.other
  17.0 16.2 %first_half.1 = (f32[65536,128]{1,0:T(8,128)S(1)}, bf16[2,272,256]{2,1,0:T(8,128)(2,1)S(1)}, bf16[3,272,256]{2,1,0:T(8,128)(2,1)S(1)}) custom-call(s32[5]{0:T(128)S(1)} %stack.31.me, s32[73728]{0:T(1024)S(1)} %bitcast.54, bf16[96,32768]{1,0:T(8,128)(2,1)} %features.1, bf16[96,32768]{1,0:T(8,128)(2,1)} %collective-permute-done.3.other, ...), custom_call_target="tpu_custom_call" | custom-call | tf_op jit(solution)/shard_map/first_half/pallas_call | solution.py:391
  33.1 1.9 %collective-permute-start.4 = (bf16[3,272,256]{2,1,0:T(8,128)(2,1)S(1)}, bf16[3,272,256]{2,1,0:T(8,128)(2,1)S(1)}, u32[]{:S(2)}, u32[]{:S(2)}) collective-permute-start(bf16[3,272,256]{2,1,0:T(8,128)(2,1)S(1)} %get-tuple-element.62.sent.weight), channel_id=1, source_target_pairs={{0,2},{2,0},{4,6},{6,4},{8,10},{10,8},{12,14},{14,12},{1,3},{3,1},... | collective-permute-start | bytes 1253384 | tf_op jit(solution)/shard_map/ppermute | solution.py:487
  35.0 0.0 copy-start.4
  35.0 0.0 copy-start.10
  35.0 0.0 copy-start.1
  35.0 0.0 copy-start.2
  35.0 0.0 copy-start.3
  35.0 0.0 copy-start.5
  35.1 0.0 copy-start.6
  35.1 0.0 copy-start.7
  35.1 0.0 copy-start.8
  35.1 0.0 copy-start.11
  35.1 0.0 copy-start.12
  35.1 0.0 copy-start.13
  35.1 9.3 %second_half.1 = (bf16[2,272,256]{2,1,0:T(8,128)(2,1)}, bf16[2,272,256]{2,1,0:T(8,128)(2,1)}) custom-call(s32[5]{0:T(128)S(1)} %stack.31.me, s32[73728]{0:T(1024)S(1)} %bitcast.55, f32[65536,128]{1,0:T(8,128)S(1)} %get-tuple-element.63.table), custom_call_target="tpu_custom_call" | custom-call | tf_op jit(solution)/shard_map/second_half/pallas_call | solution.py:409
  44.5 0.3 collective-permute-start.5
  44.7 0.0 copy-done.4
  44.7 0.1 copy.37.out_weight
  44.8 0.0 copy-done.10
  44.9 0.1 copy.36.counts
  44.9 0.6 add_reduce_fusion.3
  45.6 0.7 %add_reduce_fusion.2 = s32[]{:T(128)} fusion(s32[1,32]{1,0:T(1,128)S(1)} %collective-permute-done.got_1), kind=kLoop, calls=%fused_computation.42 | loop fusion | flops 63 | bytes 132 | tf_op jit(solution)/shard_map/reduce_sum | solution.py:517
  47.5 0.0 collective-permute-done.4.got.weight_got
  47.5 0.0 copy-start
  47.5 0.9 %copy-done = bf16[2,272,256]{2,1,0:T(8,128)(2,1)S(1)} copy-done((bf16[2,272,256]{2,1,0:T(8,128)(2,1)S(1)}, bf16[2,272,256]{2,1,0:T(8,128)(2,1)}, u32[]{:S(2)}) %copy-start) | copy-done | bytes 278552
  48.5 0.9 %project_far.1 = (bf16[272,256]{1,0:T(8,128)(2,1)S(1)}, bf16[272,256]{1,0:T(8,128)(2,1)S(1)}, bf16[2,272,256]{2,1,0:T(8,128)(2,1)S(1)}) custom-call(s32[5]{0:T(128)S(1)} %stack.31.me, bf16[2,272,256]{2,1,0:T(8,128)(2,1)S(1)} %get-tuple-element.61.keep, bf16[3,272,256]{2,1,0:T(8,128)(2,1)S(1)} %collective-permute-done.4.got.weight_got, ...), custom_call_target="tpu_custom_call" | custom-call | tf_op jit(solution)/shard_map/project_far/pallas_call | solution.py:424
  49.4 1.9 %collective-permute-done.5.got = bf16[2,272,256]{2,1,0:T(8,128)(2,1)S(1)} collective-permute-done((bf16[2,272,256]{2,1,0:T(8,128)(2,1)}, bf16[2,272,256]{2,1,0:T(8,128)(2,1)S(1)}, u32[]{:S(2)}, u32[]{:S(2)}) %collective-permute-start.5) | collective-permute-done | bytes 278560 | tf_op jit(solution)/shard_map/ppermute | solution.py:487
  51.3 0.8 %project_near.1 = (f32[272,256]{1,0:T(8,128)S(1)}, bf16[272,256]{1,0:T(8,128)(2,1)S(1)}) custom-call(s32[5]{0:T(128)S(1)} %stack.31.me, bf16[2,272,256]{2,1,0:T(8,128)(2,1)S(1)} %get-tuple-element.65.keep, bf16[2,272,256]{2,1,0:T(8,128)(2,1)S(1)} %collective-permute-done.5.got, bf16[3,272,256]{2,1,0:T(8,128)(2,1)S(1)} %get-tuple-element.62.sent.weight, ...), custom_call_target="tpu_custom_call" | custom-call | tf_op jit(solution)/shard_map/project_near/pallas_call | solution.py:437
  52.2 1.6 %collective-permute-start.8 = (bf16[272,256]{1,0:T(8,128)(2,1)S(1)}, bf16[272,256]{1,0:T(8,128)(2,1)S(1)}, u32[]{:S(2)}, u32[]{:S(2)}) collective-permute-start(bf16[272,256]{1,0:T(8,128)(2,1)S(1)} %get-tuple-element.70), channel_id=1, source_target_pairs={{0,4},{2,6},{4,0},{6,2},{8,12},{10,14},{12,8},{14,10},{1,5},{3,7},... | collective-permute-start | bytes 417800 | tf_op jit(solution)/shard_map/ppermute | solution.py:487
  53.8 2.6 %collective-permute-start.6 = (bf16[272,256]{1,0:T(8,128)(2,1)S(1)}, bf16[272,256]{1,0:T(8,128)(2,1)S(1)}, u32[]{:S(2)}, u32[]{:S(2)}) collective-permute-start(bf16[272,256]{1,0:T(8,128)(2,1)S(1)} %get-tuple-element.68), channel_id=1, source_target_pairs={{0,8},{2,10},{4,12},{6,14},{8,0},{10,2},{12,4},{14,6},{1,9},{3,11}... | collective-permute-start | bytes 417800 | tf_op jit(solution)/shard_map/ppermute | solution.py:487
  56.4 0.2 collective-permute-start.7
  56.6 0.1 add_reduce_fusion.1
  56.7 0.6 reduce_max.16
  58.0 0.1 add_reduce_fusion
  58.1 0.6 reduce_max.20
  59.4 0.2 collective-permute-done.8.c
  59.6 1.9 %collective-permute-done.6.a = bf16[272,256]{1,0:T(8,128)(2,1)S(1)} collective-permute-done((bf16[272,256]{1,0:T(8,128)(2,1)S(1)}, bf16[272,256]{1,0:T(8,128)(2,1)S(1)}, u32[]{:S(2)}, u32[]{:S(2)}) %collective-permute-start.6) | collective-permute-done | bytes 139296 | tf_op jit(solution)/shard_map/ppermute | solution.py:487
  61.5 1.8 %collective-permute-done.7.b = bf16[272,256]{1,0:T(8,128)(2,1)S(1)} collective-permute-done((bf16[272,256]{1,0:T(8,128)(2,1)S(1)}, bf16[272,256]{1,0:T(8,128)(2,1)S(1)}, u32[]{:S(2)}, u32[]{:S(2)}) %collective-permute-start.7) | collective-permute-done | bytes 139296 | tf_op jit(solution)/shard_map/ppermute | solution.py:487
  63.3 0.0 copy-done.1
  63.3 0.0 copy-done.2
  63.4 0.0 copy-done.3
  63.4 0.0 copy-done.5
  63.4 0.0 copy-done.6
  63.4 0.0 copy-done.7
  63.4 0.0 copy-done.8
  63.4 0.0 copy-done.11
  63.4 0.0 copy-done.12
  63.4 0.0 copy-done.13
  63.4 0.7 %layer_two.1 = f32[32,153]{1,0:T(8,128)S(1)} custom-call(f32[272,256]{1,0:T(8,128)S(1)} %get-tuple-element.67.mine, bf16[272,256]{1,0:T(8,128)(2,1)S(1)} %collective-permute-done.6.a, bf16[272,256]{1,0:T(8,128)(2,1)S(1)} %collective-permute-done.7.b, bf16[272,256]{1,0:T(8,128)(2,1)S(1)} %collective-permute-done.8.c, s32[32,1]{1,0:T(8,128)S(1)} %copy.36.counts, ...), custom_call_target="tpu_custom_call" | custom-call | tf_op jit(solution)/shard_map/layer_two/pallas_call | solution.py:450
  64.1 0.1 conditional.1
  64.3 0.0 copy-start.9
  64.3 0.6 copy-done.9
Async XLA Ops:
  0.0 16.9 %collective-permute-start.3 = (bf16[96,32768]{1,0:T(8,128)(2,1)}, bf16[96,32768]{1,0:T(8,128)(2,1)}, u32[]{:S(2)}, u32[]{:S(2)}) collective-permute-start(bf16[96,32768]{1,0:T(8,128)(2,1)} %features.1), channel_id=1, source_target_pairs={{0,1},{1,0},{2,3},{3,2},{4,5},{5,4},{6,7},{7,6},{8,9},{9,8},{10,11... | collective-permute-start | bytes 18874376 | tf_op jit(solution)/shard_map/ppermute | solution.py:489
  0.5 4.1 %collective-permute-start = (s32[1,32]{1,0:T(1,128)}, s32[1,32]{1,0:T(1,128)S(1)}, u32[]{:S(2)}, u32[]{:S(2)}) collective-permute-start(s32[1,32]{1,0:T(1,128)} %bitcast.63), channel_id=1, source_target_pairs={{0,2},{2,0},{4,6},{6,4},{8,10},{10,8},{12,14},{14,12},{1,3},{3,1},... | collective-permute-start | bytes 392 | tf_op jit(solution)/shard_map/ppermute | solution.py:487
  5.3 3.7 %collective-permute-start.1 = (s32[2,32]{1,0:T(2,128)S(1)}, s32[2,32]{1,0:T(2,128)S(1)}, u32[]{:S(2)}, u32[]{:S(2)}) collective-permute-start(s32[2,32]{1,0:T(2,128)S(1)} %pad_add_fusion.1), channel_id=1, source_target_pairs={{0,4},{2,6},{4,0},{6,2},{8,12},{10,14},{12,8},{14,10},{1,5},{3,7},... | collective-permute-start | bytes 776 | tf_op jit(solution)/shard_map/ppermute | solution.py:487
  9.6 4.6 %collective-permute-start.2 = (s32[4,32]{1,0:T(4,128)S(1)}, s32[4,32]{1,0:T(4,128)S(1)}, u32[]{:S(2)}, u32[]{:S(2)}) collective-permute-start(s32[4,32]{1,0:T(4,128)S(1)} %pad_add_fusion), channel_id=1, source_target_pairs={{0,8},{2,10},{4,12},{6,14},{8,0},{10,2},{12,4},{14,6},{1,9},{3,11}... | collective-permute-start | bytes 1544 | tf_op jit(solution)/shard_map/ppermute | solution.py:487
  33.1 14.4 %collective-permute-start.4 = (bf16[3,272,256]{2,1,0:T(8,128)(2,1)S(1)}, bf16[3,272,256]{2,1,0:T(8,128)(2,1)S(1)}, u32[]{:S(2)}, u32[]{:S(2)}) collective-permute-start(bf16[3,272,256]{2,1,0:T(8,128)(2,1)S(1)} %get-tuple-element.62.sent.weight), channel_id=1, source_target_pairs={{0,2},{2,0},{4,6},{6,4},{8,10},{10,8},{12,14},{14,12},{1,3},{3,1},... | collective-permute-start | bytes 1253384 | tf_op jit(solution)/shard_map/ppermute | solution.py:487
  35.0 9.7 %copy-start.4 = (bf16[256,153]{0,1:T(8,128)(2,1)S(1)}, bf16[256,153]{0,1:T(8,128)(2,1)}, u32[]{:S(2)}) copy-start(bf16[256,153]{0,1:T(8,128)(2,1)} %param.26) | copy-start | bytes 235012
  35.0 9.8 %copy-start.10 = (s32[32]{0:T(128)S(1)}, s32[32]{0:T(128)}, u32[]{:S(2)}) copy-start(s32[32]{0:T(128)} %param.19) | copy-start | bytes 388
  35.0 28.3 %copy-start.1 = (s32[15,2816]{1,0:T(8,128)S(1)}, s32[15,2816]{1,0:T(8,128)}, u32[]{:S(2)}) copy-start(s32[15,2816]{1,0:T(8,128)} %neighbour_ids.1) | copy-start | bytes 506884
  35.0 28.3 %copy-start.2 = (bf16[256,256]{1,0:T(8,128)(2,1)S(1)}, bf16[256,256]{1,0:T(8,128)(2,1)}, u32[]{:S(2)}) copy-start(bf16[256,256]{1,0:T(8,128)(2,1)} %neigh_two.1) | copy-start | bytes 393220
  35.0 28.3 %copy-start.3 = (bf16[256,256]{1,0:T(8,128)(2,1)S(1)}, bf16[256,256]{1,0:T(8,128)(2,1)}, u32[]{:S(2)}) copy-start(bf16[256,256]{1,0:T(8,128)(2,1)} %self_two.1) | copy-start | bytes 393220
  35.0 28.3 %copy-start.5 = (bf16[96,256]{1,0:T(8,128)(2,1)S(1)}, bf16[96,256]{1,0:T(8,128)(2,1)}, u32[]{:S(2)}) copy-start(bf16[96,256]{1,0:T(8,128)(2,1)} %self_one.1) | copy-start | bytes 147460
  35.1 28.3 %copy-start.6 = (bf16[96,256]{1,0:T(8,128)(2,1)S(1)}, bf16[96,256]{1,0:T(8,128)(2,1)}, u32[]{:S(2)}) copy-start(bf16[96,256]{1,0:T(8,128)(2,1)} %neigh_one.1) | copy-start | bytes 147460
  35.1 28.3 %copy-start.7 = (s32[2816]{0:T(1024)S(1)}, s32[2816]{0:T(1024)}, u32[]{:S(2)}) copy-start(s32[2816]{0:T(1024)} %self_ids.1) | copy-start | bytes 33796
  35.1 28.3 %copy-start.8 = (s32[2816]{0:T(1024)S(1)}, s32[2816]{0:T(1024)}, u32[]{:S(2)}) copy-start(s32[2816]{0:T(1024)} %count_one.1) | copy-start | bytes 33796
  35.1 28.3 %copy-start.11 = (f32[256]{0:T(256)S(1)}, f32[256]{0:T(256)}, u32[]{:S(2)}) copy-start(f32[256]{0:T(256)} %param.25) | copy-start | bytes 3076
  35.1 28.3 %copy-start.12 = (f32[153]{0:T(256)S(1)}, f32[153]{0:T(256)}, u32[]{:S(2)}) copy-start(f32[153]{0:T(256)} %param.27) | copy-start | bytes 1840
  35.1 28.3 %copy-start.13 = (f32[256]{0:T(256)S(1)}, f32[256]{0:T(256)}, u32[]{:S(2)}) copy-start(f32[256]{0:T(256)} %param.22) | copy-start | bytes 3076
  44.5 6.8 %collective-permute-start.5 = (bf16[2,272,256]{2,1,0:T(8,128)(2,1)}, bf16[2,272,256]{2,1,0:T(8,128)(2,1)S(1)}, u32[]{:S(2)}, u32[]{:S(2)}) collective-permute-start(bf16[2,272,256]{2,1,0:T(8,128)(2,1)} %get-tuple-element.66), channel_id=1, source_target_pairs={{0,2},{2,0},{4,6},{6,4},{8,10},{10,8},{12,14},{14,12},{1,3},{3,1},... | collective-permute-start | bytes 835592 | tf_op jit(solution)/shard_map/ppermute | solution.py:487
  47.5 1.0 %copy-start = (bf16[2,272,256]{2,1,0:T(8,128)(2,1)S(1)}, bf16[2,272,256]{2,1,0:T(8,128)(2,1)}, u32[]{:S(2)}) copy-start(bf16[2,272,256]{2,1,0:T(8,128)(2,1)} %get-tuple-element.64.later) | copy-start | bytes 835588
  52.2 7.5 %collective-permute-start.8 = (bf16[272,256]{1,0:T(8,128)(2,1)S(1)}, bf16[272,256]{1,0:T(8,128)(2,1)S(1)}, u32[]{:S(2)}, u32[]{:S(2)}) collective-permute-start(bf16[272,256]{1,0:T(8,128)(2,1)S(1)} %get-tuple-element.70), channel_id=1, source_target_pairs={{0,4},{2,6},{4,0},{6,2},{8,12},{10,14},{12,8},{14,10},{1,5},{3,7},... | collective-permute-start | bytes 417800 | tf_op jit(solution)/shard_map/ppermute | solution.py:487
  53.8 7.7 %collective-permute-start.6 = (bf16[272,256]{1,0:T(8,128)(2,1)S(1)}, bf16[272,256]{1,0:T(8,128)(2,1)S(1)}, u32[]{:S(2)}, u32[]{:S(2)}) collective-permute-start(bf16[272,256]{1,0:T(8,128)(2,1)S(1)} %get-tuple-element.68), channel_id=1, source_target_pairs={{0,8},{2,10},{4,12},{6,14},{8,0},{10,2},{12,4},{14,6},{1,9},{3,11}... | collective-permute-start | bytes 417800 | tf_op jit(solution)/shard_map/ppermute | solution.py:487
  56.4 7.0 %collective-permute-start.7 = (bf16[272,256]{1,0:T(8,128)(2,1)S(1)}, bf16[272,256]{1,0:T(8,128)(2,1)S(1)}, u32[]{:S(2)}, u32[]{:S(2)}) collective-permute-start(bf16[272,256]{1,0:T(8,128)(2,1)S(1)} %get-tuple-element.69), channel_id=1, source_target_pairs={{0,12},{2,14},{4,8},{6,10},{8,4},{10,6},{12,0},{14,2},{1,13},{3,15... | collective-permute-start | bytes 417800 | tf_op jit(solution)/shard_map/ppermute | solution.py:487
  64.3 0.6 copy-start.9

commit v4 on v3

--- a/solution.py
+++ b/solution.py
@@ -11,7 +11,7 @@
 CAP = 272
 UNROLL = 8
 POSITIONS = 10 * 128
-FIRST_MIB = 18
+FIRST_MIB = 12
 LANES = 128
 MIB = 2**20
 BF16 = jnp.bfloat16
@@ -117,7 +117,7 @@
 
 
 def order_kernel(
-    per_seed, me, own, got_1, got_2, got_4, self_ids, neighbour_ids, count_one, lists, counts_rel
+    per_seed, me, own, got_1, got_2, got_4, self_ids, neighbour_ids, count_one, lists, most, counts_rel
 ):
     owners, seeds = counts_rel.shape
     fanout = neighbour_ids.shape[0]
@@ -134,6 +134,7 @@
         [counts_rel[pl.ds(jnp.bitwise_xor(mine, c), 1), :] for c in range(owners)], axis=0
     ).astype(F32)
     needs = (counts + 1.0).astype(BF16)
+    most[0] = jnp.max(jnp.sum(counts + 1.0, axis=1, keepdims=True)).astype(I32)
     before = (iota((seeds, seeds), 0) < iota((seeds, seeds), 1)).astype(BF16)
     offset = jnp.dot(needs, before, preferred_element_type=F32)
     off_hi = jnp.floor(offset * (1.0 / 16.0))
@@ -265,31 +266,59 @@
     return copies
 
 
+def turn_staged(copies, staged, table, base):
+    part = staged.shape[2]
+    for b, copy in enumerate(copies):
+        copy.wait()
+        turn(staged.at[b], table, pl.multiple_of(base + b * part, part))
+
+
+def own_kernel(which, halves, me, features, *refs):
+    table, staged, sems = refs[-3:]
+    length = features.shape[1]
+    half = length // halves
+    copies = stage(features.at[:, pl.ds(which * half, half)], staged, sems)
+    turn_staged(copies, staged, table, me[2] * length + which * half)
+
+
+def join_kernel(*refs):
+    *parts, out = refs
+    at = 0
+    for part in parts:
+        out[at : at + part.shape[0], :] = part[...]
+        at += part.shape[0]
+
+
+def hand_out(keep, send, keep_hbm, send_hbm, sems):
+    copies = [
+        pltpu.make_async_copy(send, send_hbm, sems.at[0]),
+        pltpu.make_async_copy(keep, keep_hbm, sems.at[1]),
+    ]
+    start_all(copies)
+    for copy in copies:
+        copy.wait()
+
+
 def first_kernel(
-    fanout, me, lists, features, other, self_one, neigh_one, table, keep, send, *scratch
+    fanout, me, lists, table_in, other, self_one, neigh_one, table, keep_hbm, send_hbm, *scratch
 ):
+    del table_in
     ids = scratch[: fanout + 1]
-    places, begins, self_rows, mean_rows, sems = scratch[fanout + 1 : -4]
-    staged_0, sems_0, staged_1, sems_1 = scratch[-4:]
+    places, begins, self_rows, mean_rows, sems = scratch[fanout + 1 : fanout + 6]
+    staged, staged_sems, keep, send, out_sems = scratch[fanout + 6 :]
     width, length = other.shape
     x, h, rep = me[0], me[1], me[2]
-    stages = [
-        (stage(features, staged_0, sems_0), staged_0, rep * length),
-        (stage(other, staged_1, sems_1), staged_1, (1 - rep) * length),
-    ]
+    staging = stage(other, staged, staged_sems)
     copies = list_copies(fanout, h, lists, ids, places, begins, sems)
     self_rows[...] = jnp.zeros_like(self_rows)
     mean_rows[...] = jnp.zeros_like(mean_rows)
     send[2, :, :] = jnp.zeros(send.shape[1:], BF16)
     send[2, 0:width, :] = self_one[...]
     send[2, LANES : LANES + width, :] = neigh_one[...]
-    for parts, staged, base in stages:
-        length_of = staged.shape[2]
-        for b, part in enumerate(parts):
-            part.wait()
-            turn(staged.at[b], table, pl.multiple_of(base + b * length_of, length_of))
+    turn_staged(staging, staged, table, (1 - rep) * length)
     look_up(fanout, copies, table, ids, places, begins, self_rows, mean_rows)
     write_out(x, width, self_rows, mean_rows, keep, send)
+    hand_out(keep, send, keep_hbm, send_hbm, out_sems)
 
 
 def second_kernel(fanout, width, me, lists, table, keep_hbm, send_hbm, *scratch):
@@ -301,13 +330,7 @@
     mean_rows[...] = jnp.zeros_like(mean_rows)
     look_up(fanout, copies, table, ids, places, begins, self_rows, mean_rows)
     write_out(x, width, self_rows, mean_rows, keep, send)
-    outs = [
-        pltpu.make_async_copy(send, send_hbm, out_sems.at[0]),
-        pltpu.make_async_copy(keep, keep_hbm, out_sems.at[1]),
-    ]
-    start_all(outs)
-    for copy in outs:
-        copy.wait()
+    hand_out(keep, send, keep_hbm, send_hbm, out_sems)
 
 
 def project(zl, keep, got, weight, weight_got, outs):
@@ -318,14 +341,14 @@
         ).astype(out.dtype)
 
 
-def project_far_kernel(me, keep, got, sent, later, out_0, out_1, loaded, sem):
-    copy = pltpu.make_async_copy(later, loaded, sem)
+def project_far_kernel(me, keep, got, sent, out_0, out_1):
+    project(me[3], keep, got, sent, got, (out_0, out_1))
+
+
+def project_near_kernel(me, keep_hbm, got, weight, weight_got, out_0, out_1, keep, sem):
+    copy = pltpu.make_async_copy(keep_hbm, keep, sem)
     copy.start()
-    project(me[3], keep, got, sent, got, (out_0, out_1))
     copy.wait()
-
-
-def project_near_kernel(me, keep, got, weight, weight_got, out_0, out_1):
     project(me[3], keep, got, weight, weight_got, (out_0, out_1))
 
 
@@ -334,8 +357,10 @@
 ):
     pre = mine[...] + a[...].astype(F32) + b[...].astype(F32) + c[...].astype(F32)
     hidden = jnp.maximum(pre + bias_one[...], 0.0).astype(BF16)
-    seeds = counts.shape[0]
-    count = counts[...]
+    seeds = counts.shape[1]
+    same = iota((seeds, seeds), 0) == iota((seeds, seeds), 1)
+    count = jnp.sum(jnp.where(same, counts[...].astype(F32), 0.0), axis=1, keepdims=True)
+    count = count.astype(I32)
     earlier = (iota((seeds, seeds), 0) > iota((seeds, seeds), 1)).astype(BF16)
     needs = jnp.broadcast_to((count + 1).astype(F32), (seeds, LANES)).astype(BF16)
     offset = jnp.dot(earlier, needs, preferred_element_type=F32)[:, 0:1].astype(I32)
@@ -351,7 +376,10 @@
         + bias_two[...]
     )
     hidden_two = jnp.maximum(pre_two, 0.0).astype(BF16)
-    out[...] = jnp.dot(hidden_two, out_weight[...], preferred_element_type=F32) + out_bias[...]
+    logits = lax.dot_general(
+        hidden_two, out_weight[...], (((1,), (1,)), ((), ())), preferred_element_type=F32
+    )
+    out[...] = logits + out_bias[...]
 
 
 def params(limit):
@@ -364,16 +392,16 @@
 
 def order_call(per_seed, me, own, got, self_ids, neighbour_ids, count_one):
     owners = sum(x.shape[0] for x in (own, *got))
-    lists = pl.pallas_call(
+    lists, most = pl.pallas_call(
         functools.partial(order_kernel, per_seed),
-        out_shape=shape((2, neighbour_ids.shape[0] + 3, 16, LANES), I32),
+        out_shape=(shape((2, neighbour_ids.shape[0] + 3, 16, LANES), I32), shape((1,), I32)),
         in_specs=[SMEM] + [VMEM] * 7,
-        out_specs=VMEM,
+        out_specs=(VMEM, SMEM),
         scratch_shapes=[pltpu.VMEM((owners, own.shape[1]), I32)],
         compiler_params=params(10),
         name="order",
     )(me, own, *got, self_ids, neighbour_ids, count_one)
-    return lists.reshape(-1)
+    return lists.reshape(-1), most[0]
 
 
 def list_scratch(fanout):
@@ -385,22 +413,56 @@
     )
 
 
-def first_call(fanout, me, lists, features, other, self_one, neigh_one):
+def own_call(which, halves, me, features, *table):
     width, length = features.shape
-    staging = [pltpu.VMEM((4, width, length // 4), BF16), pltpu.SemaphoreType.DMA((4,))]
+    parts = 4 // halves
+    return pl.pallas_call(
+        functools.partial(own_kernel, which, halves),
+        out_shape=shape((2 * length, LANES), F32),
+        in_specs=[SMEM, HBM] + [VMEM] * len(table),
+        out_specs=VMEM,
+        scratch_shapes=[
+            pltpu.VMEM((parts, width, length // 4), BF16),
+            pltpu.SemaphoreType.DMA((parts,)),
+        ],
+        input_output_aliases={2: 0} if table else {},
+        compiler_params=params(FIRST_MIB),
+        name="own_rows",
+    )(me, features, *table)
+
+
+def join_call(*parts):
+    rows = sum(part.shape[0] for part in parts)
+    return pl.pallas_call(
+        join_kernel,
+        out_shape=shape((rows, parts[0].shape[1]), parts[0].dtype),
+        in_specs=[VMEM] * len(parts),
+        out_specs=VMEM,
+        compiler_params=params(1),
+        name="join",
+    )(*parts)
+
+
+def first_call(fanout, me, lists, table, other, self_one, neigh_one):
+    width, length = other.shape
+    keep, send = (2, CAP, 2 * LANES), (3, CAP, 2 * LANES)
     return pl.pallas_call(
         functools.partial(first_kernel, fanout),
-        out_shape=(
-            shape((2 * length, LANES), F32),
-            shape((2, CAP, 2 * LANES), BF16),
-            shape((3, CAP, 2 * LANES), BF16),
-        ),
-        in_specs=[SMEM, ANY, ANY, ANY, VMEM, VMEM],
-        out_specs=(VMEM, VMEM, VMEM),
-        scratch_shapes=list_scratch(fanout) + staging + staging,
+        out_shape=(shape((2 * length, LANES), F32), pltpu.HBM(keep, BF16), pltpu.HBM(send, BF16)),
+        in_specs=[SMEM, ANY, VMEM, HBM, VMEM, VMEM],
+        out_specs=(VMEM, HBM, HBM),
+        scratch_shapes=list_scratch(fanout)
+        + [
+            pltpu.VMEM((4, width, length // 4), BF16),
+            pltpu.SemaphoreType.DMA((4,)),
+            pltpu.VMEM(keep, BF16),
+            pltpu.VMEM(send, BF16),
+            pltpu.SemaphoreType.DMA((2,)),
+        ],
+        input_output_aliases={2: 0},
         compiler_params=params(FIRST_MIB),
         name="first_half",
-    )(me, lists, features, other, self_one, neigh_one)
+    )(me, lists, table, other, self_one, neigh_one)
 
 
 def second_call(fanout, width, me, lists, table):
@@ -419,17 +481,16 @@
     )(me, lists, table)
 
 
-def project_far_call(me, keep, got, sent, later):
+def project_far_call(me, keep, got, sent):
     part = shape((CAP, sent.shape[2]), BF16)
     return pl.pallas_call(
         project_far_kernel,
-        out_shape=(part, part, shape(later.shape, BF16)),
-        in_specs=[SMEM, VMEM, VMEM, VMEM, ANY],
-        out_specs=(VMEM, VMEM, VMEM),
-        scratch_shapes=[pltpu.SemaphoreType.DMA],
+        out_shape=(part, part),
+        in_specs=[SMEM, VMEM, VMEM, VMEM],
+        out_specs=(VMEM, VMEM),
         compiler_params=params(10),
         name="project_far",
-    )(me, keep, got, sent, later)
+    )(me, keep, got, sent)
 
 
 def project_near_call(me, keep, got, weight, weight_got):
@@ -437,15 +498,16 @@
     return pl.pallas_call(
         project_near_kernel,
         out_shape=(shape(dims, F32), shape(dims, BF16)),
-        in_specs=[SMEM, VMEM, VMEM, VMEM, VMEM],
+        in_specs=[SMEM, HBM, VMEM, VMEM, VMEM],
         out_specs=(VMEM, VMEM),
+        scratch_shapes=[pltpu.VMEM(keep.shape, BF16), pltpu.SemaphoreType.DMA],
         compiler_params=params(10),
         name="project_near",
     )(me, keep, got, weight, weight_got)
 
 
 def last_call(*args):
-    seeds = args[4].shape[0]
+    seeds = args[4].shape[1]
     classes = args[-1].shape[1]
     return pl.pallas_call(
         last_kernel,
@@ -487,34 +549,35 @@
         return lax.ppermute(value, "col", [(i, i ^ bit) for i in range(owners)])
 
     other = lax.ppermute(features, "rep", [(0, 1), (1, 0)])
+    held = pltpu.with_memory_space_constraint(features, pltpu.HBM)
     own = count_two[None, :]
     got_1 = across(own, 1)
-    got_2 = across(jnp.concatenate([own, got_1], axis=0), 2)
-    got_4 = across(jnp.concatenate([own, got_1, got_2], axis=0), 4)
+    table, got_1 = lax.optimization_barrier((own_call(0, 1, me, held), got_1))
+    got_2 = across(join_call(own, got_1), 2)
+    got_4 = across(join_call(own, got_1, got_2), 4)
     got = (got_1, got_2, got_4)
-    lists = order_call(per_seed, me, own, got, self_ids, neighbour_ids, count_one)
+    lists, most = order_call(per_seed, me, own, got, self_ids, neighbour_ids, count_one)
     table, keep_far, send_far = first_call(
-        fanout, me, lists, features, other, self_one, neigh_one
+        fanout, me, lists, table, other, self_one, neigh_one
     )
     got_far = across(send_far, 1)
     keep_near, send_near = second_call(fanout, width, me, lists, table)
     got_near = across(send_near, 1)
-    far_0, far_1, keep_near = project_far_call(me, keep_far, got_far, send_far, keep_near)
+    far_0, far_1 = project_far_call(me, keep_far, got_far, send_far)
     far = [across(far_0, 4), across(far_1, 6)]
     near_0, near_1 = project_near_call(me, keep_near, got_near, send_far, got_far)
     far.append(across(near_1, 2))
     fast = last_call(
         near_0,
         *far,
-        count_two[:, None],
+        own,
         bias_one[None, :],
         self_two,
         neigh_two,
         bias_two[None, :],
-        out_weight,
+        out_weight.T,
         out_bias[None, :],
     )
-    most = functools.reduce(jnp.maximum, [jnp.max(jnp.sum(x + 1, axis=1)) for x in (own, *got)])
     return lax.cond(
         most > CAP,
         lambda: general(

time: 65 us -> 58.6 us (0.902)
  other arithmetic: 4.12 us -> 0 us
  waiting for transfers between devices: 10.5 us -> 7.56 us
  Pallas kernels: 30.7 us -> 33.2 us
  between operations: 2.83 us -> 0.87 us
    pallas_call x2 -> x5, Pallas kernels: 3.67 us -> 8.91 us  [the longest x1 5.23 us: own_call(): pl.pallas_call(functools.partial(own_kernel, which, halves), out_shape=sh...]
    ppermute x8, waiting for transfers between devices: 10.5 us -> 7.56 us  [across(): return lax.ppermute(value, 'col', [(i, i ^ bit) for i in range(owners)])]
    pallas_call x1, Pallas kernels: 16.2 us -> 13.4 us  [first_call(): pl.pallas_call(functools.partial(first_kernel, fanout), out_shape=(shape(...]
    reduce_sum x4 -> x0, other arithmetic: 1.51 us -> none  [main(): jnp.sum(x + 1, axis=1)]
    concatenate x2 -> x0, other arithmetic: 1.33 us -> none  [the longest x1 0.66 us: main(): got_4 = across(jnp.concatenate([own, got_1, got_2], axis=0), 4)]
    reduce_max x2 -> x0, other arithmetic: 1.27 us -> none  [main(): jnp.max(jnp.sum(x + 1, axis=1))]
    unnamed x29 -> x32, local copies, waits for them, and re-layouts: 1.72 us -> 1.63 us
  transfers between devices with their start and end apart: 9 -> 9, of which waited for: 7 -> 5; matrix products, arithmetic and copies ran while one was open for 7% -> 0% of each run, Pallas kernels for 20% -> 32%
where the time goes in v4:
time: 58.6 us; the launch traced here: 58.8 us
  Pallas kernels  33.2 us (57%)
  starting transfers between devices  15.3 us (26%)
  waiting for transfers between devices  7.56 us (13%)
  local copies, waits for them, and re-layouts  1.72 us (3%)
  between operations  0.87 us (1%)
    ppermute x8, starting transfers between devices, across(): return lax.ppermute(value, 'col', [(i, i ^ bit) for i in range(owners)])  14.9 us
    pallas_call x1, Pallas kernels, first_call(): pl.pallas_call(functools.partial(first_kernel, fanout), out_shape=(shape(...  13.4 us
    pallas_call x1, Pallas kernels, second_call(): pl.pallas_call(functools.partial(second_kernel, fanout, width), out_shape...  9.2 us
    ppermute x8, waiting for transfers between devices, across(): return lax.ppermute(value, 'col', [(i, i ^ bit) for i in range(owners)])  7.56 us
    pallas_call x1, Pallas kernels, own_call(): pl.pallas_call(functools.partial(own_kernel, which, halves), out_shape=sh...  5.23 us
    pallas_call x1, Pallas kernels, order_call(): pl.pallas_call(functools.partial(order_kernel, per_seed), out_shape=(shap...  2.83 us
    unnamed x32, local copies, waits for them, and re-layouts  1.63 us
  transfers between devices with their start and end apart: 9, of which 5 were waited for; matrix products, arithmetic and copies ran while one was open for 0% of the time, Pallas kernels for 32%

profile of v4, /device:TPU:0, one launch (start us, length us, event | category | flops | bytes accessed | tf_op | source)
XLA Modules:
  0.0 58.8 jit_solution(7790840058257378166)
XLA Ops:
  0.0 0.5 collective-permute-start.3
  0.5 2.5 %collective-permute-start = (s32[1,32]{1,0:T(1,128)}, s32[1,32]{1,0:T(1,128)S(1)}, u32[]{:S(2)}, u32[]{:S(2)}) collective-permute-start(s32[1,32]{1,0:T(1,128)} %bitcast.65), channel_id=1, source_target_pairs={{0,2},{2,0},{4,6},{6,4},{8,10},{10,8},{12,14},{14,12},{1,3},{3,1},... | collective-permute-start | bytes 392 | tf_op jit(solution)/shard_map/ppermute | solution.py:549
  2.9 0.1 stack.31.me
  3.0 0.0 copy-start.12
  3.0 0.0 copy-start.3
  3.0 0.0 copy-start.9
  3.0 0.0 copy-start.10
  3.0 0.0 copy-start.7
  3.1 0.0 copy-start.8
  3.1 5.2 %own_rows.1.table_in = f32[65536,128]{1,0:T(8,128)S(1)} custom-call(s32[5]{0:T(128)S(1)} %stack.31.me, bf16[96,32768]{1,0:T(8,128)(2,1)} %features.1), custom_call_target="tpu_custom_call" | custom-call | tf_op jit(solution)/shard_map/own_rows/pallas_call | solution.py:419
  8.3 0.0 collective-permute-done.refs_1_.got_1
  8.3 0.0 copy-done.12
  8.3 1.6 %collective-permute-start.1 = (s32[2,32]{1,0:T(2,128)S(1)}, s32[2,32]{1,0:T(2,128)S(1)}, u32[]{:S(2)}, u32[]{:S(2)}) collective-permute-start(s32[2,32]{1,0:T(2,128)S(1)} %join.2), channel_id=1, source_target_pairs={{0,4},{2,6},{4,0},{6,2},{8,12},{10,14},{12,8},{14,10},{1,5},{3,7},... | collective-permute-start | bytes 776 | tf_op jit(solution)/shard_map/ppermute | solution.py:549
  10.0 2.0 %collective-permute-done.1.refs_2_.got_2 = s32[2,32]{1,0:T(2,128)S(1)} collective-permute-done((s32[2,32]{1,0:T(2,128)S(1)}, s32[2,32]{1,0:T(2,128)S(1)}, u32[]{:S(2)}, u32[]{:S(2)}) %collective-permute-start.1) | collective-permute-done | bytes 288 | tf_op jit(solution)/shard_map/ppermute | solution.py:549
  12.0 2.6 %collective-permute-start.2 = (s32[4,32]{1,0:T(4,128)S(1)}, s32[4,32]{1,0:T(4,128)S(1)}, u32[]{:S(2)}, u32[]{:S(2)}) collective-permute-start(s32[4,32]{1,0:T(4,128)S(1)} %join.3), channel_id=1, source_target_pairs={{0,8},{2,10},{4,12},{6,14},{8,0},{10,2},{12,4},{14,6},{1,9},{3,11}... | collective-permute-start | bytes 1544 | tf_op jit(solution)/shard_map/ppermute | solution.py:549
  14.6 1.9 %collective-permute-done.2.got_4 = s32[4,32]{1,0:T(4,128)S(1)} collective-permute-done((s32[4,32]{1,0:T(4,128)S(1)}, s32[4,32]{1,0:T(4,128)S(1)}, u32[]{:S(2)}, u32[]{:S(2)}) %collective-permute-start.2) | collective-permute-done | bytes 544 | tf_op jit(solution)/shard_map/ppermute | solution.py:549
  16.5 0.0 copy-done.3
  16.5 0.0 copy-done.9
  16.5 0.0 copy-done.10
  16.5 2.8 %order.1 = (s32[2,18,16,128]{3,2,1,0:T(8,128)S(1)}, s32[1]{0:T(128)}) custom-call(s32[5]{0:T(128)S(1)} %stack.31.me, s32[1,32]{1,0:T(1,128)S(1)} %bitcast.68, s32[1,32]{1,0:T(1,128)S(1)} %collective-permute-done.refs_1_.got_1, s32[2,32]{1,0:T(2,128)S(1)} %collective-permute-done.1.refs_2_.got_2, s32[4,32]{1,0:T(4,128)S(1)} %collective-permute-done.2.got_4, ...), custom_call_target="tpu_custom_call" | custom-call | tf_op jit(solution)/shard_map/order/pallas_call | solution.py:395
  19.3 0.0 collective-permute-done.3.other
  19.3 0.0 copy-done.7
  19.3 0.0 copy-done.8
  19.3 13.4 %first_half.1 = (f32[65536,128]{1,0:T(8,128)S(1)}, bf16[2,272,256]{2,1,0:T(8,128)(2,1)}, bf16[3,272,256]{2,1,0:T(8,128)(2,1)}) custom-call(s32[5]{0:T(128)S(1)} %stack.31.me, s32[73728]{0:T(1024)S(1)} %bitcast.55, f32[65536,128]{1,0:T(8,128)S(1)} %own_rows.1.table_in, ...), custom_call_target="tpu_custom_call", output_to_operand_aliasing={{0}: (2, {})} | custom-call | tf_op jit(solution)/shard_map/first_half/pallas_call | solution.py:449
  32.8 0.3 collective-permute-start.5
  33.0 0.0 copy-start
  33.0 0.0 copy-start.2
  33.0 0.0 copy-start.4
  33.0 0.0 copy-start.5
  33.0 0.0 copy-start.6
  33.1 0.0 copy-start.13
  33.1 0.0 copy-start.14
  33.1 0.0 copy-start.15
  33.1 9.2 %second_half.1 = (bf16[2,272,256]{2,1,0:T(8,128)(2,1)}, bf16[2,272,256]{2,1,0:T(8,128)(2,1)}) custom-call(s32[5]{0:T(128)S(1)} %stack.31.me, s32[73728]{0:T(1024)S(1)} %bitcast.56, f32[65536,128]{1,0:T(8,128)S(1)} %get-tuple-element.68.table), custom_call_target="tpu_custom_call" | custom-call | tf_op jit(solution)/shard_map/second_half/pallas_call | solution.py:471
  42.3 1.9 %collective-permute-start.4 = (bf16[2,272,256]{2,1,0:T(8,128)(2,1)}, bf16[2,272,256]{2,1,0:T(8,128)(2,1)S(1)}, u32[]{:S(2)}, u32[]{:S(2)}) collective-permute-start(bf16[2,272,256]{2,1,0:T(8,128)(2,1)} %get-tuple-element.70), channel_id=1, source_target_pairs={{0,2},{2,0},{4,6},{6,4},{8,10},{10,8},{12,14},{14,12},{1,3},{3,1},... | collective-permute-start | bytes 835592 | tf_op jit(solution)/shard_map/ppermute | solution.py:549
  44.2 0.0 collective-permute-done.5.weight_got.got
  44.2 0.0 copy-done
  44.2 0.0 copy-done.2
  44.2 0.8 %project_far.1 = (bf16[272,256]{1,0:T(8,128)(2,1)S(1)}, bf16[272,256]{1,0:T(8,128)(2,1)S(1)}) custom-call(s32[5]{0:T(128)S(1)} %stack.31.me, bf16[2,272,256]{2,1,0:T(8,128)(2,1)S(1)} %copy-done.2, bf16[3,272,256]{2,1,0:T(8,128)(2,1)S(1)} %collective-permute-done.5.weight_got.got, bf16[3,272,256]{2,1,0:T(8,128)(2,1)S(1)} %copy-done), custom_call_target="tpu_custom_call" | custom-call | tf_op jit(solution)/shard_map/project_far/pallas_call | solution.py:486
  45.1 2.7 %collective-permute-start.6 = (bf16[272,256]{1,0:T(8,128)(2,1)S(1)}, bf16[272,256]{1,0:T(8,128)(2,1)S(1)}, u32[]{:S(2)}, u32[]{:S(2)}) collective-permute-start(bf16[272,256]{1,0:T(8,128)(2,1)S(1)} %get-tuple-element.74), channel_id=1, source_target_pairs={{0,8},{2,10},{4,12},{6,14},{8,0},{10,2},{12,4},{14,6},{1,9},{3,11}... | collective-permute-start | bytes 417800 | tf_op jit(solution)/shard_map/ppermute | solution.py:549
  47.7 1.3 %collective-permute-start.7 = (bf16[272,256]{1,0:T(8,128)(2,1)S(1)}, bf16[272,256]{1,0:T(8,128)(2,1)S(1)}, u32[]{:S(2)}, u32[]{:S(2)}) collective-permute-start(bf16[272,256]{1,0:T(8,128)(2,1)S(1)} %get-tuple-element.75), channel_id=1, source_target_pairs={{0,12},{2,14},{4,8},{6,10},{8,4},{10,6},{12,0},{14,2},{1,13},{3,15... | collective-permute-start | bytes 417800 | tf_op jit(solution)/shard_map/ppermute | solution.py:549
  49.1 0.1 collective-permute-done.4.got
  49.1 0.0 copy-start.1
  49.1 1.0 %copy-done.1 = bf16[2,272,256]{2,1,0:T(8,128)(2,1)S(1)} copy-done((bf16[2,272,256]{2,1,0:T(8,128)(2,1)S(1)}, bf16[2,272,256]{2,1,0:T(8,128)(2,1)}, u32[]{:S(2)}) %copy-start.1) | copy-done | bytes 278552
  50.1 0.9 %project_near.1 = (f32[272,256]{1,0:T(8,128)S(1)}, bf16[272,256]{1,0:T(8,128)(2,1)S(1)}) custom-call(s32[5]{0:T(128)S(1)} %stack.31.me, bf16[2,272,256]{2,1,0:T(8,128)(2,1)S(1)} %copy-done.1, bf16[2,272,256]{2,1,0:T(8,128)(2,1)S(1)} %collective-permute-done.4.got, bf16[3,272,256]{2,1,0:T(8,128)(2,1)S(1)} %copy-done, ...), custom_call_target="tpu_custom_call" | custom-call | tf_op jit(solution)/shard_map/project_near/pallas_call | solution.py:498
  51.0 2.0 %collective-permute-start.8 = (bf16[272,256]{1,0:T(8,128)(2,1)S(1)}, bf16[272,256]{1,0:T(8,128)(2,1)S(1)}, u32[]{:S(2)}, u32[]{:S(2)}) collective-permute-start(bf16[272,256]{1,0:T(8,128)(2,1)S(1)} %get-tuple-element.76), channel_id=1, source_target_pairs={{0,4},{2,6},{4,0},{6,2},{8,12},{10,14},{12,8},{14,10},{1,5},{3,7},... | collective-permute-start | bytes 417800 | tf_op jit(solution)/shard_map/ppermute | solution.py:549
  53.6 2.4 %collective-permute-done.6.a = bf16[272,256]{1,0:T(8,128)(2,1)S(1)} collective-permute-done((bf16[272,256]{1,0:T(8,128)(2,1)S(1)}, bf16[272,256]{1,0:T(8,128)(2,1)S(1)}, u32[]{:S(2)}, u32[]{:S(2)}) %collective-permute-start.6) | collective-permute-done | bytes 139296 | tf_op jit(solution)/shard_map/ppermute | solution.py:549
  56.0 0.0 collective-permute-done.7.b
  56.0 1.2 %collective-permute-done.8.c = bf16[272,256]{1,0:T(8,128)(2,1)S(1)} collective-permute-done((bf16[272,256]{1,0:T(8,128)(2,1)S(1)}, bf16[272,256]{1,0:T(8,128)(2,1)S(1)}, u32[]{:S(2)}, u32[]{:S(2)}) %collective-permute-start.8) | collective-permute-done | bytes 139296 | tf_op jit(solution)/shard_map/ppermute | solution.py:549
  57.2 0.0 copy-done.4
  57.2 0.0 copy-done.5
  57.2 0.0 copy-done.6
  57.2 0.0 copy-done.13
  57.2 0.0 copy-done.14
  57.3 0.0 copy-done.15
  57.3 0.7 %layer_two.1 = f32[32,153]{1,0:T(8,128)S(1)} custom-call(f32[272,256]{1,0:T(8,128)S(1)} %get-tuple-element.72.mine, bf16[272,256]{1,0:T(8,128)(2,1)S(1)} %collective-permute-done.6.a, bf16[272,256]{1,0:T(8,128)(2,1)S(1)} %collective-permute-done.7.b, bf16[272,256]{1,0:T(8,128)(2,1)S(1)} %collective-permute-done.8.c, s32[1,32]{1,0:T(1,128)S(1)} %bitcast.69, ...), custom_call_target="tpu_custom_call" | custom-call | tf_op jit(solution)/shard_map/layer_two/pallas_call | solution.py:512
  58.0 0.1 conditional.1
  58.1 0.0 copy-start.11
  58.2 0.6 %copy-done.11 = f32[32,153]{1,0:T(8,128)} copy-done((f32[32,153]{1,0:T(8,128)}, f32[32,153]{1,0:T(8,128)S(1)}, u32[]{:S(2)}) %copy-start.11) | copy-done | bytes 19608
  (2 shorter events, 0.0 us)
Async XLA Ops:
  0.0 19.3 %collective-permute-start.3 = (bf16[96,32768]{1,0:T(8,128)(2,1)}, bf16[96,32768]{1,0:T(8,128)(2,1)}, u32[]{:S(2)}, u32[]{:S(2)}) collective-permute-start(bf16[96,32768]{1,0:T(8,128)(2,1)} %features.1), channel_id=1, source_target_pairs={{0,1},{1,0},{2,3},{3,2},{4,5},{5,4},{6,7},{7,6},{8,9},{9,8},{10,11... | collective-permute-start | bytes 18874376 | tf_op jit(solution)/shard_map/ppermute | solution.py:551
  0.5 7.8 %collective-permute-start = (s32[1,32]{1,0:T(1,128)}, s32[1,32]{1,0:T(1,128)S(1)}, u32[]{:S(2)}, u32[]{:S(2)}) collective-permute-start(s32[1,32]{1,0:T(1,128)} %bitcast.65), channel_id=1, source_target_pairs={{0,2},{2,0},{4,6},{6,4},{8,10},{10,8},{12,14},{14,12},{1,3},{3,1},... | collective-permute-start | bytes 392 | tf_op jit(solution)/shard_map/ppermute | solution.py:549
  3.0 5.3 %copy-start.12 = (s32[32]{0:T(128)S(1)}, s32[32]{0:T(128)}, u32[]{:S(2)}) copy-start(s32[32]{0:T(128)} %param.19) | copy-start | bytes 388
  3.0 13.4 %copy-start.3 = (s32[15,2816]{1,0:T(8,128)S(1)}, s32[15,2816]{1,0:T(8,128)}, u32[]{:S(2)}) copy-start(s32[15,2816]{1,0:T(8,128)} %neighbour_ids.1) | copy-start | bytes 506884
  3.0 13.4 %copy-start.9 = (s32[2816]{0:T(1024)S(1)}, s32[2816]{0:T(1024)}, u32[]{:S(2)}) copy-start(s32[2816]{0:T(1024)} %count_one.1) | copy-start | bytes 33796
  3.0 13.4 %copy-start.10 = (s32[2816]{0:T(1024)S(1)}, s32[2816]{0:T(1024)}, u32[]{:S(2)}) copy-start(s32[2816]{0:T(1024)} %self_ids.1) | copy-start | bytes 33796
  3.0 16.3 %copy-start.7 = (bf16[96,256]{1,0:T(8,128)(2,1)S(1)}, bf16[96,256]{1,0:T(8,128)(2,1)}, u32[]{:S(2)}) copy-start(bf16[96,256]{1,0:T(8,128)(2,1)} %self_one.1) | copy-start | bytes 147460
  3.1 16.3 %copy-start.8 = (bf16[96,256]{1,0:T(8,128)(2,1)S(1)}, bf16[96,256]{1,0:T(8,128)(2,1)}, u32[]{:S(2)}) copy-start(bf16[96,256]{1,0:T(8,128)(2,1)} %neigh_one.1) | copy-start | bytes 147460
  8.3 3.6 %collective-permute-start.1 = (s32[2,32]{1,0:T(2,128)S(1)}, s32[2,32]{1,0:T(2,128)S(1)}, u32[]{:S(2)}, u32[]{:S(2)}) collective-permute-start(s32[2,32]{1,0:T(2,128)S(1)} %join.2), channel_id=1, source_target_pairs={{0,4},{2,6},{4,0},{6,2},{8,12},{10,14},{12,8},{14,10},{1,5},{3,7},... | collective-permute-start | bytes 776 | tf_op jit(solution)/shard_map/ppermute | solution.py:549
  12.0 4.5 %collective-permute-start.2 = (s32[4,32]{1,0:T(4,128)S(1)}, s32[4,32]{1,0:T(4,128)S(1)}, u32[]{:S(2)}, u32[]{:S(2)}) collective-permute-start(s32[4,32]{1,0:T(4,128)S(1)} %join.3), channel_id=1, source_target_pairs={{0,8},{2,10},{4,12},{6,14},{8,0},{10,2},{12,4},{14,6},{1,9},{3,11}... | collective-permute-start | bytes 1544 | tf_op jit(solution)/shard_map/ppermute | solution.py:549
  32.8 11.4 %collective-permute-start.5 = (bf16[3,272,256]{2,1,0:T(8,128)(2,1)}, bf16[3,272,256]{2,1,0:T(8,128)(2,1)S(1)}, u32[]{:S(2)}, u32[]{:S(2)}) collective-permute-start(bf16[3,272,256]{2,1,0:T(8,128)(2,1)} %get-tuple-element.71.weight.sent), channel_id=1, source_target_pairs={{0,2},{2,0},{4,6},{6,4},{8,10},{10,8},{12,14},{14,12},{1,3},{3,1},... | collective-permute-start | bytes 1253384 | tf_op jit(solution)/shard_map/ppermute | solution.py:549
  33.0 11.2 %copy-start = (bf16[3,272,256]{2,1,0:T(8,128)(2,1)S(1)}, bf16[3,272,256]{2,1,0:T(8,128)(2,1)}, u32[]{:S(2)}) copy-start(bf16[3,272,256]{2,1,0:T(8,128)(2,1)} %get-tuple-element.71.weight.sent) | copy-start | bytes 1253380
  33.0 11.2 %copy-start.2 = (bf16[2,272,256]{2,1,0:T(8,128)(2,1)S(1)}, bf16[2,272,256]{2,1,0:T(8,128)(2,1)}, u32[]{:S(2)}) copy-start(bf16[2,272,256]{2,1,0:T(8,128)(2,1)} %get-tuple-element.73.keep) | copy-start | bytes 835588
  33.0 24.2 %copy-start.4 = (bf16[256,256]{1,0:T(8,128)(2,1)S(1)}, bf16[256,256]{1,0:T(8,128)(2,1)}, u32[]{:S(2)}) copy-start(bf16[256,256]{1,0:T(8,128)(2,1)} %neigh_two.1) | copy-start | bytes 393220
  33.0 24.2 %copy-start.5 = (bf16[256,256]{1,0:T(8,128)(2,1)S(1)}, bf16[256,256]{1,0:T(8,128)(2,1)}, u32[]{:S(2)}) copy-start(bf16[256,256]{1,0:T(8,128)(2,1)} %self_two.1) | copy-start | bytes 393220
  33.0 24.2 %copy-start.6 = (bf16[256,153]{0,1:T(8,128)(2,1)S(1)}, bf16[256,153]{0,1:T(8,128)(2,1)}, u32[]{:S(2)}) copy-start(bf16[256,153]{0,1:T(8,128)(2,1)} %param.26) | copy-start | bytes 235012
  33.1 24.2 %copy-start.13 = (f32[256]{0:T(256)S(1)}, f32[256]{0:T(256)}, u32[]{:S(2)}) copy-start(f32[256]{0:T(256)} %param.25) | copy-start | bytes 3076
  33.1 24.2 %copy-start.14 = (f32[153]{0:T(256)S(1)}, f32[153]{0:T(256)}, u32[]{:S(2)}) copy-start(f32[153]{0:T(256)} %param.27) | copy-start | bytes 1840
  33.1 24.2 %copy-start.15 = (f32[256]{0:T(256)S(1)}, f32[256]{0:T(256)}, u32[]{:S(2)}) copy-start(f32[256]{0:T(256)} %param.22) | copy-start | bytes 3076
  42.3 6.8 %collective-permute-start.4 = (bf16[2,272,256]{2,1,0:T(8,128)(2,1)}, bf16[2,272,256]{2,1,0:T(8,128)(2,1)S(1)}, u32[]{:S(2)}, u32[]{:S(2)}) collective-permute-start(bf16[2,272,256]{2,1,0:T(8,128)(2,1)} %get-tuple-element.70), channel_id=1, source_target_pairs={{0,2},{2,0},{4,6},{6,4},{8,10},{10,8},{12,14},{14,12},{1,3},{3,1},... | collective-permute-start | bytes 835592 | tf_op jit(solution)/shard_map/ppermute | solution.py:549
  45.1 11.0 %collective-permute-start.6 = (bf16[272,256]{1,0:T(8,128)(2,1)S(1)}, bf16[272,256]{1,0:T(8,128)(2,1)S(1)}, u32[]{:S(2)}, u32[]{:S(2)}) collective-permute-start(bf16[272,256]{1,0:T(8,128)(2,1)S(1)} %get-tuple-element.74), channel_id=1, source_target_pairs={{0,8},{2,10},{4,12},{6,14},{8,0},{10,2},{12,4},{14,6},{1,9},{3,11}... | collective-permute-start | bytes 417800 | tf_op jit(solution)/shard_map/ppermute | solution.py:549
  47.7 8.3 %collective-permute-start.7 = (bf16[272,256]{1,0:T(8,128)(2,1)S(1)}, bf16[272,256]{1,0:T(8,128)(2,1)S(1)}, u32[]{:S(2)}, u32[]{:S(2)}) collective-permute-start(bf16[272,256]{1,0:T(8,128)(2,1)S(1)} %get-tuple-element.75), channel_id=1, source_target_pairs={{0,12},{2,14},{4,8},{6,10},{8,4},{10,6},{12,0},{14,2},{1,13},{3,15... | collective-permute-start | bytes 417800 | tf_op jit(solution)/shard_map/ppermute | solution.py:549
  49.1 1.0 %copy-start.1 = (bf16[2,272,256]{2,1,0:T(8,128)(2,1)S(1)}, bf16[2,272,256]{2,1,0:T(8,128)(2,1)}, u32[]{:S(2)}) copy-start(bf16[2,272,256]{2,1,0:T(8,128)(2,1)} %get-tuple-element.69.keep_hbm) | copy-start | bytes 835588
  51.0 6.2 %collective-permute-start.8 = (bf16[272,256]{1,0:T(8,128)(2,1)S(1)}, bf16[272,256]{1,0:T(8,128)(2,1)S(1)}, u32[]{:S(2)}, u32[]{:S(2)}) collective-permute-start(bf16[272,256]{1,0:T(8,128)(2,1)S(1)} %get-tuple-element.76), channel_id=1, source_target_pairs={{0,4},{2,6},{4,0},{6,2},{8,12},{10,14},{12,8},{14,10},{1,5},{3,7},... | collective-permute-start | bytes 417800 | tf_op jit(solution)/shard_map/ppermute | solution.py:549
  58.1 0.6 %copy-start.11 = (f32[32,153]{1,0:T(8,128)}, f32[32,153]{1,0:T(8,128)S(1)}, u32[]{:S(2)}) copy-start(f32[32,153]{1,0:T(8,128)S(1)} %get-tuple-element.156) | copy-start | bytes 58756

commit v5 on v4

--- a/solution.py
+++ b/solution.py
@@ -12,6 +12,7 @@
 UNROLL = 8
 POSITIONS = 10 * 128
 FIRST_MIB = 12
+OWN_MIB = 18
 LANES = 128
 MIB = 2**20
 BF16 = jnp.bfloat16
@@ -135,18 +136,14 @@
     ).astype(F32)
     needs = (counts + 1.0).astype(BF16)
     most[0] = jnp.max(jnp.sum(counts + 1.0, axis=1, keepdims=True)).astype(I32)
-    before = (iota((seeds, seeds), 0) < iota((seeds, seeds), 1)).astype(BF16)
-    offset = jnp.dot(needs, before, preferred_element_type=F32)
-    off_hi = jnp.floor(offset * (1.0 / 16.0))
-    off_lo = offset - off_hi * 16.0
-    shift = iota((seeds, per_owner), 1) - iota((seeds, per_owner), 0) * per_seed
-    spread = ((shift >= 0) & (shift < per_seed)).astype(BF16)
-    place = jnp.dot(iota((8, seeds), 1).astype(BF16), spread, preferred_element_type=F32)
-    t = iota((owners, per_owner), 1).astype(F32) - place[0:1, :] * per_seed
-    of_row = jnp.dot(counts.astype(BF16), spread, preferred_element_type=F32)
-    row_hi = jnp.dot(off_hi.astype(BF16), spread, preferred_element_type=F32)
-    row_lo = jnp.dot(off_lo.astype(BF16), spread, preferred_element_type=F32)
-    slot = row_hi * 16.0 + row_lo + t
+    column = iota((seeds, per_owner), 1).astype(F32)
+    seed_of = jnp.floor((column + 0.5) * (1.0 / per_seed))
+    seed = iota((seeds, per_owner), 0).astype(F32)
+    t = column[0:1, :] - seed_of[0:1, :] * per_seed
+    of_row = jnp.dot(
+        counts.astype(BF16), (seed == seed_of).astype(BF16), preferred_element_type=F32
+    )
+    slot = t + jnp.dot(needs, (seed < seed_of).astype(BF16), preferred_element_type=F32)
     used = (t <= of_row) & (slot < CAP)
     slot = slot.astype(I32)
     keys = [
@@ -341,14 +338,14 @@
         ).astype(out.dtype)
 
 
-def project_far_kernel(me, keep, got, sent, out_0, out_1):
+def project_far_kernel(me, keep, got, sent, later, out_0, out_1, loaded, sem):
+    copy = pltpu.make_async_copy(later, loaded, sem)
+    copy.start()
     project(me[3], keep, got, sent, got, (out_0, out_1))
-
-
-def project_near_kernel(me, keep_hbm, got, weight, weight_got, out_0, out_1, keep, sem):
-    copy = pltpu.make_async_copy(keep_hbm, keep, sem)
-    copy.start()
     copy.wait()
+
+
+def project_near_kernel(me, keep, got, weight, weight_got, out_0, out_1):
     project(me[3], keep, got, weight, weight_got, (out_0, out_1))
 
 
@@ -415,18 +412,18 @@
 
 def own_call(which, halves, me, features, *table):
     width, length = features.shape
-    parts = 4 // halves
+    parts = 8 // halves
     return pl.pallas_call(
         functools.partial(own_kernel, which, halves),
         out_shape=shape((2 * length, LANES), F32),
         in_specs=[SMEM, HBM] + [VMEM] * len(table),
         out_specs=VMEM,
         scratch_shapes=[
-            pltpu.VMEM((parts, width, length // 4), BF16),
+            pltpu.VMEM((parts, width, length // 8), BF16),
             pltpu.SemaphoreType.DMA((parts,)),
         ],
         input_output_aliases={2: 0} if table else {},
-        compiler_params=params(FIRST_MIB),
+        compiler_params=params(FIRST_MIB if table else OWN_MIB),
         name="own_rows",
     )(me, features, *table)
 
@@ -453,8 +450,8 @@
         out_specs=(VMEM, HBM, HBM),
         scratch_shapes=list_scratch(fanout)
         + [
-            pltpu.VMEM((4, width, length // 4), BF16),
-            pltpu.SemaphoreType.DMA((4,)),
+            pltpu.VMEM((8, width, length // 8), BF16),
+            pltpu.SemaphoreType.DMA((8,)),
             pltpu.VMEM(keep, BF16),
             pltpu.VMEM(send, BF16),
             pltpu.SemaphoreType.DMA((2,)),
@@ -481,16 +478,17 @@
     )(me, lists, table)
 
 
-def project_far_call(me, keep, got, sent):
+def project_far_call(me, keep, got, sent, later):
     part = shape((CAP, sent.shape[2]), BF16)
     return pl.pallas_call(
         project_far_kernel,
-        out_shape=(part, part),
-        in_specs=[SMEM, VMEM, VMEM, VMEM],
-        out_specs=(VMEM, VMEM),
+        out_shape=(part, part, shape(later.shape, BF16)),
+        in_specs=[SMEM, VMEM, VMEM, VMEM, HBM],
+        out_specs=(VMEM, VMEM, VMEM),
+        scratch_shapes=[pltpu.SemaphoreType.DMA],
         compiler_params=params(10),
         name="project_far",
-    )(me, keep, got, sent)
+    )(me, keep, got, sent, pltpu.with_memory_space_constraint(later, pltpu.HBM))
 
 
 def project_near_call(me, keep, got, weight, weight_got):
@@ -498,9 +496,8 @@
     return pl.pallas_call(
         project_near_kernel,
         out_shape=(shape(dims, F32), shape(dims, BF16)),
-        in_specs=[SMEM, HBM, VMEM, VMEM, VMEM],
+        in_specs=[SMEM, VMEM, VMEM, VMEM, VMEM],
         out_specs=(VMEM, VMEM),
-        scratch_shapes=[pltpu.VMEM(keep.shape, BF16), pltpu.SemaphoreType.DMA],
         compiler_params=params(10),
         name="project_near",
     )(me, keep, got, weight, weight_got)
@@ -552,8 +549,9 @@
     held = pltpu.with_memory_space_constraint(features, pltpu.HBM)
     own = count_two[None, :]
     got_1 = across(own, 1)
-    table, got_1 = lax.optimization_barrier((own_call(0, 1, me, held), got_1))
+    table, got_1 = lax.optimization_barrier((own_call(0, 2, me, held), got_1))
     got_2 = across(join_call(own, got_1), 2)
+    table, got_2 = lax.optimization_barrier((own_call(1, 2, me, held, table), got_2))
     got_4 = across(join_call(own, got_1, got_2), 4)
     got = (got_1, got_2, got_4)
     lists, most = order_call(per_seed, me, own, got, self_ids, neighbour_ids, count_one)
@@ -563,7 +561,7 @@
     got_far = across(send_far, 1)
     keep_near, send_near = second_call(fanout, width, me, lists, table)
     got_near = across(send_near, 1)
-    far_0, far_1 = project_far_call(me, keep_far, got_far, send_far)
+    far_0, far_1, keep_near = project_far_call(me, keep_far, got_far, send_far, keep_near)
     far = [across(far_0, 4), across(far_1, 6)]
     near_0, near_1 = project_near_call(me, keep_near, got_near, send_far, got_far)
     far.append(across(near_1, 2))

time: 58.6 us -> 59.1 us (level); the launches traced: 58.8 us -> 58.4 us
  starting transfers between devices: 15.3 us -> 12.7 us
  waiting for transfers between devices: 7.56 us -> 9.44 us
  Pallas kernels: 33.2 us -> 34.5 us
  local copies, waits for them, and re-layouts: 1.72 us -> 0.77 us
    ppermute x8, starting transfers between devices: 14.9 us -> 12.3 us  [across(): return lax.ppermute(value, 'col', [(i, i ^ bit) for i in range(owners)])]
    ppermute x8, waiting for transfers between devices: 7.56 us -> 9.44 us  [across(): return lax.ppermute(value, 'col', [(i, i ^ bit) for i in range(owners)])]
    pallas_call x1 -> x2, Pallas kernels: 5.23 us -> 6.66 us  [own_call(): pl.pallas_call(functools.partial(own_kernel, which, halves), out_shape=sh...]
    unnamed x32 -> x30, local copies, waits for them, and re-layouts: 1.63 us -> 0.68 us
    pallas_call x1, Pallas kernels: 13.4 us -> 12.7 us  [first_call(): pl.pallas_call(functools.partial(first_kernel, fanout), out_shape=(shape(...]
    pallas_call x1, Pallas kernels: 0.85 us -> 1.53 us  [project_far_call(): pl.pallas_call(project_far_kernel, out_shape=(part, part, shape(later.sha...]
  transfers between devices with their start and end apart: 9 -> 9, of which waited for: 5 -> 4; matrix products, arithmetic and copies ran while one was open for 0% -> 0% of each run, Pallas kernels for 32% -> 36%
where the time goes in v5:
time: 59.1 us; the launch traced here: 58.4 us
  Pallas kernels  34.5 us (58%)
  starting transfers between devices  12.7 us (21%)
  waiting for transfers between devices  9.44 us (16%)
  between operations  0.91 us (2%)
  local copies, waits for them, and re-layouts  0.77 us (1%)
    pallas_call x1, Pallas kernels, first_call(): pl.pallas_call(functools.partial(first_kernel, fanout), out_shape=(shape(...  12.7 us
    ppermute x8, starting transfers between devices, across(): return lax.ppermute(value, 'col', [(i, i ^ bit) for i in range(owners)])  12.3 us
    ppermute x8, waiting for transfers between devices, across(): return lax.ppermute(value, 'col', [(i, i ^ bit) for i in range(owners)])  9.44 us
    pallas_call x1, Pallas kernels, second_call(): pl.pallas_call(functools.partial(second_kernel, fanout, width), out_shape...  9.23 us
    pallas_call x2, Pallas kernels, own_call(): pl.pallas_call(functools.partial(own_kernel, which, halves), out_shape=sh...  6.66 us
    pallas_call x1, Pallas kernels, order_call(): pl.pallas_call(functools.partial(order_kernel, per_seed), out_shape=(shap...  2.73 us
    pallas_call x1, Pallas kernels, project_far_call(): pl.pallas_call(project_far_kernel, out_shape=(part, part, shape(later.sha...  1.53 us
  transfers between devices with their start and end apart: 9, of which 4 were waited for; matrix products, arithmetic and copies ran while one was open for 0% of the time, Pallas kernels for 36%

profile of v5, /device:TPU:0, one launch (start us, length us, event | category | flops | bytes accessed | tf_op | source)
XLA Modules:
  0.0 58.4 jit_solution(1917659709793598359)
XLA Ops:
  0.0 0.5 collective-permute-start.3
  0.5 2.5 %collective-permute-start = (s32[1,32]{1,0:T(1,128)}, s32[1,32]{1,0:T(1,128)S(1)}, u32[]{:S(2)}, u32[]{:S(2)}) collective-permute-start(s32[1,32]{1,0:T(1,128)} %bitcast.65), channel_id=1, source_target_pairs={{0,2},{2,0},{4,6},{6,4},{8,10},{10,8},{12,14},{14,12},{1,3},{3,1},... | collective-permute-start | bytes 392 | tf_op jit(solution)/shard_map/ppermute | solution.py:546
  2.9 0.1 stack.31.me
  3.0 0.0 copy-start.11
  3.0 3.3 %own_rows.2.refs_0_ = f32[65536,128]{1,0:T(8,128)S(1)} custom-call(s32[5]{0:T(128)S(1)} %stack.31.me, bf16[96,32768]{1,0:T(8,128)(2,1)} %features.3), custom_call_target="tpu_custom_call" | custom-call | tf_op jit(solution)/shard_map/own_rows/pallas_call | solution.py:416
  6.4 0.0 collective-permute-done.refs_1_.got_1
  6.4 0.0 copy-done.11
  6.4 0.0 copy-start.2
  6.4 0.0 copy-start.8
  6.4 0.0 copy-start.9
  6.4 0.0 copy-start.6
  6.4 0.0 copy-start.7
  6.5 1.6 %collective-permute-start.1 = (s32[2,32]{1,0:T(2,128)S(1)}, s32[2,32]{1,0:T(2,128)S(1)}, u32[]{:S(2)}, u32[]{:S(2)}) collective-permute-start(s32[2,32]{1,0:T(2,128)S(1)} %join.2), channel_id=1, source_target_pairs={{0,4},{2,6},{4,0},{6,2},{8,12},{10,14},{12,8},{14,10},{1,5},{3,7},... | collective-permute-start | bytes 776 | tf_op jit(solution)/shard_map/ppermute | solution.py:546
  8.1 3.3 %own_rows.3.table_in = f32[65536,128]{1,0:T(8,128)S(1)} custom-call(s32[5]{0:T(128)S(1)} %stack.31.me, bf16[96,32768]{1,0:T(8,128)(2,1)} %features.3, f32[65536,128]{1,0:T(8,128)S(1)} %own_rows.2.refs_0_), custom_call_target="tpu_custom_call", output_to_operand_aliasing={{}: (2, {})} | custom-call | tf_op jit(solution)/shard_map/own_rows/pallas_call | solution.py:416
  11.4 0.0 collective-permute-done.1.refs_2_.got_2
  11.5 2.7 %collective-permute-start.2 = (s32[4,32]{1,0:T(4,128)S(1)}, s32[4,32]{1,0:T(4,128)S(1)}, u32[]{:S(2)}, u32[]{:S(2)}) collective-permute-start(s32[4,32]{1,0:T(4,128)S(1)} %join.3), channel_id=1, source_target_pairs={{0,8},{2,10},{4,12},{6,14},{8,0},{10,2},{12,4},{14,6},{1,9},{3,11}... | collective-permute-start | bytes 1544 | tf_op jit(solution)/shard_map/ppermute | solution.py:546
  14.1 1.9 %collective-permute-done.2.got_4 = s32[4,32]{1,0:T(4,128)S(1)} collective-permute-done((s32[4,32]{1,0:T(4,128)S(1)}, s32[4,32]{1,0:T(4,128)S(1)}, u32[]{:S(2)}, u32[]{:S(2)}) %collective-permute-start.2) | collective-permute-done | bytes 544 | tf_op jit(solution)/shard_map/ppermute | solution.py:546
  16.0 0.0 copy-done.2
  16.0 0.0 copy-done.8
  16.0 0.0 copy-done.9
  16.0 2.7 %order.1 = (s32[2,18,16,128]{3,2,1,0:T(8,128)S(1)}, s32[1]{0:T(128)}) custom-call(s32[5]{0:T(128)S(1)} %stack.31.me, s32[1,32]{1,0:T(1,128)S(1)} %bitcast.68, s32[1,32]{1,0:T(1,128)S(1)} %collective-permute-done.refs_1_.got_1, s32[2,32]{1,0:T(2,128)S(1)} %collective-permute-done.1.refs_2_.got_2, s32[4,32]{1,0:T(4,128)S(1)} %collective-permute-done.2.got_4, ...), custom_call_target="tpu_custom_call" | custom-call | tf_op jit(solution)/shard_map/order/pallas_call | solution.py:392
  18.8 0.0 collective-permute-done.3.other
  18.8 0.0 copy-done.6
  18.8 0.0 copy-done.7
  18.8 12.7 %first_half.1 = (f32[65536,128]{1,0:T(8,128)S(1)}, bf16[2,272,256]{2,1,0:T(8,128)(2,1)}, bf16[3,272,256]{2,1,0:T(8,128)(2,1)}) custom-call(s32[5]{0:T(128)S(1)} %stack.31.me, s32[73728]{0:T(1024)S(1)} %bitcast.55, f32[65536,128]{1,0:T(8,128)S(1)} %own_rows.3.table_in, ...), custom_call_target="tpu_custom_call", output_to_operand_aliasing={{0}: (2, {})} | custom-call | tf_op jit(solution)/shard_map/first_half/pallas_call | solution.py:446
  31.5 0.6 %collective-permute-start.4 = (bf16[3,272,256]{2,1,0:T(8,128)(2,1)}, bf16[3,272,256]{2,1,0:T(8,128)(2,1)S(1)}, u32[]{:S(2)}, u32[]{:S(2)}) collective-permute-start(bf16[3,272,256]{2,1,0:T(8,128)(2,1)} %get-tuple-element.74.sent.weight), channel_id=1, source_target_pairs={{0,2},{2,0},{4,6},{6,4},{8,10},{10,8},{12,14},{14,12},{1,3},{3,1},... | collective-permute-start | bytes 1253384 | tf_op jit(solution)/shard_map/ppermute | solution.py:546
  32.1 0.0 copy-start
  32.1 0.0 copy-start.1
  32.1 0.0 copy-start.3
  32.1 0.0 copy-start.4
  32.1 0.0 copy-start.5
  32.1 0.0 copy-start.12
  32.1 0.0 copy-start.13
  32.2 0.0 copy-start.14
  32.2 9.2 %second_half.1 = (bf16[2,272,256]{2,1,0:T(8,128)(2,1)}, bf16[2,272,256]{2,1,0:T(8,128)(2,1)}) custom-call(s32[5]{0:T(128)S(1)} %stack.31.me, s32[73728]{0:T(1024)S(1)} %bitcast.56, f32[65536,128]{1,0:T(8,128)S(1)} %get-tuple-element.75.table), custom_call_target="tpu_custom_call" | custom-call | tf_op jit(solution)/shard_map/second_half/pallas_call | solution.py:468
  41.4 1.6 %collective-permute-start.5 = (bf16[2,272,256]{2,1,0:T(8,128)(2,1)}, bf16[2,272,256]{2,1,0:T(8,128)(2,1)S(1)}, u32[]{:S(2)}, u32[]{:S(2)}) collective-permute-start(bf16[2,272,256]{2,1,0:T(8,128)(2,1)} %get-tuple-element.78), channel_id=1, source_target_pairs={{0,2},{2,0},{4,6},{6,4},{8,10},{10,8},{12,14},{14,12},{1,3},{3,1},... | collective-permute-start | bytes 835592 | tf_op jit(solution)/shard_map/ppermute | solution.py:546
  43.0 0.0 collective-permute-done.4.got.weight_got
  43.0 0.0 copy-done
  43.0 0.0 copy-done.1
  43.0 1.5 %project_far.1 = (bf16[272,256]{1,0:T(8,128)(2,1)S(1)}, bf16[272,256]{1,0:T(8,128)(2,1)S(1)}, bf16[2,272,256]{2,1,0:T(8,128)(2,1)S(1)}) custom-call(s32[5]{0:T(128)S(1)} %stack.31.me, bf16[2,272,256]{2,1,0:T(8,128)(2,1)S(1)} %copy-done.1, bf16[3,272,256]{2,1,0:T(8,128)(2,1)S(1)} %collective-permute-done.4.got.weight_got, bf16[3,272,256]{2,1,0:T(8,128)(2,1)S(1)} %copy-done, ...), custom_call_target="tpu_custom_call" | custom-call | tf_op jit(solution)/shard_map/project_far/pallas_call | solution.py:483
  44.5 2.7 %collective-permute-start.6 = (bf16[272,256]{1,0:T(8,128)(2,1)S(1)}, bf16[272,256]{1,0:T(8,128)(2,1)S(1)}, u32[]{:S(2)}, u32[]{:S(2)}) collective-permute-start(bf16[272,256]{1,0:T(8,128)(2,1)S(1)} %get-tuple-element.80), channel_id=1, source_target_pairs={{0,8},{2,10},{4,12},{6,14},{8,0},{10,2},{12,4},{14,6},{1,9},{3,11}... | collective-permute-start | bytes 417800 | tf_op jit(solution)/shard_map/ppermute | solution.py:546
  47.2 0.2 collective-permute-start.7
  47.4 1.1 %collective-permute-done.5.got = bf16[2,272,256]{2,1,0:T(8,128)(2,1)S(1)} collective-permute-done((bf16[2,272,256]{2,1,0:T(8,128)(2,1)}, bf16[2,272,256]{2,1,0:T(8,128)(2,1)S(1)}, u32[]{:S(2)}, u32[]{:S(2)}) %collective-permute-start.5) | collective-permute-done | bytes 278560 | tf_op jit(solution)/shard_map/ppermute | solution.py:546
  48.5 0.8 %project_near.1 = (f32[272,256]{1,0:T(8,128)S(1)}, bf16[272,256]{1,0:T(8,128)(2,1)S(1)}) custom-call(s32[5]{0:T(128)S(1)} %stack.31.me, bf16[2,272,256]{2,1,0:T(8,128)(2,1)S(1)} %get-tuple-element.77.keep, bf16[2,272,256]{2,1,0:T(8,128)(2,1)S(1)} %collective-permute-done.5.got, bf16[3,272,256]{2,1,0:T(8,128)(2,1)S(1)} %copy-done, ...), custom_call_target="tpu_custom_call" | custom-call | tf_op jit(solution)/shard_map/project_near/pallas_call | solution.py:496
  49.3 0.5 collective-permute-start.8
  50.5 5.9 %collective-permute-done.6.a = bf16[272,256]{1,0:T(8,128)(2,1)S(1)} collective-permute-done((bf16[272,256]{1,0:T(8,128)(2,1)S(1)}, bf16[272,256]{1,0:T(8,128)(2,1)S(1)}, u32[]{:S(2)}, u32[]{:S(2)}) %collective-permute-start.6) | collective-permute-done | bytes 139296 | tf_op jit(solution)/shard_map/ppermute | solution.py:546
  56.4 0.0 collective-permute-done.7.b
  56.4 0.5 collective-permute-done.8.c
  56.9 0.0 copy-done.3
  56.9 0.0 copy-done.4
  56.9 0.0 copy-done.5
  56.9 0.0 copy-done.12
  56.9 0.0 copy-done.13
  56.9 0.0 copy-done.14
  57.0 0.7 %layer_two.1 = f32[32,153]{1,0:T(8,128)S(1)} custom-call(f32[272,256]{1,0:T(8,128)S(1)} %get-tuple-element.79.mine, bf16[272,256]{1,0:T(8,128)(2,1)S(1)} %collective-permute-done.6.a, bf16[272,256]{1,0:T(8,128)(2,1)S(1)} %collective-permute-done.7.b, bf16[272,256]{1,0:T(8,128)(2,1)S(1)} %collective-permute-done.8.c, s32[1,32]{1,0:T(1,128)S(1)} %bitcast.69, ...), custom_call_target="tpu_custom_call" | custom-call | tf_op jit(solution)/shard_map/layer_two/pallas_call | solution.py:509
  57.7 0.1 conditional.1
  57.8 0.0 copy-start.10
  57.8 0.6 %copy-done.10 = f32[32,153]{1,0:T(8,128)} copy-done((f32[32,153]{1,0:T(8,128)}, f32[32,153]{1,0:T(8,128)S(1)}, u32[]{:S(2)}) %copy-start.10) | copy-done | bytes 19608
  (2 shorter events, 0.0 us)
Async XLA Ops:
  0.0 18.8 %collective-permute-start.3 = (bf16[96,32768]{1,0:T(8,128)(2,1)}, bf16[96,32768]{1,0:T(8,128)(2,1)}, u32[]{:S(2)}, u32[]{:S(2)}) collective-permute-start(bf16[96,32768]{1,0:T(8,128)(2,1)} %features.3), channel_id=1, source_target_pairs={{0,1},{1,0},{2,3},{3,2},{4,5},{5,4},{6,7},{7,6},{8,9},{9,8},{10,11... | collective-permute-start | bytes 18874376 | tf_op jit(solution)/shard_map/ppermute | solution.py:548
  0.5 5.9 %collective-permute-start = (s32[1,32]{1,0:T(1,128)}, s32[1,32]{1,0:T(1,128)S(1)}, u32[]{:S(2)}, u32[]{:S(2)}) collective-permute-start(s32[1,32]{1,0:T(1,128)} %bitcast.65), channel_id=1, source_target_pairs={{0,2},{2,0},{4,6},{6,4},{8,10},{10,8},{12,14},{14,12},{1,3},{3,1},... | collective-permute-start | bytes 392 | tf_op jit(solution)/shard_map/ppermute | solution.py:546
  3.0 3.4 %copy-start.11 = (s32[32]{0:T(128)S(1)}, s32[32]{0:T(128)}, u32[]{:S(2)}) copy-start(s32[32]{0:T(128)} %param.19) | copy-start | bytes 388
  6.4 9.6 %copy-start.2 = (s32[15,2816]{1,0:T(8,128)S(1)}, s32[15,2816]{1,0:T(8,128)}, u32[]{:S(2)}) copy-start(s32[15,2816]{1,0:T(8,128)} %neighbour_ids.1) | copy-start | bytes 506884
  6.4 9.6 %copy-start.8 = (s32[2816]{0:T(1024)S(1)}, s32[2816]{0:T(1024)}, u32[]{:S(2)}) copy-start(s32[2816]{0:T(1024)} %count_one.1) | copy-start | bytes 33796
  6.4 9.6 %copy-start.9 = (s32[2816]{0:T(1024)S(1)}, s32[2816]{0:T(1024)}, u32[]{:S(2)}) copy-start(s32[2816]{0:T(1024)} %self_ids.1) | copy-start | bytes 33796
  6.4 12.3 %copy-start.6 = (bf16[96,256]{1,0:T(8,128)(2,1)S(1)}, bf16[96,256]{1,0:T(8,128)(2,1)}, u32[]{:S(2)}) copy-start(bf16[96,256]{1,0:T(8,128)(2,1)} %self_one.1) | copy-start | bytes 147460
  6.4 12.3 %copy-start.7 = (bf16[96,256]{1,0:T(8,128)(2,1)S(1)}, bf16[96,256]{1,0:T(8,128)(2,1)}, u32[]{:S(2)}) copy-start(bf16[96,256]{1,0:T(8,128)(2,1)} %neigh_one.1) | copy-start | bytes 147460
  6.5 5.0 %collective-permute-start.1 = (s32[2,32]{1,0:T(2,128)S(1)}, s32[2,32]{1,0:T(2,128)S(1)}, u32[]{:S(2)}, u32[]{:S(2)}) collective-permute-start(s32[2,32]{1,0:T(2,128)S(1)} %join.2), channel_id=1, source_target_pairs={{0,4},{2,6},{4,0},{6,2},{8,12},{10,14},{12,8},{14,10},{1,5},{3,7},... | collective-permute-start | bytes 776 | tf_op jit(solution)/shard_map/ppermute | solution.py:546
  11.5 4.5 %collective-permute-start.2 = (s32[4,32]{1,0:T(4,128)S(1)}, s32[4,32]{1,0:T(4,128)S(1)}, u32[]{:S(2)}, u32[]{:S(2)}) collective-permute-start(s32[4,32]{1,0:T(4,128)S(1)} %join.3), channel_id=1, source_target_pairs={{0,8},{2,10},{4,12},{6,14},{8,0},{10,2},{12,4},{14,6},{1,9},{3,11}... | collective-permute-start | bytes 1544 | tf_op jit(solution)/shard_map/ppermute | solution.py:546
  31.5 11.5 %collective-permute-start.4 = (bf16[3,272,256]{2,1,0:T(8,128)(2,1)}, bf16[3,272,256]{2,1,0:T(8,128)(2,1)S(1)}, u32[]{:S(2)}, u32[]{:S(2)}) collective-permute-start(bf16[3,272,256]{2,1,0:T(8,128)(2,1)} %get-tuple-element.74.sent.weight), channel_id=1, source_target_pairs={{0,2},{2,0},{4,6},{6,4},{8,10},{10,8},{12,14},{14,12},{1,3},{3,1},... | collective-permute-start | bytes 1253384 | tf_op jit(solution)/shard_map/ppermute | solution.py:546
  32.1 10.9 %copy-start = (bf16[3,272,256]{2,1,0:T(8,128)(2,1)S(1)}, bf16[3,272,256]{2,1,0:T(8,128)(2,1)}, u32[]{:S(2)}) copy-start(bf16[3,272,256]{2,1,0:T(8,128)(2,1)} %get-tuple-element.74.sent.weight) | copy-start | bytes 1253380
  32.1 10.9 %copy-start.1 = (bf16[2,272,256]{2,1,0:T(8,128)(2,1)S(1)}, bf16[2,272,256]{2,1,0:T(8,128)(2,1)}, u32[]{:S(2)}) copy-start(bf16[2,272,256]{2,1,0:T(8,128)(2,1)} %get-tuple-element.73.keep) | copy-start | bytes 835588
  32.1 24.8 %copy-start.3 = (bf16[256,256]{1,0:T(8,128)(2,1)S(1)}, bf16[256,256]{1,0:T(8,128)(2,1)}, u32[]{:S(2)}) copy-start(bf16[256,256]{1,0:T(8,128)(2,1)} %neigh_two.1) | copy-start | bytes 393220
  32.1 24.8 %copy-start.4 = (bf16[256,256]{1,0:T(8,128)(2,1)S(1)}, bf16[256,256]{1,0:T(8,128)(2,1)}, u32[]{:S(2)}) copy-start(bf16[256,256]{1,0:T(8,128)(2,1)} %self_two.1) | copy-start | bytes 393220
  32.1 24.8 %copy-start.5 = (bf16[256,153]{0,1:T(8,128)(2,1)S(1)}, bf16[256,153]{0,1:T(8,128)(2,1)}, u32[]{:S(2)}) copy-start(bf16[256,153]{0,1:T(8,128)(2,1)} %param.26) | copy-start | bytes 235012
  32.1 24.8 %copy-start.12 = (f32[256]{0:T(256)S(1)}, f32[256]{0:T(256)}, u32[]{:S(2)}) copy-start(f32[256]{0:T(256)} %param.25) | copy-start | bytes 3076
  32.1 24.8 %copy-start.13 = (f32[153]{0:T(256)S(1)}, f32[153]{0:T(256)}, u32[]{:S(2)}) copy-start(f32[153]{0:T(256)} %param.27) | copy-start | bytes 1840
  32.2 24.8 %copy-start.14 = (f32[256]{0:T(256)S(1)}, f32[256]{0:T(256)}, u32[]{:S(2)}) copy-start(f32[256]{0:T(256)} %param.22) | copy-start | bytes 3076
  41.4 7.1 %collective-permute-start.5 = (bf16[2,272,256]{2,1,0:T(8,128)(2,1)}, bf16[2,272,256]{2,1,0:T(8,128)(2,1)S(1)}, u32[]{:S(2)}, u32[]{:S(2)}) collective-permute-start(bf16[2,272,256]{2,1,0:T(8,128)(2,1)} %get-tuple-element.78), channel_id=1, source_target_pairs={{0,2},{2,0},{4,6},{6,4},{8,10},{10,8},{12,14},{14,12},{1,3},{3,1},... | collective-permute-start | bytes 835592 | tf_op jit(solution)/shard_map/ppermute | solution.py:546
  44.5 11.9 %collective-permute-start.6 = (bf16[272,256]{1,0:T(8,128)(2,1)S(1)}, bf16[272,256]{1,0:T(8,128)(2,1)S(1)}, u32[]{:S(2)}, u32[]{:S(2)}) collective-permute-start(bf16[272,256]{1,0:T(8,128)(2,1)S(1)} %get-tuple-element.80), channel_id=1, source_target_pairs={{0,8},{2,10},{4,12},{6,14},{8,0},{10,2},{12,4},{14,6},{1,9},{3,11}... | collective-permute-start | bytes 417800 | tf_op jit(solution)/shard_map/ppermute | solution.py:546
  47.2 9.2 %collective-permute-start.7 = (bf16[272,256]{1,0:T(8,128)(2,1)S(1)}, bf16[272,256]{1,0:T(8,128)(2,1)S(1)}, u32[]{:S(2)}, u32[]{:S(2)}) collective-permute-start(bf16[272,256]{1,0:T(8,128)(2,1)S(1)} %get-tuple-element.81), channel_id=1, source_target_pairs={{0,12},{2,14},{4,8},{6,10},{8,4},{10,6},{12,0},{14,2},{1,13},{3,15... | collective-permute-start | bytes 417800 | tf_op jit(solution)/shard_map/ppermute | solution.py:546
  49.3 7.6 %collective-permute-start.8 = (bf16[272,256]{1,0:T(8,128)(2,1)S(1)}, bf16[272,256]{1,0:T(8,128)(2,1)S(1)}, u32[]{:S(2)}, u32[]{:S(2)}) collective-permute-start(bf16[272,256]{1,0:T(8,128)(2,1)S(1)} %get-tuple-element.82), channel_id=1, source_target_pairs={{0,4},{2,6},{4,0},{6,2},{8,12},{10,14},{12,8},{14,10},{1,5},{3,7},... | collective-permute-start | bytes 417800 | tf_op jit(solution)/shard_map/ppermute | solution.py:546
  57.8 0.6 %copy-start.10 = (f32[32,153]{1,0:T(8,128)}, f32[32,153]{1,0:T(8,128)S(1)}, u32[]{:S(2)}) copy-start(f32[32,153]{1,0:T(8,128)S(1)} %get-tuple-element.162) | copy-start | bytes 58756

commit v6 on v5

--- a/solution.py
+++ b/solution.py
@@ -118,7 +118,7 @@
 
 
 def order_kernel(
-    per_seed, me, own, got_1, got_2, got_4, self_ids, neighbour_ids, count_one, lists, most, counts_rel
+    per_seed, me, own, got_1, got_2, got_4, got_6, self_ids, neighbour_ids, count_one, lists, most, counts_rel
 ):
     owners, seeds = counts_rel.shape
     fanout = neighbour_ids.shape[0]
@@ -128,7 +128,8 @@
     counts_rel[0:1, :] = own[...]
     counts_rel[1:2, :] = got_1[...]
     counts_rel[2:4, :] = got_2[...]
-    counts_rel[4:8, :] = got_4[...]
+    counts_rel[4:6, :] = got_4[...]
+    counts_rel[6:8, :] = got_6[...]
     own_ids = self_ids[...].reshape(1, owners * per_owner)
     ones = count_one[...].reshape(1, owners * per_owner)
     counts = jnp.concatenate(
@@ -338,14 +339,14 @@
         ).astype(out.dtype)
 
 
-def project_far_kernel(me, keep, got, sent, later, out_0, out_1, loaded, sem):
-    copy = pltpu.make_async_copy(later, loaded, sem)
+def project_far_kernel(me, keep, got, sent, out_0, out_1):
+    project(me[3], keep, got, sent, got, (out_0, out_1))
+
+
+def project_near_kernel(me, keep_hbm, got, weight, weight_got, out_0, out_1, keep, sem):
+    copy = pltpu.make_async_copy(keep_hbm, keep, sem)
     copy.start()
-    project(me[3], keep, got, sent, got, (out_0, out_1))
     copy.wait()
-
-
-def project_near_kernel(me, keep, got, weight, weight_got, out_0, out_1):
     project(me[3], keep, got, weight, weight_got, (out_0, out_1))
 
 
@@ -392,7 +393,7 @@
     lists, most = pl.pallas_call(
         functools.partial(order_kernel, per_seed),
         out_shape=(shape((2, neighbour_ids.shape[0] + 3, 16, LANES), I32), shape((1,), I32)),
-        in_specs=[SMEM] + [VMEM] * 7,
+        in_specs=[SMEM] + [VMEM] * 8,
         out_specs=(VMEM, SMEM),
         scratch_shapes=[pltpu.VMEM((owners, own.shape[1]), I32)],
         compiler_params=params(10),
@@ -478,17 +479,16 @@
     )(me, lists, table)
 
 
-def project_far_call(me, keep, got, sent, later):
+def project_far_call(me, keep, got, sent):
     part = shape((CAP, sent.shape[2]), BF16)
     return pl.pallas_call(
         project_far_kernel,
-        out_shape=(part, part, shape(later.shape, BF16)),
-        in_specs=[SMEM, VMEM, VMEM, VMEM, HBM],
-        out_specs=(VMEM, VMEM, VMEM),
-        scratch_shapes=[pltpu.SemaphoreType.DMA],
+        out_shape=(part, part),
+        in_specs=[SMEM, VMEM, VMEM, VMEM],
+        out_specs=(VMEM, VMEM),
         compiler_params=params(10),
         name="project_far",
-    )(me, keep, got, sent, pltpu.with_memory_space_constraint(later, pltpu.HBM))
+    )(me, keep, got, sent)
 
 
 def project_near_call(me, keep, got, weight, weight_got):
@@ -496,8 +496,9 @@
     return pl.pallas_call(
         project_near_kernel,
         out_shape=(shape(dims, F32), shape(dims, BF16)),
-        in_specs=[SMEM, VMEM, VMEM, VMEM, VMEM],
+        in_specs=[SMEM, HBM, VMEM, VMEM, VMEM],
         out_specs=(VMEM, VMEM),
+        scratch_shapes=[pltpu.VMEM(keep.shape, BF16), pltpu.SemaphoreType.DMA],
         compiler_params=params(10),
         name="project_near",
     )(me, keep, got, weight, weight_got)
@@ -550,19 +551,20 @@
     own = count_two[None, :]
     got_1 = across(own, 1)
     table, got_1 = lax.optimization_barrier((own_call(0, 2, me, held), got_1))
-    got_2 = across(join_call(own, got_1), 2)
-    table, got_2 = lax.optimization_barrier((own_call(1, 2, me, held, table), got_2))
-    got_4 = across(join_call(own, got_1, got_2), 4)
-    got = (got_1, got_2, got_4)
+    pair = join_call(own, got_1)
+    got = tuple(across(pair, bit) for bit in (4, 6, 2))
+    table, *got = lax.optimization_barrier((own_call(1, 2, me, held, table), *got))
+    got = (got_1, got[2], got[0], got[1])
     lists, most = order_call(per_seed, me, own, got, self_ids, neighbour_ids, count_one)
     table, keep_far, send_far = first_call(
         fanout, me, lists, table, other, self_one, neigh_one
     )
     got_far = across(send_far, 1)
     keep_near, send_near = second_call(fanout, width, me, lists, table)
+    far_0, far_1 = project_far_call(me, keep_far, got_far, send_far)
+    far_0, far_1, send_near = lax.optimization_barrier((far_0, far_1, send_near))
+    far = [across(far_0, 4), across(far_1, 6)]
     got_near = across(send_near, 1)
-    far_0, far_1, keep_near = project_far_call(me, keep_far, got_far, send_far, keep_near)
-    far = [across(far_0, 4), across(far_1, 6)]
     near_0, near_1 = project_near_call(me, keep_near, got_near, send_far, got_far)
     far.append(across(near_1, 2))
     fast = last_call(

time: 59.1 us -> 58 us (0.981); the launches traced: 58.4 us -> 58.2 us
  waiting for transfers between devices: 9.44 us -> 7.93 us
  starting transfers between devices: 12.7 us -> 14 us
  Pallas kernels: 34.5 us -> 33.5 us
  local copies, waits for them, and re-layouts: 0.77 us -> 1.72 us
    ppermute x8 -> x9, waiting for transfers between devices: 9.44 us -> 7.93 us  [across(): return lax.ppermute(value, 'col', [(i, i ^ bit) for i in range(owners)])]
    ppermute x8 -> x9, starting transfers between devices: 12.3 us -> 13.6 us  [across(): return lax.ppermute(value, 'col', [(i, i ^ bit) for i in range(owners)])]
    unnamed x30 -> x32, local copies, waits for them, and re-layouts: 0.68 us -> 1.64 us
    pallas_call x1, Pallas kernels: 1.53 us -> 0.84 us  [project_far_call(): pl.pallas_call(project_far_kernel, out_shape=(part, part), in_specs=[SMEM...]
  transfers between devices with their start and end apart: 9 -> 10, of which waited for: 4 -> 5; matrix products, arithmetic and copies ran while one was open for 0% -> 0% of each run, Pallas kernels for 36% -> 33%
where the time goes in v6:
time: 58 us; the launch traced here: 58.2 us
  Pallas kernels  33.5 us (58%)
  starting transfers between devices  14 us (24%)
  waiting for transfers between devices  7.93 us (14%)
  local copies, waits for them, and re-layouts  1.72 us (3%)
  between operations  0.91 us (2%)
    ppermute x9, starting transfers between devices, across(): return lax.ppermute(value, 'col', [(i, i ^ bit) for i in range(owners)])  13.6 us
    pallas_call x1, Pallas kernels, first_call(): pl.pallas_call(functools.partial(first_kernel, fanout), out_shape=(shape(...  12.5 us
    pallas_call x1, Pallas kernels, second_call(): pl.pallas_call(functools.partial(second_kernel, fanout, width), out_shape...  9.1 us
    ppermute x9, waiting for transfers between devices, across(): return lax.ppermute(value, 'col', [(i, i ^ bit) for i in range(owners)])  7.93 us
    pallas_call x2, Pallas kernels, own_call(): pl.pallas_call(functools.partial(own_kernel, which, halves), out_shape=sh...  6.66 us
    pallas_call x1, Pallas kernels, order_call(): pl.pallas_call(functools.partial(order_kernel, per_seed), out_shape=(shap...  2.72 us
    unnamed x32, local copies, waits for them, and re-layouts  1.64 us
  transfers between devices with their start and end apart: 10, of which 5 were waited for; matrix products, arithmetic and copies ran while one was open for 0% of the time, Pallas kernels for 33%

profile of v6, /device:TPU:0, one launch (start us, length us, event | category | flops | bytes accessed | tf_op | source)
XLA Modules:
  0.0 58.2 jit_solution(3295896032651619182)
XLA Ops:
  0.0 0.5 collective-permute-start.4
  0.5 2.5 %collective-permute-start = (s32[1,32]{1,0:T(1,128)}, s32[1,32]{1,0:T(1,128)S(1)}, u32[]{:S(2)}, u32[]{:S(2)}) collective-permute-start(s32[1,32]{1,0:T(1,128)} %bitcast.65), channel_id=1, source_target_pairs={{0,2},{2,0},{4,6},{6,4},{8,10},{10,8},{12,14},{14,12},{1,3},{3,1},... | collective-permute-start | bytes 392 | tf_op jit(solution)/shard_map/ppermute | solution.py:547
  2.9 0.1 stack.31.me
  3.0 0.0 copy-start.12
  3.0 3.3 %own_rows.2.refs_0_ = f32[65536,128]{1,0:T(8,128)S(1)} custom-call(s32[5]{0:T(128)S(1)} %stack.31.me, bf16[96,32768]{1,0:T(8,128)(2,1)} %features.3), custom_call_target="tpu_custom_call" | custom-call | tf_op jit(solution)/shard_map/own_rows/pallas_call | solution.py:417
  6.4 0.0 collective-permute-done.refs_1_.got_1
  6.4 0.0 copy-done.12
  6.4 0.0 copy-start.3
  6.4 0.0 copy-start.9
  6.4 0.0 copy-start.10
  6.4 0.0 copy-start.7
  6.4 0.0 copy-start.8
  6.5 2.7 %collective-permute-start.1 = (s32[2,32]{1,0:T(2,128)S(1)}, s32[2,32]{1,0:T(2,128)S(1)}, u32[]{:S(2)}, u32[]{:S(2)}) collective-permute-start(s32[2,32]{1,0:T(2,128)S(1)} %join.1), channel_id=1, source_target_pairs={{0,8},{2,10},{4,12},{6,14},{8,0},{10,2},{12,4},{14,6},{1,9},{3,11}... | collective-permute-start | bytes 776 | tf_op jit(solution)/shard_map/ppermute | solution.py:547
  9.1 1.3 %collective-permute-start.2 = (s32[2,32]{1,0:T(2,128)S(1)}, s32[2,32]{1,0:T(2,128)S(1)}, u32[]{:S(2)}, u32[]{:S(2)}) collective-permute-start(s32[2,32]{1,0:T(2,128)S(1)} %join.1), channel_id=1, source_target_pairs={{0,12},{2,14},{4,8},{6,10},{8,4},{10,6},{12,0},{14,2},{1,13},{3,15... | collective-permute-start | bytes 776 | tf_op jit(solution)/shard_map/ppermute | solution.py:547
  10.5 0.2 collective-permute-start.3
  10.7 3.3 %own_rows.3.table_in = f32[65536,128]{1,0:T(8,128)S(1)} custom-call(s32[5]{0:T(128)S(1)} %stack.31.me, bf16[96,32768]{1,0:T(8,128)(2,1)} %features.3, f32[65536,128]{1,0:T(8,128)S(1)} %own_rows.2.refs_0_), custom_call_target="tpu_custom_call", output_to_operand_aliasing={{}: (2, {})} | custom-call | tf_op jit(solution)/shard_map/own_rows/pallas_call | solution.py:417
  14.0 0.0 collective-permute-done.1.got_4
  14.0 0.4 collective-permute-done.2.got_6
  14.5 0.0 collective-permute-done.3.got_2
  14.5 0.0 copy-done.3
  14.5 0.0 copy-done.9
  14.5 0.0 copy-done.10
  14.5 2.7 %order.1 = (s32[2,18,16,128]{3,2,1,0:T(8,128)S(1)}, s32[1]{0:T(128)}) custom-call(s32[5]{0:T(128)S(1)} %stack.31.me, s32[1,32]{1,0:T(1,128)S(1)} %bitcast.67, s32[1,32]{1,0:T(1,128)S(1)} %collective-permute-done.refs_1_.got_1, s32[2,32]{1,0:T(2,128)S(1)} %collective-permute-done.3.got_2, s32[2,32]{1,0:T(2,128)S(1)} %collective-permute-done.1.got_4, ...), custom_call_target="tpu_custom_call" | custom-call | tf_op jit(solution)/shard_map/order/pallas_call | solution.py:393
  17.2 0.0 collective-permute-done.4.other
  17.2 0.0 copy-done.7
  17.3 0.0 copy-done.8
  17.3 12.5 %first_half.1 = (f32[65536,128]{1,0:T(8,128)S(1)}, bf16[2,272,256]{2,1,0:T(8,128)(2,1)}, bf16[3,272,256]{2,1,0:T(8,128)(2,1)}) custom-call(s32[5]{0:T(128)S(1)} %stack.31.me, s32[73728]{0:T(1024)S(1)} %bitcast.55, f32[65536,128]{1,0:T(8,128)S(1)} %own_rows.3.table_in, ...), custom_call_target="tpu_custom_call", output_to_operand_aliasing={{0}: (2, {})} | custom-call | tf_op jit(solution)/shard_map/first_half/pallas_call | solution.py:447
  29.8 0.6 %collective-permute-start.5 = (bf16[3,272,256]{2,1,0:T(8,128)(2,1)}, bf16[3,272,256]{2,1,0:T(8,128)(2,1)S(1)}, u32[]{:S(2)}, u32[]{:S(2)}) collective-permute-start(bf16[3,272,256]{2,1,0:T(8,128)(2,1)} %get-tuple-element.82.sent.weight), channel_id=1, source_target_pairs={{0,2},{2,0},{4,6},{6,4},{8,10},{10,8},{12,14},{14,12},{1,3},{3,1},... | collective-permute-start | bytes 1253384 | tf_op jit(solution)/shard_map/ppermute | solution.py:547
  30.4 0.0 copy-start
  30.4 0.0 copy-start.2
  30.4 0.0 copy-start.4
  30.4 0.0 copy-start.5
  30.4 0.0 copy-start.6
  30.4 0.0 copy-start.13
  30.4 0.0 copy-start.14
  30.4 0.0 copy-start.15
  30.4 9.1 %second_half.1 = (bf16[2,272,256]{2,1,0:T(8,128)(2,1)}, bf16[2,272,256]{2,1,0:T(8,128)(2,1)}) custom-call(s32[5]{0:T(128)S(1)} %stack.31.me, s32[73728]{0:T(1024)S(1)} %bitcast.56, f32[65536,128]{1,0:T(8,128)S(1)} %get-tuple-element.79.table), custom_call_target="tpu_custom_call" | custom-call | tf_op jit(solution)/shard_map/second_half/pallas_call | solution.py:469
  39.5 1.7 %collective-permute-done.5.got.weight_got = bf16[3,272,256]{2,1,0:T(8,128)(2,1)S(1)} collective-permute-done((bf16[3,272,256]{2,1,0:T(8,128)(2,1)}, bf16[3,272,256]{2,1,0:T(8,128)(2,1)S(1)}, u32[]{:S(2)}, u32[]{:S(2)}) %collective-permute-start.5) | collective-permute-done | bytes 417824 | tf_op jit(solution)/shard_map/ppermute | solution.py:547
  41.2 0.0 copy-done
  41.2 0.0 copy-done.2
  41.2 0.8 %project_far.1 = (bf16[272,256]{1,0:T(8,128)(2,1)S(1)}, bf16[272,256]{1,0:T(8,128)(2,1)S(1)}) custom-call(s32[5]{0:T(128)S(1)} %stack.31.me, bf16[2,272,256]{2,1,0:T(8,128)(2,1)S(1)} %copy-done.2, bf16[3,272,256]{2,1,0:T(8,128)(2,1)S(1)} %collective-permute-done.5.got.weight_got, bf16[3,272,256]{2,1,0:T(8,128)(2,1)S(1)} %copy-done), custom_call_target="tpu_custom_call" | custom-call | tf_op jit(solution)/shard_map/project_far/pallas_call | solution.py:484
  42.1 0.6 %collective-permute-start.6 = (bf16[2,272,256]{2,1,0:T(8,128)(2,1)}, bf16[2,272,256]{2,1,0:T(8,128)(2,1)S(1)}, u32[]{:S(2)}, u32[]{:S(2)}) collective-permute-start(bf16[2,272,256]{2,1,0:T(8,128)(2,1)} %get-tuple-element.86), channel_id=1, source_target_pairs={{0,2},{2,0},{4,6},{6,4},{8,10},{10,8},{12,14},{14,12},{1,3},{3,1},... | collective-permute-start | bytes 835592 | tf_op jit(solution)/shard_map/ppermute | solution.py:547
  42.7 2.6 %collective-permute-start.7 = (bf16[272,256]{1,0:T(8,128)(2,1)S(1)}, bf16[272,256]{1,0:T(8,128)(2,1)S(1)}, u32[]{:S(2)}, u32[]{:S(2)}) collective-permute-start(bf16[272,256]{1,0:T(8,128)(2,1)S(1)} %get-tuple-element.88), channel_id=1, source_target_pairs={{0,8},{2,10},{4,12},{6,14},{8,0},{10,2},{12,4},{14,6},{1,9},{3,11}... | collective-permute-start | bytes 417800 | tf_op jit(solution)/shard_map/ppermute | solution.py:547
  45.3 1.2 %collective-permute-start.8 = (bf16[272,256]{1,0:T(8,128)(2,1)S(1)}, bf16[272,256]{1,0:T(8,128)(2,1)S(1)}, u32[]{:S(2)}, u32[]{:S(2)}) collective-permute-start(bf16[272,256]{1,0:T(8,128)(2,1)S(1)} %get-tuple-element.89), channel_id=1, source_target_pairs={{0,12},{2,14},{4,8},{6,10},{8,4},{10,6},{12,0},{14,2},{1,13},{3,15... | collective-permute-start | bytes 417800 | tf_op jit(solution)/shard_map/ppermute | solution.py:547
  46.6 3.1 %collective-permute-done.6.got = bf16[2,272,256]{2,1,0:T(8,128)(2,1)S(1)} collective-permute-done((bf16[2,272,256]{2,1,0:T(8,128)(2,1)}, bf16[2,272,256]{2,1,0:T(8,128)(2,1)S(1)}, u32[]{:S(2)}, u32[]{:S(2)}) %collective-permute-start.6) | collective-permute-done | bytes 278560 | tf_op jit(solution)/shard_map/ppermute | solution.py:547
  49.7 0.0 copy-start.1
  49.7 1.0 %copy-done.1 = bf16[2,272,256]{2,1,0:T(8,128)(2,1)S(1)} copy-done((bf16[2,272,256]{2,1,0:T(8,128)(2,1)S(1)}, bf16[2,272,256]{2,1,0:T(8,128)(2,1)}, u32[]{:S(2)}) %copy-start.1) | copy-done | bytes 278552
  50.6 0.9 %project_near.1 = (f32[272,256]{1,0:T(8,128)S(1)}, bf16[272,256]{1,0:T(8,128)(2,1)S(1)}) custom-call(s32[5]{0:T(128)S(1)} %stack.31.me, bf16[2,272,256]{2,1,0:T(8,128)(2,1)S(1)} %copy-done.1, bf16[2,272,256]{2,1,0:T(8,128)(2,1)S(1)} %collective-permute-done.6.got, bf16[3,272,256]{2,1,0:T(8,128)(2,1)S(1)} %copy-done, ...), custom_call_target="tpu_custom_call" | custom-call | tf_op jit(solution)/shard_map/project_near/pallas_call | solution.py:496
  51.5 1.8 %collective-permute-start.9 = (bf16[272,256]{1,0:T(8,128)(2,1)S(1)}, bf16[272,256]{1,0:T(8,128)(2,1)S(1)}, u32[]{:S(2)}, u32[]{:S(2)}) collective-permute-start(bf16[272,256]{1,0:T(8,128)(2,1)S(1)} %get-tuple-element.90), channel_id=1, source_target_pairs={{0,4},{2,6},{4,0},{6,2},{8,12},{10,14},{12,8},{14,10},{1,5},{3,7},... | collective-permute-start | bytes 417800 | tf_op jit(solution)/shard_map/ppermute | solution.py:547
  54.0 0.9 %collective-permute-done.7.a = bf16[272,256]{1,0:T(8,128)(2,1)S(1)} collective-permute-done((bf16[272,256]{1,0:T(8,128)(2,1)S(1)}, bf16[272,256]{1,0:T(8,128)(2,1)S(1)}, u32[]{:S(2)}, u32[]{:S(2)}) %collective-permute-start.7) | collective-permute-done | bytes 139296 | tf_op jit(solution)/shard_map/ppermute | solution.py:547
  54.9 0.0 collective-permute-done.8.b
  54.9 1.8 %collective-permute-done.9.c = bf16[272,256]{1,0:T(8,128)(2,1)S(1)} collective-permute-done((bf16[272,256]{1,0:T(8,128)(2,1)S(1)}, bf16[272,256]{1,0:T(8,128)(2,1)S(1)}, u32[]{:S(2)}, u32[]{:S(2)}) %collective-permute-start.9) | collective-permute-done | bytes 139296 | tf_op jit(solution)/shard_map/ppermute | solution.py:547
  56.7 0.0 copy-done.4
  56.7 0.0 copy-done.5
  56.7 0.0 copy-done.6
  56.7 0.0 copy-done.13
  56.7 0.0 copy-done.14
  56.7 0.0 copy-done.15
  56.7 0.7 %layer_two.1 = f32[32,153]{1,0:T(8,128)S(1)} custom-call(f32[272,256]{1,0:T(8,128)S(1)} %get-tuple-element.87.mine, bf16[272,256]{1,0:T(8,128)(2,1)S(1)} %collective-permute-done.7.a, bf16[272,256]{1,0:T(8,128)(2,1)S(1)} %collective-permute-done.8.b, bf16[272,256]{1,0:T(8,128)(2,1)S(1)} %collective-permute-done.9.c, s32[1,32]{1,0:T(1,128)S(1)} %bitcast.68, ...), custom_call_target="tpu_custom_call" | custom-call | tf_op jit(solution)/shard_map/layer_two/pallas_call | solution.py:510
  57.4 0.1 conditional.1
  57.6 0.0 copy-start.11
  57.6 0.6 %copy-done.11 = f32[32,153]{1,0:T(8,128)} copy-done((f32[32,153]{1,0:T(8,128)}, f32[32,153]{1,0:T(8,128)S(1)}, u32[]{:S(2)}) %copy-start.11) | copy-done | bytes 19608
  (1 shorter events, 0.0 us)
Async XLA Ops:
  0.0 17.2 %collective-permute-start.4 = (bf16[96,32768]{1,0:T(8,128)(2,1)}, bf16[96,32768]{1,0:T(8,128)(2,1)}, u32[]{:S(2)}, u32[]{:S(2)}) collective-permute-start(bf16[96,32768]{1,0:T(8,128)(2,1)} %features.3), channel_id=1, source_target_pairs={{0,1},{1,0},{2,3},{3,2},{4,5},{5,4},{6,7},{7,6},{8,9},{9,8},{10,11... | collective-permute-start | bytes 18874376 | tf_op jit(solution)/shard_map/ppermute | solution.py:549
  0.5 5.9 %collective-permute-start = (s32[1,32]{1,0:T(1,128)}, s32[1,32]{1,0:T(1,128)S(1)}, u32[]{:S(2)}, u32[]{:S(2)}) collective-permute-start(s32[1,32]{1,0:T(1,128)} %bitcast.65), channel_id=1, source_target_pairs={{0,2},{2,0},{4,6},{6,4},{8,10},{10,8},{12,14},{14,12},{1,3},{3,1},... | collective-permute-start | bytes 392 | tf_op jit(solution)/shard_map/ppermute | solution.py:547
  3.0 3.4 %copy-start.12 = (s32[32]{0:T(128)S(1)}, s32[32]{0:T(128)}, u32[]{:S(2)}) copy-start(s32[32]{0:T(128)} %param.19) | copy-start | bytes 388
  6.4 8.1 %copy-start.3 = (s32[15,2816]{1,0:T(8,128)S(1)}, s32[15,2816]{1,0:T(8,128)}, u32[]{:S(2)}) copy-start(s32[15,2816]{1,0:T(8,128)} %neighbour_ids.1) | copy-start | bytes 506884
  6.4 8.1 %copy-start.9 = (s32[2816]{0:T(1024)S(1)}, s32[2816]{0:T(1024)}, u32[]{:S(2)}) copy-start(s32[2816]{0:T(1024)} %count_one.1) | copy-start | bytes 33796
  6.4 8.1 %copy-start.10 = (s32[2816]{0:T(1024)S(1)}, s32[2816]{0:T(1024)}, u32[]{:S(2)}) copy-start(s32[2816]{0:T(1024)} %self_ids.1) | copy-start | bytes 33796
  6.4 10.8 %copy-start.7 = (bf16[96,256]{1,0:T(8,128)(2,1)S(1)}, bf16[96,256]{1,0:T(8,128)(2,1)}, u32[]{:S(2)}) copy-start(bf16[96,256]{1,0:T(8,128)(2,1)} %self_one.1) | copy-start | bytes 147460
  6.4 10.8 %copy-start.8 = (bf16[96,256]{1,0:T(8,128)(2,1)S(1)}, bf16[96,256]{1,0:T(8,128)(2,1)}, u32[]{:S(2)}) copy-start(bf16[96,256]{1,0:T(8,128)(2,1)} %neigh_one.1) | copy-start | bytes 147460
  6.5 7.6 %collective-permute-start.1 = (s32[2,32]{1,0:T(2,128)S(1)}, s32[2,32]{1,0:T(2,128)S(1)}, u32[]{:S(2)}, u32[]{:S(2)}) collective-permute-start(s32[2,32]{1,0:T(2,128)S(1)} %join.1), channel_id=1, source_target_pairs={{0,8},{2,10},{4,12},{6,14},{8,0},{10,2},{12,4},{14,6},{1,9},{3,11}... | collective-permute-start | bytes 776 | tf_op jit(solution)/shard_map/ppermute | solution.py:547
  9.1 5.4 %collective-permute-start.2 = (s32[2,32]{1,0:T(2,128)S(1)}, s32[2,32]{1,0:T(2,128)S(1)}, u32[]{:S(2)}, u32[]{:S(2)}) collective-permute-start(s32[2,32]{1,0:T(2,128)S(1)} %join.1), channel_id=1, source_target_pairs={{0,12},{2,14},{4,8},{6,10},{8,4},{10,6},{12,0},{14,2},{1,13},{3,15... | collective-permute-start | bytes 776 | tf_op jit(solution)/shard_map/ppermute | solution.py:547
  10.5 4.0 %collective-permute-start.3 = (s32[2,32]{1,0:T(2,128)S(1)}, s32[2,32]{1,0:T(2,128)S(1)}, u32[]{:S(2)}, u32[]{:S(2)}) collective-permute-start(s32[2,32]{1,0:T(2,128)S(1)} %join.1), channel_id=1, source_target_pairs={{0,4},{2,6},{4,0},{6,2},{8,12},{10,14},{12,8},{14,10},{1,5},{3,7},... | collective-permute-start | bytes 776 | tf_op jit(solution)/shard_map/ppermute | solution.py:547
  29.8 11.5 %collective-permute-start.5 = (bf16[3,272,256]{2,1,0:T(8,128)(2,1)}, bf16[3,272,256]{2,1,0:T(8,128)(2,1)S(1)}, u32[]{:S(2)}, u32[]{:S(2)}) collective-permute-start(bf16[3,272,256]{2,1,0:T(8,128)(2,1)} %get-tuple-element.82.sent.weight), channel_id=1, source_target_pairs={{0,2},{2,0},{4,6},{6,4},{8,10},{10,8},{12,14},{14,12},{1,3},{3,1},... | collective-permute-start | bytes 1253384 | tf_op jit(solution)/shard_map/ppermute | solution.py:547
  30.4 10.9 %copy-start = (bf16[3,272,256]{2,1,0:T(8,128)(2,1)S(1)}, bf16[3,272,256]{2,1,0:T(8,128)(2,1)}, u32[]{:S(2)}) copy-start(bf16[3,272,256]{2,1,0:T(8,128)(2,1)} %get-tuple-element.82.sent.weight) | copy-start | bytes 1253380
  30.4 10.9 %copy-start.2 = (bf16[2,272,256]{2,1,0:T(8,128)(2,1)S(1)}, bf16[2,272,256]{2,1,0:T(8,128)(2,1)}, u32[]{:S(2)}) copy-start(bf16[2,272,256]{2,1,0:T(8,128)(2,1)} %get-tuple-element.81.keep) | copy-start | bytes 835588
  30.4 26.3 %copy-start.4 = (bf16[256,256]{1,0:T(8,128)(2,1)S(1)}, bf16[256,256]{1,0:T(8,128)(2,1)}, u32[]{:S(2)}) copy-start(bf16[256,256]{1,0:T(8,128)(2,1)} %neigh_two.1) | copy-start | bytes 393220
  30.4 26.3 %copy-start.5 = (bf16[256,256]{1,0:T(8,128)(2,1)S(1)}, bf16[256,256]{1,0:T(8,128)(2,1)}, u32[]{:S(2)}) copy-start(bf16[256,256]{1,0:T(8,128)(2,1)} %self_two.1) | copy-start | bytes 393220
  30.4 26.3 %copy-start.6 = (bf16[256,153]{0,1:T(8,128)(2,1)S(1)}, bf16[256,153]{0,1:T(8,128)(2,1)}, u32[]{:S(2)}) copy-start(bf16[256,153]{0,1:T(8,128)(2,1)} %param.26) | copy-start | bytes 235012
  30.4 26.3 %copy-start.13 = (f32[256]{0:T(256)S(1)}, f32[256]{0:T(256)}, u32[]{:S(2)}) copy-start(f32[256]{0:T(256)} %param.25) | copy-start | bytes 3076
  30.4 26.3 %copy-start.14 = (f32[153]{0:T(256)S(1)}, f32[153]{0:T(256)}, u32[]{:S(2)}) copy-start(f32[153]{0:T(256)} %param.27) | copy-start | bytes 1840
  30.4 26.3 %copy-start.15 = (f32[256]{0:T(256)S(1)}, f32[256]{0:T(256)}, u32[]{:S(2)}) copy-start(f32[256]{0:T(256)} %param.22) | copy-start | bytes 3076
  42.1 7.6 %collective-permute-start.6 = (bf16[2,272,256]{2,1,0:T(8,128)(2,1)}, bf16[2,272,256]{2,1,0:T(8,128)(2,1)S(1)}, u32[]{:S(2)}, u32[]{:S(2)}) collective-permute-start(bf16[2,272,256]{2,1,0:T(8,128)(2,1)} %get-tuple-element.86), channel_id=1, source_target_pairs={{0,2},{2,0},{4,6},{6,4},{8,10},{10,8},{12,14},{14,12},{1,3},{3,1},... | collective-permute-start | bytes 835592 | tf_op jit(solution)/shard_map/ppermute | solution.py:547
  42.7 12.2 %collective-permute-start.7 = (bf16[272,256]{1,0:T(8,128)(2,1)S(1)}, bf16[272,256]{1,0:T(8,128)(2,1)S(1)}, u32[]{:S(2)}, u32[]{:S(2)}) collective-permute-start(bf16[272,256]{1,0:T(8,128)(2,1)S(1)} %get-tuple-element.88), channel_id=1, source_target_pairs={{0,8},{2,10},{4,12},{6,14},{8,0},{10,2},{12,4},{14,6},{1,9},{3,11}... | collective-permute-start | bytes 417800 | tf_op jit(solution)/shard_map/ppermute | solution.py:547
  45.3 9.6 %collective-permute-start.8 = (bf16[272,256]{1,0:T(8,128)(2,1)S(1)}, bf16[272,256]{1,0:T(8,128)(2,1)S(1)}, u32[]{:S(2)}, u32[]{:S(2)}) collective-permute-start(bf16[272,256]{1,0:T(8,128)(2,1)S(1)} %get-tuple-element.89), channel_id=1, source_target_pairs={{0,12},{2,14},{4,8},{6,10},{8,4},{10,6},{12,0},{14,2},{1,13},{3,15... | collective-permute-start | bytes 417800 | tf_op jit(solution)/shard_map/ppermute | solution.py:547
  49.7 1.0 %copy-start.1 = (bf16[2,272,256]{2,1,0:T(8,128)(2,1)S(1)}, bf16[2,272,256]{2,1,0:T(8,128)(2,1)}, u32[]{:S(2)}) copy-start(bf16[2,272,256]{2,1,0:T(8,128)(2,1)} %get-tuple-element.80.keep_hbm) | copy-start | bytes 835588
  51.5 5.1 %collective-permute-start.9 = (bf16[272,256]{1,0:T(8,128)(2,1)S(1)}, bf16[272,256]{1,0:T(8,128)(2,1)S(1)}, u32[]{:S(2)}, u32[]{:S(2)}) collective-permute-start(bf16[272,256]{1,0:T(8,128)(2,1)S(1)} %get-tuple-element.90), channel_id=1, source_target_pairs={{0,4},{2,6},{4,0},{6,2},{8,12},{10,14},{12,8},{14,10},{1,5},{3,7},... | collective-permute-start | bytes 417800 | tf_op jit(solution)/shard_map/ppermute | solution.py:547
  57.6 0.6 %copy-start.11 = (f32[32,153]{1,0:T(8,128)}, f32[32,153]{1,0:T(8,128)S(1)}, u32[]{:S(2)}) copy-start(f32[32,153]{1,0:T(8,128)S(1)} %get-tuple-element.172) | copy-start | bytes 58756

commit v7 on v6

--- a/solution.py
+++ b/solution.py
@@ -105,7 +105,7 @@
 def turn(source, table, base):
     width, length = source.shape
     step = 512
-    unroll = 4
+    unroll = 8
 
     def body(i, carry):
         for u in range(unroll):
@@ -298,7 +298,7 @@
 
 
 def first_kernel(
-    fanout, me, lists, table_in, other, self_one, neigh_one, table, keep_hbm, send_hbm, *scratch
+    fanout, me, lists, table_in, other, table, keep_hbm, send_hbm, *scratch
 ):
     del table_in
     ids = scratch[: fanout + 1]
@@ -310,9 +310,6 @@
     copies = list_copies(fanout, h, lists, ids, places, begins, sems)
     self_rows[...] = jnp.zeros_like(self_rows)
     mean_rows[...] = jnp.zeros_like(mean_rows)
-    send[2, :, :] = jnp.zeros(send.shape[1:], BF16)
-    send[2, 0:width, :] = self_one[...]
-    send[2, LANES : LANES + width, :] = neigh_one[...]
     turn_staged(staging, staged, table, (1 - rep) * length)
     look_up(fanout, copies, table, ids, places, begins, self_rows, mean_rows)
     write_out(x, width, self_rows, mean_rows, keep, send)
@@ -331,23 +328,29 @@
     hand_out(keep, send, keep_hbm, send_hbm, out_sems)
 
 
-def project(zl, keep, got, weight, weight_got, outs):
-    for which, out in ((zl, outs[0]), (1 - zl, outs[1])):
-        out[...] = (
-            jnp.dot(keep[which], weight[2, 0 : 2 * LANES, :], preferred_element_type=F32)
-            + jnp.dot(got[which], weight_got[2, 0 : 2 * LANES, :], preferred_element_type=F32)
-        ).astype(out.dtype)
-
-
-def project_far_kernel(me, keep, got, sent, out_0, out_1):
-    project(me[3], keep, got, sent, got, (out_0, out_1))
-
-
-def project_near_kernel(me, keep_hbm, got, weight, weight_got, out_0, out_1, keep, sem):
-    copy = pltpu.make_async_copy(keep_hbm, keep, sem)
-    copy.start()
-    copy.wait()
-    project(me[3], keep, got, weight, weight_got, (out_0, out_1))
+def partial(rows, self_one, neigh_one):
+    width = self_one.shape[0]
+    return jnp.dot(rows[:, 0:width], self_one[...], preferred_element_type=F32) + jnp.dot(
+        rows[:, LANES : LANES + width], neigh_one[...], preferred_element_type=F32
+    )
+
+
+def far_kernel(me, keep, got, self_one, neigh_one, self_got, neigh_got, out_0, out_1):
+    zl = me[3]
+    for which, out in ((zl, out_0), (1 - zl, out_1)):
+        total = partial(keep[which], self_one, neigh_one) + partial(got[which], self_got, neigh_got)
+        out[...] = total.astype(BF16)
+
+
+def own_near_kernel(keep, self_one, neigh_one, out):
+    for z in range(2):
+        out[z, :, :] = partial(keep[z], self_one, neigh_one)
+
+
+def near_kernel(me, own, got, self_got, neigh_got, out_0, out_1):
+    zl = me[3]
+    out_0[...] = own[zl] + partial(got[zl], self_got, neigh_got)
+    out_1[...] = (own[1 - zl] + partial(got[1 - zl], self_got, neigh_got)).astype(BF16)
 
 
 def last_kernel(
@@ -441,26 +444,26 @@
     )(*parts)
 
 
-def first_call(fanout, me, lists, table, other, self_one, neigh_one):
+def first_call(fanout, me, lists, table, other):
     width, length = other.shape
-    keep, send = (2, CAP, 2 * LANES), (3, CAP, 2 * LANES)
+    dims = (2, CAP, 2 * LANES)
     return pl.pallas_call(
         functools.partial(first_kernel, fanout),
-        out_shape=(shape((2 * length, LANES), F32), pltpu.HBM(keep, BF16), pltpu.HBM(send, BF16)),
-        in_specs=[SMEM, ANY, VMEM, HBM, VMEM, VMEM],
+        out_shape=(shape((2 * length, LANES), F32), pltpu.HBM(dims, BF16), pltpu.HBM(dims, BF16)),
+        in_specs=[SMEM, ANY, VMEM, HBM],
         out_specs=(VMEM, HBM, HBM),
         scratch_shapes=list_scratch(fanout)
         + [
             pltpu.VMEM((8, width, length // 8), BF16),
             pltpu.SemaphoreType.DMA((8,)),
-            pltpu.VMEM(keep, BF16),
-            pltpu.VMEM(send, BF16),
+            pltpu.VMEM(dims, BF16),
+            pltpu.VMEM(dims, BF16),
             pltpu.SemaphoreType.DMA((2,)),
         ],
         input_output_aliases={2: 0},
         compiler_params=params(FIRST_MIB),
         name="first_half",
-    )(me, lists, table, other, self_one, neigh_one)
+    )(me, lists, table, other)
 
 
 def second_call(fanout, width, me, lists, table):
@@ -479,29 +482,39 @@
     )(me, lists, table)
 
 
-def project_far_call(me, keep, got, sent):
-    part = shape((CAP, sent.shape[2]), BF16)
-    return pl.pallas_call(
-        project_far_kernel,
+def far_call(me, keep, got, *weights):
+    part = shape((CAP, weights[0].shape[1]), BF16)
+    return pl.pallas_call(
+        far_kernel,
         out_shape=(part, part),
-        in_specs=[SMEM, VMEM, VMEM, VMEM],
+        in_specs=[SMEM] + [VMEM] * 6,
         out_specs=(VMEM, VMEM),
         compiler_params=params(10),
         name="project_far",
-    )(me, keep, got, sent)
-
-
-def project_near_call(me, keep, got, weight, weight_got):
-    dims = (CAP, weight.shape[2])
-    return pl.pallas_call(
-        project_near_kernel,
+    )(me, keep, got, *weights)
+
+
+def own_near_call(keep, *weights):
+    return pl.pallas_call(
+        own_near_kernel,
+        out_shape=shape((2, CAP, weights[0].shape[1]), F32),
+        in_specs=[VMEM] * 3,
+        out_specs=VMEM,
+        compiler_params=params(10),
+        name="project_own_near",
+    )(keep, *weights)
+
+
+def near_call(me, own, got, *weights):
+    dims = (CAP, weights[0].shape[1])
+    return pl.pallas_call(
+        near_kernel,
         out_shape=(shape(dims, F32), shape(dims, BF16)),
-        in_specs=[SMEM, HBM, VMEM, VMEM, VMEM],
+        in_specs=[SMEM] + [VMEM] * 4,
         out_specs=(VMEM, VMEM),
-        scratch_shapes=[pltpu.VMEM(keep.shape, BF16), pltpu.SemaphoreType.DMA],
         compiler_params=params(10),
         name="project_near",
-    )(me, keep, got, weight, weight_got)
+    )(me, own, got, *weights)
 
 
 def last_call(*args):
@@ -550,26 +563,28 @@
     held = pltpu.with_memory_space_constraint(features, pltpu.HBM)
     own = count_two[None, :]
     got_1 = across(own, 1)
-    table, got_1 = lax.optimization_barrier((own_call(0, 2, me, held), got_1))
+    weights_got = (across(self_one, 1), across(neigh_one, 1))
+    table, got_1, weights_got = lax.optimization_barrier(
+        (own_call(0, 2, me, held), got_1, weights_got)
+    )
     pair = join_call(own, got_1)
     got = tuple(across(pair, bit) for bit in (4, 6, 2))
-    table, *got = lax.optimization_barrier((own_call(1, 2, me, held, table), *got))
+    table, got = lax.optimization_barrier((own_call(1, 2, me, held, table), got))
     got = (got_1, got[2], got[0], got[1])
     lists, most = order_call(per_seed, me, own, got, self_ids, neighbour_ids, count_one)
-    table, keep_far, send_far = first_call(
-        fanout, me, lists, table, other, self_one, neigh_one
-    )
+    table, keep_far, send_far = first_call(fanout, me, lists, table, other)
     got_far = across(send_far, 1)
     keep_near, send_near = second_call(fanout, width, me, lists, table)
-    far_0, far_1 = project_far_call(me, keep_far, got_far, send_far)
-    far_0, far_1, send_near = lax.optimization_barrier((far_0, far_1, send_near))
-    far = [across(far_0, 4), across(far_1, 6)]
+    far = far_call(me, keep_far, got_far, self_one, neigh_one, *weights_got)
+    far, send_near, keep_near = lax.optimization_barrier((far, send_near, keep_near))
+    far_got = [across(far[0], 4), across(far[1], 6)]
     got_near = across(send_near, 1)
-    near_0, near_1 = project_near_call(me, keep_near, got_near, send_far, got_far)
-    far.append(across(near_1, 2))
+    own_near = own_near_call(keep_near, self_one, neigh_one)
+    near = near_call(me, own_near, got_near, *weights_got)
+    far_got.append(across(near[1], 2))
     fast = last_call(
-        near_0,
-        *far,
+        near[0],
+        *far_got,
         own,
         bias_one[None, :],
         self_two,

time: 58 us -> 59.2 us (1.021)
  starting transfers between devices: 14 us -> 16.5 us
  waiting for transfers between devices: 7.93 us -> 6.4 us
    ppermute x9 -> x11, starting transfers between devices: 13.6 us -> 16 us  [across(): return lax.ppermute(value, 'col', [(i, i ^ bit) for i in range(owners)])]
    ppermute x9 -> x11, waiting for transfers between devices: 7.93 us -> 6.39 us  [across(): return lax.ppermute(value, 'col', [(i, i ^ bit) for i in range(owners)])]
    pallas_call x2 -> x3, Pallas kernels: 1.75 us -> 2.06 us  [the longest x1 0.96 us: far_call(): pl.pallas_call(far_kernel, out_shape=(part, part), in_specs=[SMEM] + [VME...]
    unnamed x32 -> x30, local copies, waits for them, and re-layouts: 1.64 us -> 1.63 us
  transfers between devices with their start and end apart: 10 -> 12, of which waited for: 5 -> 4; matrix products, arithmetic and copies ran while one was open for 0% -> 0% of each run, Pallas kernels for 33% -> 32%
where the time goes in v7:
time: 59.2 us; the launch traced here: 59.1 us
  Pallas kernels  33.5 us (57%)
  starting transfers between devices  16.5 us (28%)
  waiting for transfers between devices  6.4 us (11%)
  local copies, waits for them, and re-layouts  1.72 us (3%)
  between operations  0.94 us (2%)
    ppermute x11, starting transfers between devices, across(): return lax.ppermute(value, 'col', [(i, i ^ bit) for i in range(owners)])  16 us
    pallas_call x1, Pallas kernels, first_call(): pl.pallas_call(functools.partial(first_kernel, fanout), out_shape=(shape(...  12.6 us
    pallas_call x1, Pallas kernels, second_call(): pl.pallas_call(functools.partial(second_kernel, fanout, width), out_shape...  9.13 us
    ppermute x11, waiting for transfers between devices, across(): return lax.ppermute(value, 'col', [(i, i ^ bit) for i in range(owners)])  6.39 us
    pallas_call x2, Pallas kernels, own_call(): pl.pallas_call(functools.partial(own_kernel, which, halves), out_shape=sh...  6.22 us
    pallas_call x1, Pallas kernels, order_call(): pl.pallas_call(functools.partial(order_kernel, per_seed), out_shape=(shap...  2.72 us
    unnamed x30, local copies, waits for them, and re-layouts  1.63 us
  transfers between devices with their start and end apart: 12, of which 4 were waited for; matrix products, arithmetic and copies ran while one was open for 0% of the time, Pallas kernels for 32%

profile of v7, /device:TPU:0, one launch (start us, length us, event | category | flops | bytes accessed | tf_op | source)
XLA Modules:
  0.0 59.1 jit_solution(5125902749846427690)
XLA Ops:
  0.0 0.5 collective-permute-start.6
  0.5 2.5 %collective-permute-start.1 = (bf16[96,256]{1,0:T(8,128)(2,1)}, bf16[96,256]{1,0:T(8,128)(2,1)S(1)}, u32[]{:S(2)}, u32[]{:S(2)}) collective-permute-start(bf16[96,256]{1,0:T(8,128)(2,1)} %self_one.3), channel_id=1, source_target_pairs={{0,2},{2,0},{4,6},{6,4},{8,10},{10,8},{12,14},{14,12},{1,3},{3,1},... | collective-permute-start | bytes 147464 | tf_op jit(solution)/shard_map/ppermute | solution.py:560
  2.9 0.1 collective-permute-start.2
  3.0 2.0 %collective-permute-start = (s32[1,32]{1,0:T(1,128)}, s32[1,32]{1,0:T(1,128)S(1)}, u32[]{:S(2)}, u32[]{:S(2)}) collective-permute-start(s32[1,32]{1,0:T(1,128)} %bitcast.65), channel_id=1, source_target_pairs={{0,2},{2,0},{4,6},{6,4},{8,10},{10,8},{12,14},{14,12},{1,3},{3,1},... | collective-permute-start | bytes 392 | tf_op jit(solution)/shard_map/ppermute | solution.py:560
  5.0 0.1 stack.31.me
  5.1 0.0 copy-start.11
  5.1 3.1 %own_rows.2.refs_0_ = f32[65536,128]{1,0:T(8,128)S(1)} custom-call(s32[5]{0:T(128)S(1)} %stack.31.me, bf16[96,32768]{1,0:T(8,128)(2,1)} %features.3), custom_call_target="tpu_custom_call" | custom-call | tf_op jit(solution)/shard_map/own_rows/pallas_call | solution.py:420
  8.2 0.0 collective-permute-done.refs_1_.got_1
  8.2 0.0 collective-permute-done.1.self_got
  8.2 0.0 collective-permute-done.2.neigh_got
  8.2 0.0 copy-done.11
  8.2 0.0 copy-start.2
  8.2 0.0 copy-start.8
  8.3 0.0 copy-start.9
  8.3 2.7 %collective-permute-start.3 = (s32[2,32]{1,0:T(2,128)S(1)}, s32[2,32]{1,0:T(2,128)S(1)}, u32[]{:S(2)}, u32[]{:S(2)}) collective-permute-start(s32[2,32]{1,0:T(2,128)S(1)} %join.1), channel_id=1, source_target_pairs={{0,8},{2,10},{4,12},{6,14},{8,0},{10,2},{12,4},{14,6},{1,9},{3,11}... | collective-permute-start | bytes 776 | tf_op jit(solution)/shard_map/ppermute | solution.py:560
  10.9 1.3 %collective-permute-start.4 = (s32[2,32]{1,0:T(2,128)S(1)}, s32[2,32]{1,0:T(2,128)S(1)}, u32[]{:S(2)}, u32[]{:S(2)}) collective-permute-start(s32[2,32]{1,0:T(2,128)S(1)} %join.1), channel_id=1, source_target_pairs={{0,12},{2,14},{4,8},{6,10},{8,4},{10,6},{12,0},{14,2},{1,13},{3,15... | collective-permute-start | bytes 776 | tf_op jit(solution)/shard_map/ppermute | solution.py:560
  12.3 0.2 collective-permute-start.5
  12.5 3.1 %own_rows.3.table_in = f32[65536,128]{1,0:T(8,128)S(1)} custom-call(s32[5]{0:T(128)S(1)} %stack.31.me, bf16[96,32768]{1,0:T(8,128)(2,1)} %features.3, f32[65536,128]{1,0:T(8,128)S(1)} %own_rows.2.refs_0_), custom_call_target="tpu_custom_call", output_to_operand_aliasing={{}: (2, {})} | custom-call | tf_op jit(solution)/shard_map/own_rows/pallas_call | solution.py:420
  15.6 0.0 collective-permute-done.3.got_4
  15.6 0.7 %collective-permute-done.4.got_6 = s32[2,32]{1,0:T(2,128)S(1)} collective-permute-done((s32[2,32]{1,0:T(2,128)S(1)}, s32[2,32]{1,0:T(2,128)S(1)}, u32[]{:S(2)}, u32[]{:S(2)}) %collective-permute-start.4) | collective-permute-done | bytes 288 | tf_op jit(solution)/shard_map/ppermute | solution.py:560
  16.3 0.0 collective-permute-done.5.got_2
  16.3 0.0 copy-done.2
  16.3 0.0 copy-done.8
  16.3 0.0 copy-done.9
  16.3 2.7 %order.1 = (s32[2,18,16,128]{3,2,1,0:T(8,128)S(1)}, s32[1]{0:T(128)}) custom-call(s32[5]{0:T(128)S(1)} %stack.31.me, s32[1,32]{1,0:T(1,128)S(1)} %bitcast.67, s32[1,32]{1,0:T(1,128)S(1)} %collective-permute-done.refs_1_.got_1, s32[2,32]{1,0:T(2,128)S(1)} %collective-permute-done.5.got_2, s32[2,32]{1,0:T(2,128)S(1)} %collective-permute-done.3.got_4, ...), custom_call_target="tpu_custom_call" | custom-call | tf_op jit(solution)/shard_map/order/pallas_call | solution.py:396
  19.0 0.0 collective-permute-done.6.other
  19.0 12.6 %first_half.1 = (f32[65536,128]{1,0:T(8,128)S(1)}, bf16[2,272,256]{2,1,0:T(8,128)(2,1)}, bf16[2,272,256]{2,1,0:T(8,128)(2,1)}) custom-call(s32[5]{0:T(128)S(1)} %stack.31.me, s32[73728]{0:T(1024)S(1)} %bitcast.55, f32[65536,128]{1,0:T(8,128)S(1)} %own_rows.3.table_in, bf16[96,32768]{1,0:T(8,128)(2,1)} %collective-permute-done.6.other), custom_call_target="tpu_custom_call", output_to_operand_aliasing={{0}: (2, {})} | custom-call | tf_op jit(solution)/shard_map/first_half/pallas_call | solution.py:450
  31.6 0.6 %collective-permute-start.7 = (bf16[2,272,256]{2,1,0:T(8,128)(2,1)}, bf16[2,272,256]{2,1,0:T(8,128)(2,1)S(1)}, u32[]{:S(2)}, u32[]{:S(2)}) collective-permute-start(bf16[2,272,256]{2,1,0:T(8,128)(2,1)} %get-tuple-element.83), channel_id=1, source_target_pairs={{0,2},{2,0},{4,6},{6,4},{8,10},{10,8},{12,14},{14,12},{1,3},{3,1},... | collective-permute-start | bytes 835592 | tf_op jit(solution)/shard_map/ppermute | solution.py:560
  32.2 0.0 copy-start
  32.2 0.0 copy-start.5
  32.2 0.0 copy-start.6
  32.2 0.0 copy-start.3
  32.3 0.0 copy-start.4
  32.3 0.0 copy-start.7
  32.3 0.0 copy-start.12
  32.3 0.0 copy-start.13
  32.3 0.0 copy-start.14
  32.3 9.1 %second_half.1 = (bf16[2,272,256]{2,1,0:T(8,128)(2,1)}, bf16[2,272,256]{2,1,0:T(8,128)(2,1)}) custom-call(s32[5]{0:T(128)S(1)} %stack.31.me, s32[73728]{0:T(1024)S(1)} %bitcast.56, f32[65536,128]{1,0:T(8,128)S(1)} %get-tuple-element.88.table), custom_call_target="tpu_custom_call" | custom-call | tf_op jit(solution)/shard_map/second_half/pallas_call | solution.py:472
  41.5 0.0 collective-permute-done.7.got
  41.5 0.0 copy-done
  41.5 0.0 copy-done.5
  41.5 0.0 copy-done.6
  41.5 1.0 %project_far.1 = (bf16[272,256]{1,0:T(8,128)(2,1)S(1)}, bf16[272,256]{1,0:T(8,128)(2,1)S(1)}) custom-call(s32[5]{0:T(128)S(1)} %stack.31.me, bf16[2,272,256]{2,1,0:T(8,128)(2,1)S(1)} %copy-done, bf16[2,272,256]{2,1,0:T(8,128)(2,1)S(1)} %collective-permute-done.7.got, bf16[96,256]{1,0:T(8,128)(2,1)S(1)} %copy-done.5, bf16[96,256]{1,0:T(8,128)(2,1)S(1)} %copy-done.6, ...), custom_call_target="tpu_custom_call" | custom-call | tf_op jit(solution)/shard_map/project_far/pallas_call | solution.py:487
  42.5 1.6 %collective-permute-start.8 = (bf16[2,272,256]{2,1,0:T(8,128)(2,1)}, bf16[2,272,256]{2,1,0:T(8,128)(2,1)S(1)}, u32[]{:S(2)}, u32[]{:S(2)}) collective-permute-start(bf16[2,272,256]{2,1,0:T(8,128)(2,1)} %get-tuple-element.92), channel_id=1, source_target_pairs={{0,2},{2,0},{4,6},{6,4},{8,10},{10,8},{12,14},{14,12},{1,3},{3,1},... | collective-permute-start | bytes 835592 | tf_op jit(solution)/shard_map/ppermute | solution.py:560
  44.0 1.0 %copy-done.1 = bf16[2,272,256]{2,1,0:T(8,128)(2,1)S(1)} copy-done((bf16[2,272,256]{2,1,0:T(8,128)(2,1)S(1)}, bf16[2,272,256]{2,1,0:T(8,128)(2,1)}, u32[]{:S(2)}) %copy-start.1) | copy-done | bytes 278552
  45.0 0.3 project_own_near.1.own
  45.3 2.2 %collective-permute-start.9 = (bf16[272,256]{1,0:T(8,128)(2,1)S(1)}, bf16[272,256]{1,0:T(8,128)(2,1)S(1)}, u32[]{:S(2)}, u32[]{:S(2)}) collective-permute-start(bf16[272,256]{1,0:T(8,128)(2,1)S(1)} %get-tuple-element.94), channel_id=1, source_target_pairs={{0,8},{2,10},{4,12},{6,14},{8,0},{10,2},{12,4},{14,6},{1,9},{3,11}... | collective-permute-start | bytes 417800 | tf_op jit(solution)/shard_map/ppermute | solution.py:560
  47.5 1.3 %collective-permute-start.10 = (bf16[272,256]{1,0:T(8,128)(2,1)S(1)}, bf16[272,256]{1,0:T(8,128)(2,1)S(1)}, u32[]{:S(2)}, u32[]{:S(2)}) collective-permute-start(bf16[272,256]{1,0:T(8,128)(2,1)S(1)} %get-tuple-element.95), channel_id=1, source_target_pairs={{0,12},{2,14},{4,8},{6,10},{8,4},{10,6},{12,0},{14,2},{1,13},{3,15... | collective-permute-start | bytes 417800 | tf_op jit(solution)/shard_map/ppermute | solution.py:560
  48.8 0.4 collective-permute-done.8.got
  49.3 0.8 %project_near.1 = (f32[272,256]{1,0:T(8,128)S(1)}, bf16[272,256]{1,0:T(8,128)(2,1)S(1)}) custom-call(s32[5]{0:T(128)S(1)} %stack.31.me, f32[2,272,256]{2,1,0:T(8,128)S(1)} %project_own_near.1.own, bf16[2,272,256]{2,1,0:T(8,128)(2,1)S(1)} %collective-permute-done.8.got, bf16[96,256]{1,0:T(8,128)(2,1)S(1)} %collective-permute-done.1.self_got, ...), custom_call_target="tpu_custom_call" | custom-call | tf_op jit(solution)/shard_map/project_near/pallas_call | solution.py:510
  50.1 1.5 %collective-permute-start.11 = (bf16[272,256]{1,0:T(8,128)(2,1)S(1)}, bf16[272,256]{1,0:T(8,128)(2,1)S(1)}, u32[]{:S(2)}, u32[]{:S(2)}) collective-permute-start(bf16[272,256]{1,0:T(8,128)(2,1)S(1)} %get-tuple-element.96), channel_id=1, source_target_pairs={{0,4},{2,6},{4,0},{6,2},{8,12},{10,14},{12,8},{14,10},{1,5},{3,7},... | collective-permute-start | bytes 417800 | tf_op jit(solution)/shard_map/ppermute | solution.py:560
  52.3 4.6 %collective-permute-done.9.a = bf16[272,256]{1,0:T(8,128)(2,1)S(1)} collective-permute-done((bf16[272,256]{1,0:T(8,128)(2,1)S(1)}, bf16[272,256]{1,0:T(8,128)(2,1)S(1)}, u32[]{:S(2)}, u32[]{:S(2)}) %collective-permute-start.9) | collective-permute-done | bytes 139296 | tf_op jit(solution)/shard_map/ppermute | solution.py:560
  56.9 0.0 collective-permute-done.10.b
  56.9 0.7 %collective-permute-done.11.c = bf16[272,256]{1,0:T(8,128)(2,1)S(1)} collective-permute-done((bf16[272,256]{1,0:T(8,128)(2,1)S(1)}, bf16[272,256]{1,0:T(8,128)(2,1)S(1)}, u32[]{:S(2)}, u32[]{:S(2)}) %collective-permute-start.11) | collective-permute-done | bytes 139296 | tf_op jit(solution)/shard_map/ppermute | solution.py:560
  57.6 0.0 copy-done.3
  57.6 0.0 copy-done.4
  57.6 0.0 copy-done.7
  57.6 0.0 copy-done.12
  57.6 0.0 copy-done.13
  57.6 0.0 copy-done.14
  57.6 0.7 %layer_two.1 = f32[32,153]{1,0:T(8,128)S(1)} custom-call(f32[272,256]{1,0:T(8,128)S(1)} %get-tuple-element.93.mine, bf16[272,256]{1,0:T(8,128)(2,1)S(1)} %collective-permute-done.9.a, bf16[272,256]{1,0:T(8,128)(2,1)S(1)} %collective-permute-done.10.b, bf16[272,256]{1,0:T(8,128)(2,1)S(1)} %collective-permute-done.11.c, s32[1,32]{1,0:T(1,128)S(1)} %bitcast.68, ...), custom_call_target="tpu_custom_call" | custom-call | tf_op jit(solution)/shard_map/layer_two/pallas_call | solution.py:523
  58.4 0.1 conditional.1
  58.5 0.0 copy-start.10
  58.5 0.6 %copy-done.10 = f32[32,153]{1,0:T(8,128)} copy-done((f32[32,153]{1,0:T(8,128)}, f32[32,153]{1,0:T(8,128)S(1)}, u32[]{:S(2)}) %copy-start.10) | copy-done | bytes 19608
  (2 shorter events, 0.0 us)
Async XLA Ops:
  0.0 19.0 %collective-permute-start.6 = (bf16[96,32768]{1,0:T(8,128)(2,1)}, bf16[96,32768]{1,0:T(8,128)(2,1)}, u32[]{:S(2)}, u32[]{:S(2)}) collective-permute-start(bf16[96,32768]{1,0:T(8,128)(2,1)} %features.3), channel_id=1, source_target_pairs={{0,1},{1,0},{2,3},{3,2},{4,5},{5,4},{6,7},{7,6},{8,9},{9,8},{10,11... | collective-permute-start | bytes 18874376 | tf_op jit(solution)/shard_map/ppermute | solution.py:562
  0.5 7.7 %collective-permute-start.1 = (bf16[96,256]{1,0:T(8,128)(2,1)}, bf16[96,256]{1,0:T(8,128)(2,1)S(1)}, u32[]{:S(2)}, u32[]{:S(2)}) collective-permute-start(bf16[96,256]{1,0:T(8,128)(2,1)} %self_one.3), channel_id=1, source_target_pairs={{0,2},{2,0},{4,6},{6,4},{8,10},{10,8},{12,14},{14,12},{1,3},{3,1},... | collective-permute-start | bytes 147464 | tf_op jit(solution)/shard_map/ppermute | solution.py:560
  2.9 5.3 %collective-permute-start.2 = (bf16[96,256]{1,0:T(8,128)(2,1)}, bf16[96,256]{1,0:T(8,128)(2,1)S(1)}, u32[]{:S(2)}, u32[]{:S(2)}) collective-permute-start(bf16[96,256]{1,0:T(8,128)(2,1)} %neigh_one.3), channel_id=1, source_target_pairs={{0,2},{2,0},{4,6},{6,4},{8,10},{10,8},{12,14},{14,12},{1,3},{3,1},... | collective-permute-start | bytes 147464 | tf_op jit(solution)/shard_map/ppermute | solution.py:560
  3.0 5.2 %collective-permute-start = (s32[1,32]{1,0:T(1,128)}, s32[1,32]{1,0:T(1,128)S(1)}, u32[]{:S(2)}, u32[]{:S(2)}) collective-permute-start(s32[1,32]{1,0:T(1,128)} %bitcast.65), channel_id=1, source_target_pairs={{0,2},{2,0},{4,6},{6,4},{8,10},{10,8},{12,14},{14,12},{1,3},{3,1},... | collective-permute-start | bytes 392 | tf_op jit(solution)/shard_map/ppermute | solution.py:560
  5.1 3.2 %copy-start.11 = (s32[32]{0:T(128)S(1)}, s32[32]{0:T(128)}, u32[]{:S(2)}) copy-start(s32[32]{0:T(128)} %param.19) | copy-start | bytes 388
  8.2 8.1 %copy-start.2 = (s32[15,2816]{1,0:T(8,128)S(1)}, s32[15,2816]{1,0:T(8,128)}, u32[]{:S(2)}) copy-start(s32[15,2816]{1,0:T(8,128)} %neighbour_ids.1) | copy-start | bytes 506884
  8.2 8.1 %copy-start.8 = (s32[2816]{0:T(1024)S(1)}, s32[2816]{0:T(1024)}, u32[]{:S(2)}) copy-start(s32[2816]{0:T(1024)} %count_one.1) | copy-start | bytes 33796
  8.3 8.0 %copy-start.9 = (s32[2816]{0:T(1024)S(1)}, s32[2816]{0:T(1024)}, u32[]{:S(2)}) copy-start(s32[2816]{0:T(1024)} %self_ids.1) | copy-start | bytes 33796
  8.3 7.4 %collective-permute-start.3 = (s32[2,32]{1,0:T(2,128)S(1)}, s32[2,32]{1,0:T(2,128)S(1)}, u32[]{:S(2)}, u32[]{:S(2)}) collective-permute-start(s32[2,32]{1,0:T(2,128)S(1)} %join.1), channel_id=1, source_target_pairs={{0,8},{2,10},{4,12},{6,14},{8,0},{10,2},{12,4},{14,6},{1,9},{3,11}... | collective-permute-start | bytes 776 | tf_op jit(solution)/shard_map/ppermute | solution.py:560
  10.9 5.4 %collective-permute-start.4 = (s32[2,32]{1,0:T(2,128)S(1)}, s32[2,32]{1,0:T(2,128)S(1)}, u32[]{:S(2)}, u32[]{:S(2)}) collective-permute-start(s32[2,32]{1,0:T(2,128)S(1)} %join.1), channel_id=1, source_target_pairs={{0,12},{2,14},{4,8},{6,10},{8,4},{10,6},{12,0},{14,2},{1,13},{3,15... | collective-permute-start | bytes 776 | tf_op jit(solution)/shard_map/ppermute | solution.py:560
  12.3 4.0 %collective-permute-start.5 = (s32[2,32]{1,0:T(2,128)S(1)}, s32[2,32]{1,0:T(2,128)S(1)}, u32[]{:S(2)}, u32[]{:S(2)}) collective-permute-start(s32[2,32]{1,0:T(2,128)S(1)} %join.1), channel_id=1, source_target_pairs={{0,4},{2,6},{4,0},{6,2},{8,12},{10,14},{12,8},{14,10},{1,5},{3,7},... | collective-permute-start | bytes 776 | tf_op jit(solution)/shard_map/ppermute | solution.py:560
  31.6 9.8 %collective-permute-start.7 = (bf16[2,272,256]{2,1,0:T(8,128)(2,1)}, bf16[2,272,256]{2,1,0:T(8,128)(2,1)S(1)}, u32[]{:S(2)}, u32[]{:S(2)}) collective-permute-start(bf16[2,272,256]{2,1,0:T(8,128)(2,1)} %get-tuple-element.83), channel_id=1, source_target_pairs={{0,2},{2,0},{4,6},{6,4},{8,10},{10,8},{12,14},{14,12},{1,3},{3,1},... | collective-permute-start | bytes 835592 | tf_op jit(solution)/shard_map/ppermute | solution.py:560
  32.2 9.2 %copy-start = (bf16[2,272,256]{2,1,0:T(8,128)(2,1)S(1)}, bf16[2,272,256]{2,1,0:T(8,128)(2,1)}, u32[]{:S(2)}) copy-start(bf16[2,272,256]{2,1,0:T(8,128)(2,1)} %get-tuple-element.82.keep) | copy-start | bytes 835588
  32.2 9.2 %copy-start.5 = (bf16[96,256]{1,0:T(8,128)(2,1)S(1)}, bf16[96,256]{1,0:T(8,128)(2,1)}, u32[]{:S(2)}) copy-start(bf16[96,256]{1,0:T(8,128)(2,1)} %self_one.3) | copy-start | bytes 147460
  32.2 9.2 %copy-start.6 = (bf16[96,256]{1,0:T(8,128)(2,1)S(1)}, bf16[96,256]{1,0:T(8,128)(2,1)}, u32[]{:S(2)}) copy-start(bf16[96,256]{1,0:T(8,128)(2,1)} %neigh_one.3) | copy-start | bytes 147460
  32.2 25.3 %copy-start.3 = (bf16[256,256]{1,0:T(8,128)(2,1)S(1)}, bf16[256,256]{1,0:T(8,128)(2,1)}, u32[]{:S(2)}) copy-start(bf16[256,256]{1,0:T(8,128)(2,1)} %neigh_two.1) | copy-start | bytes 393220
  32.3 25.3 %copy-start.4 = (bf16[256,256]{1,0:T(8,128)(2,1)S(1)}, bf16[256,256]{1,0:T(8,128)(2,1)}, u32[]{:S(2)}) copy-start(bf16[256,256]{1,0:T(8,128)(2,1)} %self_two.1) | copy-start | bytes 393220
  32.3 25.3 %copy-start.7 = (bf16[256,153]{0,1:T(8,128)(2,1)S(1)}, bf16[256,153]{0,1:T(8,128)(2,1)}, u32[]{:S(2)}) copy-start(bf16[256,153]{0,1:T(8,128)(2,1)} %param.26) | copy-start | bytes 235012
  32.3 25.3 %copy-start.12 = (f32[256]{0:T(256)S(1)}, f32[256]{0:T(256)}, u32[]{:S(2)}) copy-start(f32[256]{0:T(256)} %param.25) | copy-start | bytes 3076
  32.3 25.3 %copy-start.13 = (f32[153]{0:T(256)S(1)}, f32[153]{0:T(256)}, u32[]{:S(2)}) copy-start(f32[153]{0:T(256)} %param.27) | copy-start | bytes 1840
  32.3 25.3 %copy-start.14 = (f32[256]{0:T(256)S(1)}, f32[256]{0:T(256)}, u32[]{:S(2)}) copy-start(f32[256]{0:T(256)} %param.22) | copy-start | bytes 3076
  42.5 6.8 %collective-permute-start.8 = (bf16[2,272,256]{2,1,0:T(8,128)(2,1)}, bf16[2,272,256]{2,1,0:T(8,128)(2,1)S(1)}, u32[]{:S(2)}, u32[]{:S(2)}) collective-permute-start(bf16[2,272,256]{2,1,0:T(8,128)(2,1)} %get-tuple-element.92), channel_id=1, source_target_pairs={{0,2},{2,0},{4,6},{6,4},{8,10},{10,8},{12,14},{14,12},{1,3},{3,1},... | collective-permute-start | bytes 835592 | tf_op jit(solution)/shard_map/ppermute | solution.py:560
  44.0 1.0 %copy-start.1 = (bf16[2,272,256]{2,1,0:T(8,128)(2,1)S(1)}, bf16[2,272,256]{2,1,0:T(8,128)(2,1)}, u32[]{:S(2)}) copy-start(bf16[2,272,256]{2,1,0:T(8,128)(2,1)} %get-tuple-element.91.keep) | copy-start | bytes 835588
  45.3 11.7 %collective-permute-start.9 = (bf16[272,256]{1,0:T(8,128)(2,1)S(1)}, bf16[272,256]{1,0:T(8,128)(2,1)S(1)}, u32[]{:S(2)}, u32[]{:S(2)}) collective-permute-start(bf16[272,256]{1,0:T(8,128)(2,1)S(1)} %get-tuple-element.94), channel_id=1, source_target_pairs={{0,8},{2,10},{4,12},{6,14},{8,0},{10,2},{12,4},{14,6},{1,9},{3,11}... | collective-permute-start | bytes 417800 | tf_op jit(solution)/shard_map/ppermute | solution.py:560
  47.5 9.4 %collective-permute-start.10 = (bf16[272,256]{1,0:T(8,128)(2,1)S(1)}, bf16[272,256]{1,0:T(8,128)(2,1)S(1)}, u32[]{:S(2)}, u32[]{:S(2)}) collective-permute-start(bf16[272,256]{1,0:T(8,128)(2,1)S(1)} %get-tuple-element.95), channel_id=1, source_target_pairs={{0,12},{2,14},{4,8},{6,10},{8,4},{10,6},{12,0},{14,2},{1,13},{3,15... | collective-permute-start | bytes 417800 | tf_op jit(solution)/shard_map/ppermute | solution.py:560
  50.1 7.5 %collective-permute-start.11 = (bf16[272,256]{1,0:T(8,128)(2,1)S(1)}, bf16[272,256]{1,0:T(8,128)(2,1)S(1)}, u32[]{:S(2)}, u32[]{:S(2)}) collective-permute-start(bf16[272,256]{1,0:T(8,128)(2,1)S(1)} %get-tuple-element.96), channel_id=1, source_target_pairs={{0,4},{2,6},{4,0},{6,2},{8,12},{10,14},{12,8},{14,10},{1,5},{3,7},... | collective-permute-start | bytes 417800 | tf_op jit(solution)/shard_map/ppermute | solution.py:560
  58.5 0.6 %copy-start.10 = (f32[32,153]{1,0:T(8,128)}, f32[32,153]{1,0:T(8,128)S(1)}, u32[]{:S(2)}) copy-start(f32[32,153]{1,0:T(8,128)S(1)} %get-tuple-element.181) | copy-start | bytes 58756

commit v8 on v7

--- a/solution.py
+++ b/solution.py
@@ -328,29 +328,28 @@
     hand_out(keep, send, keep_hbm, send_hbm, out_sems)
 
 
-def partial(rows, self_one, neigh_one):
-    width = self_one.shape[0]
-    return jnp.dot(rows[:, 0:width], self_one[...], preferred_element_type=F32) + jnp.dot(
-        rows[:, LANES : LANES + width], neigh_one[...], preferred_element_type=F32
-    )
-
-
-def far_kernel(me, keep, got, self_one, neigh_one, self_got, neigh_got, out_0, out_1):
+def partial(rows, weights):
+    width = weights.shape[0] // 2
+    return jnp.dot(rows[:, 0:width], weights[0:width, :], preferred_element_type=F32) + jnp.dot(
+        rows[:, LANES : LANES + width], weights[width:, :], preferred_element_type=F32
+    )
+
+
+def far_kernel(me, keep, got, weights, weights_got, out_0, out_1):
     zl = me[3]
     for which, out in ((zl, out_0), (1 - zl, out_1)):
-        total = partial(keep[which], self_one, neigh_one) + partial(got[which], self_got, neigh_got)
+        total = partial(keep[which], weights) + partial(got[which], weights_got)
         out[...] = total.astype(BF16)
 
 
-def own_near_kernel(keep, self_one, neigh_one, out):
-    for z in range(2):
-        out[z, :, :] = partial(keep[z], self_one, neigh_one)
-
-
-def near_kernel(me, own, got, self_got, neigh_got, out_0, out_1):
+def near_kernel(me, keep_hbm, got, weights, weights_got, out_0, out_1, keep, sem):
+    copy = pltpu.make_async_copy(keep_hbm, keep, sem)
+    copy.start()
     zl = me[3]
-    out_0[...] = own[zl] + partial(got[zl], self_got, neigh_got)
-    out_1[...] = (own[1 - zl] + partial(got[1 - zl], self_got, neigh_got)).astype(BF16)
+    theirs = partial(got[zl], weights_got), partial(got[1 - zl], weights_got)
+    copy.wait()
+    out_0[...] = partial(keep[zl], weights) + theirs[0]
+    out_1[...] = (partial(keep[1 - zl], weights) + theirs[1]).astype(BF16)
 
 
 def last_kernel(
@@ -482,39 +481,29 @@
     )(me, lists, table)
 
 
-def far_call(me, keep, got, *weights):
-    part = shape((CAP, weights[0].shape[1]), BF16)
+def far_call(me, keep, got, weights, weights_got):
+    part = shape((CAP, weights.shape[1]), BF16)
     return pl.pallas_call(
         far_kernel,
         out_shape=(part, part),
-        in_specs=[SMEM] + [VMEM] * 6,
+        in_specs=[SMEM] + [VMEM] * 4,
         out_specs=(VMEM, VMEM),
         compiler_params=params(10),
         name="project_far",
-    )(me, keep, got, *weights)
-
-
-def own_near_call(keep, *weights):
-    return pl.pallas_call(
-        own_near_kernel,
-        out_shape=shape((2, CAP, weights[0].shape[1]), F32),
-        in_specs=[VMEM] * 3,
-        out_specs=VMEM,
-        compiler_params=params(10),
-        name="project_own_near",
-    )(keep, *weights)
-
-
-def near_call(me, own, got, *weights):
-    dims = (CAP, weights[0].shape[1])
+    )(me, keep, got, weights, weights_got)
+
+
+def near_call(me, keep, got, weights, weights_got):
+    dims = (CAP, weights.shape[1])
     return pl.pallas_call(
         near_kernel,
         out_shape=(shape(dims, F32), shape(dims, BF16)),
-        in_specs=[SMEM] + [VMEM] * 4,
+        in_specs=[SMEM, HBM] + [VMEM] * 3,
         out_specs=(VMEM, VMEM),
+        scratch_shapes=[pltpu.VMEM(keep.shape, BF16), pltpu.SemaphoreType.DMA],
         compiler_params=params(10),
         name="project_near",
-    )(me, own, got, *weights)
+    )(me, pltpu.with_memory_space_constraint(keep, pltpu.HBM), got, weights, weights_got)
 
 
 def last_call(*args):
@@ -563,24 +552,26 @@
     held = pltpu.with_memory_space_constraint(features, pltpu.HBM)
     own = count_two[None, :]
     got_1 = across(own, 1)
-    weights_got = (across(self_one, 1), across(neigh_one, 1))
-    table, got_1, weights_got = lax.optimization_barrier(
-        (own_call(0, 2, me, held), got_1, weights_got)
+    weights = join_call(self_one, neigh_one)
+    table, got_1, weights = lax.optimization_barrier(
+        (own_call(0, 2, me, held), got_1, weights)
     )
     pair = join_call(own, got_1)
     got = tuple(across(pair, bit) for bit in (4, 6, 2))
-    table, got = lax.optimization_barrier((own_call(1, 2, me, held, table), got))
+    weights_got = across(weights, 1)
+    table, got, weights_got = lax.optimization_barrier(
+        (own_call(1, 2, me, held, table), got, weights_got)
+    )
     got = (got_1, got[2], got[0], got[1])
     lists, most = order_call(per_seed, me, own, got, self_ids, neighbour_ids, count_one)
     table, keep_far, send_far = first_call(fanout, me, lists, table, other)
     got_far = across(send_far, 1)
     keep_near, send_near = second_call(fanout, width, me, lists, table)
-    far = far_call(me, keep_far, got_far, self_one, neigh_one, *weights_got)
-    far, send_near, keep_near = lax.optimization_barrier((far, send_near, keep_near))
+    far = far_call(me, keep_far, got_far, weights, weights_got)
+    far, send_near = lax.optimization_barrier((far, send_near))
     far_got = [across(far[0], 4), across(far[1], 6)]
     got_near = across(send_near, 1)
-    own_near = own_near_call(keep_near, self_one, neigh_one)
-    near = near_call(me, own_near, got_near, *weights_got)
+    near = near_call(me, keep_near, got_near, weights, weights_got)
     far_got.append(across(near[1], 2))
     fast = last_call(
         near[0],

time: 59.2 us -> 57.8 us (0.976)
  starting transfers between devices: 16.5 us -> 15.1 us
  local copies, waits for them, and re-layouts: 1.72 us -> 0.75 us
  Pallas kernels: 33.5 us -> 34.2 us
    ppermute x11 -> x10, starting transfers between devices: 16 us -> 14.6 us  [across(): return lax.ppermute(value, 'col', [(i, i ^ bit) for i in range(owners)])]
    pallas_call x1, Pallas kernels: 0.83 us -> 1.8 us  [near_call(): pl.pallas_call(near_kernel, out_shape=(shape(dims, F32), shape(dims, BF16...]
    unnamed x30 -> x28, local copies, waits for them, and re-layouts: 1.63 us -> 0.67 us
    ppermute x11 -> x10, waiting for transfers between devices: 6.39 us -> 6.58 us  [across(): return lax.ppermute(value, 'col', [(i, i ^ bit) for i in range(owners)])]
  transfers between devices with their start and end apart: 12 -> 11, of which waited for: 4 -> 4; matrix products, arithmetic and copies ran while one was open for 0% -> 0% of each run, Pallas kernels for 32% -> 35%
where the time goes in v8:
time: 57.8 us; the launch traced here: 57.7 us
  Pallas kernels  34.2 us (59%)
  starting transfers between devices  15.1 us (26%)
  waiting for transfers between devices  6.59 us (11%)
  between operations  0.89 us (2%)
  local copies, waits for them, and re-layouts  0.75 us (1%)
    ppermute x10, starting transfers between devices, across(): return lax.ppermute(value, 'col', [(i, i ^ bit) for i in range(owners)])  14.6 us
    pallas_call x1, Pallas kernels, first_call(): pl.pallas_call(functools.partial(first_kernel, fanout), out_shape=(shape(...  12.2 us
    pallas_call x1, Pallas kernels, second_call(): pl.pallas_call(functools.partial(second_kernel, fanout, width), out_shape...  9.6 us
    ppermute x10, waiting for transfers between devices, across(): return lax.ppermute(value, 'col', [(i, i ^ bit) for i in range(owners)])  6.58 us
    pallas_call x2, Pallas kernels, own_call(): pl.pallas_call(functools.partial(own_kernel, which, halves), out_shape=sh...  6.22 us
    pallas_call x1, Pallas kernels, order_call(): pl.pallas_call(functools.partial(order_kernel, per_seed), out_shape=(shap...  2.73 us
    pallas_call x1, Pallas kernels, near_call(): pl.pallas_call(near_kernel, out_shape=(shape(dims, F32), shape(dims, BF16...  1.8 us
  transfers between devices with their start and end apart: 11, of which 4 were waited for; matrix products, arithmetic and copies ran while one was open for 0% of the time, Pallas kernels for 35%

profile of v8, /device:TPU:0, one launch (start us, length us, event | category | flops | bytes accessed | tf_op | source)
XLA Modules:
  0.0 57.7 jit_solution(13116848616520397998)
XLA Ops:
  0.0 0.5 collective-permute-start.5
  0.5 2.5 %collective-permute-start = (s32[1,32]{1,0:T(1,128)}, s32[1,32]{1,0:T(1,128)S(1)}, u32[]{:S(2)}, u32[]{:S(2)}) collective-permute-start(s32[1,32]{1,0:T(1,128)} %bitcast.65), channel_id=1, source_target_pairs={{0,2},{2,0},{4,6},{6,4},{8,10},{10,8},{12,14},{14,12},{1,3},{3,1},... | collective-permute-start | bytes 392 | tf_op jit(solution)/shard_map/ppermute | solution.py:549
  2.9 0.1 stack.31.me
  3.0 0.0 copy-start.5
  3.0 0.0 copy-start.6
  3.0 0.0 copy-start.10
  3.0 3.1 %own_rows.2.refs_0_ = f32[65536,128]{1,0:T(8,128)S(1)} custom-call(s32[5]{0:T(128)S(1)} %stack.31.me, bf16[96,32768]{1,0:T(8,128)(2,1)} %features.3), custom_call_target="tpu_custom_call" | custom-call | tf_op jit(solution)/shard_map/own_rows/pallas_call | solution.py:419
  6.2 0.0 copy-done.5
  6.2 0.0 copy-done.6
  6.2 0.0 collective-permute-done.refs_1_.got_1
  6.2 0.4 collective-permute-start.4
  6.6 0.0 copy-done.10
  6.6 0.0 copy-start.1
  6.6 0.0 copy-start.7
  6.6 0.0 copy-start.8
  6.6 2.8 %collective-permute-start.1 = (s32[2,32]{1,0:T(2,128)S(1)}, s32[2,32]{1,0:T(2,128)S(1)}, u32[]{:S(2)}, u32[]{:S(2)}) collective-permute-start(s32[2,32]{1,0:T(2,128)S(1)} %join.3), channel_id=1, source_target_pairs={{0,8},{2,10},{4,12},{6,14},{8,0},{10,2},{12,4},{14,6},{1,9},{3,11}... | collective-permute-start | bytes 776 | tf_op jit(solution)/shard_map/ppermute | solution.py:549
  9.5 1.3 %collective-permute-start.2 = (s32[2,32]{1,0:T(2,128)S(1)}, s32[2,32]{1,0:T(2,128)S(1)}, u32[]{:S(2)}, u32[]{:S(2)}) collective-permute-start(s32[2,32]{1,0:T(2,128)S(1)} %join.3), channel_id=1, source_target_pairs={{0,12},{2,14},{4,8},{6,10},{8,4},{10,6},{12,0},{14,2},{1,13},{3,15... | collective-permute-start | bytes 776 | tf_op jit(solution)/shard_map/ppermute | solution.py:549
  10.8 0.2 collective-permute-start.3
  11.1 3.1 %own_rows.3.table_in = f32[65536,128]{1,0:T(8,128)S(1)} custom-call(s32[5]{0:T(128)S(1)} %stack.31.me, bf16[96,32768]{1,0:T(8,128)(2,1)} %features.3, f32[65536,128]{1,0:T(8,128)S(1)} %own_rows.2.refs_0_), custom_call_target="tpu_custom_call", output_to_operand_aliasing={{}: (2, {})} | custom-call | tf_op jit(solution)/shard_map/own_rows/pallas_call | solution.py:419
  14.2 0.0 collective-permute-done.1.got_4
  14.2 0.7 %collective-permute-done.2.got_6 = s32[2,32]{1,0:T(2,128)S(1)} collective-permute-done((s32[2,32]{1,0:T(2,128)S(1)}, s32[2,32]{1,0:T(2,128)S(1)}, u32[]{:S(2)}, u32[]{:S(2)}) %collective-permute-start.2) | collective-permute-done | bytes 288 | tf_op jit(solution)/shard_map/ppermute | solution.py:549
  14.8 0.0 collective-permute-done.3.got_2
  14.9 0.0 collective-permute-done.4.weights_got
  14.9 0.0 copy-done.1
  14.9 0.0 copy-done.7
  14.9 0.0 copy-done.8
  14.9 2.7 %order.1 = (s32[2,18,16,128]{3,2,1,0:T(8,128)S(1)}, s32[1]{0:T(128)}) custom-call(s32[5]{0:T(128)S(1)} %stack.31.me, s32[1,32]{1,0:T(1,128)S(1)} %bitcast.67, s32[1,32]{1,0:T(1,128)S(1)} %collective-permute-done.refs_1_.got_1, s32[2,32]{1,0:T(2,128)S(1)} %collective-permute-done.3.got_2, s32[2,32]{1,0:T(2,128)S(1)} %collective-permute-done.1.got_4, ...), custom_call_target="tpu_custom_call" | custom-call | tf_op jit(solution)/shard_map/order/pallas_call | solution.py:395
  17.6 0.0 collective-permute-done.5.other
  17.6 12.2 %first_half.1 = (f32[65536,128]{1,0:T(8,128)S(1)}, bf16[2,272,256]{2,1,0:T(8,128)(2,1)}, bf16[2,272,256]{2,1,0:T(8,128)(2,1)}) custom-call(s32[5]{0:T(128)S(1)} %stack.31.me, s32[73728]{0:T(1024)S(1)} %bitcast.55, f32[65536,128]{1,0:T(8,128)S(1)} %own_rows.3.table_in, bf16[96,32768]{1,0:T(8,128)(2,1)} %collective-permute-done.5.other), custom_call_target="tpu_custom_call", output_to_operand_aliasing={{0}: (2, {})} | custom-call | tf_op jit(solution)/shard_map/first_half/pallas_call | solution.py:449
  29.8 1.6 %collective-permute-start.6 = (bf16[2,272,256]{2,1,0:T(8,128)(2,1)}, bf16[2,272,256]{2,1,0:T(8,128)(2,1)S(1)}, u32[]{:S(2)}, u32[]{:S(2)}) collective-permute-start(bf16[2,272,256]{2,1,0:T(8,128)(2,1)} %get-tuple-element.85), channel_id=1, source_target_pairs={{0,2},{2,0},{4,6},{6,4},{8,10},{10,8},{12,14},{14,12},{1,3},{3,1},... | collective-permute-start | bytes 835592 | tf_op jit(solution)/shard_map/ppermute | solution.py:549
  31.4 0.0 copy-start
  31.4 0.0 copy-start.2
  31.4 0.0 copy-start.3
  31.4 0.0 copy-start.4
  31.4 0.0 copy-start.11
  31.4 0.0 copy-start.12
  31.4 0.0 copy-start.13
  31.4 9.6 %second_half.1 = (bf16[2,272,256]{2,1,0:T(8,128)(2,1)}, bf16[2,272,256]{2,1,0:T(8,128)(2,1)}) custom-call(s32[5]{0:T(128)S(1)} %stack.31.me, s32[73728]{0:T(1024)S(1)} %bitcast.56, f32[65536,128]{1,0:T(8,128)S(1)} %get-tuple-element.82.table), custom_call_target="tpu_custom_call" | custom-call | tf_op jit(solution)/shard_map/second_half/pallas_call | solution.py:471
  41.0 0.0 collective-permute-done.6.got
  41.0 0.0 copy-done
  41.0 1.0 %project_far.1 = (bf16[272,256]{1,0:T(8,128)(2,1)S(1)}, bf16[272,256]{1,0:T(8,128)(2,1)S(1)}) custom-call(s32[5]{0:T(128)S(1)} %stack.31.me, bf16[2,272,256]{2,1,0:T(8,128)(2,1)S(1)} %copy-done, bf16[2,272,256]{2,1,0:T(8,128)(2,1)S(1)} %collective-permute-done.6.got, bf16[192,256]{1,0:T(8,128)(2,1)S(1)} %join.2.weights, ...), custom_call_target="tpu_custom_call" | custom-call | tf_op jit(solution)/shard_map/project_far/pallas_call | solution.py:486
  42.0 0.6 %collective-permute-start.7 = (bf16[2,272,256]{2,1,0:T(8,128)(2,1)}, bf16[2,272,256]{2,1,0:T(8,128)(2,1)S(1)}, u32[]{:S(2)}, u32[]{:S(2)}) collective-permute-start(bf16[2,272,256]{2,1,0:T(8,128)(2,1)} %get-tuple-element.90), channel_id=1, source_target_pairs={{0,2},{2,0},{4,6},{6,4},{8,10},{10,8},{12,14},{14,12},{1,3},{3,1},... | collective-permute-start | bytes 835592 | tf_op jit(solution)/shard_map/ppermute | solution.py:549
  42.6 2.2 %collective-permute-start.8 = (bf16[272,256]{1,0:T(8,128)(2,1)S(1)}, bf16[272,256]{1,0:T(8,128)(2,1)S(1)}, u32[]{:S(2)}, u32[]{:S(2)}) collective-permute-start(bf16[272,256]{1,0:T(8,128)(2,1)S(1)} %get-tuple-element.92), channel_id=1, source_target_pairs={{0,8},{2,10},{4,12},{6,14},{8,0},{10,2},{12,4},{14,6},{1,9},{3,11}... | collective-permute-start | bytes 417800 | tf_op jit(solution)/shard_map/ppermute | solution.py:549
  44.8 1.3 %collective-permute-start.9 = (bf16[272,256]{1,0:T(8,128)(2,1)S(1)}, bf16[272,256]{1,0:T(8,128)(2,1)S(1)}, u32[]{:S(2)}, u32[]{:S(2)}) collective-permute-start(bf16[272,256]{1,0:T(8,128)(2,1)S(1)} %get-tuple-element.93), channel_id=1, source_target_pairs={{0,12},{2,14},{4,8},{6,10},{8,4},{10,6},{12,0},{14,2},{1,13},{3,15... | collective-permute-start | bytes 417800 | tf_op jit(solution)/shard_map/ppermute | solution.py:549
  46.1 2.9 %collective-permute-done.7.got = bf16[2,272,256]{2,1,0:T(8,128)(2,1)S(1)} collective-permute-done((bf16[2,272,256]{2,1,0:T(8,128)(2,1)}, bf16[2,272,256]{2,1,0:T(8,128)(2,1)S(1)}, u32[]{:S(2)}, u32[]{:S(2)}) %collective-permute-start.7) | collective-permute-done | bytes 278560 | tf_op jit(solution)/shard_map/ppermute | solution.py:549
  49.0 1.8 %project_near.1 = (f32[272,256]{1,0:T(8,128)S(1)}, bf16[272,256]{1,0:T(8,128)(2,1)S(1)}) custom-call(s32[5]{0:T(128)S(1)} %stack.31.me, bf16[2,272,256]{2,1,0:T(8,128)(2,1)} %get-tuple-element.83.keep_hbm, bf16[2,272,256]{2,1,0:T(8,128)(2,1)S(1)} %collective-permute-done.7.got, bf16[192,256]{1,0:T(8,128)(2,1)S(1)} %join.2.weights, ...), custom_call_target="tpu_custom_call" | custom-call | tf_op jit(solution)/shard_map/project_near/pallas_call | solution.py:498
  50.8 1.6 %collective-permute-start.10 = (bf16[272,256]{1,0:T(8,128)(2,1)S(1)}, bf16[272,256]{1,0:T(8,128)(2,1)S(1)}, u32[]{:S(2)}, u32[]{:S(2)}) collective-permute-start(bf16[272,256]{1,0:T(8,128)(2,1)S(1)} %get-tuple-element.94), channel_id=1, source_target_pairs={{0,4},{2,6},{4,0},{6,2},{8,12},{10,14},{12,8},{14,10},{1,5},{3,7},... | collective-permute-start | bytes 417800 | tf_op jit(solution)/shard_map/ppermute | solution.py:549
  53.1 1.4 %collective-permute-done.8.a = bf16[272,256]{1,0:T(8,128)(2,1)S(1)} collective-permute-done((bf16[272,256]{1,0:T(8,128)(2,1)S(1)}, bf16[272,256]{1,0:T(8,128)(2,1)S(1)}, u32[]{:S(2)}, u32[]{:S(2)}) %collective-permute-start.8) | collective-permute-done | bytes 139296 | tf_op jit(solution)/shard_map/ppermute | solution.py:549
  54.4 0.0 collective-permute-done.9.b
  54.4 1.7 %collective-permute-done.10.c = bf16[272,256]{1,0:T(8,128)(2,1)S(1)} collective-permute-done((bf16[272,256]{1,0:T(8,128)(2,1)S(1)}, bf16[272,256]{1,0:T(8,128)(2,1)S(1)}, u32[]{:S(2)}, u32[]{:S(2)}) %collective-permute-start.10) | collective-permute-done | bytes 139296 | tf_op jit(solution)/shard_map/ppermute | solution.py:549
  56.1 0.0 copy-done.2
  56.1 0.0 copy-done.3
  56.1 0.0 copy-done.4
  56.1 0.0 copy-done.11
  56.2 0.0 copy-done.12
  56.2 0.0 copy-done.13
  56.2 0.7 %layer_two.1 = f32[32,153]{1,0:T(8,128)S(1)} custom-call(f32[272,256]{1,0:T(8,128)S(1)} %get-tuple-element.91.mine, bf16[272,256]{1,0:T(8,128)(2,1)S(1)} %collective-permute-done.8.a, bf16[272,256]{1,0:T(8,128)(2,1)S(1)} %collective-permute-done.9.b, bf16[272,256]{1,0:T(8,128)(2,1)S(1)} %collective-permute-done.10.c, s32[1,32]{1,0:T(1,128)S(1)} %bitcast.68, ...), custom_call_target="tpu_custom_call" | custom-call | tf_op jit(solution)/shard_map/layer_two/pallas_call | solution.py:512
  56.9 0.1 conditional.1
  57.0 0.0 copy-start.9
  57.1 0.6 %copy-done.9 = f32[32,153]{1,0:T(8,128)} copy-done((f32[32,153]{1,0:T(8,128)}, f32[32,153]{1,0:T(8,128)S(1)}, u32[]{:S(2)}) %copy-start.9) | copy-done | bytes 19608
  (2 shorter events, 0.0 us)
Async XLA Ops:
  0.0 17.6 %collective-permute-start.5 = (bf16[96,32768]{1,0:T(8,128)(2,1)}, bf16[96,32768]{1,0:T(8,128)(2,1)}, u32[]{:S(2)}, u32[]{:S(2)}) collective-permute-start(bf16[96,32768]{1,0:T(8,128)(2,1)} %features.3), channel_id=1, source_target_pairs={{0,1},{1,0},{2,3},{3,2},{4,5},{5,4},{6,7},{7,6},{8,9},{9,8},{10,11... | collective-permute-start | bytes 18874376 | tf_op jit(solution)/shard_map/ppermute | solution.py:551
  0.5 5.7 %collective-permute-start = (s32[1,32]{1,0:T(1,128)}, s32[1,32]{1,0:T(1,128)S(1)}, u32[]{:S(2)}, u32[]{:S(2)}) collective-permute-start(s32[1,32]{1,0:T(1,128)} %bitcast.65), channel_id=1, source_target_pairs={{0,2},{2,0},{4,6},{6,4},{8,10},{10,8},{12,14},{14,12},{1,3},{3,1},... | collective-permute-start | bytes 392 | tf_op jit(solution)/shard_map/ppermute | solution.py:549
  3.0 3.1 %copy-start.5 = (bf16[96,256]{1,0:T(8,128)(2,1)S(1)}, bf16[96,256]{1,0:T(8,128)(2,1)}, u32[]{:S(2)}) copy-start(bf16[96,256]{1,0:T(8,128)(2,1)} %refs_0_.1) | copy-start | bytes 147460
  3.0 3.1 %copy-start.6 = (bf16[96,256]{1,0:T(8,128)(2,1)S(1)}, bf16[96,256]{1,0:T(8,128)(2,1)}, u32[]{:S(2)}) copy-start(bf16[96,256]{1,0:T(8,128)(2,1)} %refs_1_.1) | copy-start | bytes 147460
  3.0 3.6 %copy-start.10 = (s32[32]{0:T(128)S(1)}, s32[32]{0:T(128)}, u32[]{:S(2)}) copy-start(s32[32]{0:T(128)} %param.19) | copy-start | bytes 388
  6.2 8.7 %collective-permute-start.4 = (bf16[192,256]{1,0:T(8,128)(2,1)S(1)}, bf16[192,256]{1,0:T(8,128)(2,1)S(1)}, u32[]{:S(2)}, u32[]{:S(2)}) collective-permute-start(bf16[192,256]{1,0:T(8,128)(2,1)S(1)} %join.2.weights), channel_id=1, source_target_pairs={{0,2},{2,0},{4,6},{6,4},{8,10},{10,8},{12,14},{14,12},{1,3},{3,1},... | collective-permute-start | bytes 294920 | tf_op jit(solution)/shard_map/ppermute | solution.py:549
  6.6 8.2 %copy-start.1 = (s32[15,2816]{1,0:T(8,128)S(1)}, s32[15,2816]{1,0:T(8,128)}, u32[]{:S(2)}) copy-start(s32[15,2816]{1,0:T(8,128)} %neighbour_ids.1) | copy-start | bytes 506884
  6.6 8.2 %copy-start.7 = (s32[2816]{0:T(1024)S(1)}, s32[2816]{0:T(1024)}, u32[]{:S(2)}) copy-start(s32[2816]{0:T(1024)} %count_one.1) | copy-start | bytes 33796
  6.6 8.2 %copy-start.8 = (s32[2816]{0:T(1024)S(1)}, s32[2816]{0:T(1024)}, u32[]{:S(2)}) copy-start(s32[2816]{0:T(1024)} %self_ids.1) | copy-start | bytes 33796
  6.6 7.5 %collective-permute-start.1 = (s32[2,32]{1,0:T(2,128)S(1)}, s32[2,32]{1,0:T(2,128)S(1)}, u32[]{:S(2)}, u32[]{:S(2)}) collective-permute-start(s32[2,32]{1,0:T(2,128)S(1)} %join.3), channel_id=1, source_target_pairs={{0,8},{2,10},{4,12},{6,14},{8,0},{10,2},{12,4},{14,6},{1,9},{3,11}... | collective-permute-start | bytes 776 | tf_op jit(solution)/shard_map/ppermute | solution.py:549
  9.5 5.4 %collective-permute-start.2 = (s32[2,32]{1,0:T(2,128)S(1)}, s32[2,32]{1,0:T(2,128)S(1)}, u32[]{:S(2)}, u32[]{:S(2)}) collective-permute-start(s32[2,32]{1,0:T(2,128)S(1)} %join.3), channel_id=1, source_target_pairs={{0,12},{2,14},{4,8},{6,10},{8,4},{10,6},{12,0},{14,2},{1,13},{3,15... | collective-permute-start | bytes 776 | tf_op jit(solution)/shard_map/ppermute | solution.py:549
  10.8 4.0 %collective-permute-start.3 = (s32[2,32]{1,0:T(2,128)S(1)}, s32[2,32]{1,0:T(2,128)S(1)}, u32[]{:S(2)}, u32[]{:S(2)}) collective-permute-start(s32[2,32]{1,0:T(2,128)S(1)} %join.3), channel_id=1, source_target_pairs={{0,4},{2,6},{4,0},{6,2},{8,12},{10,14},{12,8},{14,10},{1,5},{3,7},... | collective-permute-start | bytes 776 | tf_op jit(solution)/shard_map/ppermute | solution.py:549
  29.8 11.2 %collective-permute-start.6 = (bf16[2,272,256]{2,1,0:T(8,128)(2,1)}, bf16[2,272,256]{2,1,0:T(8,128)(2,1)S(1)}, u32[]{:S(2)}, u32[]{:S(2)}) collective-permute-start(bf16[2,272,256]{2,1,0:T(8,128)(2,1)} %get-tuple-element.85), channel_id=1, source_target_pairs={{0,2},{2,0},{4,6},{6,4},{8,10},{10,8},{12,14},{14,12},{1,3},{3,1},... | collective-permute-start | bytes 835592 | tf_op jit(solution)/shard_map/ppermute | solution.py:549
  31.4 9.7 %copy-start = (bf16[2,272,256]{2,1,0:T(8,128)(2,1)S(1)}, bf16[2,272,256]{2,1,0:T(8,128)(2,1)}, u32[]{:S(2)}) copy-start(bf16[2,272,256]{2,1,0:T(8,128)(2,1)} %get-tuple-element.84.keep) | copy-start | bytes 835588
  31.4 24.8 %copy-start.2 = (bf16[256,256]{1,0:T(8,128)(2,1)S(1)}, bf16[256,256]{1,0:T(8,128)(2,1)}, u32[]{:S(2)}) copy-start(bf16[256,256]{1,0:T(8,128)(2,1)} %neigh_two.1) | copy-start | bytes 393220
  31.4 24.8 %copy-start.3 = (bf16[256,256]{1,0:T(8,128)(2,1)S(1)}, bf16[256,256]{1,0:T(8,128)(2,1)}, u32[]{:S(2)}) copy-start(bf16[256,256]{1,0:T(8,128)(2,1)} %self_two.1) | copy-start | bytes 393220
  31.4 24.8 %copy-start.4 = (bf16[256,153]{0,1:T(8,128)(2,1)S(1)}, bf16[256,153]{0,1:T(8,128)(2,1)}, u32[]{:S(2)}) copy-start(bf16[256,153]{0,1:T(8,128)(2,1)} %param.26) | copy-start | bytes 235012
  31.4 24.8 %copy-start.11 = (f32[256]{0:T(256)S(1)}, f32[256]{0:T(256)}, u32[]{:S(2)}) copy-start(f32[256]{0:T(256)} %param.25) | copy-start | bytes 3076
  31.4 24.8 %copy-start.12 = (f32[153]{0:T(256)S(1)}, f32[153]{0:T(256)}, u32[]{:S(2)}) copy-start(f32[153]{0:T(256)} %param.27) | copy-start | bytes 1840
  31.4 24.8 %copy-start.13 = (f32[256]{0:T(256)S(1)}, f32[256]{0:T(256)}, u32[]{:S(2)}) copy-start(f32[256]{0:T(256)} %param.22) | copy-start | bytes 3076
  42.0 7.0 %collective-permute-start.7 = (bf16[2,272,256]{2,1,0:T(8,128)(2,1)}, bf16[2,272,256]{2,1,0:T(8,128)(2,1)S(1)}, u32[]{:S(2)}, u32[]{:S(2)}) collective-permute-start(bf16[2,272,256]{2,1,0:T(8,128)(2,1)} %get-tuple-element.90), channel_id=1, source_target_pairs={{0,2},{2,0},{4,6},{6,4},{8,10},{10,8},{12,14},{14,12},{1,3},{3,1},... | collective-permute-start | bytes 835592 | tf_op jit(solution)/shard_map/ppermute | solution.py:549
  42.6 11.8 %collective-permute-start.8 = (bf16[272,256]{1,0:T(8,128)(2,1)S(1)}, bf16[272,256]{1,0:T(8,128)(2,1)S(1)}, u32[]{:S(2)}, u32[]{:S(2)}) collective-permute-start(bf16[272,256]{1,0:T(8,128)(2,1)S(1)} %get-tuple-element.92), channel_id=1, source_target_pairs={{0,8},{2,10},{4,12},{6,14},{8,0},{10,2},{12,4},{14,6},{1,9},{3,11}... | collective-permute-start | bytes 417800 | tf_op jit(solution)/shard_map/ppermute | solution.py:549
  44.8 9.7 %collective-permute-start.9 = (bf16[272,256]{1,0:T(8,128)(2,1)S(1)}, bf16[272,256]{1,0:T(8,128)(2,1)S(1)}, u32[]{:S(2)}, u32[]{:S(2)}) collective-permute-start(bf16[272,256]{1,0:T(8,128)(2,1)S(1)} %get-tuple-element.93), channel_id=1, source_target_pairs={{0,12},{2,14},{4,8},{6,10},{8,4},{10,6},{12,0},{14,2},{1,13},{3,15... | collective-permute-start | bytes 417800 | tf_op jit(solution)/shard_map/ppermute | solution.py:549
  50.8 5.3 %collective-permute-start.10 = (bf16[272,256]{1,0:T(8,128)(2,1)S(1)}, bf16[272,256]{1,0:T(8,128)(2,1)S(1)}, u32[]{:S(2)}, u32[]{:S(2)}) collective-permute-start(bf16[272,256]{1,0:T(8,128)(2,1)S(1)} %get-tuple-element.94), channel_id=1, source_target_pairs={{0,4},{2,6},{4,0},{6,2},{8,12},{10,14},{12,8},{14,10},{1,5},{3,7},... | collective-permute-start | bytes 417800 | tf_op jit(solution)/shard_map/ppermute | solution.py:549
  57.0 0.6 %copy-start.9 = (f32[32,153]{1,0:T(8,128)}, f32[32,153]{1,0:T(8,128)S(1)}, u32[]{:S(2)}) copy-start(f32[32,153]{1,0:T(8,128)S(1)} %get-tuple-element.177) | copy-start | bytes 58756

commit v9 on v8

--- a/solution.py
+++ b/solution.py
@@ -244,14 +244,11 @@
         lax.fori_loop(0, jnp.right_shift(end - begin, UNROLL.bit_length() - 1), body, 0)
 
 
-def write_out(x, width, self_rows, mean_rows, keep, send):
+def block_of(z, side, width, self_rows, mean_rows):
     valid = iota((CAP, LANES), 1) < width
-    for z in range(2):
-        for ref, side in ((keep, x), (send, 1 - x)):
-            at = pl.multiple_of((z * 2 + side) * CAP, CAP)
-            for part, rows in enumerate((self_rows, mean_rows)):
-                block = jnp.where(valid, rows[pl.ds(at, CAP), :], 0.0).astype(BF16)
-                ref[z, :, part * LANES : (part + 1) * LANES] = block
+    at = pl.multiple_of((z * 2 + side) * CAP, CAP)
+    parts = [jnp.where(valid, rows[pl.ds(at, CAP), :], 0.0) for rows in (self_rows, mean_rows)]
+    return jnp.concatenate(parts, axis=1).astype(BF16)
 
 
 def stage(source, staged, sems):
@@ -287,12 +284,12 @@
         at += part.shape[0]
 
 
-def hand_out(keep, send, keep_hbm, send_hbm, sems):
-    copies = [
-        pltpu.make_async_copy(send, send_hbm, sems.at[0]),
-        pltpu.make_async_copy(keep, keep_hbm, sems.at[1]),
-    ]
-    start_all(copies)
+def hand_out(blocks, sems):
+    copies = []
+    for i, (make, scratch, out) in enumerate(blocks):
+        scratch[...] = make()
+        copies.append(pltpu.make_async_copy(scratch, out, sems.at[i]))
+        copies[-1].start()
     for copy in copies:
         copy.wait()
 
@@ -312,20 +309,38 @@
     mean_rows[...] = jnp.zeros_like(mean_rows)
     turn_staged(staging, staged, table, (1 - rep) * length)
     look_up(fanout, copies, table, ids, places, begins, self_rows, mean_rows)
-    write_out(x, width, self_rows, mean_rows, keep, send)
-    hand_out(keep, send, keep_hbm, send_hbm, out_sems)
-
-
-def second_kernel(fanout, width, me, lists, table, keep_hbm, send_hbm, *scratch):
+    hand_out(
+        [
+            (
+                functools.partial(block_of, z, side, width, self_rows, mean_rows),
+                held.at[z],
+                out.at[z],
+            )
+            for held, out, side in ((send, send_hbm, 1 - x), (keep, keep_hbm, x))
+            for z in range(2)
+        ],
+        out_sems,
+    )
+
+
+def second_kernel(fanout, width, me, lists, table, *refs):
+    outs, scratch = refs[:4], refs[4:]
     ids = scratch[: fanout + 1]
-    places, begins, self_rows, mean_rows, sems, keep, send, out_sems = scratch[fanout + 1 :]
-    x, h = me[0], 1 - me[1]
+    places, begins, self_rows, mean_rows, sems = scratch[fanout + 1 : fanout + 6]
+    *held, out_sems = scratch[fanout + 6 :]
+    x, h, zl = me[0], 1 - me[1], me[3]
     copies = list_copies(fanout, h, lists, ids, places, begins, sems)
     self_rows[...] = jnp.zeros_like(self_rows)
     mean_rows[...] = jnp.zeros_like(mean_rows)
     look_up(fanout, copies, table, ids, places, begins, self_rows, mean_rows)
-    write_out(x, width, self_rows, mean_rows, keep, send)
-    hand_out(keep, send, keep_hbm, send_hbm, out_sems)
+    sides = ((1 - zl, 1 - x), (zl, 1 - x), (1 - zl, x), (zl, x))
+    hand_out(
+        [
+            (functools.partial(block_of, z, side, width, self_rows, mean_rows), one, out)
+            for (z, side), one, out in zip(sides, held, outs)
+        ],
+        out_sems,
+    )
 
 
 def partial(rows, weights):
@@ -342,14 +357,12 @@
         out[...] = total.astype(BF16)
 
 
-def near_kernel(me, keep_hbm, got, weights, weights_got, out_0, out_1, keep, sem):
+def near_kernel(keep_hbm, got, weights, weights_got, out, keep, sem):
     copy = pltpu.make_async_copy(keep_hbm, keep, sem)
     copy.start()
-    zl = me[3]
-    theirs = partial(got[zl], weights_got), partial(got[1 - zl], weights_got)
+    theirs = partial(got, weights_got)
     copy.wait()
-    out_0[...] = partial(keep[zl], weights) + theirs[0]
-    out_1[...] = (partial(keep[1 - zl], weights) + theirs[1]).astype(BF16)
+    out[...] = (partial(keep, weights) + theirs).astype(out.dtype)
 
 
 def last_kernel(
@@ -457,7 +470,7 @@
             pltpu.SemaphoreType.DMA((8,)),
             pltpu.VMEM(dims, BF16),
             pltpu.VMEM(dims, BF16),
-            pltpu.SemaphoreType.DMA((2,)),
+            pltpu.SemaphoreType.DMA((4,)),
         ],
         input_output_aliases={2: 0},
         compiler_params=params(FIRST_MIB),
@@ -466,16 +479,15 @@
 
 
 def second_call(fanout, width, me, lists, table):
-    dims = (2, CAP, 2 * LANES)
-    halves = pltpu.HBM(dims, BF16)
+    dims = (CAP, 2 * LANES)
     return pl.pallas_call(
         functools.partial(second_kernel, fanout, width),
-        out_shape=(halves, halves),
+        out_shape=(pltpu.HBM(dims, BF16),) * 4,
         in_specs=[SMEM, ANY, VMEM],
-        out_specs=(HBM, HBM),
+        out_specs=(HBM,) * 4,
         scratch_shapes=list_scratch(fanout)
-        + [pltpu.VMEM(dims, BF16) for _ in range(2)]
-        + [pltpu.SemaphoreType.DMA((2,))],
+        + [pltpu.VMEM(dims, BF16) for _ in range(4)]
+        + [pltpu.SemaphoreType.DMA((4,))],
         compiler_params=params(10),
         name="second_half",
     )(me, lists, table)
@@ -493,17 +505,16 @@
     )(me, keep, got, weights, weights_got)
 
 
-def near_call(me, keep, got, weights, weights_got):
-    dims = (CAP, weights.shape[1])
+def near_call(keep, got, weights, weights_got, kind):
     return pl.pallas_call(
         near_kernel,
-        out_shape=(shape(dims, F32), shape(dims, BF16)),
-        in_specs=[SMEM, HBM] + [VMEM] * 3,
-        out_specs=(VMEM, VMEM),
+        out_shape=shape((CAP, weights.shape[1]), kind),
+        in_specs=[HBM] + [VMEM] * 3,
+        out_specs=VMEM,
         scratch_shapes=[pltpu.VMEM(keep.shape, BF16), pltpu.SemaphoreType.DMA],
         compiler_params=params(10),
         name="project_near",
-    )(me, pltpu.with_memory_space_constraint(keep, pltpu.HBM), got, weights, weights_got)
+    )(pltpu.with_memory_space_constraint(keep, pltpu.HBM), got, weights, weights_got)
 
 
 def last_call(*args):
@@ -566,15 +577,17 @@
     lists, most = order_call(per_seed, me, own, got, self_ids, neighbour_ids, count_one)
     table, keep_far, send_far = first_call(fanout, me, lists, table, other)
     got_far = across(send_far, 1)
-    keep_near, send_near = second_call(fanout, width, me, lists, table)
+    send_on, send_own, keep_on, keep_own = second_call(fanout, width, me, lists, table)
     far = far_call(me, keep_far, got_far, weights, weights_got)
-    far, send_near = lax.optimization_barrier((far, send_near))
+    far, send_on, send_own = lax.optimization_barrier((far, send_on, send_own))
     far_got = [across(far[0], 4), across(far[1], 6)]
-    got_near = across(send_near, 1)
-    near = near_call(me, keep_near, got_near, weights, weights_got)
-    far_got.append(across(near[1], 2))
+    got_on = across(send_on, 1)
+    got_own = across(send_own, 1)
+    near = near_call(keep_on, got_on, weights, weights_got, BF16)
+    far_got.append(across(near, 2))
+    mine = near_call(keep_own, got_own, weights, weights_got, F32)
     fast = last_call(
-        near[0],
+        mine,
         *far_got,
         own,
         bias_one[None, :],

time: 57.8 us -> 57.5 us (level)
  waiting for transfers between devices: 6.59 us -> 4.97 us
  starting transfers between devices: 15.1 us -> 16.6 us
    ppermute x10 -> x11, waiting for transfers between devices: 6.58 us -> 4.96 us  [across(): return lax.ppermute(value, 'col', [(i, i ^ bit) for i in range(owners)])]
    ppermute x10 -> x11, starting transfers between devices: 14.6 us -> 16.1 us  [across(): return lax.ppermute(value, 'col', [(i, i ^ bit) for i in range(owners)])]
    pallas_call x1, Pallas kernels: 9.6 us -> 8.78 us  [second_call(): pl.pallas_call(functools.partial(second_kernel, fanout, width), out_shape...]
    pallas_call x1 -> x2, Pallas kernels: 1.8 us -> 2.39 us  [near_call(): pl.pallas_call(near_kernel, out_shape=shape((CAP, weights.shape[1]), kind...]
  transfers between devices with their start and end apart: 11 -> 12, of which waited for: 4 -> 4; matrix products, arithmetic and copies ran while one was open for 0% -> 0% of each run, Pallas kernels for 35% -> 35%
where the time goes in v9:
time: 57.5 us; the launch traced here: 57.2 us
  Pallas kernels  33.9 us (59%)
  starting transfers between devices  16.6 us (29%)
  waiting for transfers between devices  4.97 us (9%)
  between operations  0.91 us (2%)
  local copies, waits for them, and re-layouts  0.75 us (1%)
    ppermute x11, starting transfers between devices, across(): return lax.ppermute(value, 'col', [(i, i ^ bit) for i in range(owners)])  16.1 us
    pallas_call x1, Pallas kernels, first_call(): pl.pallas_call(functools.partial(first_kernel, fanout), out_shape=(shape(...  12.1 us
    pallas_call x1, Pallas kernels, second_call(): pl.pallas_call(functools.partial(second_kernel, fanout, width), out_shape...  8.78 us
    pallas_call x2, Pallas kernels, own_call(): pl.pallas_call(functools.partial(own_kernel, which, halves), out_shape=sh...  6.22 us
    ppermute x11, waiting for transfers between devices, across(): return lax.ppermute(value, 'col', [(i, i ^ bit) for i in range(owners)])  4.96 us
    pallas_call x1, Pallas kernels, order_call(): pl.pallas_call(functools.partial(order_kernel, per_seed), out_shape=(shap...  2.73 us
    pallas_call x2, Pallas kernels, near_call(): pl.pallas_call(near_kernel, out_shape=shape((CAP, weights.shape[1]), kind...  2.39 us
  transfers between devices with their start and end apart: 12, of which 4 were waited for; matrix products, arithmetic and copies ran while one was open for 0% of the time, Pallas kernels for 35%

profile of v9, /device:TPU:0, one launch (start us, length us, event | category | flops | bytes accessed | tf_op | source)
XLA Modules:
  0.0 57.2 jit_solution(379460707637005467)
XLA Ops:
  0.0 0.5 collective-permute-start.5
  0.5 2.5 %collective-permute-start = (s32[1,32]{1,0:T(1,128)}, s32[1,32]{1,0:T(1,128)S(1)}, u32[]{:S(2)}, u32[]{:S(2)}) collective-permute-start(s32[1,32]{1,0:T(1,128)} %bitcast.65), channel_id=1, source_target_pairs={{0,2},{2,0},{4,6},{6,4},{8,10},{10,8},{12,14},{14,12},{1,3},{3,1},... | collective-permute-start | bytes 392 | tf_op jit(solution)/shard_map/ppermute | solution.py:560
  2.9 0.1 stack.31.me
  3.0 0.0 copy-start.5
  3.0 0.0 copy-start.6
  3.0 0.0 copy-start.10
  3.0 3.1 %own_rows.2.refs_0_ = f32[65536,128]{1,0:T(8,128)S(1)} custom-call(s32[5]{0:T(128)S(1)} %stack.31.me, bf16[96,32768]{1,0:T(8,128)(2,1)} %features.3), custom_call_target="tpu_custom_call" | custom-call | tf_op jit(solution)/shard_map/own_rows/pallas_call | solution.py:432
  6.2 0.0 copy-done.5
  6.2 0.0 copy-done.6
  6.2 0.0 collective-permute-done.refs_1_.got_1
  6.2 0.4 collective-permute-start.4
  6.6 0.0 copy-done.10
  6.6 0.0 copy-start.1
  6.6 0.0 copy-start.7
  6.6 0.0 copy-start.8
  6.6 2.8 %collective-permute-start.1 = (s32[2,32]{1,0:T(2,128)S(1)}, s32[2,32]{1,0:T(2,128)S(1)}, u32[]{:S(2)}, u32[]{:S(2)}) collective-permute-start(s32[2,32]{1,0:T(2,128)S(1)} %join.3), channel_id=1, source_target_pairs={{0,8},{2,10},{4,12},{6,14},{8,0},{10,2},{12,4},{14,6},{1,9},{3,11}... | collective-permute-start | bytes 776 | tf_op jit(solution)/shard_map/ppermute | solution.py:560
  9.5 1.3 %collective-permute-start.2 = (s32[2,32]{1,0:T(2,128)S(1)}, s32[2,32]{1,0:T(2,128)S(1)}, u32[]{:S(2)}, u32[]{:S(2)}) collective-permute-start(s32[2,32]{1,0:T(2,128)S(1)} %join.3), channel_id=1, source_target_pairs={{0,12},{2,14},{4,8},{6,10},{8,4},{10,6},{12,0},{14,2},{1,13},{3,15... | collective-permute-start | bytes 776 | tf_op jit(solution)/shard_map/ppermute | solution.py:560
  10.8 0.2 collective-permute-start.3
  11.1 3.1 %own_rows.3.table_in = f32[65536,128]{1,0:T(8,128)S(1)} custom-call(s32[5]{0:T(128)S(1)} %stack.31.me, bf16[96,32768]{1,0:T(8,128)(2,1)} %features.3, f32[65536,128]{1,0:T(8,128)S(1)} %own_rows.2.refs_0_), custom_call_target="tpu_custom_call", output_to_operand_aliasing={{}: (2, {})} | custom-call | tf_op jit(solution)/shard_map/own_rows/pallas_call | solution.py:432
  14.2 0.0 collective-permute-done.1.got_4
  14.2 0.7 %collective-permute-done.2.got_6 = s32[2,32]{1,0:T(2,128)S(1)} collective-permute-done((s32[2,32]{1,0:T(2,128)S(1)}, s32[2,32]{1,0:T(2,128)S(1)}, u32[]{:S(2)}, u32[]{:S(2)}) %collective-permute-start.2) | collective-permute-done | bytes 288 | tf_op jit(solution)/shard_map/ppermute | solution.py:560
  14.8 0.0 collective-permute-done.3.got_2
  14.9 0.0 collective-permute-done.4.weights_got
  14.9 0.0 copy-done.1
  14.9 0.0 copy-done.7
  14.9 0.0 copy-done.8
  14.9 2.7 %order.1 = (s32[2,18,16,128]{3,2,1,0:T(8,128)S(1)}, s32[1]{0:T(128)}) custom-call(s32[5]{0:T(128)S(1)} %stack.31.me, s32[1,32]{1,0:T(1,128)S(1)} %bitcast.67, s32[1,32]{1,0:T(1,128)S(1)} %collective-permute-done.refs_1_.got_1, s32[2,32]{1,0:T(2,128)S(1)} %collective-permute-done.3.got_2, s32[2,32]{1,0:T(2,128)S(1)} %collective-permute-done.1.got_4, ...), custom_call_target="tpu_custom_call" | custom-call | tf_op jit(solution)/shard_map/order/pallas_call | solution.py:408
  17.6 0.0 collective-permute-done.5.other
  17.6 12.1 %first_half.1 = (f32[65536,128]{1,0:T(8,128)S(1)}, bf16[2,272,256]{2,1,0:T(8,128)(2,1)}, bf16[2,272,256]{2,1,0:T(8,128)(2,1)}) custom-call(s32[5]{0:T(128)S(1)} %stack.31.me, s32[73728]{0:T(1024)S(1)} %bitcast.55, f32[65536,128]{1,0:T(8,128)S(1)} %own_rows.3.table_in, bf16[96,32768]{1,0:T(8,128)(2,1)} %collective-permute-done.5.other), custom_call_target="tpu_custom_call", output_to_operand_aliasing={{0}: (2, {})} | custom-call | tf_op jit(solution)/shard_map/first_half/pallas_call | solution.py:462
  29.7 1.6 %collective-permute-start.6 = (bf16[2,272,256]{2,1,0:T(8,128)(2,1)}, bf16[2,272,256]{2,1,0:T(8,128)(2,1)S(1)}, u32[]{:S(2)}, u32[]{:S(2)}) collective-permute-start(bf16[2,272,256]{2,1,0:T(8,128)(2,1)} %get-tuple-element.86), channel_id=1, source_target_pairs={{0,2},{2,0},{4,6},{6,4},{8,10},{10,8},{12,14},{14,12},{1,3},{3,1},... | collective-permute-start | bytes 835592 | tf_op jit(solution)/shard_map/ppermute | solution.py:560
  31.2 0.0 copy-start
  31.2 0.0 copy-start.2
  31.2 0.0 copy-start.3
  31.2 0.0 copy-start.4
  31.3 0.0 copy-start.11
  31.3 0.0 copy-start.12
  31.3 0.0 copy-start.13
  31.3 8.8 %second_half.1 = (bf16[272,256]{1,0:T(8,128)(2,1)}, bf16[272,256]{1,0:T(8,128)(2,1)}, bf16[272,256]{1,0:T(8,128)(2,1)}, bf16[272,256]{1,0:T(8,128)(2,1)}) custom-call(s32[5]{0:T(128)S(1)} %stack.31.me, s32[73728]{0:T(1024)S(1)} %bitcast.56, f32[65536,128]{1,0:T(8,128)S(1)} %get-tuple-element.83.table), custom_call_target="tpu_custom_call" | custom-call | tf_op jit(solution)/shard_map/second_half/pallas_call | solution.py:483
  40.1 0.0 collective-permute-done.6.got
  40.1 0.0 copy-done
  40.1 1.0 %project_far.1 = (bf16[272,256]{1,0:T(8,128)(2,1)S(1)}, bf16[272,256]{1,0:T(8,128)(2,1)S(1)}) custom-call(s32[5]{0:T(128)S(1)} %stack.31.me, bf16[2,272,256]{2,1,0:T(8,128)(2,1)S(1)} %copy-done, bf16[2,272,256]{2,1,0:T(8,128)(2,1)S(1)} %collective-permute-done.6.got, bf16[192,256]{1,0:T(8,128)(2,1)S(1)} %join.2.weights, ...), custom_call_target="tpu_custom_call" | custom-call | tf_op jit(solution)/shard_map/project_far/pallas_call | solution.py:498
  41.1 0.6 %collective-permute-start.10 = (bf16[272,256]{1,0:T(8,128)(2,1)}, bf16[272,256]{1,0:T(8,128)(2,1)S(1)}, u32[]{:S(2)}, u32[]{:S(2)}) collective-permute-start(bf16[272,256]{1,0:T(8,128)(2,1)} %get-tuple-element.96), channel_id=1, source_target_pairs={{0,2},{2,0},{4,6},{6,4},{8,10},{10,8},{12,14},{14,12},{1,3},{3,1},... | collective-permute-start | bytes 417800 | tf_op jit(solution)/shard_map/ppermute | solution.py:560
  41.7 1.5 %collective-permute-start.7 = (bf16[272,256]{1,0:T(8,128)(2,1)}, bf16[272,256]{1,0:T(8,128)(2,1)S(1)}, u32[]{:S(2)}, u32[]{:S(2)}) collective-permute-start(bf16[272,256]{1,0:T(8,128)(2,1)} %get-tuple-element.92), channel_id=1, source_target_pairs={{0,2},{2,0},{4,6},{6,4},{8,10},{10,8},{12,14},{14,12},{1,3},{3,1},... | collective-permute-start | bytes 417800 | tf_op jit(solution)/shard_map/ppermute | solution.py:560
  43.2 2.2 %collective-permute-start.8 = (bf16[272,256]{1,0:T(8,128)(2,1)S(1)}, bf16[272,256]{1,0:T(8,128)(2,1)S(1)}, u32[]{:S(2)}, u32[]{:S(2)}) collective-permute-start(bf16[272,256]{1,0:T(8,128)(2,1)S(1)} %get-tuple-element.93), channel_id=1, source_target_pairs={{0,8},{2,10},{4,12},{6,14},{8,0},{10,2},{12,4},{14,6},{1,9},{3,11}... | collective-permute-start | bytes 417800 | tf_op jit(solution)/shard_map/ppermute | solution.py:560
  45.3 1.3 %collective-permute-start.9 = (bf16[272,256]{1,0:T(8,128)(2,1)S(1)}, bf16[272,256]{1,0:T(8,128)(2,1)S(1)}, u32[]{:S(2)}, u32[]{:S(2)}) collective-permute-start(bf16[272,256]{1,0:T(8,128)(2,1)S(1)} %get-tuple-element.94), channel_id=1, source_target_pairs={{0,12},{2,14},{4,8},{6,10},{8,4},{10,6},{12,0},{14,2},{1,13},{3,15... | collective-permute-start | bytes 417800 | tf_op jit(solution)/shard_map/ppermute | solution.py:560
  46.7 0.6 %collective-permute-done.10.got = bf16[272,256]{1,0:T(8,128)(2,1)S(1)} collective-permute-done((bf16[272,256]{1,0:T(8,128)(2,1)}, bf16[272,256]{1,0:T(8,128)(2,1)S(1)}, u32[]{:S(2)}, u32[]{:S(2)}) %collective-permute-start.10) | collective-permute-done | bytes 139296 | tf_op jit(solution)/shard_map/ppermute | solution.py:560
  47.3 1.2 %project_near.3 = bf16[272,256]{1,0:T(8,128)(2,1)S(1)} custom-call(bf16[272,256]{1,0:T(8,128)(2,1)} %get-tuple-element.95.keep_hbm, bf16[272,256]{1,0:T(8,128)(2,1)S(1)} %collective-permute-done.10.got, bf16[192,256]{1,0:T(8,128)(2,1)S(1)} %join.2.weights, bf16[192,256]{1,0:T(8,128)(2,1)S(1)} %collective-permute-done.4.weights_got), custom_call_target="tpu_custom_call" | custom-call | tf_op jit(solution)/shard_map/project_near/pallas_call | solution.py:509
  48.5 1.6 %collective-permute-start.11 = (bf16[272,256]{1,0:T(8,128)(2,1)S(1)}, bf16[272,256]{1,0:T(8,128)(2,1)S(1)}, u32[]{:S(2)}, u32[]{:S(2)}) collective-permute-start(bf16[272,256]{1,0:T(8,128)(2,1)S(1)} %project_near.3), channel_id=1, source_target_pairs={{0,4},{2,6},{4,0},{6,2},{8,12},{10,14},{12,8},{14,10},{1,5},{3,7},... | collective-permute-start | bytes 417800 | tf_op jit(solution)/shard_map/ppermute | solution.py:560
  50.8 0.0 collective-permute-done.7.got
  50.8 1.2 %project_near.2.mine = f32[272,256]{1,0:T(8,128)S(1)} custom-call(bf16[272,256]{1,0:T(8,128)(2,1)} %get-tuple-element.84.keep_hbm, bf16[272,256]{1,0:T(8,128)(2,1)S(1)} %collective-permute-done.7.got, bf16[192,256]{1,0:T(8,128)(2,1)S(1)} %join.2.weights, bf16[192,256]{1,0:T(8,128)(2,1)S(1)} %collective-permute-done.4.weights_got), custom_call_target="tpu_custom_call" | custom-call | tf_op jit(solution)/shard_map/project_near/pallas_call | solution.py:509
  52.0 3.2 %collective-permute-done.8.a = bf16[272,256]{1,0:T(8,128)(2,1)S(1)} collective-permute-done((bf16[272,256]{1,0:T(8,128)(2,1)S(1)}, bf16[272,256]{1,0:T(8,128)(2,1)S(1)}, u32[]{:S(2)}, u32[]{:S(2)}) %collective-permute-start.8) | collective-permute-done | bytes 139296 | tf_op jit(solution)/shard_map/ppermute | solution.py:560
  55.2 0.0 collective-permute-done.9.b
  55.2 0.5 collective-permute-done.11.c
  55.7 0.0 copy-done.2
  55.7 0.0 copy-done.3
  55.7 0.0 copy-done.4
  55.7 0.0 copy-done.11
  55.7 0.0 copy-done.12
  55.7 0.0 copy-done.13
  55.7 0.7 %layer_two.1 = f32[32,153]{1,0:T(8,128)S(1)} custom-call(f32[272,256]{1,0:T(8,128)S(1)} %project_near.2.mine, bf16[272,256]{1,0:T(8,128)(2,1)S(1)} %collective-permute-done.8.a, bf16[272,256]{1,0:T(8,128)(2,1)S(1)} %collective-permute-done.9.b, bf16[272,256]{1,0:T(8,128)(2,1)S(1)} %collective-permute-done.11.c, s32[1,32]{1,0:T(1,128)S(1)} %bitcast.68, ...), custom_call_target="tpu_custom_call" | custom-call | tf_op jit(solution)/shard_map/layer_two/pallas_call | solution.py:523
  56.4 0.1 conditional.1
  56.6 0.0 copy-start.9
  56.6 0.6 %copy-done.9 = f32[32,153]{1,0:T(8,128)} copy-done((f32[32,153]{1,0:T(8,128)}, f32[32,153]{1,0:T(8,128)S(1)}, u32[]{:S(2)}) %copy-start.9) | copy-done | bytes 19608
  (2 shorter events, 0.0 us)
Async XLA Ops:
  0.0 17.6 %collective-permute-start.5 = (bf16[96,32768]{1,0:T(8,128)(2,1)}, bf16[96,32768]{1,0:T(8,128)(2,1)}, u32[]{:S(2)}, u32[]{:S(2)}) collective-permute-start(bf16[96,32768]{1,0:T(8,128)(2,1)} %features.3), channel_id=1, source_target_pairs={{0,1},{1,0},{2,3},{3,2},{4,5},{5,4},{6,7},{7,6},{8,9},{9,8},{10,11... | collective-permute-start | bytes 18874376 | tf_op jit(solution)/shard_map/ppermute | solution.py:562
  0.5 5.7 %collective-permute-start = (s32[1,32]{1,0:T(1,128)}, s32[1,32]{1,0:T(1,128)S(1)}, u32[]{:S(2)}, u32[]{:S(2)}) collective-permute-start(s32[1,32]{1,0:T(1,128)} %bitcast.65), channel_id=1, source_target_pairs={{0,2},{2,0},{4,6},{6,4},{8,10},{10,8},{12,14},{14,12},{1,3},{3,1},... | collective-permute-start | bytes 392 | tf_op jit(solution)/shard_map/ppermute | solution.py:560
  3.0 3.1 %copy-start.5 = (bf16[96,256]{1,0:T(8,128)(2,1)S(1)}, bf16[96,256]{1,0:T(8,128)(2,1)}, u32[]{:S(2)}) copy-start(bf16[96,256]{1,0:T(8,128)(2,1)} %refs_0_.1) | copy-start | bytes 147460
  3.0 3.1 %copy-start.6 = (bf16[96,256]{1,0:T(8,128)(2,1)S(1)}, bf16[96,256]{1,0:T(8,128)(2,1)}, u32[]{:S(2)}) copy-start(bf16[96,256]{1,0:T(8,128)(2,1)} %refs_1_.1) | copy-start | bytes 147460
  3.0 3.6 %copy-start.10 = (s32[32]{0:T(128)S(1)}, s32[32]{0:T(128)}, u32[]{:S(2)}) copy-start(s32[32]{0:T(128)} %param.19) | copy-start | bytes 388
  6.2 8.7 %collective-permute-start.4 = (bf16[192,256]{1,0:T(8,128)(2,1)S(1)}, bf16[192,256]{1,0:T(8,128)(2,1)S(1)}, u32[]{:S(2)}, u32[]{:S(2)}) collective-permute-start(bf16[192,256]{1,0:T(8,128)(2,1)S(1)} %join.2.weights), channel_id=1, source_target_pairs={{0,2},{2,0},{4,6},{6,4},{8,10},{10,8},{12,14},{14,12},{1,3},{3,1},... | collective-permute-start | bytes 294920 | tf_op jit(solution)/shard_map/ppermute | solution.py:560
  6.6 8.2 %copy-start.1 = (s32[15,2816]{1,0:T(8,128)S(1)}, s32[15,2816]{1,0:T(8,128)}, u32[]{:S(2)}) copy-start(s32[15,2816]{1,0:T(8,128)} %neighbour_ids.1) | copy-start | bytes 506884
  6.6 8.2 %copy-start.7 = (s32[2816]{0:T(1024)S(1)}, s32[2816]{0:T(1024)}, u32[]{:S(2)}) copy-start(s32[2816]{0:T(1024)} %count_one.1) | copy-start | bytes 33796
  6.6 8.2 %copy-start.8 = (s32[2816]{0:T(1024)S(1)}, s32[2816]{0:T(1024)}, u32[]{:S(2)}) copy-start(s32[2816]{0:T(1024)} %self_ids.1) | copy-start | bytes 33796
  6.6 7.5 %collective-permute-start.1 = (s32[2,32]{1,0:T(2,128)S(1)}, s32[2,32]{1,0:T(2,128)S(1)}, u32[]{:S(2)}, u32[]{:S(2)}) collective-permute-start(s32[2,32]{1,0:T(2,128)S(1)} %join.3), channel_id=1, source_target_pairs={{0,8},{2,10},{4,12},{6,14},{8,0},{10,2},{12,4},{14,6},{1,9},{3,11}... | collective-permute-start | bytes 776 | tf_op jit(solution)/shard_map/ppermute | solution.py:560
  9.5 5.4 %collective-permute-start.2 = (s32[2,32]{1,0:T(2,128)S(1)}, s32[2,32]{1,0:T(2,128)S(1)}, u32[]{:S(2)}, u32[]{:S(2)}) collective-permute-start(s32[2,32]{1,0:T(2,128)S(1)} %join.3), channel_id=1, source_target_pairs={{0,12},{2,14},{4,8},{6,10},{8,4},{10,6},{12,0},{14,2},{1,13},{3,15... | collective-permute-start | bytes 776 | tf_op jit(solution)/shard_map/ppermute | solution.py:560
  10.8 4.0 %collective-permute-start.3 = (s32[2,32]{1,0:T(2,128)S(1)}, s32[2,32]{1,0:T(2,128)S(1)}, u32[]{:S(2)}, u32[]{:S(2)}) collective-permute-start(s32[2,32]{1,0:T(2,128)S(1)} %join.3), channel_id=1, source_target_pairs={{0,4},{2,6},{4,0},{6,2},{8,12},{10,14},{12,8},{14,10},{1,5},{3,7},... | collective-permute-start | bytes 776 | tf_op jit(solution)/shard_map/ppermute | solution.py:560
  29.7 10.4 %collective-permute-start.6 = (bf16[2,272,256]{2,1,0:T(8,128)(2,1)}, bf16[2,272,256]{2,1,0:T(8,128)(2,1)S(1)}, u32[]{:S(2)}, u32[]{:S(2)}) collective-permute-start(bf16[2,272,256]{2,1,0:T(8,128)(2,1)} %get-tuple-element.86), channel_id=1, source_target_pairs={{0,2},{2,0},{4,6},{6,4},{8,10},{10,8},{12,14},{14,12},{1,3},{3,1},... | collective-permute-start | bytes 835592 | tf_op jit(solution)/shard_map/ppermute | solution.py:560
  31.2 8.9 %copy-start = (bf16[2,272,256]{2,1,0:T(8,128)(2,1)S(1)}, bf16[2,272,256]{2,1,0:T(8,128)(2,1)}, u32[]{:S(2)}) copy-start(bf16[2,272,256]{2,1,0:T(8,128)(2,1)} %get-tuple-element.85.keep) | copy-start | bytes 835588
  31.2 24.4 %copy-start.2 = (bf16[256,256]{1,0:T(8,128)(2,1)S(1)}, bf16[256,256]{1,0:T(8,128)(2,1)}, u32[]{:S(2)}) copy-start(bf16[256,256]{1,0:T(8,128)(2,1)} %neigh_two.1) | copy-start | bytes 393220
  31.2 24.4 %copy-start.3 = (bf16[256,256]{1,0:T(8,128)(2,1)S(1)}, bf16[256,256]{1,0:T(8,128)(2,1)}, u32[]{:S(2)}) copy-start(bf16[256,256]{1,0:T(8,128)(2,1)} %self_two.1) | copy-start | bytes 393220
  31.2 24.4 %copy-start.4 = (bf16[256,153]{0,1:T(8,128)(2,1)S(1)}, bf16[256,153]{0,1:T(8,128)(2,1)}, u32[]{:S(2)}) copy-start(bf16[256,153]{0,1:T(8,128)(2,1)} %param.26) | copy-start | bytes 235012
  31.3 24.4 %copy-start.11 = (f32[256]{0:T(256)S(1)}, f32[256]{0:T(256)}, u32[]{:S(2)}) copy-start(f32[256]{0:T(256)} %param.25) | copy-start | bytes 3076
  31.3 24.4 %copy-start.12 = (f32[153]{0:T(256)S(1)}, f32[153]{0:T(256)}, u32[]{:S(2)}) copy-start(f32[153]{0:T(256)} %param.27) | copy-start | bytes 1840
  31.3 24.4 %copy-start.13 = (f32[256]{0:T(256)S(1)}, f32[256]{0:T(256)}, u32[]{:S(2)}) copy-start(f32[256]{0:T(256)} %param.22) | copy-start | bytes 3076
  41.1 6.2 %collective-permute-start.10 = (bf16[272,256]{1,0:T(8,128)(2,1)}, bf16[272,256]{1,0:T(8,128)(2,1)S(1)}, u32[]{:S(2)}, u32[]{:S(2)}) collective-permute-start(bf16[272,256]{1,0:T(8,128)(2,1)} %get-tuple-element.96), channel_id=1, source_target_pairs={{0,2},{2,0},{4,6},{6,4},{8,10},{10,8},{12,14},{14,12},{1,3},{3,1},... | collective-permute-start | bytes 417800 | tf_op jit(solution)/shard_map/ppermute | solution.py:560
  41.7 9.1 %collective-permute-start.7 = (bf16[272,256]{1,0:T(8,128)(2,1)}, bf16[272,256]{1,0:T(8,128)(2,1)S(1)}, u32[]{:S(2)}, u32[]{:S(2)}) collective-permute-start(bf16[272,256]{1,0:T(8,128)(2,1)} %get-tuple-element.92), channel_id=1, source_target_pairs={{0,2},{2,0},{4,6},{6,4},{8,10},{10,8},{12,14},{14,12},{1,3},{3,1},... | collective-permute-start | bytes 417800 | tf_op jit(solution)/shard_map/ppermute | solution.py:560
  43.2 12.0 %collective-permute-start.8 = (bf16[272,256]{1,0:T(8,128)(2,1)S(1)}, bf16[272,256]{1,0:T(8,128)(2,1)S(1)}, u32[]{:S(2)}, u32[]{:S(2)}) collective-permute-start(bf16[272,256]{1,0:T(8,128)(2,1)S(1)} %get-tuple-element.93), channel_id=1, source_target_pairs={{0,8},{2,10},{4,12},{6,14},{8,0},{10,2},{12,4},{14,6},{1,9},{3,11}... | collective-permute-start | bytes 417800 | tf_op jit(solution)/shard_map/ppermute | solution.py:560
  45.3 9.8 %collective-permute-start.9 = (bf16[272,256]{1,0:T(8,128)(2,1)S(1)}, bf16[272,256]{1,0:T(8,128)(2,1)S(1)}, u32[]{:S(2)}, u32[]{:S(2)}) collective-permute-start(bf16[272,256]{1,0:T(8,128)(2,1)S(1)} %get-tuple-element.94), channel_id=1, source_target_pairs={{0,12},{2,14},{4,8},{6,10},{8,4},{10,6},{12,0},{14,2},{1,13},{3,15... | collective-permute-start | bytes 417800 | tf_op jit(solution)/shard_map/ppermute | solution.py:560
  48.5 7.2 %collective-permute-start.11 = (bf16[272,256]{1,0:T(8,128)(2,1)S(1)}, bf16[272,256]{1,0:T(8,128)(2,1)S(1)}, u32[]{:S(2)}, u32[]{:S(2)}) collective-permute-start(bf16[272,256]{1,0:T(8,128)(2,1)S(1)} %project_near.3), channel_id=1, source_target_pairs={{0,4},{2,6},{4,0},{6,2},{8,12},{10,14},{12,8},{14,10},{1,5},{3,7},... | collective-permute-start | bytes 417800 | tf_op jit(solution)/shard_map/ppermute | solution.py:560
  56.6 0.6 %copy-start.9 = (f32[32,153]{1,0:T(8,128)}, f32[32,153]{1,0:T(8,128)S(1)}, u32[]{:S(2)}) copy-start(f32[32,153]{1,0:T(8,128)S(1)} %get-tuple-element.180) | copy-start | bytes 58756

commit v10 on v8

--- a/solution.py
+++ b/solution.py
@@ -245,13 +245,20 @@
 
 
 def write_out(x, width, self_rows, mean_rows, keep, send):
-    valid = iota((CAP, LANES), 1) < width
-    for z in range(2):
-        for ref, side in ((keep, x), (send, 1 - x)):
+    lane = iota((CAP, LANES), 1)
+    rest = 2 * width - LANES
+    for ref, side in ((keep, x), (send, 1 - x)):
+        turned = []
+        for z in range(2):
             at = pl.multiple_of((z * 2 + side) * CAP, CAP)
-            for part, rows in enumerate((self_rows, mean_rows)):
-                block = jnp.where(valid, rows[pl.ds(at, CAP), :], 0.0).astype(BF16)
-                ref[z, :, part * LANES : (part + 1) * LANES] = block
+            mean = jnp.where(lane < width, mean_rows[pl.ds(at, CAP), :], 0.0)
+            turned.append(pltpu.roll(mean, width, 1))
+            own = self_rows[pl.ds(at, CAP), :]
+            ref[z, :, :] = jnp.where(lane < width, own, turned[z]).astype(BF16)
+        right = pltpu.roll(turned[1], LANES // 2, 1)
+        block = jnp.where(lane < LANES // 2, turned[0], right)
+        used = (lane < rest) | ((lane >= LANES // 2) & (lane < LANES // 2 + rest))
+        ref[2, :, :] = jnp.where(used, block, 0.0).astype(BF16)
 
 
 def stage(source, staged, sems):
@@ -328,28 +335,35 @@
     hand_out(keep, send, keep_hbm, send_hbm, out_sems)
 
 
-def partial(rows, weights):
-    width = weights.shape[0] // 2
-    return jnp.dot(rows[:, 0:width], weights[0:width, :], preferred_element_type=F32) + jnp.dot(
-        rows[:, LANES : LANES + width], weights[width:, :], preferred_element_type=F32
-    )
+def partials(blocks, weights):
+    rest = weights.shape[0] - LANES
+    return [
+        jnp.dot(blocks[z], weights[0:LANES, :], preferred_element_type=F32)
+        + jnp.dot(
+            blocks[2, :, z * LANES // 2 : z * LANES // 2 + rest],
+            weights[LANES:, :],
+            preferred_element_type=F32,
+        )
+        for z in range(2)
+    ]
 
 
 def far_kernel(me, keep, got, weights, weights_got, out_0, out_1):
     zl = me[3]
-    for which, out in ((zl, out_0), (1 - zl, out_1)):
-        total = partial(keep[which], weights) + partial(got[which], weights_got)
-        out[...] = total.astype(BF16)
+    pre = [a + b for a, b in zip(partials(keep, weights), partials(got, weights_got))]
+    out_0[...] = jnp.where(zl == 0, pre[0], pre[1]).astype(BF16)
+    out_1[...] = jnp.where(zl == 0, pre[1], pre[0]).astype(BF16)
 
 
 def near_kernel(me, keep_hbm, got, weights, weights_got, out_0, out_1, keep, sem):
     copy = pltpu.make_async_copy(keep_hbm, keep, sem)
     copy.start()
     zl = me[3]
-    theirs = partial(got[zl], weights_got), partial(got[1 - zl], weights_got)
+    theirs = partials(got, weights_got)
     copy.wait()
-    out_0[...] = partial(keep[zl], weights) + theirs[0]
-    out_1[...] = (partial(keep[1 - zl], weights) + theirs[1]).astype(BF16)
+    pre = [a + b for a, b in zip(partials(keep, weights), theirs)]
+    out_0[...] = jnp.where(zl == 0, pre[0], pre[1])
+    out_1[...] = jnp.where(zl == 0, pre[1], pre[0]).astype(BF16)
 
 
 def last_kernel(
@@ -445,7 +459,7 @@
 
 def first_call(fanout, me, lists, table, other):
     width, length = other.shape
-    dims = (2, CAP, 2 * LANES)
+    dims = (3, CAP, LANES)
     return pl.pallas_call(
         functools.partial(first_kernel, fanout),
         out_shape=(shape((2 * length, LANES), F32), pltpu.HBM(dims, BF16), pltpu.HBM(dims, BF16)),
@@ -466,7 +480,7 @@
 
 
 def second_call(fanout, width, me, lists, table):
-    dims = (2, CAP, 2 * LANES)
+    dims = (3, CAP, LANES)
     halves = pltpu.HBM(dims, BF16)
     return pl.pallas_call(
         functools.partial(second_kernel, fanout, width),
@@ -611,7 +625,7 @@
     sizes = (lax.axis_size("groups"), lax.axis_size("col"), lax.axis_size("rep"))
     small = (
         sizes == (2, 8, 2)
-        and features.shape[0] <= LANES
+        and LANES // 2 < features.shape[0] <= 3 * LANES // 4
         and features.shape[1] <= 32768
         and self_ids.shape[0] * (neighbour_ids.shape[0] + 1) <= 2**17
         and neighbour_ids.shape[0] <= 15

time: 57.8 us -> 58 us (level)
  waiting for transfers between devices: 6.59 us -> 7.73 us
    ppermute x10, waiting for transfers between devices: 6.58 us -> 7.72 us  [across(): return lax.ppermute(value, 'col', [(i, i ^ bit) for i in range(owners)])]
    pallas_call x1, Pallas kernels: 9.6 us -> 8.94 us  [second_call(): pl.pallas_call(functools.partial(second_kernel, fanout, width), out_shape...]
  transfers between devices with their start and end apart: 11 -> 11, of which waited for: 4 -> 4; matrix products, arithmetic and copies ran while one was open for 0% -> 0% of each run, Pallas kernels for 35% -> 34%
where the time goes in v10:
time: 58 us; the launch traced here: 58.4 us
  Pallas kernels  33.8 us (58%)
  starting transfers between devices  15.1 us (26%)
  waiting for transfers between devices  7.73 us (13%)
  between operations  0.89 us (2%)
  local copies, waits for them, and re-layouts  0.75 us (1%)
    ppermute x10, starting transfers between devices, across(): return lax.ppermute(value, 'col', [(i, i ^ bit) for i in range(owners)])  14.6 us
    pallas_call x1, Pallas kernels, first_call(): pl.pallas_call(functools.partial(first_kernel, fanout), out_shape=(shape(...  12.3 us
    pallas_call x1, Pallas kernels, second_call(): pl.pallas_call(functools.partial(second_kernel, fanout, width), out_shape...  8.94 us
    ppermute x10, waiting for transfers between devices, across(): return lax.ppermute(value, 'col', [(i, i ^ bit) for i in range(owners)])  7.72 us
    pallas_call x2, Pallas kernels, own_call(): pl.pallas_call(functools.partial(own_kernel, which, halves), out_shape=sh...  6.22 us
    pallas_call x1, Pallas kernels, order_call(): pl.pallas_call(functools.partial(order_kernel, per_seed), out_shape=(shap...  2.73 us
    pallas_call x1, Pallas kernels, near_call(): pl.pallas_call(near_kernel, out_shape=(shape(dims, F32), shape(dims, BF16...  1.82 us
  transfers between devices with their start and end apart: 11, of which 4 were waited for; matrix products, arithmetic and copies ran while one was open for 0% of the time, Pallas kernels for 34%

profile of v10, /device:TPU:0, one launch (start us, length us, event | category | flops | bytes accessed | tf_op | source)
XLA Modules:
  0.0 58.4 jit_solution(8301082672374144007)
XLA Ops:
  0.0 0.5 collective-permute-start.5
  0.5 2.5 %collective-permute-start = (s32[1,32]{1,0:T(1,128)}, s32[1,32]{1,0:T(1,128)S(1)}, u32[]{:S(2)}, u32[]{:S(2)}) collective-permute-start(s32[1,32]{1,0:T(1,128)} %bitcast.65), channel_id=1, source_target_pairs={{0,2},{2,0},{4,6},{6,4},{8,10},{10,8},{12,14},{14,12},{1,3},{3,1},... | collective-permute-start | bytes 392 | tf_op jit(solution)/shard_map/ppermute | solution.py:563
  2.9 0.1 stack.31.me
  3.0 0.0 copy-start.5
  3.0 0.0 copy-start.6
  3.0 0.0 copy-start.10
  3.0 3.1 %own_rows.2.refs_0_ = f32[65536,128]{1,0:T(8,128)S(1)} custom-call(s32[5]{0:T(128)S(1)} %stack.31.me, bf16[96,32768]{1,0:T(8,128)(2,1)} %features.3), custom_call_target="tpu_custom_call" | custom-call | tf_op jit(solution)/shard_map/own_rows/pallas_call | solution.py:433
  6.2 0.0 copy-done.5
  6.2 0.0 copy-done.6
  6.2 0.0 collective-permute-done.refs_1_.got_1
  6.2 0.4 collective-permute-start.4
  6.6 0.0 copy-done.10
  6.6 0.0 copy-start.1
  6.6 0.0 copy-start.7
  6.6 0.0 copy-start.8
  6.6 2.8 %collective-permute-start.1 = (s32[2,32]{1,0:T(2,128)S(1)}, s32[2,32]{1,0:T(2,128)S(1)}, u32[]{:S(2)}, u32[]{:S(2)}) collective-permute-start(s32[2,32]{1,0:T(2,128)S(1)} %join.3), channel_id=1, source_target_pairs={{0,8},{2,10},{4,12},{6,14},{8,0},{10,2},{12,4},{14,6},{1,9},{3,11}... | collective-permute-start | bytes 776 | tf_op jit(solution)/shard_map/ppermute | solution.py:563
  9.5 1.3 %collective-permute-start.2 = (s32[2,32]{1,0:T(2,128)S(1)}, s32[2,32]{1,0:T(2,128)S(1)}, u32[]{:S(2)}, u32[]{:S(2)}) collective-permute-start(s32[2,32]{1,0:T(2,128)S(1)} %join.3), channel_id=1, source_target_pairs={{0,12},{2,14},{4,8},{6,10},{8,4},{10,6},{12,0},{14,2},{1,13},{3,15... | collective-permute-start | bytes 776 | tf_op jit(solution)/shard_map/ppermute | solution.py:563
  10.8 0.2 collective-permute-start.3
  11.1 3.1 %own_rows.3.table_in = f32[65536,128]{1,0:T(8,128)S(1)} custom-call(s32[5]{0:T(128)S(1)} %stack.31.me, bf16[96,32768]{1,0:T(8,128)(2,1)} %features.3, f32[65536,128]{1,0:T(8,128)S(1)} %own_rows.2.refs_0_), custom_call_target="tpu_custom_call", output_to_operand_aliasing={{}: (2, {})} | custom-call | tf_op jit(solution)/shard_map/own_rows/pallas_call | solution.py:433
  14.2 0.0 collective-permute-done.1.got_4
  14.2 0.7 %collective-permute-done.2.got_6 = s32[2,32]{1,0:T(2,128)S(1)} collective-permute-done((s32[2,32]{1,0:T(2,128)S(1)}, s32[2,32]{1,0:T(2,128)S(1)}, u32[]{:S(2)}, u32[]{:S(2)}) %collective-permute-start.2) | collective-permute-done | bytes 288 | tf_op jit(solution)/shard_map/ppermute | solution.py:563
  14.8 0.0 collective-permute-done.3.got_2
  14.9 0.0 collective-permute-done.4.weights_got
  14.9 0.0 copy-done.1
  14.9 0.0 copy-done.7
  14.9 0.0 copy-done.8
  14.9 2.7 %order.1 = (s32[2,18,16,128]{3,2,1,0:T(8,128)S(1)}, s32[1]{0:T(128)}) custom-call(s32[5]{0:T(128)S(1)} %stack.31.me, s32[1,32]{1,0:T(1,128)S(1)} %bitcast.67, s32[1,32]{1,0:T(1,128)S(1)} %collective-permute-done.refs_1_.got_1, s32[2,32]{1,0:T(2,128)S(1)} %collective-permute-done.3.got_2, s32[2,32]{1,0:T(2,128)S(1)} %collective-permute-done.1.got_4, ...), custom_call_target="tpu_custom_call" | custom-call | tf_op jit(solution)/shard_map/order/pallas_call | solution.py:409
  17.6 0.0 collective-permute-done.5.other
  17.6 12.3 %first_half.1 = (f32[65536,128]{1,0:T(8,128)S(1)}, bf16[3,272,128]{2,1,0:T(8,128)(2,1)}, bf16[3,272,128]{2,1,0:T(8,128)(2,1)}) custom-call(s32[5]{0:T(128)S(1)} %stack.31.me, s32[73728]{0:T(1024)S(1)} %bitcast.55, f32[65536,128]{1,0:T(8,128)S(1)} %own_rows.3.table_in, bf16[96,32768]{1,0:T(8,128)(2,1)} %collective-permute-done.5.other), custom_call_target="tpu_custom_call", output_to_operand_aliasing={{0}: (2, {})} | custom-call | tf_op jit(solution)/shard_map/first_half/pallas_call | solution.py:463
  30.0 1.6 %collective-permute-start.6 = (bf16[3,272,128]{2,1,0:T(8,128)(2,1)}, bf16[3,272,128]{2,1,0:T(8,128)(2,1)S(1)}, u32[]{:S(2)}, u32[]{:S(2)}) collective-permute-start(bf16[3,272,128]{2,1,0:T(8,128)(2,1)} %get-tuple-element.85), channel_id=1, source_target_pairs={{0,2},{2,0},{4,6},{6,4},{8,10},{10,8},{12,14},{14,12},{1,3},{3,1},... | collective-permute-start | bytes 626696 | tf_op jit(solution)/shard_map/ppermute | solution.py:563
  31.5 0.0 copy-start
  31.5 0.0 copy-start.2
  31.5 0.0 copy-start.3
  31.5 0.0 copy-start.4
  31.5 0.0 copy-start.11
  31.5 0.0 copy-start.12
  31.6 0.0 copy-start.13
  31.6 8.9 %second_half.1 = (bf16[3,272,128]{2,1,0:T(8,128)(2,1)}, bf16[3,272,128]{2,1,0:T(8,128)(2,1)}) custom-call(s32[5]{0:T(128)S(1)} %stack.31.me, s32[73728]{0:T(1024)S(1)} %bitcast.56, f32[65536,128]{1,0:T(8,128)S(1)} %get-tuple-element.82.table), custom_call_target="tpu_custom_call" | custom-call | tf_op jit(solution)/shard_map/second_half/pallas_call | solution.py:485
  40.5 0.0 collective-permute-done.6.got
  40.5 0.0 copy-done
  40.5 1.0 %project_far.1 = (bf16[272,256]{1,0:T(8,128)(2,1)S(1)}, bf16[272,256]{1,0:T(8,128)(2,1)S(1)}) custom-call(s32[5]{0:T(128)S(1)} %stack.31.me, bf16[3,272,128]{2,1,0:T(8,128)(2,1)S(1)} %copy-done, bf16[3,272,128]{2,1,0:T(8,128)(2,1)S(1)} %collective-permute-done.6.got, bf16[192,256]{1,0:T(8,128)(2,1)S(1)} %join.2.weights, ...), custom_call_target="tpu_custom_call" | custom-call | tf_op jit(solution)/shard_map/project_far/pallas_call | solution.py:500
  41.6 0.6 %collective-permute-start.7 = (bf16[3,272,128]{2,1,0:T(8,128)(2,1)}, bf16[3,272,128]{2,1,0:T(8,128)(2,1)S(1)}, u32[]{:S(2)}, u32[]{:S(2)}) collective-permute-start(bf16[3,272,128]{2,1,0:T(8,128)(2,1)} %get-tuple-element.90), channel_id=1, source_target_pairs={{0,2},{2,0},{4,6},{6,4},{8,10},{10,8},{12,14},{14,12},{1,3},{3,1},... | collective-permute-start | bytes 626696 | tf_op jit(solution)/shard_map/ppermute | solution.py:563
  42.2 2.2 %collective-permute-start.8 = (bf16[272,256]{1,0:T(8,128)(2,1)S(1)}, bf16[272,256]{1,0:T(8,128)(2,1)S(1)}, u32[]{:S(2)}, u32[]{:S(2)}) collective-permute-start(bf16[272,256]{1,0:T(8,128)(2,1)S(1)} %get-tuple-element.92), channel_id=1, source_target_pairs={{0,8},{2,10},{4,12},{6,14},{8,0},{10,2},{12,4},{14,6},{1,9},{3,11}... | collective-permute-start | bytes 417800 | tf_op jit(solution)/shard_map/ppermute | solution.py:563
  44.3 1.3 %collective-permute-start.9 = (bf16[272,256]{1,0:T(8,128)(2,1)S(1)}, bf16[272,256]{1,0:T(8,128)(2,1)S(1)}, u32[]{:S(2)}, u32[]{:S(2)}) collective-permute-start(bf16[272,256]{1,0:T(8,128)(2,1)S(1)} %get-tuple-element.93), channel_id=1, source_target_pairs={{0,12},{2,14},{4,8},{6,10},{8,4},{10,6},{12,0},{14,2},{1,13},{3,15... | collective-permute-start | bytes 417800 | tf_op jit(solution)/shard_map/ppermute | solution.py:563
  45.7 2.7 %collective-permute-done.7.got = bf16[3,272,128]{2,1,0:T(8,128)(2,1)S(1)} collective-permute-done((bf16[3,272,128]{2,1,0:T(8,128)(2,1)}, bf16[3,272,128]{2,1,0:T(8,128)(2,1)S(1)}, u32[]{:S(2)}, u32[]{:S(2)}) %collective-permute-start.7) | collective-permute-done | bytes 208928 | tf_op jit(solution)/shard_map/ppermute | solution.py:563
  48.4 1.8 %project_near.1 = (f32[272,256]{1,0:T(8,128)S(1)}, bf16[272,256]{1,0:T(8,128)(2,1)S(1)}) custom-call(s32[5]{0:T(128)S(1)} %stack.31.me, bf16[3,272,128]{2,1,0:T(8,128)(2,1)} %get-tuple-element.83.keep_hbm, bf16[3,272,128]{2,1,0:T(8,128)(2,1)S(1)} %collective-permute-done.7.got, bf16[192,256]{1,0:T(8,128)(2,1)S(1)} %join.2.weights, ...), custom_call_target="tpu_custom_call" | custom-call | tf_op jit(solution)/shard_map/project_near/pallas_call | solution.py:512
  50.2 1.6 %collective-permute-start.10 = (bf16[272,256]{1,0:T(8,128)(2,1)S(1)}, bf16[272,256]{1,0:T(8,128)(2,1)S(1)}, u32[]{:S(2)}, u32[]{:S(2)}) collective-permute-start(bf16[272,256]{1,0:T(8,128)(2,1)S(1)} %get-tuple-element.94), channel_id=1, source_target_pairs={{0,4},{2,6},{4,0},{6,2},{8,12},{10,14},{12,8},{14,10},{1,5},{3,7},... | collective-permute-start | bytes 417800 | tf_op jit(solution)/shard_map/ppermute | solution.py:563
  52.5 2.5 %collective-permute-done.8.a = bf16[272,256]{1,0:T(8,128)(2,1)S(1)} collective-permute-done((bf16[272,256]{1,0:T(8,128)(2,1)S(1)}, bf16[272,256]{1,0:T(8,128)(2,1)S(1)}, u32[]{:S(2)}, u32[]{:S(2)}) %collective-permute-start.8) | collective-permute-done | bytes 139296 | tf_op jit(solution)/shard_map/ppermute | solution.py:563
  55.0 0.0 collective-permute-done.9.b
  55.0 1.8 %collective-permute-done.10.c = bf16[272,256]{1,0:T(8,128)(2,1)S(1)} collective-permute-done((bf16[272,256]{1,0:T(8,128)(2,1)S(1)}, bf16[272,256]{1,0:T(8,128)(2,1)S(1)}, u32[]{:S(2)}, u32[]{:S(2)}) %collective-permute-start.10) | collective-permute-done | bytes 139296 | tf_op jit(solution)/shard_map/ppermute | solution.py:563
  56.8 0.0 copy-done.2
  56.8 0.0 copy-done.3
  56.8 0.0 copy-done.4
  56.8 0.0 copy-done.11
  56.9 0.0 copy-done.12
  56.9 0.0 copy-done.13
  56.9 0.7 %layer_two.1 = f32[32,153]{1,0:T(8,128)S(1)} custom-call(f32[272,256]{1,0:T(8,128)S(1)} %get-tuple-element.91.mine, bf16[272,256]{1,0:T(8,128)(2,1)S(1)} %collective-permute-done.8.a, bf16[272,256]{1,0:T(8,128)(2,1)S(1)} %collective-permute-done.9.b, bf16[272,256]{1,0:T(8,128)(2,1)S(1)} %collective-permute-done.10.c, s32[1,32]{1,0:T(1,128)S(1)} %bitcast.68, ...), custom_call_target="tpu_custom_call" | custom-call | tf_op jit(solution)/shard_map/layer_two/pallas_call | solution.py:526
  57.6 0.1 conditional.1
  57.7 0.0 copy-start.9
  57.8 0.6 %copy-done.9 = f32[32,153]{1,0:T(8,128)} copy-done((f32[32,153]{1,0:T(8,128)}, f32[32,153]{1,0:T(8,128)S(1)}, u32[]{:S(2)}) %copy-start.9) | copy-done | bytes 19608
  (2 shorter events, 0.0 us)
Async XLA Ops:
  0.0 17.6 %collective-permute-start.5 = (bf16[96,32768]{1,0:T(8,128)(2,1)}, bf16[96,32768]{1,0:T(8,128)(2,1)}, u32[]{:S(2)}, u32[]{:S(2)}) collective-permute-start(bf16[96,32768]{1,0:T(8,128)(2,1)} %features.3), channel_id=1, source_target_pairs={{0,1},{1,0},{2,3},{3,2},{4,5},{5,4},{6,7},{7,6},{8,9},{9,8},{10,11... | collective-permute-start | bytes 18874376 | tf_op jit(solution)/shard_map/ppermute | solution.py:565
  0.5 5.7 %collective-permute-start = (s32[1,32]{1,0:T(1,128)}, s32[1,32]{1,0:T(1,128)S(1)}, u32[]{:S(2)}, u32[]{:S(2)}) collective-permute-start(s32[1,32]{1,0:T(1,128)} %bitcast.65), channel_id=1, source_target_pairs={{0,2},{2,0},{4,6},{6,4},{8,10},{10,8},{12,14},{14,12},{1,3},{3,1},... | collective-permute-start | bytes 392 | tf_op jit(solution)/shard_map/ppermute | solution.py:563
  3.0 3.1 %copy-start.5 = (bf16[96,256]{1,0:T(8,128)(2,1)S(1)}, bf16[96,256]{1,0:T(8,128)(2,1)}, u32[]{:S(2)}) copy-start(bf16[96,256]{1,0:T(8,128)(2,1)} %refs_0_.1) | copy-start | bytes 147460
  3.0 3.1 %copy-start.6 = (bf16[96,256]{1,0:T(8,128)(2,1)S(1)}, bf16[96,256]{1,0:T(8,128)(2,1)}, u32[]{:S(2)}) copy-start(bf16[96,256]{1,0:T(8,128)(2,1)} %refs_1_.1) | copy-start | bytes 147460
  3.0 3.6 %copy-start.10 = (s32[32]{0:T(128)S(1)}, s32[32]{0:T(128)}, u32[]{:S(2)}) copy-start(s32[32]{0:T(128)} %param.19) | copy-start | bytes 388
  6.2 8.7 %collective-permute-start.4 = (bf16[192,256]{1,0:T(8,128)(2,1)S(1)}, bf16[192,256]{1,0:T(8,128)(2,1)S(1)}, u32[]{:S(2)}, u32[]{:S(2)}) collective-permute-start(bf16[192,256]{1,0:T(8,128)(2,1)S(1)} %join.2.weights), channel_id=1, source_target_pairs={{0,2},{2,0},{4,6},{6,4},{8,10},{10,8},{12,14},{14,12},{1,3},{3,1},... | collective-permute-start | bytes 294920 | tf_op jit(solution)/shard_map/ppermute | solution.py:563
  6.6 8.2 %copy-start.1 = (s32[15,2816]{1,0:T(8,128)S(1)}, s32[15,2816]{1,0:T(8,128)}, u32[]{:S(2)}) copy-start(s32[15,2816]{1,0:T(8,128)} %neighbour_ids.1) | copy-start | bytes 506884
  6.6 8.2 %copy-start.7 = (s32[2816]{0:T(1024)S(1)}, s32[2816]{0:T(1024)}, u32[]{:S(2)}) copy-start(s32[2816]{0:T(1024)} %count_one.1) | copy-start | bytes 33796
  6.6 8.2 %copy-start.8 = (s32[2816]{0:T(1024)S(1)}, s32[2816]{0:T(1024)}, u32[]{:S(2)}) copy-start(s32[2816]{0:T(1024)} %self_ids.1) | copy-start | bytes 33796
  6.6 7.5 %collective-permute-start.1 = (s32[2,32]{1,0:T(2,128)S(1)}, s32[2,32]{1,0:T(2,128)S(1)}, u32[]{:S(2)}, u32[]{:S(2)}) collective-permute-start(s32[2,32]{1,0:T(2,128)S(1)} %join.3), channel_id=1, source_target_pairs={{0,8},{2,10},{4,12},{6,14},{8,0},{10,2},{12,4},{14,6},{1,9},{3,11}... | collective-permute-start | bytes 776 | tf_op jit(solution)/shard_map/ppermute | solution.py:563
  9.5 5.4 %collective-permute-start.2 = (s32[2,32]{1,0:T(2,128)S(1)}, s32[2,32]{1,0:T(2,128)S(1)}, u32[]{:S(2)}, u32[]{:S(2)}) collective-permute-start(s32[2,32]{1,0:T(2,128)S(1)} %join.3), channel_id=1, source_target_pairs={{0,12},{2,14},{4,8},{6,10},{8,4},{10,6},{12,0},{14,2},{1,13},{3,15... | collective-permute-start | bytes 776 | tf_op jit(solution)/shard_map/ppermute | solution.py:563
  10.8 4.0 %collective-permute-start.3 = (s32[2,32]{1,0:T(2,128)S(1)}, s32[2,32]{1,0:T(2,128)S(1)}, u32[]{:S(2)}, u32[]{:S(2)}) collective-permute-start(s32[2,32]{1,0:T(2,128)S(1)} %join.3), channel_id=1, source_target_pairs={{0,4},{2,6},{4,0},{6,2},{8,12},{10,14},{12,8},{14,10},{1,5},{3,7},... | collective-permute-start | bytes 776 | tf_op jit(solution)/shard_map/ppermute | solution.py:563
  30.0 10.6 %collective-permute-start.6 = (bf16[3,272,128]{2,1,0:T(8,128)(2,1)}, bf16[3,272,128]{2,1,0:T(8,128)(2,1)S(1)}, u32[]{:S(2)}, u32[]{:S(2)}) collective-permute-start(bf16[3,272,128]{2,1,0:T(8,128)(2,1)} %get-tuple-element.85), channel_id=1, source_target_pairs={{0,2},{2,0},{4,6},{6,4},{8,10},{10,8},{12,14},{14,12},{1,3},{3,1},... | collective-permute-start | bytes 626696 | tf_op jit(solution)/shard_map/ppermute | solution.py:563
  31.5 9.0 %copy-start = (bf16[3,272,128]{2,1,0:T(8,128)(2,1)S(1)}, bf16[3,272,128]{2,1,0:T(8,128)(2,1)}, u32[]{:S(2)}) copy-start(bf16[3,272,128]{2,1,0:T(8,128)(2,1)} %get-tuple-element.84.keep) | copy-start | bytes 626692
  31.5 25.3 %copy-start.2 = (bf16[256,256]{1,0:T(8,128)(2,1)S(1)}, bf16[256,256]{1,0:T(8,128)(2,1)}, u32[]{:S(2)}) copy-start(bf16[256,256]{1,0:T(8,128)(2,1)} %neigh_two.1) | copy-start | bytes 393220
  31.5 25.3 %copy-start.3 = (bf16[256,256]{1,0:T(8,128)(2,1)S(1)}, bf16[256,256]{1,0:T(8,128)(2,1)}, u32[]{:S(2)}) copy-start(bf16[256,256]{1,0:T(8,128)(2,1)} %self_two.1) | copy-start | bytes 393220
  31.5 25.3 %copy-start.4 = (bf16[256,153]{0,1:T(8,128)(2,1)S(1)}, bf16[256,153]{0,1:T(8,128)(2,1)}, u32[]{:S(2)}) copy-start(bf16[256,153]{0,1:T(8,128)(2,1)} %param.26) | copy-start | bytes 235012
  31.5 25.3 %copy-start.11 = (f32[256]{0:T(256)S(1)}, f32[256]{0:T(256)}, u32[]{:S(2)}) copy-start(f32[256]{0:T(256)} %param.25) | copy-start | bytes 3076
  31.5 25.3 %copy-start.12 = (f32[153]{0:T(256)S(1)}, f32[153]{0:T(256)}, u32[]{:S(2)}) copy-start(f32[153]{0:T(256)} %param.27) | copy-start | bytes 1840
  31.6 25.3 %copy-start.13 = (f32[256]{0:T(256)S(1)}, f32[256]{0:T(256)}, u32[]{:S(2)}) copy-start(f32[256]{0:T(256)} %param.22) | copy-start | bytes 3076
  41.6 6.9 %collective-permute-start.7 = (bf16[3,272,128]{2,1,0:T(8,128)(2,1)}, bf16[3,272,128]{2,1,0:T(8,128)(2,1)S(1)}, u32[]{:S(2)}, u32[]{:S(2)}) collective-permute-start(bf16[3,272,128]{2,1,0:T(8,128)(2,1)} %get-tuple-element.90), channel_id=1, source_target_pairs={{0,2},{2,0},{4,6},{6,4},{8,10},{10,8},{12,14},{14,12},{1,3},{3,1},... | collective-permute-start | bytes 626696 | tf_op jit(solution)/shard_map/ppermute | solution.py:563
  42.2 12.8 %collective-permute-start.8 = (bf16[272,256]{1,0:T(8,128)(2,1)S(1)}, bf16[272,256]{1,0:T(8,128)(2,1)S(1)}, u32[]{:S(2)}, u32[]{:S(2)}) collective-permute-start(bf16[272,256]{1,0:T(8,128)(2,1)S(1)} %get-tuple-element.92), channel_id=1, source_target_pairs={{0,8},{2,10},{4,12},{6,14},{8,0},{10,2},{12,4},{14,6},{1,9},{3,11}... | collective-permute-start | bytes 417800 | tf_op jit(solution)/shard_map/ppermute | solution.py:563
  44.3 10.6 %collective-permute-start.9 = (bf16[272,256]{1,0:T(8,128)(2,1)S(1)}, bf16[272,256]{1,0:T(8,128)(2,1)S(1)}, u32[]{:S(2)}, u32[]{:S(2)}) collective-permute-start(bf16[272,256]{1,0:T(8,128)(2,1)S(1)} %get-tuple-element.93), channel_id=1, source_target_pairs={{0,12},{2,14},{4,8},{6,10},{8,4},{10,6},{12,0},{14,2},{1,13},{3,15... | collective-permute-start | bytes 417800 | tf_op jit(solution)/shard_map/ppermute | solution.py:563
  50.2 6.6 %collective-permute-start.10 = (bf16[272,256]{1,0:T(8,128)(2,1)S(1)}, bf16[272,256]{1,0:T(8,128)(2,1)S(1)}, u32[]{:S(2)}, u32[]{:S(2)}) collective-permute-start(bf16[272,256]{1,0:T(8,128)(2,1)S(1)} %get-tuple-element.94), channel_id=1, source_target_pairs={{0,4},{2,6},{4,0},{6,2},{8,12},{10,14},{12,8},{14,10},{1,5},{3,7},... | collective-permute-start | bytes 417800 | tf_op jit(solution)/shard_map/ppermute | solution.py:563
  57.7 0.6 %copy-start.9 = (f32[32,153]{1,0:T(8,128)}, f32[32,153]{1,0:T(8,128)S(1)}, u32[]{:S(2)}) copy-start(f32[32,153]{1,0:T(8,128)S(1)} %get-tuple-element.177) | copy-start | bytes 58756

commit v11 on v10

--- a/solution.py
+++ b/solution.py
@@ -244,21 +244,20 @@
         lax.fori_loop(0, jnp.right_shift(end - begin, UNROLL.bit_length() - 1), body, 0)
 
 
-def write_out(x, width, self_rows, mean_rows, keep, send):
+def lay_out(ref, side, width, self_rows, mean_rows):
     lane = iota((CAP, LANES), 1)
     rest = 2 * width - LANES
-    for ref, side in ((keep, x), (send, 1 - x)):
-        turned = []
-        for z in range(2):
-            at = pl.multiple_of((z * 2 + side) * CAP, CAP)
-            mean = jnp.where(lane < width, mean_rows[pl.ds(at, CAP), :], 0.0)
-            turned.append(pltpu.roll(mean, width, 1))
-            own = self_rows[pl.ds(at, CAP), :]
-            ref[z, :, :] = jnp.where(lane < width, own, turned[z]).astype(BF16)
-        right = pltpu.roll(turned[1], LANES // 2, 1)
-        block = jnp.where(lane < LANES // 2, turned[0], right)
-        used = (lane < rest) | ((lane >= LANES // 2) & (lane < LANES // 2 + rest))
-        ref[2, :, :] = jnp.where(used, block, 0.0).astype(BF16)
+    turned = []
+    for z in range(2):
+        at = pl.multiple_of((z * 2 + side) * CAP, CAP)
+        mean = jnp.where(lane < width, mean_rows[pl.ds(at, CAP), :], 0.0)
+        turned.append(pltpu.roll(mean, width, 1))
+        own = self_rows[pl.ds(at, CAP), :]
+        ref[z, :, :] = jnp.where(lane < width, own, turned[z]).astype(BF16)
+    right = pltpu.roll(turned[1], LANES // 2, 1)
+    block = jnp.where(lane < LANES // 2, turned[0], right)
+    used = (lane < rest) | ((lane >= LANES // 2) & (lane < LANES // 2 + rest))
+    ref[2, :, :] = jnp.where(used, block, 0.0).astype(BF16)
 
 
 def stage(source, staged, sems):
@@ -294,12 +293,12 @@
         at += part.shape[0]
 
 
-def hand_out(keep, send, keep_hbm, send_hbm, sems):
-    copies = [
-        pltpu.make_async_copy(send, send_hbm, sems.at[0]),
-        pltpu.make_async_copy(keep, keep_hbm, sems.at[1]),
-    ]
-    start_all(copies)
+def hand_out(x, width, self_rows, mean_rows, keep, send, keep_hbm, send_hbm, sems):
+    copies = []
+    for i, (ref, out, side) in enumerate(((send, send_hbm, 1 - x), (keep, keep_hbm, x))):
+        lay_out(ref, side, width, self_rows, mean_rows)
+        copies.append(pltpu.make_async_copy(ref, out, sems.at[i]))
+        copies[-1].start()
     for copy in copies:
         copy.wait()
 
@@ -319,8 +318,7 @@
     mean_rows[...] = jnp.zeros_like(mean_rows)
     turn_staged(staging, staged, table, (1 - rep) * length)
     look_up(fanout, copies, table, ids, places, begins, self_rows, mean_rows)
-    write_out(x, width, self_rows, mean_rows, keep, send)
-    hand_out(keep, send, keep_hbm, send_hbm, out_sems)
+    hand_out(x, width, self_rows, mean_rows, keep, send, keep_hbm, send_hbm, out_sems)
 
 
 def second_kernel(fanout, width, me, lists, table, keep_hbm, send_hbm, *scratch):
@@ -331,8 +329,7 @@
     self_rows[...] = jnp.zeros_like(self_rows)
     mean_rows[...] = jnp.zeros_like(mean_rows)
     look_up(fanout, copies, table, ids, places, begins, self_rows, mean_rows)
-    write_out(x, width, self_rows, mean_rows, keep, send)
-    hand_out(keep, send, keep_hbm, send_hbm, out_sems)
+    hand_out(x, width, self_rows, mean_rows, keep, send, keep_hbm, send_hbm, out_sems)
 
 
 def partials(blocks, weights):
@@ -348,19 +345,19 @@
     ]
 
 
-def far_kernel(me, keep, got, weights, weights_got, out_0, out_1):
+def far_kernel(me, keep, got, weights, weights_got, later, out_0, out_1, loaded, sem):
+    copy = pltpu.make_async_copy(later, loaded, sem)
+    copy.start()
     zl = me[3]
     pre = [a + b for a, b in zip(partials(keep, weights), partials(got, weights_got))]
     out_0[...] = jnp.where(zl == 0, pre[0], pre[1]).astype(BF16)
     out_1[...] = jnp.where(zl == 0, pre[1], pre[0]).astype(BF16)
-
-
-def near_kernel(me, keep_hbm, got, weights, weights_got, out_0, out_1, keep, sem):
-    copy = pltpu.make_async_copy(keep_hbm, keep, sem)
-    copy.start()
+    copy.wait()
+
+
+def near_kernel(me, keep, got, weights, weights_got, out_0, out_1):
     zl = me[3]
     theirs = partials(got, weights_got)
-    copy.wait()
     pre = [a + b for a, b in zip(partials(keep, weights), theirs)]
     out_0[...] = jnp.where(zl == 0, pre[0], pre[1])
     out_1[...] = jnp.where(zl == 0, pre[1], pre[0]).astype(BF16)
@@ -495,16 +492,17 @@
     )(me, lists, table)
 
 
-def far_call(me, keep, got, weights, weights_got):
+def far_call(me, keep, got, weights, weights_got, later):
     part = shape((CAP, weights.shape[1]), BF16)
     return pl.pallas_call(
         far_kernel,
-        out_shape=(part, part),
-        in_specs=[SMEM] + [VMEM] * 4,
-        out_specs=(VMEM, VMEM),
+        out_shape=(part, part, shape(later.shape, BF16)),
+        in_specs=[SMEM] + [VMEM] * 4 + [HBM],
+        out_specs=(VMEM, VMEM, VMEM),
+        scratch_shapes=[pltpu.SemaphoreType.DMA],
         compiler_params=params(10),
         name="project_far",
-    )(me, keep, got, weights, weights_got)
+    )(me, keep, got, weights, weights_got, pltpu.with_memory_space_constraint(later, pltpu.HBM))
 
 
 def near_call(me, keep, got, weights, weights_got):
@@ -512,12 +510,11 @@
     return pl.pallas_call(
         near_kernel,
         out_shape=(shape(dims, F32), shape(dims, BF16)),
-        in_specs=[SMEM, HBM] + [VMEM] * 3,
+        in_specs=[SMEM] + [VMEM] * 4,
         out_specs=(VMEM, VMEM),
-        scratch_shapes=[pltpu.VMEM(keep.shape, BF16), pltpu.SemaphoreType.DMA],
         compiler_params=params(10),
         name="project_near",
-    )(me, pltpu.with_memory_space_constraint(keep, pltpu.HBM), got, weights, weights_got)
+    )(me, keep, got, weights, weights_got)
 
 
 def last_call(*args):
@@ -581,7 +578,7 @@
     table, keep_far, send_far = first_call(fanout, me, lists, table, other)
     got_far = across(send_far, 1)
     keep_near, send_near = second_call(fanout, width, me, lists, table)
-    far = far_call(me, keep_far, got_far, weights, weights_got)
+    *far, keep_near = far_call(me, keep_far, got_far, weights, weights_got, keep_near)
     far, send_near = lax.optimization_barrier((far, send_near))
     far_got = [across(far[0], 4), across(far[1], 6)]
     got_near = across(send_near, 1)

time: 58 us -> 57.5 us (level)
  waiting for transfers between devices: 7.73 us -> 7.13 us
    pallas_call x1, Pallas kernels: 1.82 us -> 1.01 us  [near_call(): pl.pallas_call(near_kernel, out_shape=(shape(dims, F32), shape(dims, BF16...]
    ppermute x10, waiting for transfers between devices: 7.72 us -> 7.13 us  [across(): return lax.ppermute(value, 'col', [(i, i ^ bit) for i in range(owners)])]
  transfers between devices with their start and end apart: 11 -> 11, of which waited for: 4 -> 4; matrix products, arithmetic and copies ran while one was open for 0% -> 0% of each run, Pallas kernels for 34% -> 32%
where the time goes in v11:
time: 57.5 us; the launch traced here: 57.4 us
  Pallas kernels  33.5 us (58%)
  starting transfers between devices  15 us (26%)
  waiting for transfers between devices  7.13 us (12%)
  between operations  0.89 us (2%)
  local copies, waits for them, and re-layouts  0.75 us (1%)
    ppermute x10, starting transfers between devices, across(): return lax.ppermute(value, 'col', [(i, i ^ bit) for i in range(owners)])  14.5 us
    pallas_call x1, Pallas kernels, first_call(): pl.pallas_call(functools.partial(first_kernel, fanout), out_shape=(shape(...  12.7 us
    pallas_call x1, Pallas kernels, second_call(): pl.pallas_call(functools.partial(second_kernel, fanout, width), out_shape...  8.61 us
    ppermute x10, waiting for transfers between devices, across(): return lax.ppermute(value, 'col', [(i, i ^ bit) for i in range(owners)])  7.13 us
    pallas_call x2, Pallas kernels, own_call(): pl.pallas_call(functools.partial(own_kernel, which, halves), out_shape=sh...  6.22 us
    pallas_call x1, Pallas kernels, order_call(): pl.pallas_call(functools.partial(order_kernel, per_seed), out_shape=(shap...  2.73 us
    pallas_call x1, Pallas kernels, far_call(): pl.pallas_call(far_kernel, out_shape=(part, part, shape(later.shape, BF16...  1.48 us
  transfers between devices with their start and end apart: 11, of which 4 were waited for; matrix products, arithmetic and copies ran while one was open for 0% of the time, Pallas kernels for 32%

profile of v11, /device:TPU:0, one launch (start us, length us, event | category | flops | bytes accessed | tf_op | source)
XLA Modules:
  0.0 57.4 jit_solution(5163002597639521869)
XLA Ops:
  0.0 0.5 collective-permute-start.5
  0.5 2.5 %collective-permute-start = (s32[1,32]{1,0:T(1,128)}, s32[1,32]{1,0:T(1,128)S(1)}, u32[]{:S(2)}, u32[]{:S(2)}) collective-permute-start(s32[1,32]{1,0:T(1,128)} %bitcast.65), channel_id=1, source_target_pairs={{0,2},{2,0},{4,6},{6,4},{8,10},{10,8},{12,14},{14,12},{1,3},{3,1},... | collective-permute-start | bytes 392 | tf_op jit(solution)/shard_map/ppermute | solution.py:560
  2.9 0.1 stack.31.me
  3.0 0.0 copy-start.5
  3.0 0.0 copy-start.6
  3.0 0.0 copy-start.10
  3.0 3.1 %own_rows.2.refs_0_ = f32[65536,128]{1,0:T(8,128)S(1)} custom-call(s32[5]{0:T(128)S(1)} %stack.31.me, bf16[96,32768]{1,0:T(8,128)(2,1)} %features.3), custom_call_target="tpu_custom_call" | custom-call | tf_op jit(solution)/shard_map/own_rows/pallas_call | solution.py:430
  6.2 0.0 copy-done.5
  6.2 0.0 copy-done.6
  6.2 0.0 collective-permute-done.refs_1_.got_1
  6.2 0.4 collective-permute-start.4
  6.6 0.0 copy-done.10
  6.6 0.0 copy-start.1
  6.6 0.0 copy-start.7
  6.6 0.0 copy-start.8
  6.6 2.8 %collective-permute-start.1 = (s32[2,32]{1,0:T(2,128)S(1)}, s32[2,32]{1,0:T(2,128)S(1)}, u32[]{:S(2)}, u32[]{:S(2)}) collective-permute-start(s32[2,32]{1,0:T(2,128)S(1)} %join.3), channel_id=1, source_target_pairs={{0,8},{2,10},{4,12},{6,14},{8,0},{10,2},{12,4},{14,6},{1,9},{3,11}... | collective-permute-start | bytes 776 | tf_op jit(solution)/shard_map/ppermute | solution.py:560
  9.5 1.3 %collective-permute-start.2 = (s32[2,32]{1,0:T(2,128)S(1)}, s32[2,32]{1,0:T(2,128)S(1)}, u32[]{:S(2)}, u32[]{:S(2)}) collective-permute-start(s32[2,32]{1,0:T(2,128)S(1)} %join.3), channel_id=1, source_target_pairs={{0,12},{2,14},{4,8},{6,10},{8,4},{10,6},{12,0},{14,2},{1,13},{3,15... | collective-permute-start | bytes 776 | tf_op jit(solution)/shard_map/ppermute | solution.py:560
  10.8 0.2 collective-permute-start.3
  11.1 3.1 %own_rows.3.table_in = f32[65536,128]{1,0:T(8,128)S(1)} custom-call(s32[5]{0:T(128)S(1)} %stack.31.me, bf16[96,32768]{1,0:T(8,128)(2,1)} %features.3, f32[65536,128]{1,0:T(8,128)S(1)} %own_rows.2.refs_0_), custom_call_target="tpu_custom_call", output_to_operand_aliasing={{}: (2, {})} | custom-call | tf_op jit(solution)/shard_map/own_rows/pallas_call | solution.py:430
  14.2 0.0 collective-permute-done.1.got_4
  14.2 0.7 %collective-permute-done.2.got_6 = s32[2,32]{1,0:T(2,128)S(1)} collective-permute-done((s32[2,32]{1,0:T(2,128)S(1)}, s32[2,32]{1,0:T(2,128)S(1)}, u32[]{:S(2)}, u32[]{:S(2)}) %collective-permute-start.2) | collective-permute-done | bytes 288 | tf_op jit(solution)/shard_map/ppermute | solution.py:560
  14.8 0.0 collective-permute-done.3.got_2
  14.9 0.0 collective-permute-done.4.weights_got
  14.9 0.0 copy-done.1
  14.9 0.0 copy-done.7
  14.9 0.0 copy-done.8
  14.9 2.7 %order.1 = (s32[2,18,16,128]{3,2,1,0:T(8,128)S(1)}, s32[1]{0:T(128)}) custom-call(s32[5]{0:T(128)S(1)} %stack.31.me, s32[1,32]{1,0:T(1,128)S(1)} %bitcast.67, s32[1,32]{1,0:T(1,128)S(1)} %collective-permute-done.refs_1_.got_1, s32[2,32]{1,0:T(2,128)S(1)} %collective-permute-done.3.got_2, s32[2,32]{1,0:T(2,128)S(1)} %collective-permute-done.1.got_4, ...), custom_call_target="tpu_custom_call" | custom-call | tf_op jit(solution)/shard_map/order/pallas_call | solution.py:406
  17.6 0.0 collective-permute-done.5.other
  17.6 12.7 %first_half.1 = (f32[65536,128]{1,0:T(8,128)S(1)}, bf16[3,272,128]{2,1,0:T(8,128)(2,1)}, bf16[3,272,128]{2,1,0:T(8,128)(2,1)}) custom-call(s32[5]{0:T(128)S(1)} %stack.31.me, s32[73728]{0:T(1024)S(1)} %bitcast.55, f32[65536,128]{1,0:T(8,128)S(1)} %own_rows.3.table_in, bf16[96,32768]{1,0:T(8,128)(2,1)} %collective-permute-done.5.other), custom_call_target="tpu_custom_call", output_to_operand_aliasing={{0}: (2, {})} | custom-call | tf_op jit(solution)/shard_map/first_half/pallas_call | solution.py:460
  30.3 1.6 %collective-permute-start.6 = (bf16[3,272,128]{2,1,0:T(8,128)(2,1)}, bf16[3,272,128]{2,1,0:T(8,128)(2,1)S(1)}, u32[]{:S(2)}, u32[]{:S(2)}) collective-permute-start(bf16[3,272,128]{2,1,0:T(8,128)(2,1)} %get-tuple-element.84), channel_id=1, source_target_pairs={{0,2},{2,0},{4,6},{6,4},{8,10},{10,8},{12,14},{14,12},{1,3},{3,1},... | collective-permute-start | bytes 626696 | tf_op jit(solution)/shard_map/ppermute | solution.py:560
  31.9 0.0 copy-start
  31.9 0.0 copy-start.2
  31.9 0.0 copy-start.3
  31.9 0.0 copy-start.4
  31.9 0.0 copy-start.11
  31.9 0.0 copy-start.12
  31.9 0.0 copy-start.13
  31.9 8.6 %second_half.1 = (bf16[3,272,128]{2,1,0:T(8,128)(2,1)}, bf16[3,272,128]{2,1,0:T(8,128)(2,1)}) custom-call(s32[5]{0:T(128)S(1)} %stack.31.me, s32[73728]{0:T(1024)S(1)} %bitcast.56, f32[65536,128]{1,0:T(8,128)S(1)} %get-tuple-element.86.table), custom_call_target="tpu_custom_call" | custom-call | tf_op jit(solution)/shard_map/second_half/pallas_call | solution.py:482
  40.6 0.0 collective-permute-done.6.got
  40.6 0.0 copy-done
  40.6 1.5 %project_far.1 = (bf16[272,256]{1,0:T(8,128)(2,1)S(1)}, bf16[272,256]{1,0:T(8,128)(2,1)S(1)}, bf16[3,272,128]{2,1,0:T(8,128)(2,1)S(1)}) custom-call(s32[5]{0:T(128)S(1)} %stack.31.me, bf16[3,272,128]{2,1,0:T(8,128)(2,1)S(1)} %copy-done, bf16[3,272,128]{2,1,0:T(8,128)(2,1)S(1)} %collective-permute-done.6.got, bf16[192,256]{1,0:T(8,128)(2,1)S(1)} %join.2.weights, ...), custom_call_target="tpu_custom_call" | custom-call | tf_op jit(solution)/shard_map/project_far/pallas_call | solution.py:497
  42.1 0.6 %collective-permute-start.7 = (bf16[3,272,128]{2,1,0:T(8,128)(2,1)}, bf16[3,272,128]{2,1,0:T(8,128)(2,1)S(1)}, u32[]{:S(2)}, u32[]{:S(2)}) collective-permute-start(bf16[3,272,128]{2,1,0:T(8,128)(2,1)} %get-tuple-element.92), channel_id=1, source_target_pairs={{0,2},{2,0},{4,6},{6,4},{8,10},{10,8},{12,14},{14,12},{1,3},{3,1},... | collective-permute-start | bytes 626696 | tf_op jit(solution)/shard_map/ppermute | solution.py:560
  42.7 2.2 %collective-permute-start.8 = (bf16[272,256]{1,0:T(8,128)(2,1)S(1)}, bf16[272,256]{1,0:T(8,128)(2,1)S(1)}, u32[]{:S(2)}, u32[]{:S(2)}) collective-permute-start(bf16[272,256]{1,0:T(8,128)(2,1)S(1)} %get-tuple-element.94), channel_id=1, source_target_pairs={{0,8},{2,10},{4,12},{6,14},{8,0},{10,2},{12,4},{14,6},{1,9},{3,11}... | collective-permute-start | bytes 417800 | tf_op jit(solution)/shard_map/ppermute | solution.py:560
  44.9 1.3 %collective-permute-start.9 = (bf16[272,256]{1,0:T(8,128)(2,1)S(1)}, bf16[272,256]{1,0:T(8,128)(2,1)S(1)}, u32[]{:S(2)}, u32[]{:S(2)}) collective-permute-start(bf16[272,256]{1,0:T(8,128)(2,1)S(1)} %get-tuple-element.95), channel_id=1, source_target_pairs={{0,12},{2,14},{4,8},{6,10},{8,4},{10,6},{12,0},{14,2},{1,13},{3,15... | collective-permute-start | bytes 417800 | tf_op jit(solution)/shard_map/ppermute | solution.py:560
  46.2 1.9 %collective-permute-done.7.got = bf16[3,272,128]{2,1,0:T(8,128)(2,1)S(1)} collective-permute-done((bf16[3,272,128]{2,1,0:T(8,128)(2,1)}, bf16[3,272,128]{2,1,0:T(8,128)(2,1)S(1)}, u32[]{:S(2)}, u32[]{:S(2)}) %collective-permute-start.7) | collective-permute-done | bytes 208928 | tf_op jit(solution)/shard_map/ppermute | solution.py:560
  48.2 1.0 %project_near.1 = (f32[272,256]{1,0:T(8,128)S(1)}, bf16[272,256]{1,0:T(8,128)(2,1)S(1)}) custom-call(s32[5]{0:T(128)S(1)} %stack.31.me, bf16[3,272,128]{2,1,0:T(8,128)(2,1)S(1)} %get-tuple-element.88.keep, bf16[3,272,128]{2,1,0:T(8,128)(2,1)S(1)} %collective-permute-done.7.got, bf16[192,256]{1,0:T(8,128)(2,1)S(1)} %join.2.weights, ...), custom_call_target="tpu_custom_call" | custom-call | tf_op jit(solution)/shard_map/project_near/pallas_call | solution.py:510
  49.2 1.5 %collective-permute-start.10 = (bf16[272,256]{1,0:T(8,128)(2,1)S(1)}, bf16[272,256]{1,0:T(8,128)(2,1)S(1)}, u32[]{:S(2)}, u32[]{:S(2)}) collective-permute-start(bf16[272,256]{1,0:T(8,128)(2,1)S(1)} %get-tuple-element.96), channel_id=1, source_target_pairs={{0,4},{2,6},{4,0},{6,2},{8,12},{10,14},{12,8},{14,10},{1,5},{3,7},... | collective-permute-start | bytes 417800 | tf_op jit(solution)/shard_map/ppermute | solution.py:560
  51.3 3.4 %collective-permute-done.8.a = bf16[272,256]{1,0:T(8,128)(2,1)S(1)} collective-permute-done((bf16[272,256]{1,0:T(8,128)(2,1)S(1)}, bf16[272,256]{1,0:T(8,128)(2,1)S(1)}, u32[]{:S(2)}, u32[]{:S(2)}) %collective-permute-start.8) | collective-permute-done | bytes 139296 | tf_op jit(solution)/shard_map/ppermute | solution.py:560
  54.7 0.0 collective-permute-done.9.b
  54.7 1.1 %collective-permute-done.10.c = bf16[272,256]{1,0:T(8,128)(2,1)S(1)} collective-permute-done((bf16[272,256]{1,0:T(8,128)(2,1)S(1)}, bf16[272,256]{1,0:T(8,128)(2,1)S(1)}, u32[]{:S(2)}, u32[]{:S(2)}) %collective-permute-start.10) | collective-permute-done | bytes 139296 | tf_op jit(solution)/shard_map/ppermute | solution.py:560
  55.8 0.0 copy-done.2
  55.8 0.0 copy-done.3
  55.8 0.0 copy-done.4
  55.8 0.0 copy-done.11
  55.9 0.0 copy-done.12
  55.9 0.0 copy-done.13
  55.9 0.7 %layer_two.1 = f32[32,153]{1,0:T(8,128)S(1)} custom-call(f32[272,256]{1,0:T(8,128)S(1)} %get-tuple-element.93.mine, bf16[272,256]{1,0:T(8,128)(2,1)S(1)} %collective-permute-done.8.a, bf16[272,256]{1,0:T(8,128)(2,1)S(1)} %collective-permute-done.9.b, bf16[272,256]{1,0:T(8,128)(2,1)S(1)} %collective-permute-done.10.c, s32[1,32]{1,0:T(1,128)S(1)} %bitcast.68, ...), custom_call_target="tpu_custom_call" | custom-call | tf_op jit(solution)/shard_map/layer_two/pallas_call | solution.py:523
  56.6 0.1 conditional.1
  56.7 0.0 copy-start.9
  56.8 0.6 %copy-done.9 = f32[32,153]{1,0:T(8,128)} copy-done((f32[32,153]{1,0:T(8,128)}, f32[32,153]{1,0:T(8,128)S(1)}, u32[]{:S(2)}) %copy-start.9) | copy-done | bytes 19608
  (2 shorter events, 0.0 us)
Async XLA Ops:
  0.0 17.6 %collective-permute-start.5 = (bf16[96,32768]{1,0:T(8,128)(2,1)}, bf16[96,32768]{1,0:T(8,128)(2,1)}, u32[]{:S(2)}, u32[]{:S(2)}) collective-permute-start(bf16[96,32768]{1,0:T(8,128)(2,1)} %features.3), channel_id=1, source_target_pairs={{0,1},{1,0},{2,3},{3,2},{4,5},{5,4},{6,7},{7,6},{8,9},{9,8},{10,11... | collective-permute-start | bytes 18874376 | tf_op jit(solution)/shard_map/ppermute | solution.py:562
  0.5 5.7 %collective-permute-start = (s32[1,32]{1,0:T(1,128)}, s32[1,32]{1,0:T(1,128)S(1)}, u32[]{:S(2)}, u32[]{:S(2)}) collective-permute-start(s32[1,32]{1,0:T(1,128)} %bitcast.65), channel_id=1, source_target_pairs={{0,2},{2,0},{4,6},{6,4},{8,10},{10,8},{12,14},{14,12},{1,3},{3,1},... | collective-permute-start | bytes 392 | tf_op jit(solution)/shard_map/ppermute | solution.py:560
  3.0 3.1 %copy-start.5 = (bf16[96,256]{1,0:T(8,128)(2,1)S(1)}, bf16[96,256]{1,0:T(8,128)(2,1)}, u32[]{:S(2)}) copy-start(bf16[96,256]{1,0:T(8,128)(2,1)} %refs_0_.1) | copy-start | bytes 147460
  3.0 3.1 %copy-start.6 = (bf16[96,256]{1,0:T(8,128)(2,1)S(1)}, bf16[96,256]{1,0:T(8,128)(2,1)}, u32[]{:S(2)}) copy-start(bf16[96,256]{1,0:T(8,128)(2,1)} %refs_1_.1) | copy-start | bytes 147460
  3.0 3.6 %copy-start.10 = (s32[32]{0:T(128)S(1)}, s32[32]{0:T(128)}, u32[]{:S(2)}) copy-start(s32[32]{0:T(128)} %param.19) | copy-start | bytes 388
  6.2 8.7 %collective-permute-start.4 = (bf16[192,256]{1,0:T(8,128)(2,1)S(1)}, bf16[192,256]{1,0:T(8,128)(2,1)S(1)}, u32[]{:S(2)}, u32[]{:S(2)}) collective-permute-start(bf16[192,256]{1,0:T(8,128)(2,1)S(1)} %join.2.weights), channel_id=1, source_target_pairs={{0,2},{2,0},{4,6},{6,4},{8,10},{10,8},{12,14},{14,12},{1,3},{3,1},... | collective-permute-start | bytes 294920 | tf_op jit(solution)/shard_map/ppermute | solution.py:560
  6.6 8.2 %copy-start.1 = (s32[15,2816]{1,0:T(8,128)S(1)}, s32[15,2816]{1,0:T(8,128)}, u32[]{:S(2)}) copy-start(s32[15,2816]{1,0:T(8,128)} %neighbour_ids.1) | copy-start | bytes 506884
  6.6 8.2 %copy-start.7 = (s32[2816]{0:T(1024)S(1)}, s32[2816]{0:T(1024)}, u32[]{:S(2)}) copy-start(s32[2816]{0:T(1024)} %count_one.1) | copy-start | bytes 33796
  6.6 8.2 %copy-start.8 = (s32[2816]{0:T(1024)S(1)}, s32[2816]{0:T(1024)}, u32[]{:S(2)}) copy-start(s32[2816]{0:T(1024)} %self_ids.1) | copy-start | bytes 33796
  6.6 7.5 %collective-permute-start.1 = (s32[2,32]{1,0:T(2,128)S(1)}, s32[2,32]{1,0:T(2,128)S(1)}, u32[]{:S(2)}, u32[]{:S(2)}) collective-permute-start(s32[2,32]{1,0:T(2,128)S(1)} %join.3), channel_id=1, source_target_pairs={{0,8},{2,10},{4,12},{6,14},{8,0},{10,2},{12,4},{14,6},{1,9},{3,11}... | collective-permute-start | bytes 776 | tf_op jit(solution)/shard_map/ppermute | solution.py:560
  9.5 5.4 %collective-permute-start.2 = (s32[2,32]{1,0:T(2,128)S(1)}, s32[2,32]{1,0:T(2,128)S(1)}, u32[]{:S(2)}, u32[]{:S(2)}) collective-permute-start(s32[2,32]{1,0:T(2,128)S(1)} %join.3), channel_id=1, source_target_pairs={{0,12},{2,14},{4,8},{6,10},{8,4},{10,6},{12,0},{14,2},{1,13},{3,15... | collective-permute-start | bytes 776 | tf_op jit(solution)/shard_map/ppermute | solution.py:560
  10.8 4.0 %collective-permute-start.3 = (s32[2,32]{1,0:T(2,128)S(1)}, s32[2,32]{1,0:T(2,128)S(1)}, u32[]{:S(2)}, u32[]{:S(2)}) collective-permute-start(s32[2,32]{1,0:T(2,128)S(1)} %join.3), channel_id=1, source_target_pairs={{0,4},{2,6},{4,0},{6,2},{8,12},{10,14},{12,8},{14,10},{1,5},{3,7},... | collective-permute-start | bytes 776 | tf_op jit(solution)/shard_map/ppermute | solution.py:560
  30.3 10.2 %collective-permute-start.6 = (bf16[3,272,128]{2,1,0:T(8,128)(2,1)}, bf16[3,272,128]{2,1,0:T(8,128)(2,1)S(1)}, u32[]{:S(2)}, u32[]{:S(2)}) collective-permute-start(bf16[3,272,128]{2,1,0:T(8,128)(2,1)} %get-tuple-element.84), channel_id=1, source_target_pairs={{0,2},{2,0},{4,6},{6,4},{8,10},{10,8},{12,14},{14,12},{1,3},{3,1},... | collective-permute-start | bytes 626696 | tf_op jit(solution)/shard_map/ppermute | solution.py:560
  31.9 8.7 %copy-start = (bf16[3,272,128]{2,1,0:T(8,128)(2,1)S(1)}, bf16[3,272,128]{2,1,0:T(8,128)(2,1)}, u32[]{:S(2)}) copy-start(bf16[3,272,128]{2,1,0:T(8,128)(2,1)} %get-tuple-element.83.keep) | copy-start | bytes 626692
  31.9 23.9 %copy-start.2 = (bf16[256,256]{1,0:T(8,128)(2,1)S(1)}, bf16[256,256]{1,0:T(8,128)(2,1)}, u32[]{:S(2)}) copy-start(bf16[256,256]{1,0:T(8,128)(2,1)} %neigh_two.1) | copy-start | bytes 393220
  31.9 23.9 %copy-start.3 = (bf16[256,256]{1,0:T(8,128)(2,1)S(1)}, bf16[256,256]{1,0:T(8,128)(2,1)}, u32[]{:S(2)}) copy-start(bf16[256,256]{1,0:T(8,128)(2,1)} %self_two.1) | copy-start | bytes 393220
  31.9 23.9 %copy-start.4 = (bf16[256,153]{0,1:T(8,128)(2,1)S(1)}, bf16[256,153]{0,1:T(8,128)(2,1)}, u32[]{:S(2)}) copy-start(bf16[256,153]{0,1:T(8,128)(2,1)} %param.26) | copy-start | bytes 235012
  31.9 23.9 %copy-start.11 = (f32[256]{0:T(256)S(1)}, f32[256]{0:T(256)}, u32[]{:S(2)}) copy-start(f32[256]{0:T(256)} %param.25) | copy-start | bytes 3076
  31.9 23.9 %copy-start.12 = (f32[153]{0:T(256)S(1)}, f32[153]{0:T(256)}, u32[]{:S(2)}) copy-start(f32[153]{0:T(256)} %param.27) | copy-start | bytes 1840
  31.9 23.9 %copy-start.13 = (f32[256]{0:T(256)S(1)}, f32[256]{0:T(256)}, u32[]{:S(2)}) copy-start(f32[256]{0:T(256)} %param.22) | copy-start | bytes 3076
  42.1 6.1 %collective-permute-start.7 = (bf16[3,272,128]{2,1,0:T(8,128)(2,1)}, bf16[3,272,128]{2,1,0:T(8,128)(2,1)S(1)}, u32[]{:S(2)}, u32[]{:S(2)}) collective-permute-start(bf16[3,272,128]{2,1,0:T(8,128)(2,1)} %get-tuple-element.92), channel_id=1, source_target_pairs={{0,2},{2,0},{4,6},{6,4},{8,10},{10,8},{12,14},{14,12},{1,3},{3,1},... | collective-permute-start | bytes 626696 | tf_op jit(solution)/shard_map/ppermute | solution.py:560
  42.7 12.0 %collective-permute-start.8 = (bf16[272,256]{1,0:T(8,128)(2,1)S(1)}, bf16[272,256]{1,0:T(8,128)(2,1)S(1)}, u32[]{:S(2)}, u32[]{:S(2)}) collective-permute-start(bf16[272,256]{1,0:T(8,128)(2,1)S(1)} %get-tuple-element.94), channel_id=1, source_target_pairs={{0,8},{2,10},{4,12},{6,14},{8,0},{10,2},{12,4},{14,6},{1,9},{3,11}... | collective-permute-start | bytes 417800 | tf_op jit(solution)/shard_map/ppermute | solution.py:560
  44.9 9.9 %collective-permute-start.9 = (bf16[272,256]{1,0:T(8,128)(2,1)S(1)}, bf16[272,256]{1,0:T(8,128)(2,1)S(1)}, u32[]{:S(2)}, u32[]{:S(2)}) collective-permute-start(bf16[272,256]{1,0:T(8,128)(2,1)S(1)} %get-tuple-element.95), channel_id=1, source_target_pairs={{0,12},{2,14},{4,8},{6,10},{8,4},{10,6},{12,0},{14,2},{1,13},{3,15... | collective-permute-start | bytes 417800 | tf_op jit(solution)/shard_map/ppermute | solution.py:560
  49.2 6.7 %collective-permute-start.10 = (bf16[272,256]{1,0:T(8,128)(2,1)S(1)}, bf16[272,256]{1,0:T(8,128)(2,1)S(1)}, u32[]{:S(2)}, u32[]{:S(2)}) collective-permute-start(bf16[272,256]{1,0:T(8,128)(2,1)S(1)} %get-tuple-element.96), channel_id=1, source_target_pairs={{0,4},{2,6},{4,0},{6,2},{8,12},{10,14},{12,8},{14,10},{1,5},{3,7},... | collective-permute-start | bytes 417800 | tf_op jit(solution)/shard_map/ppermute | solution.py:560
  56.7 0.6 %copy-start.9 = (f32[32,153]{1,0:T(8,128)}, f32[32,153]{1,0:T(8,128)S(1)}, u32[]{:S(2)}) copy-start(f32[32,153]{1,0:T(8,128)S(1)} %get-tuple-element.179) | copy-start | bytes 58756

commit v12 on v10

--- a/solution.py
+++ b/solution.py
@@ -367,7 +367,7 @@
 
 
 def last_kernel(
-    mine, a, b, c, counts, bias_one, self_two, neigh_two, bias_two, out_weight, out_bias, out
+    mine, a, b, c, counts, bias_one, self_two, neigh_two, bias_two, out_weight, out_bias, out_hbm, out, sem
 ):
     pre = mine[...] + a[...].astype(F32) + b[...].astype(F32) + c[...].astype(F32)
     hidden = jnp.maximum(pre + bias_one[...], 0.0).astype(BF16)
@@ -394,6 +394,9 @@
         hidden_two, out_weight[...], (((1,), (1,)), ((), ())), preferred_element_type=F32
     )
     out[...] = logits + out_bias[...]
+    copy = pltpu.make_async_copy(out, out_hbm, sem)
+    copy.start()
+    copy.wait()
 
 
 def params(limit):
@@ -525,9 +528,10 @@
     classes = args[-1].shape[1]
     return pl.pallas_call(
         last_kernel,
-        out_shape=shape((seeds, classes), F32),
+        out_shape=pltpu.HBM((seeds, classes), F32),
         in_specs=[VMEM] * len(args),
-        out_specs=VMEM,
+        out_specs=HBM,
+        scratch_shapes=[pltpu.VMEM((seeds, classes), F32), pltpu.SemaphoreType.DMA],
         compiler_params=params(10),
         name="layer_two",
     )(*args)

time: 58 us -> 58.8 us (1.014)
  Pallas kernels: 33.8 us -> 34.7 us
  local copies, waits for them, and re-layouts: 0.75 us -> 0.14 us
    pallas_call x1, Pallas kernels: 0.73 us -> 1.36 us  [last_call(): pl.pallas_call(last_kernel, out_shape=pltpu.HBM((seeds, classes), F32), i...]
    unnamed x28 -> x26, local copies, waits for them, and re-layouts: 0.67 us -> 0.06 us
where the time goes in v12:
time: 58.8 us
  Pallas kernels  34.7 us (59%)
  starting transfers between devices  15.1 us (26%)
  waiting for transfers between devices  7.62 us (13%)
  between operations  1.06 us (2%)
    ppermute x10, starting transfers between devices, across(): return lax.ppermute(value, 'col', [(i, i ^ bit) for i in range(owners)])  14.6 us
    pallas_call x1, Pallas kernels, first_call(): pl.pallas_call(functools.partial(first_kernel, fanout), out_shape=(shape(...  12.6 us
    pallas_call x1, Pallas kernels, second_call(): pl.pallas_call(functools.partial(second_kernel, fanout, width), out_shape...  8.99 us
    ppermute x10, waiting for transfers between devices, across(): return lax.ppermute(value, 'col', [(i, i ^ bit) for i in range(owners)])  7.61 us
    pallas_call x2, Pallas kernels, own_call(): pl.pallas_call(functools.partial(own_kernel, which, halves), out_shape=sh...  6.22 us
    pallas_call x1, Pallas kernels, order_call(): pl.pallas_call(functools.partial(order_kernel, per_seed), out_shape=(shap...  2.73 us
    pallas_call x1, Pallas kernels, near_call(): pl.pallas_call(near_kernel, out_shape=(shape(dims, F32), shape(dims, BF16...  1.82 us
    pallas_call x1, Pallas kernels, last_call(): pl.pallas_call(last_kernel, out_shape=pltpu.HBM((seeds, classes), F32), i...  1.36 us
  transfers between devices with their start and end apart: 11, of which 4 were waited for; matrix products, arithmetic and copies ran while one was open for 0% of the time, Pallas kernels for 34%

profile of v12, /device:TPU:0, one launch (start us, length us, event | category | flops | bytes accessed | tf_op | source)
XLA Modules:
  0.0 58.8 jit_solution(17584821043045623470)
XLA Ops:
  0.0 0.5 collective-permute-start.5
  0.5 2.5 %collective-permute-start = (s32[1,32]{1,0:T(1,128)}, s32[1,32]{1,0:T(1,128)S(1)}, u32[]{:S(2)}, u32[]{:S(2)}) collective-permute-start(s32[1,32]{1,0:T(1,128)} %bitcast.65), channel_id=1, source_target_pairs={{0,2},{2,0},{4,6},{6,4},{8,10},{10,8},{12,14},{14,12},{1,3},{3,1},... | collective-permute-start | bytes 392 | tf_op jit(solution)/shard_map/ppermute | solution.py:567
  2.9 0.1 stack.31.me
  3.0 0.0 copy-start.5
  3.0 0.0 copy-start.6
  3.0 0.0 copy-start.9
  3.0 3.1 %own_rows.2.refs_0_ = f32[65536,128]{1,0:T(8,128)S(1)} custom-call(s32[5]{0:T(128)S(1)} %stack.31.me, bf16[96,32768]{1,0:T(8,128)(2,1)} %features.3), custom_call_target="tpu_custom_call" | custom-call | tf_op jit(solution)/shard_map/own_rows/pallas_call | solution.py:436
  6.2 0.0 copy-done.5
  6.2 0.0 copy-done.6
  6.2 0.0 collective-permute-done.refs_1_.got_1
  6.2 0.4 collective-permute-start.4
  6.6 0.0 copy-done.9
  6.6 0.0 copy-start.1
  6.6 0.0 copy-start.7
  6.6 0.0 copy-start.8
  6.6 2.8 %collective-permute-start.1 = (s32[2,32]{1,0:T(2,128)S(1)}, s32[2,32]{1,0:T(2,128)S(1)}, u32[]{:S(2)}, u32[]{:S(2)}) collective-permute-start(s32[2,32]{1,0:T(2,128)S(1)} %join.3), channel_id=1, source_target_pairs={{0,8},{2,10},{4,12},{6,14},{8,0},{10,2},{12,4},{14,6},{1,9},{3,11}... | collective-permute-start | bytes 776 | tf_op jit(solution)/shard_map/ppermute | solution.py:567
  9.5 1.3 %collective-permute-start.2 = (s32[2,32]{1,0:T(2,128)S(1)}, s32[2,32]{1,0:T(2,128)S(1)}, u32[]{:S(2)}, u32[]{:S(2)}) collective-permute-start(s32[2,32]{1,0:T(2,128)S(1)} %join.3), channel_id=1, source_target_pairs={{0,12},{2,14},{4,8},{6,10},{8,4},{10,6},{12,0},{14,2},{1,13},{3,15... | collective-permute-start | bytes 776 | tf_op jit(solution)/shard_map/ppermute | solution.py:567
  10.8 0.2 collective-permute-start.3
  11.1 3.1 %own_rows.3.table_in = f32[65536,128]{1,0:T(8,128)S(1)} custom-call(s32[5]{0:T(128)S(1)} %stack.31.me, bf16[96,32768]{1,0:T(8,128)(2,1)} %features.3, f32[65536,128]{1,0:T(8,128)S(1)} %own_rows.2.refs_0_), custom_call_target="tpu_custom_call", output_to_operand_aliasing={{}: (2, {})} | custom-call | tf_op jit(solution)/shard_map/own_rows/pallas_call | solution.py:436
  14.2 0.0 collective-permute-done.1.got_4
  14.2 0.7 %collective-permute-done.2.got_6 = s32[2,32]{1,0:T(2,128)S(1)} collective-permute-done((s32[2,32]{1,0:T(2,128)S(1)}, s32[2,32]{1,0:T(2,128)S(1)}, u32[]{:S(2)}, u32[]{:S(2)}) %collective-permute-start.2) | collective-permute-done | bytes 288 | tf_op jit(solution)/shard_map/ppermute | solution.py:567
  14.8 0.0 collective-permute-done.3.got_2
  14.9 0.0 collective-permute-done.4.weights_got
  14.9 0.0 copy-done.1
  14.9 0.0 copy-done.7
  14.9 0.0 copy-done.8
  14.9 2.7 %order.1 = (s32[2,18,16,128]{3,2,1,0:T(8,128)S(1)}, s32[1]{0:T(128)}) custom-call(s32[5]{0:T(128)S(1)} %stack.31.me, s32[1,32]{1,0:T(1,128)S(1)} %bitcast.67, s32[1,32]{1,0:T(1,128)S(1)} %collective-permute-done.refs_1_.got_1, s32[2,32]{1,0:T(2,128)S(1)} %collective-permute-done.3.got_2, s32[2,32]{1,0:T(2,128)S(1)} %collective-permute-done.1.got_4, ...), custom_call_target="tpu_custom_call" | custom-call | tf_op jit(solution)/shard_map/order/pallas_call | solution.py:412
  17.6 0.0 collective-permute-done.5.other
  17.6 12.6 %first_half.1 = (f32[65536,128]{1,0:T(8,128)S(1)}, bf16[3,272,128]{2,1,0:T(8,128)(2,1)}, bf16[3,272,128]{2,1,0:T(8,128)(2,1)}) custom-call(s32[5]{0:T(128)S(1)} %stack.31.me, s32[73728]{0:T(1024)S(1)} %bitcast.55, f32[65536,128]{1,0:T(8,128)S(1)} %own_rows.3.table_in, bf16[96,32768]{1,0:T(8,128)(2,1)} %collective-permute-done.5.other), custom_call_target="tpu_custom_call", output_to_operand_aliasing={{0}: (2, {})} | custom-call | tf_op jit(solution)/shard_map/first_half/pallas_call | solution.py:466
  30.2 1.6 %collective-permute-start.6 = (bf16[3,272,128]{2,1,0:T(8,128)(2,1)}, bf16[3,272,128]{2,1,0:T(8,128)(2,1)S(1)}, u32[]{:S(2)}, u32[]{:S(2)}) collective-permute-start(bf16[3,272,128]{2,1,0:T(8,128)(2,1)} %get-tuple-element.85), channel_id=1, source_target_pairs={{0,2},{2,0},{4,6},{6,4},{8,10},{10,8},{12,14},{14,12},{1,3},{3,1},... | collective-permute-start | bytes 626696 | tf_op jit(solution)/shard_map/ppermute | solution.py:567
  31.8 0.0 copy-start
  31.8 0.0 copy-start.2
  31.8 0.0 copy-start.3
  31.8 0.0 copy-start.4
  31.8 0.0 copy-start.10
  31.8 0.0 copy-start.11
  31.8 0.0 copy-start.12
  31.8 9.0 %second_half.1 = (bf16[3,272,128]{2,1,0:T(8,128)(2,1)}, bf16[3,272,128]{2,1,0:T(8,128)(2,1)}) custom-call(s32[5]{0:T(128)S(1)} %stack.31.me, s32[73728]{0:T(1024)S(1)} %bitcast.56, f32[65536,128]{1,0:T(8,128)S(1)} %get-tuple-element.82.table), custom_call_target="tpu_custom_call" | custom-call | tf_op jit(solution)/shard_map/second_half/pallas_call | solution.py:488
  40.8 0.0 collective-permute-done.6.got
  40.8 0.0 copy-done
  40.8 1.0 %project_far.1 = (bf16[272,256]{1,0:T(8,128)(2,1)S(1)}, bf16[272,256]{1,0:T(8,128)(2,1)S(1)}) custom-call(s32[5]{0:T(128)S(1)} %stack.31.me, bf16[3,272,128]{2,1,0:T(8,128)(2,1)S(1)} %copy-done, bf16[3,272,128]{2,1,0:T(8,128)(2,1)S(1)} %collective-permute-done.6.got, bf16[192,256]{1,0:T(8,128)(2,1)S(1)} %join.2.weights, ...), custom_call_target="tpu_custom_call" | custom-call | tf_op jit(solution)/shard_map/project_far/pallas_call | solution.py:503
  41.8 0.6 %collective-permute-start.7 = (bf16[3,272,128]{2,1,0:T(8,128)(2,1)}, bf16[3,272,128]{2,1,0:T(8,128)(2,1)S(1)}, u32[]{:S(2)}, u32[]{:S(2)}) collective-permute-start(bf16[3,272,128]{2,1,0:T(8,128)(2,1)} %get-tuple-element.90), channel_id=1, source_target_pairs={{0,2},{2,0},{4,6},{6,4},{8,10},{10,8},{12,14},{14,12},{1,3},{3,1},... | collective-permute-start | bytes 626696 | tf_op jit(solution)/shard_map/ppermute | solution.py:567
  42.4 2.2 %collective-permute-start.8 = (bf16[272,256]{1,0:T(8,128)(2,1)S(1)}, bf16[272,256]{1,0:T(8,128)(2,1)S(1)}, u32[]{:S(2)}, u32[]{:S(2)}) collective-permute-start(bf16[272,256]{1,0:T(8,128)(2,1)S(1)} %get-tuple-element.92), channel_id=1, source_target_pairs={{0,8},{2,10},{4,12},{6,14},{8,0},{10,2},{12,4},{14,6},{1,9},{3,11}... | collective-permute-start | bytes 417800 | tf_op jit(solution)/shard_map/ppermute | solution.py:567
  44.6 1.3 %collective-permute-start.9 = (bf16[272,256]{1,0:T(8,128)(2,1)S(1)}, bf16[272,256]{1,0:T(8,128)(2,1)S(1)}, u32[]{:S(2)}, u32[]{:S(2)}) collective-permute-start(bf16[272,256]{1,0:T(8,128)(2,1)S(1)} %get-tuple-element.93), channel_id=1, source_target_pairs={{0,12},{2,14},{4,8},{6,10},{8,4},{10,6},{12,0},{14,2},{1,13},{3,15... | collective-permute-start | bytes 417800 | tf_op jit(solution)/shard_map/ppermute | solution.py:567
  46.0 2.6 %collective-permute-done.7.got = bf16[3,272,128]{2,1,0:T(8,128)(2,1)S(1)} collective-permute-done((bf16[3,272,128]{2,1,0:T(8,128)(2,1)}, bf16[3,272,128]{2,1,0:T(8,128)(2,1)S(1)}, u32[]{:S(2)}, u32[]{:S(2)}) %collective-permute-start.7) | collective-permute-done | bytes 208928 | tf_op jit(solution)/shard_map/ppermute | solution.py:567
  48.6 1.8 %project_near.1 = (f32[272,256]{1,0:T(8,128)S(1)}, bf16[272,256]{1,0:T(8,128)(2,1)S(1)}) custom-call(s32[5]{0:T(128)S(1)} %stack.31.me, bf16[3,272,128]{2,1,0:T(8,128)(2,1)} %get-tuple-element.83.keep_hbm, bf16[3,272,128]{2,1,0:T(8,128)(2,1)S(1)} %collective-permute-done.7.got, bf16[192,256]{1,0:T(8,128)(2,1)S(1)} %join.2.weights, ...), custom_call_target="tpu_custom_call" | custom-call | tf_op jit(solution)/shard_map/project_near/pallas_call | solution.py:515
  50.4 1.6 %collective-permute-start.10 = (bf16[272,256]{1,0:T(8,128)(2,1)S(1)}, bf16[272,256]{1,0:T(8,128)(2,1)S(1)}, u32[]{:S(2)}, u32[]{:S(2)}) collective-permute-start(bf16[272,256]{1,0:T(8,128)(2,1)S(1)} %get-tuple-element.94), channel_id=1, source_target_pairs={{0,4},{2,6},{4,0},{6,2},{8,12},{10,14},{12,8},{14,10},{1,5},{3,7},... | collective-permute-start | bytes 417800 | tf_op jit(solution)/shard_map/ppermute | solution.py:567
  52.7 2.5 %collective-permute-done.8.a = bf16[272,256]{1,0:T(8,128)(2,1)S(1)} collective-permute-done((bf16[272,256]{1,0:T(8,128)(2,1)S(1)}, bf16[272,256]{1,0:T(8,128)(2,1)S(1)}, u32[]{:S(2)}, u32[]{:S(2)}) %collective-permute-start.8) | collective-permute-done | bytes 139296 | tf_op jit(solution)/shard_map/ppermute | solution.py:567
  55.2 0.0 collective-permute-done.9.b
  55.2 1.8 %collective-permute-done.10.c = bf16[272,256]{1,0:T(8,128)(2,1)S(1)} collective-permute-done((bf16[272,256]{1,0:T(8,128)(2,1)S(1)}, bf16[272,256]{1,0:T(8,128)(2,1)S(1)}, u32[]{:S(2)}, u32[]{:S(2)}) %collective-permute-start.10) | collective-permute-done | bytes 139296 | tf_op jit(solution)/shard_map/ppermute | solution.py:567
  57.0 0.0 copy-done.2
  57.0 0.0 copy-done.3
  57.0 0.0 copy-done.4
  57.0 0.0 copy-done.10
  57.0 0.0 copy-done.11
  57.0 0.0 copy-done.12
  57.0 1.4 %layer_two.1 = f32[32,153]{1,0:T(8,128)} custom-call(f32[272,256]{1,0:T(8,128)S(1)} %get-tuple-element.91.mine, bf16[272,256]{1,0:T(8,128)(2,1)S(1)} %collective-permute-done.8.a, bf16[272,256]{1,0:T(8,128)(2,1)S(1)} %collective-permute-done.9.b, bf16[272,256]{1,0:T(8,128)(2,1)S(1)} %collective-permute-done.10.c, s32[1,32]{1,0:T(1,128)S(1)} %bitcast.68, ...), custom_call_target="tpu_custom_call" | custom-call | tf_op jit(solution)/shard_map/layer_two/pallas_call | solution.py:529
  58.4 0.2 conditional.1
  (2 shorter events, 0.0 us)
Async XLA Ops:
  0.0 17.6 %collective-permute-start.5 = (bf16[96,32768]{1,0:T(8,128)(2,1)}, bf16[96,32768]{1,0:T(8,128)(2,1)}, u32[]{:S(2)}, u32[]{:S(2)}) collective-permute-start(bf16[96,32768]{1,0:T(8,128)(2,1)} %features.3), channel_id=1, source_target_pairs={{0,1},{1,0},{2,3},{3,2},{4,5},{5,4},{6,7},{7,6},{8,9},{9,8},{10,11... | collective-permute-start | bytes 18874376 | tf_op jit(solution)/shard_map/ppermute | solution.py:569
  0.5 5.7 %collective-permute-start = (s32[1,32]{1,0:T(1,128)}, s32[1,32]{1,0:T(1,128)S(1)}, u32[]{:S(2)}, u32[]{:S(2)}) collective-permute-start(s32[1,32]{1,0:T(1,128)} %bitcast.65), channel_id=1, source_target_pairs={{0,2},{2,0},{4,6},{6,4},{8,10},{10,8},{12,14},{14,12},{1,3},{3,1},... | collective-permute-start | bytes 392 | tf_op jit(solution)/shard_map/ppermute | solution.py:567
  3.0 3.1 %copy-start.5 = (bf16[96,256]{1,0:T(8,128)(2,1)S(1)}, bf16[96,256]{1,0:T(8,128)(2,1)}, u32[]{:S(2)}) copy-start(bf16[96,256]{1,0:T(8,128)(2,1)} %refs_0_.1) | copy-start | bytes 147460
  3.0 3.1 %copy-start.6 = (bf16[96,256]{1,0:T(8,128)(2,1)S(1)}, bf16[96,256]{1,0:T(8,128)(2,1)}, u32[]{:S(2)}) copy-start(bf16[96,256]{1,0:T(8,128)(2,1)} %refs_1_.1) | copy-start | bytes 147460
  3.0 3.6 %copy-start.9 = (s32[32]{0:T(128)S(1)}, s32[32]{0:T(128)}, u32[]{:S(2)}) copy-start(s32[32]{0:T(128)} %param.19) | copy-start | bytes 388
  6.2 8.7 %collective-permute-start.4 = (bf16[192,256]{1,0:T(8,128)(2,1)S(1)}, bf16[192,256]{1,0:T(8,128)(2,1)S(1)}, u32[]{:S(2)}, u32[]{:S(2)}) collective-permute-start(bf16[192,256]{1,0:T(8,128)(2,1)S(1)} %join.2.weights), channel_id=1, source_target_pairs={{0,2},{2,0},{4,6},{6,4},{8,10},{10,8},{12,14},{14,12},{1,3},{3,1},... | collective-permute-start | bytes 294920 | tf_op jit(solution)/shard_map/ppermute | solution.py:567
  6.6 8.2 %copy-start.1 = (s32[15,2816]{1,0:T(8,128)S(1)}, s32[15,2816]{1,0:T(8,128)}, u32[]{:S(2)}) copy-start(s32[15,2816]{1,0:T(8,128)} %neighbour_ids.1) | copy-start | bytes 506884
  6.6 8.2 %copy-start.7 = (s32[2816]{0:T(1024)S(1)}, s32[2816]{0:T(1024)}, u32[]{:S(2)}) copy-start(s32[2816]{0:T(1024)} %count_one.1) | copy-start | bytes 33796
  6.6 8.2 %copy-start.8 = (s32[2816]{0:T(1024)S(1)}, s32[2816]{0:T(1024)}, u32[]{:S(2)}) copy-start(s32[2816]{0:T(1024)} %self_ids.1) | copy-start | bytes 33796
  6.6 7.5 %collective-permute-start.1 = (s32[2,32]{1,0:T(2,128)S(1)}, s32[2,32]{1,0:T(2,128)S(1)}, u32[]{:S(2)}, u32[]{:S(2)}) collective-permute-start(s32[2,32]{1,0:T(2,128)S(1)} %join.3), channel_id=1, source_target_pairs={{0,8},{2,10},{4,12},{6,14},{8,0},{10,2},{12,4},{14,6},{1,9},{3,11}... | collective-permute-start | bytes 776 | tf_op jit(solution)/shard_map/ppermute | solution.py:567
  9.5 5.4 %collective-permute-start.2 = (s32[2,32]{1,0:T(2,128)S(1)}, s32[2,32]{1,0:T(2,128)S(1)}, u32[]{:S(2)}, u32[]{:S(2)}) collective-permute-start(s32[2,32]{1,0:T(2,128)S(1)} %join.3), channel_id=1, source_target_pairs={{0,12},{2,14},{4,8},{6,10},{8,4},{10,6},{12,0},{14,2},{1,13},{3,15... | collective-permute-start | bytes 776 | tf_op jit(solution)/shard_map/ppermute | solution.py:567
  10.8 4.0 %collective-permute-start.3 = (s32[2,32]{1,0:T(2,128)S(1)}, s32[2,32]{1,0:T(2,128)S(1)}, u32[]{:S(2)}, u32[]{:S(2)}) collective-permute-start(s32[2,32]{1,0:T(2,128)S(1)} %join.3), channel_id=1, source_target_pairs={{0,4},{2,6},{4,0},{6,2},{8,12},{10,14},{12,8},{14,10},{1,5},{3,7},... | collective-permute-start | bytes 776 | tf_op jit(solution)/shard_map/ppermute | solution.py:567
  30.2 10.6 %collective-permute-start.6 = (bf16[3,272,128]{2,1,0:T(8,128)(2,1)}, bf16[3,272,128]{2,1,0:T(8,128)(2,1)S(1)}, u32[]{:S(2)}, u32[]{:S(2)}) collective-permute-start(bf16[3,272,128]{2,1,0:T(8,128)(2,1)} %get-tuple-element.85), channel_id=1, source_target_pairs={{0,2},{2,0},{4,6},{6,4},{8,10},{10,8},{12,14},{14,12},{1,3},{3,1},... | collective-permute-start | bytes 626696 | tf_op jit(solution)/shard_map/ppermute | solution.py:567
  31.8 9.1 %copy-start = (bf16[3,272,128]{2,1,0:T(8,128)(2,1)S(1)}, bf16[3,272,128]{2,1,0:T(8,128)(2,1)}, u32[]{:S(2)}) copy-start(bf16[3,272,128]{2,1,0:T(8,128)(2,1)} %get-tuple-element.84.keep) | copy-start | bytes 626692
  31.8 25.2 %copy-start.2 = (bf16[256,256]{1,0:T(8,128)(2,1)S(1)}, bf16[256,256]{1,0:T(8,128)(2,1)}, u32[]{:S(2)}) copy-start(bf16[256,256]{1,0:T(8,128)(2,1)} %neigh_two.1) | copy-start | bytes 393220
  31.8 25.2 %copy-start.3 = (bf16[256,256]{1,0:T(8,128)(2,1)S(1)}, bf16[256,256]{1,0:T(8,128)(2,1)}, u32[]{:S(2)}) copy-start(bf16[256,256]{1,0:T(8,128)(2,1)} %self_two.1) | copy-start | bytes 393220
  31.8 25.2 %copy-start.4 = (bf16[256,153]{0,1:T(8,128)(2,1)S(1)}, bf16[256,153]{0,1:T(8,128)(2,1)}, u32[]{:S(2)}) copy-start(bf16[256,153]{0,1:T(8,128)(2,1)} %param.26) | copy-start | bytes 235012
  31.8 25.3 %copy-start.10 = (f32[256]{0:T(256)S(1)}, f32[256]{0:T(256)}, u32[]{:S(2)}) copy-start(f32[256]{0:T(256)} %param.25) | copy-start | bytes 3076
  31.8 25.2 %copy-start.11 = (f32[153]{0:T(256)S(1)}, f32[153]{0:T(256)}, u32[]{:S(2)}) copy-start(f32[153]{0:T(256)} %param.27) | copy-start | bytes 1840
  31.8 25.2 %copy-start.12 = (f32[256]{0:T(256)S(1)}, f32[256]{0:T(256)}, u32[]{:S(2)}) copy-start(f32[256]{0:T(256)} %param.22) | copy-start | bytes 3076
  41.8 6.8 %collective-permute-start.7 = (bf16[3,272,128]{2,1,0:T(8,128)(2,1)}, bf16[3,272,128]{2,1,0:T(8,128)(2,1)S(1)}, u32[]{:S(2)}, u32[]{:S(2)}) collective-permute-start(bf16[3,272,128]{2,1,0:T(8,128)(2,1)} %get-tuple-element.90), channel_id=1, source_target_pairs={{0,2},{2,0},{4,6},{6,4},{8,10},{10,8},{12,14},{14,12},{1,3},{3,1},... | collective-permute-start | bytes 626696 | tf_op jit(solution)/shard_map/ppermute | solution.py:567
  42.4 12.7 %collective-permute-start.8 = (bf16[272,256]{1,0:T(8,128)(2,1)S(1)}, bf16[272,256]{1,0:T(8,128)(2,1)S(1)}, u32[]{:S(2)}, u32[]{:S(2)}) collective-permute-start(bf16[272,256]{1,0:T(8,128)(2,1)S(1)} %get-tuple-element.92), channel_id=1, source_target_pairs={{0,8},{2,10},{4,12},{6,14},{8,0},{10,2},{12,4},{14,6},{1,9},{3,11}... | collective-permute-start | bytes 417800 | tf_op jit(solution)/shard_map/ppermute | solution.py:567
  44.6 10.5 %collective-permute-start.9 = (bf16[272,256]{1,0:T(8,128)(2,1)S(1)}, bf16[272,256]{1,0:T(8,128)(2,1)S(1)}, u32[]{:S(2)}, u32[]{:S(2)}) collective-permute-start(bf16[272,256]{1,0:T(8,128)(2,1)S(1)} %get-tuple-element.93), channel_id=1, source_target_pairs={{0,12},{2,14},{4,8},{6,10},{8,4},{10,6},{12,0},{14,2},{1,13},{3,15... | collective-permute-start | bytes 417800 | tf_op jit(solution)/shard_map/ppermute | solution.py:567
  50.4 6.6 %collective-permute-start.10 = (bf16[272,256]{1,0:T(8,128)(2,1)S(1)}, bf16[272,256]{1,0:T(8,128)(2,1)S(1)}, u32[]{:S(2)}, u32[]{:S(2)}) collective-permute-start(bf16[272,256]{1,0:T(8,128)(2,1)S(1)} %get-tuple-element.94), channel_id=1, source_target_pairs={{0,4},{2,6},{4,0},{6,2},{8,12},{10,14},{12,8},{14,10},{1,5},{3,7},... | collective-permute-start | bytes 417800 | tf_op jit(solution)/shard_map/ppermute | solution.py:567

commit v13 on v10

--- a/solution.py
+++ b/solution.py
@@ -582,7 +582,6 @@
     got_far = across(send_far, 1)
     keep_near, send_near = second_call(fanout, width, me, lists, table)
     far = far_call(me, keep_far, got_far, weights, weights_got)
-    far, send_near = lax.optimization_barrier((far, send_near))
     far_got = [across(far[0], 4), across(far[1], 6)]
     got_near = across(send_near, 1)
     near = near_call(me, keep_near, got_near, weights, weights_got)

time: 58 us -> 57.6 us (level); the launches traced: 58.4 us -> 57 us
  waiting for transfers between devices: 7.73 us -> 6.1 us
    ppermute x10, waiting for transfers between devices: 7.72 us -> 6.1 us  [across(): return lax.ppermute(value, 'col', [(i, i ^ bit) for i in range(owners)])]
  transfers between devices with their start and end apart: 11 -> 11, of which waited for: 4 -> 4; matrix products, arithmetic and copies ran while one was open for 0% -> 0% of each run, Pallas kernels for 34% -> 37%
where the time goes in v13:
time: 57.6 us; the launch traced here: 57 us
  Pallas kernels  34.2 us (59%)
  starting transfers between devices  14.9 us (26%)
  waiting for transfers between devices  6.1 us (11%)
  between operations  0.88 us (2%)
  local copies, waits for them, and re-layouts  0.75 us (1%)
    ppermute x10, starting transfers between devices, across(): return lax.ppermute(value, 'col', [(i, i ^ bit) for i in range(owners)])  14.4 us
    pallas_call x1, Pallas kernels, first_call(): pl.pallas_call(functools.partial(first_kernel, fanout), out_shape=(shape(...  12.3 us
    pallas_call x1, Pallas kernels, second_call(): pl.pallas_call(functools.partial(second_kernel, fanout, width), out_shape...  9.47 us
    pallas_call x2, Pallas kernels, own_call(): pl.pallas_call(functools.partial(own_kernel, which, halves), out_shape=sh...  6.22 us
    ppermute x10, waiting for transfers between devices, across(): return lax.ppermute(value, 'col', [(i, i ^ bit) for i in range(owners)])  6.1 us
    pallas_call x1, Pallas kernels, order_call(): pl.pallas_call(functools.partial(order_kernel, per_seed), out_shape=(shap...  2.73 us
    pallas_call x1, Pallas kernels, near_call(): pl.pallas_call(near_kernel, out_shape=(shape(dims, F32), shape(dims, BF16...  1.82 us
  transfers between devices with their start and end apart: 11, of which 4 were waited for; matrix products, arithmetic and copies ran while one was open for 0% of the time, Pallas kernels for 37%

profile of v13, /device:TPU:0, one launch (start us, length us, event | category | flops | bytes accessed | tf_op | source)
XLA Modules:
  0.0 57.0 jit_solution(10459029482318786313)
XLA Ops:
  0.0 0.5 collective-permute-start.5
  0.5 2.5 %collective-permute-start = (s32[1,32]{1,0:T(1,128)}, s32[1,32]{1,0:T(1,128)S(1)}, u32[]{:S(2)}, u32[]{:S(2)}) collective-permute-start(s32[1,32]{1,0:T(1,128)} %bitcast.65), channel_id=1, source_target_pairs={{0,2},{2,0},{4,6},{6,4},{8,10},{10,8},{12,14},{14,12},{1,3},{3,1},... | collective-permute-start | bytes 392 | tf_op jit(solution)/shard_map/ppermute | solution.py:563
  2.9 0.1 stack.31.me
  3.0 0.0 copy-start.5
  3.0 0.0 copy-start.6
  3.0 0.0 copy-start.10
  3.0 3.1 %own_rows.2.refs_0_ = f32[65536,128]{1,0:T(8,128)S(1)} custom-call(s32[5]{0:T(128)S(1)} %stack.31.me, bf16[96,32768]{1,0:T(8,128)(2,1)} %features.3), custom_call_target="tpu_custom_call" | custom-call | tf_op jit(solution)/shard_map/own_rows/pallas_call | solution.py:433
  6.2 0.0 copy-done.5
  6.2 0.0 copy-done.6
  6.2 0.0 collective-permute-done.refs_1_.got_1
  6.2 0.4 collective-permute-start.4
  6.6 0.0 copy-done.10
  6.6 0.0 copy-start.1
  6.6 0.0 copy-start.7
  6.6 0.0 copy-start.8
  6.6 2.8 %collective-permute-start.1 = (s32[2,32]{1,0:T(2,128)S(1)}, s32[2,32]{1,0:T(2,128)S(1)}, u32[]{:S(2)}, u32[]{:S(2)}) collective-permute-start(s32[2,32]{1,0:T(2,128)S(1)} %join.3), channel_id=1, source_target_pairs={{0,8},{2,10},{4,12},{6,14},{8,0},{10,2},{12,4},{14,6},{1,9},{3,11}... | collective-permute-start | bytes 776 | tf_op jit(solution)/shard_map/ppermute | solution.py:563
  9.5 1.3 %collective-permute-start.2 = (s32[2,32]{1,0:T(2,128)S(1)}, s32[2,32]{1,0:T(2,128)S(1)}, u32[]{:S(2)}, u32[]{:S(2)}) collective-permute-start(s32[2,32]{1,0:T(2,128)S(1)} %join.3), channel_id=1, source_target_pairs={{0,12},{2,14},{4,8},{6,10},{8,4},{10,6},{12,0},{14,2},{1,13},{3,15... | collective-permute-start | bytes 776 | tf_op jit(solution)/shard_map/ppermute | solution.py:563
  10.8 0.2 collective-permute-start.3
  11.1 3.1 %own_rows.3.table_in = f32[65536,128]{1,0:T(8,128)S(1)} custom-call(s32[5]{0:T(128)S(1)} %stack.31.me, bf16[96,32768]{1,0:T(8,128)(2,1)} %features.3, f32[65536,128]{1,0:T(8,128)S(1)} %own_rows.2.refs_0_), custom_call_target="tpu_custom_call", output_to_operand_aliasing={{}: (2, {})} | custom-call | tf_op jit(solution)/shard_map/own_rows/pallas_call | solution.py:433
  14.2 0.0 collective-permute-done.1.got_4
  14.2 0.7 %collective-permute-done.2.got_6 = s32[2,32]{1,0:T(2,128)S(1)} collective-permute-done((s32[2,32]{1,0:T(2,128)S(1)}, s32[2,32]{1,0:T(2,128)S(1)}, u32[]{:S(2)}, u32[]{:S(2)}) %collective-permute-start.2) | collective-permute-done | bytes 288 | tf_op jit(solution)/shard_map/ppermute | solution.py:563
  14.8 0.0 collective-permute-done.3.got_2
  14.9 0.0 collective-permute-done.4.weights_got
  14.9 0.0 copy-done.1
  14.9 0.0 copy-done.7
  14.9 0.0 copy-done.8
  14.9 2.7 %order.1 = (s32[2,18,16,128]{3,2,1,0:T(8,128)S(1)}, s32[1]{0:T(128)}) custom-call(s32[5]{0:T(128)S(1)} %stack.31.me, s32[1,32]{1,0:T(1,128)S(1)} %bitcast.67, s32[1,32]{1,0:T(1,128)S(1)} %collective-permute-done.refs_1_.got_1, s32[2,32]{1,0:T(2,128)S(1)} %collective-permute-done.3.got_2, s32[2,32]{1,0:T(2,128)S(1)} %collective-permute-done.1.got_4, ...), custom_call_target="tpu_custom_call" | custom-call | tf_op jit(solution)/shard_map/order/pallas_call | solution.py:409
  17.6 0.0 collective-permute-done.5.other
  17.6 12.3 %first_half.1 = (f32[65536,128]{1,0:T(8,128)S(1)}, bf16[3,272,128]{2,1,0:T(8,128)(2,1)}, bf16[3,272,128]{2,1,0:T(8,128)(2,1)}) custom-call(s32[5]{0:T(128)S(1)} %stack.31.me, s32[73728]{0:T(1024)S(1)} %bitcast.55, f32[65536,128]{1,0:T(8,128)S(1)} %own_rows.3.table_in, bf16[96,32768]{1,0:T(8,128)(2,1)} %collective-permute-done.5.other), custom_call_target="tpu_custom_call", output_to_operand_aliasing={{0}: (2, {})} | custom-call | tf_op jit(solution)/shard_map/first_half/pallas_call | solution.py:463
  29.9 1.6 %collective-permute-start.7 = (bf16[3,272,128]{2,1,0:T(8,128)(2,1)}, bf16[3,272,128]{2,1,0:T(8,128)(2,1)S(1)}, u32[]{:S(2)}, u32[]{:S(2)}) collective-permute-start(bf16[3,272,128]{2,1,0:T(8,128)(2,1)} %get-tuple-element.85), channel_id=1, source_target_pairs={{0,2},{2,0},{4,6},{6,4},{8,10},{10,8},{12,14},{14,12},{1,3},{3,1},... | collective-permute-start | bytes 626696 | tf_op jit(solution)/shard_map/ppermute | solution.py:563
  31.4 0.0 copy-start
  31.5 0.0 copy-start.2
  31.5 0.0 copy-start.3
  31.5 0.0 copy-start.4
  31.5 0.0 copy-start.11
  31.5 0.0 copy-start.12
  31.5 0.0 copy-start.13
  31.5 9.5 %second_half.1 = (bf16[3,272,128]{2,1,0:T(8,128)(2,1)}, bf16[3,272,128]{2,1,0:T(8,128)(2,1)}) custom-call(s32[5]{0:T(128)S(1)} %stack.31.me, s32[73728]{0:T(1024)S(1)} %bitcast.56, f32[65536,128]{1,0:T(8,128)S(1)} %get-tuple-element.79.table), custom_call_target="tpu_custom_call" | custom-call | tf_op jit(solution)/shard_map/second_half/pallas_call | solution.py:485
  41.0 0.6 %collective-permute-start.6 = (bf16[3,272,128]{2,1,0:T(8,128)(2,1)}, bf16[3,272,128]{2,1,0:T(8,128)(2,1)S(1)}, u32[]{:S(2)}, u32[]{:S(2)}) collective-permute-start(bf16[3,272,128]{2,1,0:T(8,128)(2,1)} %get-tuple-element.81), channel_id=1, source_target_pairs={{0,2},{2,0},{4,6},{6,4},{8,10},{10,8},{12,14},{14,12},{1,3},{3,1},... | collective-permute-start | bytes 626696 | tf_op jit(solution)/shard_map/ppermute | solution.py:563
  41.6 0.0 collective-permute-done.7.got
  41.6 0.0 copy-done
  41.6 1.0 %project_far.1 = (bf16[272,256]{1,0:T(8,128)(2,1)S(1)}, bf16[272,256]{1,0:T(8,128)(2,1)S(1)}) custom-call(s32[5]{0:T(128)S(1)} %stack.31.me, bf16[3,272,128]{2,1,0:T(8,128)(2,1)S(1)} %copy-done, bf16[3,272,128]{2,1,0:T(8,128)(2,1)S(1)} %collective-permute-done.7.got, bf16[192,256]{1,0:T(8,128)(2,1)S(1)} %join.2.weights, ...), custom_call_target="tpu_custom_call" | custom-call | tf_op jit(solution)/shard_map/project_far/pallas_call | solution.py:500
  42.6 2.2 %collective-permute-start.8 = (bf16[272,256]{1,0:T(8,128)(2,1)S(1)}, bf16[272,256]{1,0:T(8,128)(2,1)S(1)}, u32[]{:S(2)}, u32[]{:S(2)}) collective-permute-start(bf16[272,256]{1,0:T(8,128)(2,1)S(1)} %get-tuple-element.86), channel_id=1, source_target_pairs={{0,8},{2,10},{4,12},{6,14},{8,0},{10,2},{12,4},{14,6},{1,9},{3,11}... | collective-permute-start | bytes 417800 | tf_op jit(solution)/shard_map/ppermute | solution.py:563
  44.8 1.3 %collective-permute-start.9 = (bf16[272,256]{1,0:T(8,128)(2,1)S(1)}, bf16[272,256]{1,0:T(8,128)(2,1)S(1)}, u32[]{:S(2)}, u32[]{:S(2)}) collective-permute-start(bf16[272,256]{1,0:T(8,128)(2,1)S(1)} %get-tuple-element.87), channel_id=1, source_target_pairs={{0,12},{2,14},{4,8},{6,10},{8,4},{10,6},{12,0},{14,2},{1,13},{3,15... | collective-permute-start | bytes 417800 | tf_op jit(solution)/shard_map/ppermute | solution.py:563
  46.2 0.9 %collective-permute-done.6.got = bf16[3,272,128]{2,1,0:T(8,128)(2,1)S(1)} collective-permute-done((bf16[3,272,128]{2,1,0:T(8,128)(2,1)}, bf16[3,272,128]{2,1,0:T(8,128)(2,1)S(1)}, u32[]{:S(2)}, u32[]{:S(2)}) %collective-permute-start.6) | collective-permute-done | bytes 208928 | tf_op jit(solution)/shard_map/ppermute | solution.py:563
  47.1 1.8 %project_near.1 = (f32[272,256]{1,0:T(8,128)S(1)}, bf16[272,256]{1,0:T(8,128)(2,1)S(1)}) custom-call(s32[5]{0:T(128)S(1)} %stack.31.me, bf16[3,272,128]{2,1,0:T(8,128)(2,1)} %get-tuple-element.80.keep_hbm, bf16[3,272,128]{2,1,0:T(8,128)(2,1)S(1)} %collective-permute-done.6.got, bf16[192,256]{1,0:T(8,128)(2,1)S(1)} %join.2.weights, ...), custom_call_target="tpu_custom_call" | custom-call | tf_op jit(solution)/shard_map/project_near/pallas_call | solution.py:512
  48.9 1.3 %collective-permute-start.10 = (bf16[272,256]{1,0:T(8,128)(2,1)S(1)}, bf16[272,256]{1,0:T(8,128)(2,1)S(1)}, u32[]{:S(2)}, u32[]{:S(2)}) collective-permute-start(bf16[272,256]{1,0:T(8,128)(2,1)S(1)} %get-tuple-element.88), channel_id=1, source_target_pairs={{0,4},{2,6},{4,0},{6,2},{8,12},{10,14},{12,8},{14,10},{1,5},{3,7},... | collective-permute-start | bytes 417800 | tf_op jit(solution)/shard_map/ppermute | solution.py:563
  50.9 3.8 %collective-permute-done.8.a = bf16[272,256]{1,0:T(8,128)(2,1)S(1)} collective-permute-done((bf16[272,256]{1,0:T(8,128)(2,1)S(1)}, bf16[272,256]{1,0:T(8,128)(2,1)S(1)}, u32[]{:S(2)}, u32[]{:S(2)}) %collective-permute-start.8) | collective-permute-done | bytes 139296 | tf_op jit(solution)/shard_map/ppermute | solution.py:563
  54.7 0.0 collective-permute-done.9.b
  54.7 0.8 %collective-permute-done.10.c = bf16[272,256]{1,0:T(8,128)(2,1)S(1)} collective-permute-done((bf16[272,256]{1,0:T(8,128)(2,1)S(1)}, bf16[272,256]{1,0:T(8,128)(2,1)S(1)}, u32[]{:S(2)}, u32[]{:S(2)}) %collective-permute-start.10) | collective-permute-done | bytes 139296 | tf_op jit(solution)/shard_map/ppermute | solution.py:563
  55.4 0.0 copy-done.2
  55.4 0.0 copy-done.3
  55.4 0.0 copy-done.4
  55.4 0.0 copy-done.11
  55.5 0.0 copy-done.12
  55.5 0.0 copy-done.13
  55.5 0.7 %layer_two.1 = f32[32,153]{1,0:T(8,128)S(1)} custom-call(f32[272,256]{1,0:T(8,128)S(1)} %get-tuple-element.83.mine, bf16[272,256]{1,0:T(8,128)(2,1)S(1)} %collective-permute-done.8.a, bf16[272,256]{1,0:T(8,128)(2,1)S(1)} %collective-permute-done.9.b, bf16[272,256]{1,0:T(8,128)(2,1)S(1)} %collective-permute-done.10.c, s32[1,32]{1,0:T(1,128)S(1)} %bitcast.68, ...), custom_call_target="tpu_custom_call" | custom-call | tf_op jit(solution)/shard_map/layer_two/pallas_call | solution.py:526
  56.2 0.1 conditional.1
  56.3 0.0 copy-start.9
  56.4 0.6 %copy-done.9 = f32[32,153]{1,0:T(8,128)} copy-done((f32[32,153]{1,0:T(8,128)}, f32[32,153]{1,0:T(8,128)S(1)}, u32[]{:S(2)}) %copy-start.9) | copy-done | bytes 19608
  (2 shorter events, 0.0 us)
Async XLA Ops:
  0.0 17.6 %collective-permute-start.5 = (bf16[96,32768]{1,0:T(8,128)(2,1)}, bf16[96,32768]{1,0:T(8,128)(2,1)}, u32[]{:S(2)}, u32[]{:S(2)}) collective-permute-start(bf16[96,32768]{1,0:T(8,128)(2,1)} %features.3), channel_id=1, source_target_pairs={{0,1},{1,0},{2,3},{3,2},{4,5},{5,4},{6,7},{7,6},{8,9},{9,8},{10,11... | collective-permute-start | bytes 18874376 | tf_op jit(solution)/shard_map/ppermute | solution.py:565
  0.5 5.7 %collective-permute-start = (s32[1,32]{1,0:T(1,128)}, s32[1,32]{1,0:T(1,128)S(1)}, u32[]{:S(2)}, u32[]{:S(2)}) collective-permute-start(s32[1,32]{1,0:T(1,128)} %bitcast.65), channel_id=1, source_target_pairs={{0,2},{2,0},{4,6},{6,4},{8,10},{10,8},{12,14},{14,12},{1,3},{3,1},... | collective-permute-start | bytes 392 | tf_op jit(solution)/shard_map/ppermute | solution.py:563
  3.0 3.1 %copy-start.5 = (bf16[96,256]{1,0:T(8,128)(2,1)S(1)}, bf16[96,256]{1,0:T(8,128)(2,1)}, u32[]{:S(2)}) copy-start(bf16[96,256]{1,0:T(8,128)(2,1)} %refs_0_.1) | copy-start | bytes 147460
  3.0 3.1 %copy-start.6 = (bf16[96,256]{1,0:T(8,128)(2,1)S(1)}, bf16[96,256]{1,0:T(8,128)(2,1)}, u32[]{:S(2)}) copy-start(bf16[96,256]{1,0:T(8,128)(2,1)} %refs_1_.1) | copy-start | bytes 147460
  3.0 3.6 %copy-start.10 = (s32[32]{0:T(128)S(1)}, s32[32]{0:T(128)}, u32[]{:S(2)}) copy-start(s32[32]{0:T(128)} %param.19) | copy-start | bytes 388
  6.2 8.7 %collective-permute-start.4 = (bf16[192,256]{1,0:T(8,128)(2,1)S(1)}, bf16[192,256]{1,0:T(8,128)(2,1)S(1)}, u32[]{:S(2)}, u32[]{:S(2)}) collective-permute-start(bf16[192,256]{1,0:T(8,128)(2,1)S(1)} %join.2.weights), channel_id=1, source_target_pairs={{0,2},{2,0},{4,6},{6,4},{8,10},{10,8},{12,14},{14,12},{1,3},{3,1},... | collective-permute-start | bytes 294920 | tf_op jit(solution)/shard_map/ppermute | solution.py:563
  6.6 8.2 %copy-start.1 = (s32[15,2816]{1,0:T(8,128)S(1)}, s32[15,2816]{1,0:T(8,128)}, u32[]{:S(2)}) copy-start(s32[15,2816]{1,0:T(8,128)} %neighbour_ids.1) | copy-start | bytes 506884
  6.6 8.2 %copy-start.7 = (s32[2816]{0:T(1024)S(1)}, s32[2816]{0:T(1024)}, u32[]{:S(2)}) copy-start(s32[2816]{0:T(1024)} %count_one.1) | copy-start | bytes 33796
  6.6 8.2 %copy-start.8 = (s32[2816]{0:T(1024)S(1)}, s32[2816]{0:T(1024)}, u32[]{:S(2)}) copy-start(s32[2816]{0:T(1024)} %self_ids.1) | copy-start | bytes 33796
  6.6 7.5 %collective-permute-start.1 = (s32[2,32]{1,0:T(2,128)S(1)}, s32[2,32]{1,0:T(2,128)S(1)}, u32[]{:S(2)}, u32[]{:S(2)}) collective-permute-start(s32[2,32]{1,0:T(2,128)S(1)} %join.3), channel_id=1, source_target_pairs={{0,8},{2,10},{4,12},{6,14},{8,0},{10,2},{12,4},{14,6},{1,9},{3,11}... | collective-permute-start | bytes 776 | tf_op jit(solution)/shard_map/ppermute | solution.py:563
  9.5 5.4 %collective-permute-start.2 = (s32[2,32]{1,0:T(2,128)S(1)}, s32[2,32]{1,0:T(2,128)S(1)}, u32[]{:S(2)}, u32[]{:S(2)}) collective-permute-start(s32[2,32]{1,0:T(2,128)S(1)} %join.3), channel_id=1, source_target_pairs={{0,12},{2,14},{4,8},{6,10},{8,4},{10,6},{12,0},{14,2},{1,13},{3,15... | collective-permute-start | bytes 776 | tf_op jit(solution)/shard_map/ppermute | solution.py:563
  10.8 4.0 %collective-permute-start.3 = (s32[2,32]{1,0:T(2,128)S(1)}, s32[2,32]{1,0:T(2,128)S(1)}, u32[]{:S(2)}, u32[]{:S(2)}) collective-permute-start(s32[2,32]{1,0:T(2,128)S(1)} %join.3), channel_id=1, source_target_pairs={{0,4},{2,6},{4,0},{6,2},{8,12},{10,14},{12,8},{14,10},{1,5},{3,7},... | collective-permute-start | bytes 776 | tf_op jit(solution)/shard_map/ppermute | solution.py:563
  29.9 11.7 %collective-permute-start.7 = (bf16[3,272,128]{2,1,0:T(8,128)(2,1)}, bf16[3,272,128]{2,1,0:T(8,128)(2,1)S(1)}, u32[]{:S(2)}, u32[]{:S(2)}) collective-permute-start(bf16[3,272,128]{2,1,0:T(8,128)(2,1)} %get-tuple-element.85), channel_id=1, source_target_pairs={{0,2},{2,0},{4,6},{6,4},{8,10},{10,8},{12,14},{14,12},{1,3},{3,1},... | collective-permute-start | bytes 626696 | tf_op jit(solution)/shard_map/ppermute | solution.py:563
  31.4 10.1 %copy-start = (bf16[3,272,128]{2,1,0:T(8,128)(2,1)S(1)}, bf16[3,272,128]{2,1,0:T(8,128)(2,1)}, u32[]{:S(2)}) copy-start(bf16[3,272,128]{2,1,0:T(8,128)(2,1)} %get-tuple-element.84.keep) | copy-start | bytes 626692
  31.5 24.0 %copy-start.2 = (bf16[256,256]{1,0:T(8,128)(2,1)S(1)}, bf16[256,256]{1,0:T(8,128)(2,1)}, u32[]{:S(2)}) copy-start(bf16[256,256]{1,0:T(8,128)(2,1)} %neigh_two.1) | copy-start | bytes 393220
  31.5 24.0 %copy-start.3 = (bf16[256,256]{1,0:T(8,128)(2,1)S(1)}, bf16[256,256]{1,0:T(8,128)(2,1)}, u32[]{:S(2)}) copy-start(bf16[256,256]{1,0:T(8,128)(2,1)} %self_two.1) | copy-start | bytes 393220
  31.5 24.0 %copy-start.4 = (bf16[256,153]{0,1:T(8,128)(2,1)S(1)}, bf16[256,153]{0,1:T(8,128)(2,1)}, u32[]{:S(2)}) copy-start(bf16[256,153]{0,1:T(8,128)(2,1)} %param.26) | copy-start | bytes 235012
  31.5 24.0 %copy-start.11 = (f32[256]{0:T(256)S(1)}, f32[256]{0:T(256)}, u32[]{:S(2)}) copy-start(f32[256]{0:T(256)} %param.25) | copy-start | bytes 3076
  31.5 24.0 %copy-start.12 = (f32[153]{0:T(256)S(1)}, f32[153]{0:T(256)}, u32[]{:S(2)}) copy-start(f32[153]{0:T(256)} %param.27) | copy-start | bytes 1840
  31.5 24.0 %copy-start.13 = (f32[256]{0:T(256)S(1)}, f32[256]{0:T(256)}, u32[]{:S(2)}) copy-start(f32[256]{0:T(256)} %param.22) | copy-start | bytes 3076
  41.0 6.1 %collective-permute-start.6 = (bf16[3,272,128]{2,1,0:T(8,128)(2,1)}, bf16[3,272,128]{2,1,0:T(8,128)(2,1)S(1)}, u32[]{:S(2)}, u32[]{:S(2)}) collective-permute-start(bf16[3,272,128]{2,1,0:T(8,128)(2,1)} %get-tuple-element.81), channel_id=1, source_target_pairs={{0,2},{2,0},{4,6},{6,4},{8,10},{10,8},{12,14},{14,12},{1,3},{3,1},... | collective-permute-start | bytes 626696 | tf_op jit(solution)/shard_map/ppermute | solution.py:563
  42.6 12.1 %collective-permute-start.8 = (bf16[272,256]{1,0:T(8,128)(2,1)S(1)}, bf16[272,256]{1,0:T(8,128)(2,1)S(1)}, u32[]{:S(2)}, u32[]{:S(2)}) collective-permute-start(bf16[272,256]{1,0:T(8,128)(2,1)S(1)} %get-tuple-element.86), channel_id=1, source_target_pairs={{0,8},{2,10},{4,12},{6,14},{8,0},{10,2},{12,4},{14,6},{1,9},{3,11}... | collective-permute-start | bytes 417800 | tf_op jit(solution)/shard_map/ppermute | solution.py:563
  44.8 9.8 %collective-permute-start.9 = (bf16[272,256]{1,0:T(8,128)(2,1)S(1)}, bf16[272,256]{1,0:T(8,128)(2,1)S(1)}, u32[]{:S(2)}, u32[]{:S(2)}) collective-permute-start(bf16[272,256]{1,0:T(8,128)(2,1)S(1)} %get-tuple-element.87), channel_id=1, source_target_pairs={{0,12},{2,14},{4,8},{6,10},{8,4},{10,6},{12,0},{14,2},{1,13},{3,15... | collective-permute-start | bytes 417800 | tf_op jit(solution)/shard_map/ppermute | solution.py:563
  48.9 6.6 %collective-permute-start.10 = (bf16[272,256]{1,0:T(8,128)(2,1)S(1)}, bf16[272,256]{1,0:T(8,128)(2,1)S(1)}, u32[]{:S(2)}, u32[]{:S(2)}) collective-permute-start(bf16[272,256]{1,0:T(8,128)(2,1)S(1)} %get-tuple-element.88), channel_id=1, source_target_pairs={{0,4},{2,6},{4,0},{6,2},{8,12},{10,14},{12,8},{14,10},{1,5},{3,7},... | collective-permute-start | bytes 417800 | tf_op jit(solution)/shard_map/ppermute | solution.py:563
  56.3 0.6 %copy-start.9 = (f32[32,153]{1,0:T(8,128)}, f32[32,153]{1,0:T(8,128)S(1)}, u32[]{:S(2)}) copy-start(f32[32,153]{1,0:T(8,128)S(1)} %get-tuple-element.171) | copy-start | bytes 58756
